TPU v7x, 128 devices: a whole 4x4x4 slice. The times are simulated.
128 devices in a mesh: ctx: 32 (over z, x, core), exp: 4 (over y).
Axes of the slice: x: 4, y: 4, z: 4, core: 2. Of those that a mesh axis runs over, the one named last changes fastest.
Arguments:
- hidden_in: bfloat16 [16384, 1024], P('ctx'), may hold values from -6 to 6
- teacher: bfloat16 [16384, 1024], P(('ctx', 'exp')), may hold values from -6 to 6
- valid: int32 [16384], replicated, may hold values from 0 to 1, as said below
- block_of: int32 [128], replicated, may hold values from 0 to 127, as said below
- routes: int32 [16384, 8], P(('ctx', 'exp')), may hold values from 0 to 31, all different within a row; in each aligned block of 128 rows (0 to 127, 128 to 255, ...) at most 40 rows name the same one
- gates: float32 [16384, 8], P(('ctx', 'exp')), may hold values from 0.5 to 2
- w_query: bfloat16 [1024, 1024], P('ctx', 'exp'), may hold values from -0.1875 to 0.1875
- w_key: bfloat16 [1024, 512], P('ctx', 'exp'), may hold values from -0.1875 to 0.1875
- w_value: bfloat16 [1024, 512], P('ctx', 'exp'), may hold values from -0.1875 to 0.1875
- w_out: bfloat16 [1024, 1024], P('ctx', 'exp'), may hold values from -4 to 4
- gain_attn: bfloat16 [1024], P('ctx'), may hold values from 0.5 to 1.5
- gain_query: bfloat16 [1024], P('ctx'), may hold values from 0.5 to 1.5
- gain_key: bfloat16 [512], P('ctx'), may hold values from 0.5 to 1.5
- gain_ffn: bfloat16 [1024], P('ctx'), may hold values from 0.5 to 1.5
- w_gate: bfloat16 [32, 1024, 512], P('ctx', None, 'exp'), may hold values from -0.1875 to 0.1875
- w_up: bfloat16 [32, 1024, 512], P('ctx', None, 'exp'), may hold values from -0.1875 to 0.1875
- w_down: bfloat16 [32, 512, 1024], P('ctx', 'exp'), may hold values from -0.25 to 0.25
Outputs:
- block_out: float32 [16384, 1024], P(('ctx', 'exp'))
- loss: float32 [], replicated
- grad_hidden: float32 [16384, 1024], P(('ctx', 'exp'))
- grad_w_query: float32 [1024, 1024], P('ctx', 'exp')
- grad_w_key: float32 [1024, 512], P('ctx', 'exp')
- grad_w_value: float32 [1024, 512], P('ctx', 'exp')
- grad_w_out: float32 [1024, 1024], P('ctx', 'exp')
- grad_gain_attn: float32 [1024], P('ctx')
- grad_gain_query: float32 [1024], P('ctx')
- grad_gain_key: float32 [512], P('ctx')
- grad_gain_ffn: float32 [1024], P('ctx')
- grad_w_gate: float32 [32, 1024, 512], P('ctx', None, 'exp')
- grad_w_up: float32 [32, 1024, 512], P('ctx', None, 'exp')
- grad_w_down: float32 [32, 512, 1024], P('ctx', 'exp')
Inputs may be any that keep to these rules, and one draw needn't show every extreme that they name: `valid`: the first of every 128 stored rows is 1. `block_of`: A permutation of the 128 logical blocks. Logical blocks below 64 hold the prompt in order; the others hold whole continuations of 1024 tokens in order. Each run of 4 stored blocks (one index of ctx) holds 2 prompt blocks followed by 2 continuation blocks. `routes`: each row names 8 different experts. In each aligned block of 128 rows (the rows of one device) no expert is named by more than 40 rows, and in some block an expert is named by exactly 40 rows.
All inputs are finite; a program needn't handle non-finite values.
Results may differ from a plain program's by a relative error of at most 0.014.
Values may be sent and summed in bfloat16 or wider, within the bound.
No kernel may reach another device: no remote copies, remote signals or barrier semaphores. Data moves between devices by JAX's collectives and lax.ppermute only.
A program may use at most 384 MiB of HBM per device.

v0:
```python
import jax
import jax.numpy as jnp
from jax import lax
from jax.sharding import PartitionSpec as P

HD = 64
BLK = 128
CONT_LEN = 1024


NORM_EPSILON = 1e-05
ROPE_BASE = 10000.0
MASK_FLOOR = -1e30


def places(block_table, first_row, row_count):
    block_total = block_table.shape[0]
    prompt_len = block_total * BLK // 2
    row_ids = first_row + jnp.arange(row_count, dtype=jnp.int32)
    matches = (row_ids // BLK)[:, None] == jnp.arange(block_total, dtype=jnp.int32)[None, :]
    logical = jnp.sum(jnp.where(matches, block_table[None, :], 0), axis=1)
    token_ids = logical * BLK + row_ids % BLK
    in_cont = token_ids >= prompt_len
    seq_ids = jnp.where(in_cont, 1 + (token_ids - prompt_len) // CONT_LEN, 0)
    position = jnp.where(in_cont, prompt_len + (token_ids - prompt_len) % CONT_LEN, token_ids)
    return (seq_ids, position.astype(jnp.float32))


def visibility(query_seq, query_pos, key_seq, key_pos):
    return (key_seq[None, :] == query_seq[:, None]) & (key_pos[None, :] <= query_pos[:, None]) | (
        query_seq[:, None] > 0
    ) & (key_seq[None, :] == 0)


def rope_tables(position):
    half_dim = HD // 2
    frequency = ROPE_BASE ** (-(jnp.arange(half_dim, dtype=jnp.float32) * 2.0 / HD))
    angles = position[:, None] * frequency[None, :]
    return (jnp.cos(angles)[:, None, :], jnp.sin(angles)[:, None, :])


def rotate(values, cosine, sine):
    shaped = values.reshape(values.shape[0], -1, HD)
    first_half = shaped[..., : HD // 2]
    second_half = shaped[..., HD // 2 :]
    turned = jnp.concatenate(
        [first_half * cosine - second_half * sine, second_half * cosine + first_half * sine],
        axis=-1,
    )
    return turned.reshape(values.shape)


def rotate_back(gradient, cosine, sine):
    shaped = gradient.reshape(gradient.shape[0], -1, HD)
    first_half = shaped[..., : HD // 2]
    second_half = shaped[..., HD // 2 :]
    turned = jnp.concatenate(
        [first_half * cosine + second_half * sine, second_half * cosine - first_half * sine],
        axis=-1,
    )
    return turned.reshape(gradient.shape)


def head_scores(queries_rot, key_rows, head, group, visible, scale):
    query_head = lax.dynamic_slice_in_dim(queries_rot, head * HD, HD, 1)
    key_head = lax.dynamic_slice_in_dim(key_rows, head // group * HD, HD, 1)
    raw_scores = (
        lax.dot_general(
            query_head, key_head, (((1,), (1,)), ((), ())), preferred_element_type=jnp.float32
        )
        * scale
    )
    return (jnp.where(visible, raw_scores, MASK_FLOOR), query_head, key_head)


def norm_back(grad_normed, hat_values, scale_values, gain_values):
    grad_hat = grad_normed * gain_values
    return scale_values * (
        grad_hat - hat_values * jnp.mean(grad_hat * hat_values, axis=-1, keepdims=True)
    )


def on_device(
    hidden_in,
    teacher,
    valid,
    block_of,
    routes,
    gates,
    w_query,
    w_key,
    w_value,
    w_out,
    gain_attn,
    gain_query,
    gain_key,
    gain_ffn,
    w_gate,
    w_up,
    w_down,
):
    ctx_count = lax.axis_size("ctx")
    exp_count = lax.axis_size("exp")
    dev_count = ctx_count * exp_count
    ctx_index = lax.axis_index("ctx")
    exp_index = lax.axis_index("exp")
    (
        full_query,
        full_key,
        full_value,
        full_out,
        attn_gain_low,
        query_gain_low,
        key_gain_low,
        ffn_gain_low,
    ) = (
        lax.all_gather(w_query, "ctx", axis=0, tiled=True),
        lax.all_gather(w_key, "ctx", axis=0, tiled=True),
        lax.all_gather(w_value, "ctx", axis=0, tiled=True),
        lax.all_gather(w_out, "ctx", axis=0, tiled=True),
        lax.all_gather(gain_attn, "ctx", axis=0, tiled=True),
        lax.all_gather(gain_query, "ctx", axis=0, tiled=True),
        lax.all_gather(gain_key, "ctx", axis=0, tiled=True),
        lax.all_gather(gain_ffn, "ctx", axis=0, tiled=True),
    )
    model_width = full_query.shape[0]
    head_cols = full_query.shape[1]
    kv_cols = full_key.shape[1]
    kv_total = kv_cols * exp_count
    local_heads = head_cols // HD
    local_kv = kv_cols // HD
    group = local_heads // local_kv
    ctx_rows = hidden_in.shape[0]
    own_rows = ctx_rows // exp_count
    token_total = block_of.shape[0] * BLK
    scale = HD ** (-0.5)
    attn_gain = attn_gain_low.astype(jnp.float32)
    ffn_gain = ffn_gain_low.astype(jnp.float32)
    query_gain = lax.dynamic_slice_in_dim(
        query_gain_low.astype(jnp.float32), exp_index * head_cols, head_cols
    )
    key_gain = lax.dynamic_slice_in_dim(
        key_gain_low.astype(jnp.float32), exp_index * kv_cols, kv_cols
    )
    hidden_f = hidden_in.astype(jnp.float32)
    attn_scale = lax.rsqrt(jnp.mean(hidden_f * hidden_f, axis=-1, keepdims=True) + NORM_EPSILON)
    attn_hat = hidden_f * attn_scale
    normed = (attn_hat * attn_gain).astype(jnp.bfloat16)
    query_pre = jnp.dot(normed, full_query, preferred_element_type=jnp.float32)
    key_pre = jnp.dot(normed, full_key, preferred_element_type=jnp.float32)
    value_low = jnp.dot(normed, full_value, preferred_element_type=jnp.float32).astype(jnp.bfloat16)
    query_square, key_square = lax.psum(
        (jnp.sum(query_pre * query_pre, axis=1), jnp.sum(key_pre * key_pre, axis=1)), "exp"
    )
    query_scale = lax.rsqrt(query_square / model_width + NORM_EPSILON)[:, None]
    key_scale = lax.rsqrt(key_square / kv_total + NORM_EPSILON)[:, None]
    query_hat = query_pre * query_scale
    key_hat = key_pre * key_scale
    own_seq, own_pos = places(block_of, ctx_index * ctx_rows, ctx_rows)
    all_seq, all_pos = places(block_of, 0, token_total)
    cosine, sine = rope_tables(own_pos)
    queries_rot = rotate(query_hat * query_gain, cosine, sine).astype(jnp.bfloat16)
    keys_rot = rotate(key_hat * key_gain, cosine, sine).astype(jnp.bfloat16)
    keys_all, values_all = (
        lax.all_gather(keys_rot, "ctx", axis=0, tiled=True),
        lax.all_gather(value_low, "ctx", axis=0, tiled=True),
    )
    visible = visibility(own_seq, own_pos, all_seq, all_pos)

    def forward_head(head, carry):
        head_out, log_norm = carry
        scores, query_head, key_head = head_scores(
            queries_rot, keys_all, head, group, visible, scale
        )
        value_head = lax.dynamic_slice_in_dim(values_all, head // group * HD, HD, 1)
        row_peak = jnp.max(scores, axis=1, keepdims=True)
        shifted_exp = jnp.exp(scores - row_peak)
        row_total = jnp.sum(shifted_exp, axis=1, keepdims=True)
        weights = (shifted_exp / row_total).astype(jnp.bfloat16)
        mixed_rows = jnp.dot(weights, value_head, preferred_element_type=jnp.float32)
        head_out = lax.dynamic_update_slice_in_dim(head_out, mixed_rows, head * HD, 1)
        log_norm = lax.dynamic_update_slice_in_dim(
            log_norm, (row_peak + jnp.log(row_total))[:, 0][None, :], head, 0
        )
        return (head_out, log_norm)

    head_out, log_norm = lax.fori_loop(
        0,
        local_heads,
        forward_head,
        (
            jnp.zeros((ctx_rows, head_cols), jnp.float32),
            jnp.zeros((local_heads, ctx_rows), jnp.float32),
        ),
    )
    heads_low = head_out.astype(jnp.bfloat16)
    branch_part = lax.dot_general(
        heads_low, full_out, (((1,), (1,)), ((), ())), preferred_element_type=jnp.float32
    )
    attn_rows = lax.psum_scatter(branch_part, "exp", scatter_dimension=0, tiled=True)
    hidden_rows = lax.dynamic_slice_in_dim(hidden_f, exp_index * own_rows, own_rows, 0)
    resid = hidden_rows + attn_rows
    ffn_scale = lax.rsqrt(jnp.mean(resid * resid, axis=-1, keepdims=True) + NORM_EPSILON)
    ffn_hat = resid * ffn_scale
    normed_ffn = (ffn_hat * ffn_gain).astype(jnp.bfloat16)
    top_count = routes.shape[1]
    local_experts = w_gate.shape[0]
    expert_total = ctx_count * local_experts
    capacity = max(2, own_rows * top_count * 5 // (expert_total * 4))
    route_flat = routes.reshape(-1)
    one_hot = (route_flat[:, None] == jnp.arange(expert_total, dtype=jnp.int32)[None, :]).astype(
        jnp.int32
    )
    slot_rank = jnp.sum(jnp.cumsum(one_hot, axis=0) * one_hot, axis=1) - 1
    slot_ids = route_flat * capacity + slot_rank
    copy_token = jnp.arange(route_flat.shape[0], dtype=jnp.int32) // top_count
    gate_flat = gates.reshape(-1)[:, None]

    def dispatch_rows(copies):
        placed = (
            jnp.zeros((expert_total * capacity, model_width), jnp.bfloat16).at[slot_ids].set(copies)
        )
        placed = placed.reshape(ctx_count, 1, local_experts * capacity, model_width)
        spread = jnp.broadcast_to(
            placed, (ctx_count, exp_count, local_experts * capacity, model_width)
        )
        return spread.reshape(dev_count, local_experts * capacity, model_width)

    def collect(arrived):
        shaped = arrived.reshape(ctx_count, exp_count, local_experts * capacity, model_width)
        summed = jnp.sum(shaped, axis=1, dtype=jnp.float32)
        return summed.reshape(expert_total * capacity, model_width)

    received = lax.all_to_all(
        dispatch_rows(normed_ffn[copy_token]),
        ("ctx", "exp"),
        split_axis=0,
        concat_axis=0,
        tiled=True,
    )
    expert_in = received.reshape(dev_count, local_experts, capacity, model_width)
    gate_pre = jnp.einsum("sjmd,jdf->sjmf", expert_in, w_gate, preferred_element_type=jnp.float32)
    up_pre = jnp.einsum("sjmd,jdf->sjmf", expert_in, w_up, preferred_element_type=jnp.float32)
    gate_sig = jax.nn.sigmoid(gate_pre)
    gate_act = gate_pre * gate_sig
    hidden_act = (gate_act * up_pre).astype(jnp.bfloat16)
    partial_out = jnp.einsum(
        "sjmf,jfd->sjmd", hidden_act, w_down, preferred_element_type=jnp.float32
    ).astype(jnp.bfloat16)
    returned = lax.all_to_all(
        partial_out.reshape(dev_count, local_experts * capacity, model_width),
        ("ctx", "exp"),
        split_axis=0,
        concat_axis=0,
        tiled=True,
    )
    copy_out = collect(returned)[slot_ids]
    moe_rows = jnp.sum((gate_flat * copy_out).reshape(own_rows, top_count, model_width), axis=1)
    block_out = resid + moe_rows
    row_start = (ctx_index * exp_count + exp_index) * own_rows
    row_valid = lax.dynamic_slice_in_dim(valid, row_start, own_rows, 0).astype(jnp.float32)
    valid_count = jnp.sum(valid.astype(jnp.float32))
    misfit = block_out - teacher.astype(jnp.float32)
    local_loss = jnp.sum(row_valid[:, None] * misfit * misfit)
    out_grad_rows = misfit * row_valid[:, None] * (token_total / valid_count)
    copy_grad = (gate_flat * out_grad_rows[copy_token]).astype(jnp.bfloat16)
    grad_in = lax.all_to_all(
        dispatch_rows(copy_grad), ("ctx", "exp"), split_axis=0, concat_axis=0, tiled=True
    )
    grad_copies = grad_in.reshape(dev_count, local_experts, capacity, model_width)
    grad_w_down = jnp.einsum(
        "sjmf,sjmd->jfd", hidden_act, grad_copies, preferred_element_type=jnp.float32
    )
    act_grad = jnp.einsum("sjmd,jfd->sjmf", grad_copies, w_down, preferred_element_type=jnp.float32)
    gate_grad = (act_grad * up_pre * gate_sig * (1.0 + gate_pre * (1.0 - gate_sig))).astype(
        jnp.bfloat16
    )
    up_grad = (act_grad * gate_act).astype(jnp.bfloat16)
    grad_w_gate = jnp.einsum(
        "sjmd,sjmf->jdf", expert_in, gate_grad, preferred_element_type=jnp.float32
    )
    grad_w_up = jnp.einsum("sjmd,sjmf->jdf", expert_in, up_grad, preferred_element_type=jnp.float32)
    input_part = jnp.einsum(
        "sjmf,jdf->sjmd", gate_grad, w_gate, preferred_element_type=jnp.float32
    ) + jnp.einsum("sjmf,jdf->sjmd", up_grad, w_up, preferred_element_type=jnp.float32)
    arrived_grad = lax.all_to_all(
        input_part.astype(jnp.bfloat16).reshape(dev_count, local_experts * capacity, model_width),
        ("ctx", "exp"),
        split_axis=0,
        concat_axis=0,
        tiled=True,
    )
    ffn_normed_grad = jnp.sum(
        collect(arrived_grad)[slot_ids].reshape(own_rows, top_count, model_width), axis=1
    )
    ffn_gain_part = jnp.sum(ffn_normed_grad * ffn_hat, axis=0)
    resid_grad = out_grad_rows + norm_back(ffn_normed_grad, ffn_hat, ffn_scale, ffn_gain)
    branch_grad = lax.all_gather(resid_grad.astype(jnp.bfloat16), "exp", axis=0, tiled=True)
    grad_out = lax.dot_general(
        branch_grad, heads_low, (((0,), (0,)), ((), ())), preferred_element_type=jnp.float32
    )
    out_grad = jnp.dot(branch_grad, full_out, preferred_element_type=jnp.float32).astype(
        jnp.bfloat16
    )
    contract_rows = (((0,), (0,)), ((), ()))
    contract_cols = (((1,), (1,)), ((), ()))

    def head_probs(head, key_rows, value_rows, mask_rows):
        scores, query_head, key_head = head_scores(
            queries_rot, key_rows, head, group, mask_rows, scale
        )
        value_head = lax.dynamic_slice_in_dim(value_rows, head // group * HD, HD, 1)
        out_grad_head = lax.dynamic_slice_in_dim(out_grad, head * HD, HD, 1)
        log_row = lax.dynamic_slice_in_dim(log_norm, head, 1, 0)[0][:, None]
        probs = jnp.exp(scores - log_row)
        prob_grad = lax.dot_general(
            out_grad_head, value_head, contract_cols, preferred_element_type=jnp.float32
        )
        return (probs, prob_grad, query_head, key_head, out_grad_head)

    def backward_head(head, carry):
        query_grad, pair_grad = carry
        probs, prob_grad, query_head, key_head, out_grad_head = head_probs(
            head, keys_all, values_all, visible
        )
        delta_row = jnp.sum(probs * prob_grad, axis=1, keepdims=True)
        score_grad = (probs * (prob_grad - delta_row)).astype(jnp.bfloat16)
        query_part = jnp.dot(score_grad, key_head, preferred_element_type=jnp.float32) * scale
        key_part = (
            lax.dot_general(
                score_grad, query_head, contract_rows, preferred_element_type=jnp.float32
            )
            * scale
        )
        value_part = lax.dot_general(
            probs.astype(jnp.bfloat16),
            out_grad_head,
            contract_rows,
            preferred_element_type=jnp.float32,
        )
        query_grad = lax.dynamic_update_slice_in_dim(query_grad, query_part, head * HD, 1)
        kv_col = head // group * HD
        key_old = lax.dynamic_slice_in_dim(pair_grad, kv_col, HD, 1)
        pair_grad = lax.dynamic_update_slice_in_dim(pair_grad, key_old + key_part, kv_col, 1)
        value_old = lax.dynamic_slice_in_dim(pair_grad, kv_cols + kv_col, HD, 1)
        pair_grad = lax.dynamic_update_slice_in_dim(
            pair_grad, value_old + value_part, kv_cols + kv_col, 1
        )
        return (query_grad, pair_grad)

    query_grad, pair_grad = lax.fori_loop(
        0,
        local_heads,
        backward_head,
        (
            jnp.zeros((ctx_rows, head_cols), jnp.float32),
            jnp.zeros((token_total, 2 * kv_cols), jnp.float32),
        ),
    )
    own_pair_grad = lax.psum_scatter(pair_grad, "ctx", scatter_dimension=0, tiled=True)
    key_rot_grad = own_pair_grad[:, :kv_cols]
    value_grad = own_pair_grad[:, kv_cols:].astype(jnp.bfloat16)
    query_n_grad = rotate_back(query_grad, cosine, sine)
    key_n_grad = rotate_back(key_rot_grad, cosine, sine)
    query_gain_part = jnp.sum(query_n_grad * query_hat, axis=0)
    key_gain_part = jnp.sum(key_n_grad * key_hat, axis=0)
    query_hat_grad = query_n_grad * query_gain
    key_hat_grad = key_n_grad * key_gain
    query_stat, key_stat = lax.psum(
        (jnp.sum(query_hat_grad * query_hat, axis=1), jnp.sum(key_hat_grad * key_hat, axis=1)),
        "exp",
    )
    query_low = (
        query_scale * (query_hat_grad - query_hat * (query_stat / model_width)[:, None])
    ).astype(jnp.bfloat16)
    key_low = (key_scale * (key_hat_grad - key_hat * (key_stat / kv_total)[:, None])).astype(
        jnp.bfloat16
    )
    grad_query = lax.dot_general(
        normed, query_low, contract_rows, preferred_element_type=jnp.float32
    )
    grad_key = lax.dot_general(normed, key_low, contract_rows, preferred_element_type=jnp.float32)
    grad_value = lax.dot_general(
        normed, value_grad, contract_rows, preferred_element_type=jnp.float32
    )
    normed_part = lax.dot_general(
        query_low, full_query, contract_cols, preferred_element_type=jnp.float32
    )
    normed_part = normed_part + lax.dot_general(
        key_low, full_key, contract_cols, preferred_element_type=jnp.float32
    )
    normed_part = normed_part + lax.dot_general(
        value_grad, full_value, contract_cols, preferred_element_type=jnp.float32
    )
    attn_gain_part = jnp.sum(normed_part * attn_hat, axis=0)
    query_gain_full = lax.dynamic_update_slice_in_dim(
        jnp.zeros((model_width,), jnp.float32), query_gain_part, exp_index * head_cols, 0
    )
    key_gain_full = lax.dynamic_update_slice_in_dim(
        jnp.zeros((kv_total,), jnp.float32), key_gain_part, exp_index * kv_cols, 0
    )
    gain_rows = jnp.stack([attn_gain_part, query_gain_full, ffn_gain_part], axis=0)
    normed_rows, gain_sum, key_gain_sum, loss_part = (
        lax.psum_scatter(normed_part, "exp", scatter_dimension=0, tiled=True),
        lax.psum_scatter(
            jnp.broadcast_to(gain_rows[None], (exp_count, 3, model_width)),
            "exp",
            scatter_dimension=0,
            tiled=True,
        ),
        lax.psum_scatter(
            jnp.broadcast_to(key_gain_full[None], (exp_count, kv_total)),
            "exp",
            scatter_dimension=0,
            tiled=True,
        ),
        lax.psum_scatter(
            jnp.full((exp_count,), local_loss), "exp", scatter_dimension=0, tiled=True
        ),
    )
    own_hat = lax.dynamic_slice_in_dim(attn_hat, exp_index * own_rows, own_rows, 0)
    own_scale = lax.dynamic_slice_in_dim(attn_scale, exp_index * own_rows, own_rows, 0)
    grad_hidden = resid_grad + norm_back(normed_rows, own_hat, own_scale, attn_gain)
    shards = (
        lax.psum_scatter(grad_query, "ctx", scatter_dimension=0, tiled=True),
        lax.psum_scatter(grad_key, "ctx", scatter_dimension=0, tiled=True),
        lax.psum_scatter(grad_value, "ctx", scatter_dimension=0, tiled=True),
        lax.psum_scatter(grad_out, "ctx", scatter_dimension=0, tiled=True),
        lax.psum_scatter(gain_sum[0, 0], "ctx", scatter_dimension=0, tiled=True),
        lax.psum_scatter(gain_sum[0, 1], "ctx", scatter_dimension=0, tiled=True),
        lax.psum_scatter(key_gain_sum[0], "ctx", scatter_dimension=0, tiled=True),
        lax.psum_scatter(gain_sum[0, 2], "ctx", scatter_dimension=0, tiled=True),
        lax.psum_scatter(
            jnp.full((ctx_count,), loss_part[0]), "ctx", scatter_dimension=0, tiled=True
        ),
    )
    loss = shards[8][0] / (valid_count * model_width)
    return (
        block_out,
        loss,
        grad_hidden,
        shards[0],
        shards[1],
        shards[2],
        shards[3],
        shards[4],
        shards[5],
        shards[6],
        shards[7],
        grad_w_gate,
        grad_w_up,
        grad_w_down,
    )


def solution(mesh):
    return jax.shard_map(
        on_device,
        mesh=mesh,
        in_specs=(
            P("ctx", None),
            P(("ctx", "exp"), None),
            P(),
            P(),
            P(("ctx", "exp"), None),
            P(("ctx", "exp"), None),
            P("ctx", "exp"),
            P("ctx", "exp"),
            P("ctx", "exp"),
            P("ctx", "exp"),
            P("ctx"),
            P("ctx"),
            P("ctx"),
            P("ctx"),
            P("ctx", None, "exp"),
            P("ctx", None, "exp"),
            P("ctx", "exp", None),
        ),
        out_specs=(
            P(("ctx", "exp"), None),
            P(),
            P(("ctx", "exp"), None),
            P("ctx", "exp"),
            P("ctx", "exp"),
            P("ctx", "exp"),
            P("ctx", "exp"),
            P("ctx"),
            P("ctx"),
            P("ctx"),
            P("ctx"),
            P("ctx", None, "exp"),
            P("ctx", None, "exp"),
            P("ctx", "exp", None),
        ),
        check_vma=False,
    )
```

profile of v0, /device:TPU:0, one launch (start us, length us, event | category | flops | bytes accessed | tf_op | source)
XLA Modules:
  0.0 2147.4 jit_solution(1769108885371592016)
XLA Ops:
  15.9 70.0 %all-reduce.16 = (bf16[1024]{0:T(1024)(128)(2,1)S(1)}, bf16[1024]{0:T(1024)(128)(2,1)S(1)}, bf16[512]{0:T(512)(128)(2,1)S(1)}, bf16[1024]{0:T(1024)(128)(2,1)}) all-reduce(bf16[1024]{0:T(1024)(128)(2,1)S(1)} %dynamic-update-slice, bf16[1024]{0:T(1024)(128)(2,1)S(1)} %dynamic-update-slice.1, ...), channel_id=1, replica_groups=mesh['ctx'=32,'exp'=4] {'ctx'}, use_global_device_ids=true, to_apply=%add | all-reduce | flops 3584 | bytes 14336
  85.9 22.4 %all_gather.36 = bf16[1024,128]{1,0:T(8,128)(2,1)S(1)} all-gather(bf16[32,128]{1,0:T(8,128)(2,1)} %param.28), channel_id=1, replica_groups=mesh['ctx'=32,'exp'=4] {'ctx'}, dimensions={0}, use_global_device_ids=true | all-gather | bytes 270336 | tf_op jit(solution)/shard_map/all_gather | solution.py:118
  108.3 24.2 %all_gather.34 = bf16[1024,256]{1,0:T(8,128)(2,1)S(1)} all-gather(bf16[32,256]{1,0:T(8,128)(2,1)} %param.27), channel_id=1, replica_groups=mesh['ctx'=32,'exp'=4] {'ctx'}, dimensions={0}, use_global_device_ids=true | all-gather | bytes 540672 | tf_op jit(solution)/shard_map/all_gather | solution.py:117
  148.9 22.5 %all_gather.39 = bf16[1024,128]{1,0:T(8,128)(2,1)S(1)} all-gather(bf16[32,128]{1,0:T(8,128)(2,1)S(1)} %copy-done.61), channel_id=1, replica_groups=mesh['ctx'=32,'exp'=4] {'ctx'}, dimensions={0}, use_global_device_ids=true | all-gather | bytes 270336 | tf_op jit(solution)/shard_map/all_gather | solution.py:119
  175.0 26.5 %all_gather.41 = bf16[1024,256]{1,0:T(8,128)(2,1)} all-gather(bf16[32,256]{1,0:T(8,128)(2,1)S(1)} %copy-done.55), channel_id=1, replica_groups=mesh['ctx'=32,'exp'=4] {'ctx'}, dimensions={0}, use_global_device_ids=true | all-gather | bytes 540672 | tf_op jit(solution)/shard_map/all_gather | solution.py:120
  214.4 29.8 %all-gather.6.cloned.1.call-done = bf16[16384,128]{1,0:T(8,128)(2,1)} async-done(((bf16[512,128]{1,0:T(8,128)(2,1)}), bf16[16384,128]{1,0:T(8,128)(2,1)}) %all-gather.6.cloned.1.call-update) | async-done | bytes 4194320 | tf_op jit(solution)/shard_map/all_gather | solution.py:166
  244.1 210.3 %while.36 = (s32[]{:T(128)}, bf16[512,256]{0,1:T(8,128)(2,1)S(1)}, f32[4,512]{1,0:T(4,128)}, bf16[512,256]{1,0:T(8,128)(2,1)}, bf16[16384,128]{1,0:T(8,128)(2,1)...) while((s32[]{:T(128)}, bf16[512,256]{0,1:T(8,128)(2,1)S(1)}, ...), condition=%wide.region_10.11_spmd.clone, body=%wide.region_7.10_spmd.clone.sunk | while | flops 2256535040 | bytes 109486952 | solution.py:187
  244.3 22.1 %fusion.161 = (f32[512]{0:T(512)S(1)}, f32[512,16384]{1,0:T(8,128)}) fusion(bf16[16384,128]{1,0:T(8,128)(2,1)} %get-tuple-element.884, s32[]{:T(128)S(6)} %select_n.413, bf16[512,256]{1,0:T(8,128)(2,1)} %get-tuple-element.883, s32[]{:T(128)S(6)} %select_n.411, pred[16384]{0:T(1024)(128)(4,1)} %get-tuple-element.890, ...), kind=kOutput, calls=%fused_computation.245.clone.1 | convolution fusion | flops 1140850176 | bytes 38033928 | tf_op jit(solution)/shard_map/while/body/eval_jaxpr/dot_general | solution.py:68
  296.8 22.1 %fusion.161 = (f32[512]{0:T(512)S(1)}, f32[512,16384]{1,0:T(8,128)}) fusion(bf16[16384,128]{1,0:T(8,128)(2,1)} %get-tuple-element.884, s32[]{:T(128)S(6)} %select_n.413, bf16[512,256]{1,0:T(8,128)(2,1)} %get-tuple-element.883, s32[]{:T(128)S(6)} %select_n.411, pred[16384]{0:T(1024)(128)(4,1)} %get-tuple-element.890, ...), kind=kOutput, calls=%fused_computation.245.clone.1 | convolution fusion | flops 1140850176 | bytes 38033928 | tf_op jit(solution)/shard_map/while/body/eval_jaxpr/dot_general | solution.py:68
  349.2 22.1 %fusion.161 = (f32[512]{0:T(512)S(1)}, f32[512,16384]{1,0:T(8,128)}) fusion(bf16[16384,128]{1,0:T(8,128)(2,1)} %get-tuple-element.884, s32[]{:T(128)S(6)} %select_n.413, bf16[512,256]{1,0:T(8,128)(2,1)} %get-tuple-element.883, s32[]{:T(128)S(6)} %select_n.411, pred[16384]{0:T(1024)(128)(4,1)} %get-tuple-element.890, ...), kind=kOutput, calls=%fused_computation.245.clone.1 | convolution fusion | flops 1140850176 | bytes 38033928 | tf_op jit(solution)/shard_map/while/body/eval_jaxpr/dot_general | solution.py:68
  401.6 22.1 %fusion.161 = (f32[512]{0:T(512)S(1)}, f32[512,16384]{1,0:T(8,128)}) fusion(bf16[16384,128]{1,0:T(8,128)(2,1)} %get-tuple-element.884, s32[]{:T(128)S(6)} %select_n.413, bf16[512,256]{1,0:T(8,128)(2,1)} %get-tuple-element.883, s32[]{:T(128)S(6)} %select_n.411, pred[16384]{0:T(1024)(128)(4,1)} %get-tuple-element.890, ...), kind=kOutput, calls=%fused_computation.245.clone.1 | convolution fusion | flops 1140850176 | bytes 38033928 | tf_op jit(solution)/shard_map/while/body/eval_jaxpr/dot_general | solution.py:68
  468.1 17.5 reduce-scatter.8.cloned.1.call-done
  508.9 128.3 %all_to_all.20 = bf16[128,40,1024]{2,1,0:T(8,128)(2,1)S(1)} all-to-all(bf16[128,40,1024]{2,1,0:T(8,128)(2,1)} %bitcast.208), channel_id=1, replica_groups=mesh['ctx'=32,'exp'=4] {'ctx','exp'}, dimensions={0} | all-to-all | bytes 20971520 | tf_op jit(solution)/shard_map/all_to_all | solution.py:234
  675.0 122.9 %all-to-all-done.1 = bf16[128,40,1024]{2,1,0:T(8,128)(2,1)} async-done(((bf16[128,40,1024]{2,1,0:T(8,128)(2,1)}), bf16[128,40,1024]{2,1,0:T(8,128)(2,1)}, u32[]{:S(2)}, u32[]{:S(2)}) %all-to-all-start.1) | async-done | bytes 10485792 | tf_op jit(solution)/shard_map/all_to_all | solution.py:250
  844.5 129.3 %all_to_all.21 = bf16[128,40,1024]{2,1,0:T(8,128)(2,1)S(1)} all-to-all(bf16[128,40,1024]{2,1,0:T(8,128)(2,1)} %bitcast.209), channel_id=1, replica_groups=mesh['ctx'=32,'exp'=4] {'ctx','exp'}, dimensions={0} | all-to-all | bytes 20971520 | tf_op jit(solution)/shard_map/all_to_all | solution.py:267
  1013.1 125.7 %all_to_all.22 = bf16[128,40,1024]{2,1,0:T(8,128)(2,1)} all-to-all(bf16[128,40,1024]{2,1,0:T(8,128)(2,1)} %copy.92), channel_id=1, replica_groups=mesh['ctx'=32,'exp'=4] {'ctx','exp'}, dimensions={0} | all-to-all | bytes 20971520 | tf_op jit(solution)/shard_map/all_to_all | solution.py:286
  1163.3 20.3 all-gather.8.cloned.1.call-done
  1193.2 460.6 %while.37 = (s32[]{:T(128)}, f32[512,256]{0,1:T(8,128)S(1)}, f32[16384,256]{0,1:T(8,128)}, bf16[512,256]{1,0:T(8,128)(2,1)}, bf16[16384,128]{1,0:T(8,128)(2,1)},...) while((s32[]{:T(128)}, f32[512,256]{0,1:T(8,128)S(1)}, ...), condition=%wide.region_29.30_spmd.clone, body=%wide.region_27.29_spmd.clone.sunk | while | flops 5489327616 | bytes 298613760 | solution.py:351
  1209.9 28.6 %multiply_reduce_fusion.12 = (f32[512]{0:T(512)S(1)}, f32[512,16384]{1,0:T(8,128)}) fusion(f32[512,16384]{1,0:T(8,128)} %fusion.172, f32[512]{0:T(512)S(1)} %bitcast.220, bf16[16384,128]{1,0:T(8,128)(2,1)S(1)} %copy-done.3, s32[]{:T(128)S(6)} %select_n.416, bf16[512,256]{1,0:T(8,128)(2,1)} %get-tuple-element.943, s32[]{:T(128)S(6)} %select_n.414, ...), kind=kOutput, calls=%fused_computation.21.clone.1 | convolution fusion | flops 1157627392 | bytes 71590408 | tf_op jit(solution)/shard_map/while/body/eval_jaxpr/dot_general | solution.py:68
  1238.5 27.4 %multiply_convert_fusion.14 = bf16[512,16384]{1,0:T(8,128)(2,1)} fusion(f32[512,16384]{1,0:T(8,128)} %get-tuple-element.842, f32[512,16384]{1,0:T(8,128)} %fusion.172, f32[512]{0:T(512)S(1)} %get-tuple-element.843), kind=kLoop, calls=%fused_computation.20.clone.1 | loop fusion | flops 25165824 | bytes 83888128 | tf_op jit(solution)/shard_map/while/body/eval_jaxpr/convert_element_type | solution.py:327
  1291.8 16.9 fusion.175
  1324.9 28.6 %multiply_reduce_fusion.12 = (f32[512]{0:T(512)S(1)}, f32[512,16384]{1,0:T(8,128)}) fusion(f32[512,16384]{1,0:T(8,128)} %fusion.172, f32[512]{0:T(512)S(1)} %bitcast.220, bf16[16384,128]{1,0:T(8,128)(2,1)S(1)} %copy-done.3, s32[]{:T(128)S(6)} %select_n.416, bf16[512,256]{1,0:T(8,128)(2,1)} %get-tuple-element.943, s32[]{:T(128)S(6)} %select_n.414, ...), kind=kOutput, calls=%fused_computation.21.clone.1 | convolution fusion | flops 1157627392 | bytes 71590408 | tf_op jit(solution)/shard_map/while/body/eval_jaxpr/dot_general | solution.py:68
  1353.5 27.4 %multiply_convert_fusion.14 = bf16[512,16384]{1,0:T(8,128)(2,1)} fusion(f32[512,16384]{1,0:T(8,128)} %get-tuple-element.842, f32[512,16384]{1,0:T(8,128)} %fusion.172, f32[512]{0:T(512)S(1)} %get-tuple-element.843), kind=kLoop, calls=%fused_computation.20.clone.1 | loop fusion | flops 25165824 | bytes 83888128 | tf_op jit(solution)/shard_map/while/body/eval_jaxpr/convert_element_type | solution.py:327
  1406.8 16.9 fusion.175
  1439.9 28.6 %multiply_reduce_fusion.12 = (f32[512]{0:T(512)S(1)}, f32[512,16384]{1,0:T(8,128)}) fusion(f32[512,16384]{1,0:T(8,128)} %fusion.172, f32[512]{0:T(512)S(1)} %bitcast.220, bf16[16384,128]{1,0:T(8,128)(2,1)S(1)} %copy-done.3, s32[]{:T(128)S(6)} %select_n.416, bf16[512,256]{1,0:T(8,128)(2,1)} %get-tuple-element.943, s32[]{:T(128)S(6)} %select_n.414, ...), kind=kOutput, calls=%fused_computation.21.clone.1 | convolution fusion | flops 1157627392 | bytes 71590408 | tf_op jit(solution)/shard_map/while/body/eval_jaxpr/dot_general | solution.py:68
  1468.5 27.4 %multiply_convert_fusion.14 = bf16[512,16384]{1,0:T(8,128)(2,1)} fusion(f32[512,16384]{1,0:T(8,128)} %get-tuple-element.842, f32[512,16384]{1,0:T(8,128)} %fusion.172, f32[512]{0:T(512)S(1)} %get-tuple-element.843), kind=kLoop, calls=%fused_computation.20.clone.1 | loop fusion | flops 25165824 | bytes 83888128 | tf_op jit(solution)/shard_map/while/body/eval_jaxpr/convert_element_type | solution.py:327
  1554.9 28.6 %multiply_reduce_fusion.12 = (f32[512]{0:T(512)S(1)}, f32[512,16384]{1,0:T(8,128)}) fusion(f32[512,16384]{1,0:T(8,128)} %fusion.172, f32[512]{0:T(512)S(1)} %bitcast.220, bf16[16384,128]{1,0:T(8,128)(2,1)S(1)} %copy-done.3, s32[]{:T(128)S(6)} %select_n.416, bf16[512,256]{1,0:T(8,128)(2,1)} %get-tuple-element.943, s32[]{:T(128)S(6)} %select_n.414, ...), kind=kOutput, calls=%fused_computation.21.clone.1 | convolution fusion | flops 1157627392 | bytes 71590408 | tf_op jit(solution)/shard_map/while/body/eval_jaxpr/dot_general | solution.py:68
  1583.5 27.4 %multiply_convert_fusion.14 = bf16[512,16384]{1,0:T(8,128)(2,1)} fusion(f32[512,16384]{1,0:T(8,128)} %get-tuple-element.842, f32[512,16384]{1,0:T(8,128)} %fusion.172, f32[512]{0:T(512)S(1)} %get-tuple-element.843), kind=kLoop, calls=%fused_computation.20.clone.1 | loop fusion | flops 25165824 | bytes 83888128 | tf_op jit(solution)/shard_map/while/body/eval_jaxpr/convert_element_type | solution.py:327
  1655.7 113.9 %reduce-scatter.10.cloned.1.call-done = f32[512,256]{0,1:T(8,128)} async-done(((f32[16384,256]{0,1:T(8,128)}), f32[512,256]{0,1:T(8,128)}) %reduce-scatter.10.cloned.1.call-update) | async-done | bytes 524304 | tf_op jit(solution)/shard_map/reduce_scatter | solution.py:360
  1837.4 123.9 %all-reduce.12 = (f32[32]{0:T(128)S(1)}, f32[1024]{0:T(1024)S(1)}, f32[1024]{0:T(1024)S(1)}, f32[512]{0:T(512)S(1)}, f32[1024]{0:T(1024)S(1)}) all-reduce(f32[32]{0:T(128)S(1)} %broadcast_in_dim.151, f32[1024]{0:T(1024)S(1)} %bitcast.230, f32[1024]{0:T(1024)S(1)} %bitcast.229, ...), channel_id=4, replica_groups=mesh['ctx'=32,'exp'=4] {'ctx'}, use_global_device_ids=true, to_apply=%region_21.22.clone | all-reduce | flops 3616 | bytes 28928
  1977.2 80.8 %reduce-scatter.18.cloned.1.call-done = f32[32,128]{1,0:T(8,128)} async-done(((f32[1024,128]{1,0:T(8,128)}), f32[32,128]{1,0:T(8,128)}) %reduce-scatter.18.cloned.1.call-update) | async-done | bytes 16400 | tf_op jit(solution)/shard_map/reduce_scatter | solution.py:427
  2057.9 81.3 %reduce-scatter.14.cloned.1.call-done = f32[32,256]{1,0:T(8,128)} async-done(((f32[1024,256]{1,0:T(8,128)}), f32[32,256]{1,0:T(8,128)}) %reduce-scatter.14.cloned.1.call-update) | async-done | bytes 32784 | tf_op jit(solution)/shard_map/reduce_scatter | solution.py:425
  (364 shorter events, 639.4 us)
Async XLA Ops:
  7.2 640.3 %copy-start = (bf16[1,128,1024]{2,1,0:T(8,128)(2,1)S(1)}, bf16[1,128,1024]{2,1,0:T(8,128)(2,1)}, u32[]{:S(2)}) copy-start(bf16[1,128,1024]{2,1,0:T(8,128)(2,1)} %param.37) | copy-start | bytes 786436
  7.2 200.8 %all-gather.4.cloned.1.call-start = ((), (), s32[]{:S(2)}) async-start(), calls=%async_computation.11 | async-start | bytes 4325376 | tf_op jit(solution)/shard_map/all_gather | solution.py:165
  9.9 139.0 %copy-start.61 = (bf16[32,128]{1,0:T(8,128)(2,1)S(1)}, bf16[32,128]{1,0:T(8,128)(2,1)}, u32[]{:S(2)}) copy-start(bf16[32,128]{1,0:T(8,128)(2,1)} %param.29) | copy-start | bytes 24580
  9.9 162.1 %copy-start.9 = (bf16[512,1024]{1,0:T(8,128)(2,1)S(1)}, bf16[512,1024]{1,0:T(8,128)(2,1)}, u32[]{:S(2)}) copy-start(bf16[512,1024]{1,0:T(8,128)(2,1)} %param.21) | copy-start | bytes 3145732
  11.5 161.7 %copy-start.62 = (f32[512]{0:T(512)}, f32[512]{0:T(512)S(1)}, u32[]{:S(2)}) copy-start(f32[512]{0:T(512)S(1)} %add_rsqrt_fusion.2) | copy-start | bytes 6148
  85.9 87.3 %copy-start.48 = (f32[1024]{0:T(1024)}, f32[1024]{0:T(1024)S(1)}, u32[]{:S(2)}) copy-start(f32[1024]{0:T(1024)S(1)} %convert_element_type.143) | copy-start | bytes 12292
  134.6 39.5 %copy-start.15 = (f32[512,128]{0,1:T(8,128)}, f32[512,128]{0,1:T(8,128)S(1)}, u32[]{:S(2)}) copy-start(f32[512,128]{0,1:T(8,128)S(1)} %get-tuple-element.675) | copy-start | bytes 786436
  136.5 70.0 %copy-start.12 = (f32[512,256]{0,1:T(8,128)}, f32[512,256]{0,1:T(8,128)S(1)}, u32[]{:S(2)}) copy-start(f32[512,256]{0,1:T(8,128)S(1)} %get-tuple-element.673) | copy-start | bytes 1572868
  136.5 64.9 %copy-start.70 = (s32[128]{0:T(128)S(1)}, s32[128]{0:T(128)}, u32[]{:S(2)}) copy-start(s32[128]{0:T(128)} %param.24) | copy-start | bytes 1540
  147.4 59.1 %copy-start.50 = (f32[512]{0:T(512)}, f32[512]{0:T(512)S(1)}, u32[]{:S(2)}) copy-start(f32[512]{0:T(512)S(1)} %add_rsqrt_fusion) | copy-start | bytes 6148
  147.8 59.4 %copy-start.25 = (f32[512,32]{0,1:T(8,128)}, f32[512,32]{0,1:T(8,128)S(1)}, u32[]{:S(2)}) copy-start(f32[512,32]{0,1:T(8,128)S(1)} %get-tuple-element.668) | copy-start | bytes 196612
  147.9 59.4 %copy-start.27 = (f32[512,32]{0,1:T(8,128)}, f32[512,32]{0,1:T(8,128)S(1)}, u32[]{:S(2)}) copy-start(f32[512,32]{0,1:T(8,128)S(1)} %get-tuple-element.669) | copy-start | bytes 196612
  148.9 95.3 %all-gather.6.cloned.1.call-start = ((), (), s32[]{:S(2)}) async-start(), calls=%async_computation.12 | async-start | bytes 4325376 | tf_op jit(solution)/shard_map/all_gather | solution.py:166
  173.3 312.3 %reduce-scatter.8.cloned.1.call-start = ((), (), s32[]{:S(2)}) async-start(), calls=%async_computation.13 | async-start | bytes 2621440 | tf_op jit(solution)/shard_map/reduce_scatter | solution.py:200
  173.4 41.0 %copy-start.52 = (f32[512]{0:T(512)}, f32[512]{0:T(512)S(1)}, u32[]{:S(2)}) copy-start(f32[512]{0:T(512)S(1)} %add_rsqrt_fusion.1) | copy-start | bytes 6148
  244.1 210.4 %copy-start.19 = (bf16[1024,256]{1,0:T(8,128)(2,1)S(1)}, bf16[1024,256]{1,0:T(8,128)(2,1)}, u32[]{:S(2)}) copy-start(bf16[1024,256]{1,0:T(8,128)(2,1)} %all_gather.41) | copy-start | bytes 1572868
  508.9 128.3 %copy-start.34 = (bf16[1,1024,128]{2,1,0:T(8,128)(2,1)S(1)}, bf16[1,1024,128]{2,1,0:T(8,128)(2,1)}, u32[]{:S(2)}) copy-start(bf16[1,1024,128]{2,1,0:T(8,128)(2,1)} %param.36) | copy-start | bytes 786436
  666.8 131.1 %all-to-all-start.1 = ((bf16[128,40,1024]{2,1,0:T(8,128)(2,1)}), bf16[128,40,1024]{2,1,0:T(8,128)(2,1)}, u32[]{:S(2)}, u32[]{:S(2)}) async-start(bf16[128,40,1024]{2,1,0:T(8,128)(2,1)} %copy.86), calls=%async_computation.2 | async-start | bytes 20971520 | tf_op jit(solution)/shard_map/all_to_all | solution.py:250
  672.9 510.8 %all-gather.8.cloned.1.call-start = ((), (), s32[]{:S(2)}) async-start(), calls=%async_computation.14 | async-start | bytes 1310720 | tf_op jit(solution)/shard_map/all_gather | solution.py:298
  844.5 129.3 %copy-start.6 = (f32[128,40,128]{2,1,0:T(8,128)S(1)}, f32[128,40,128]{2,1,0:T(8,128)}, u32[]{:S(2)}) copy-start(f32[128,40,128]{2,1,0:T(8,128)} %copy-done.5) | copy-start | bytes 7864324
  1163.3 606.4 %reduce-scatter.10.cloned.1.call-start = ((), (), s32[]{:S(2)}) async-start(), calls=%async_computation.15 | async-start | bytes 17301504 | tf_op jit(solution)/shard_map/reduce_scatter | solution.py:360
  1653.9 116.8 %copy-start.16 = (f32[512,128]{0,1:T(8,128)S(1)}, f32[512,128]{0,1:T(8,128)}, u32[]{:S(2)}) copy-start(f32[512,128]{0,1:T(8,128)} %copy-done.15) | copy-start | bytes 786436
  1653.9 116.8 %copy-start.51 = (f32[512]{0:T(512)S(1)}, f32[512]{0:T(512)}, u32[]{:S(2)}) copy-start(f32[512]{0:T(512)} %copy-done.50) | copy-start | bytes 6148
  1653.9 116.8 %copy-start.65 = (f32[128]{0:T(128)S(1)}, f32[128]{0:T(128)}, u32[]{:S(2)}) copy-start(f32[128]{0:T(128)} %copy-done.64) | copy-start | bytes 1540
  1653.9 130.2 %copy-start.37 = (bf16[1024,128]{1,0:T(8,128)(2,1)S(1)}, bf16[1024,128]{1,0:T(8,128)(2,1)}, u32[]{:S(2)}) copy-start(bf16[1024,128]{1,0:T(8,128)(2,1)} %copy-done.36) | copy-start | bytes 786436
  1654.0 311.6 %reduce-scatter.12.cloned.1.call-start = ((), (), s32[]{:S(2)}) async-start(), calls=%async_computation.16 | async-start | bytes 2621440 | tf_op jit(solution)/shard_map/reduce_scatter | solution.py:404
  1787.9 181.2 %reduce-scatter.20.cloned.1.call-start = ((), (), s32[]{:S(2)}) async-start(), calls=%async_computation.20 | async-start | bytes 1081344 | tf_op jit(solution)/shard_map/reduce_scatter | solution.py:428
  1789.5 187.7 %reduce-scatter.16.cloned.1.call-start = ((), (), s32[]{:S(2)}) async-start(), calls=%async_computation.18 | async-start | bytes 540672 | tf_op jit(solution)/shard_map/reduce_scatter | solution.py:426
  1793.6 264.3 %reduce-scatter.18.cloned.1.call-start = ((), (), s32[]{:S(2)}) async-start(), calls=%async_computation.19 | async-start | bytes 540672 | tf_op jit(solution)/shard_map/reduce_scatter | solution.py:427
  1803.3 335.9 %reduce-scatter.14.cloned.1.call-start = ((), (), s32[]{:S(2)}) async-start(), calls=%async_computation.17 | async-start | bytes 1081344 | tf_op jit(solution)/shard_map/reduce_scatter | solution.py:425
  1811.6 155.3 %copy-start.22 = (f32[128,1024]{1,0:T(8,128)S(1)}, f32[128,1024]{1,0:T(8,128)}, u32[]{:S(2)}) copy-start(f32[128,1024]{1,0:T(8,128)} %get-tuple-element.640) | copy-start | bytes 1572868
  1811.6 327.6 %copy-start.1 = (bf16[1,128,1024]{2,1,0:T(8,128)(2,1)S(1)}, bf16[1,128,1024]{2,1,0:T(8,128)(2,1)}, u32[]{:S(2)}) copy-start(bf16[1,128,1024]{2,1,0:T(8,128)(2,1)} %param.37) | copy-start | bytes 786436
  (61 other events, 419.8 us)
Sparse Core Ops, SparseCore 0:
  149.0 46.2 all-gather.3
  198.1 46.0 all-gather.5
  456.5 29.0 reduce-scatter.7
  1163.4 20.2 all-gather.7
  1654.0 115.5 reduce-scatter.9
  1788.0 26.8 reduce-scatter.11
  1818.9 77.3 reduce-scatter.19
  1900.7 76.4 reduce-scatter.15
  1981.6 76.2 reduce-scatter.17
  2062.3 76.9 reduce-scatter.13
where the time goes:
time: 2160 us; the launch traced here: 2150 us
  blocking collectives  710 us (33%)
  matrix products  574 us (27%)
  waiting for transfers between devices  475 us (22%)
  other arithmetic  242 us (11%)
  local copies, waits for them, and re-layouts  118 us (5%)
    unnamed x3, blocking collectives  209 us
    dot_general x8, matrix products, head_scores(): lax.dot_general(query_head, key_head, (((1,), (1,)), ((), ())), preferred...  203 us
    all_to_all x1, blocking collectives, on_device(): lax.all_to_all(dispatch_rows(copy_grad), ('ctx', 'exp'), split_axis=0, co...  129 us
    all_to_all x1, blocking collectives, on_device(): lax.all_to_all(dispatch_rows(normed_ffn[copy_token]), ('ctx', 'exp'), spl...  128 us
    all_to_all x1, blocking collectives, on_device(): lax.all_to_all(input_part.astype(jnp.bfloat16).reshape(dev_count, local_e...  126 us
    all_to_all x1, waiting for transfers between devices, on_device(): lax.all_to_all(partial_out.reshape(dev_count, local_experts * capacity, m...  123 us
    reduce_scatter x1, waiting for transfers between devices, on_device(): lax.psum_scatter(pair_grad, 'ctx', scatter_dimension=0, tiled=True)  114 us
    convert_element_type x4, other arithmetic, backward_head(): score_grad = (probs * (prob_grad - delta_row)).astype(jnp.bfloat16)  110 us
  transfers between devices with their start and end apart: 11, of which 8 were waited for; matrix products, arithmetic and copies ran while one was open for 3% of the time, Pallas kernels for 0%

commit v1 on v0

v1 whole, which is shorter than its diff:
```python
import functools

import jax
import jax.numpy as jnp
from jax import lax
from jax.experimental import pallas as pl
from jax.experimental.pallas import tpu as pltpu
from jax.sharding import PartitionSpec as P

HD = 64
BLK = 128
CONT_LEN = 1024
CONT_BLKS = CONT_LEN // BLK
LANES = 128

NORM_EPSILON = 1e-05
ROPE_BASE = 10000.0
MASK_FLOOR = -1e30
F32 = jnp.float32
BF16 = jnp.bfloat16
NT = (((1,), (1,)), ((), ()))
NN = (((1,), (0,)), ((), ()))
TN = (((0,), (0,)), ((), ()))


def dot(left, right, dims):
    return lax.dot_general(left, right, dims, preferred_element_type=F32)


def key_ranges(block, half, tile_blocks):
    cont = block >= half
    inner = jnp.where(cont, (block - half) % CONT_BLKS, 0)
    n_a = jnp.where(cont, half // tile_blocks, block // tile_blocks)
    cont_base = half + (block - half) // CONT_BLKS * CONT_BLKS
    base = jnp.where(cont, cont_base, block // tile_blocks * tile_blocks) * BLK
    return n_a, base, inner // tile_blocks


def gather_blocks(table, total, moves):
    def start(i, carry):
        to = pl.multiple_of(table[i] * BLK, BLK)
        for source, target, sem in moves:
            pltpu.make_async_copy(source(i), target(to), sem).start()
        return carry

    lax.fori_loop(0, total, start, 0)


def wait_all(ref, sem):
    pltpu.make_async_copy(ref, ref, sem).wait()


def rows_of(ref, per_ctx):
    def place(i):
        first = i // 4 * per_ctx + i % 4 * BLK
        return ref.at[pl.ds(pl.multiple_of(first, 16), BLK)]

    return place


def causal(shape, key_first, query_first, rows_are_queries):
    row = lax.broadcasted_iota(jnp.int32, shape, 0) % BLK
    col = lax.broadcasted_iota(jnp.int32, shape, 1)
    if rows_are_queries:
        return key_first + col <= query_first + row
    return key_first + row <= query_first + col


def to_half(tile, source, target):
    values = tile.astype(F32)
    if source != target:
        values = pltpu.roll(values, HD, 1)
    lane = lax.broadcasted_iota(jnp.int32, values.shape, 1)
    return jnp.where(lane // HD == target, values, 0.0)


def turn(tile, cosine, sine):
    lane = lax.broadcasted_iota(jnp.int32, tile.shape, 1)
    ahead = pltpu.roll(tile, LANES - HD // 2, 1)
    behind = pltpu.roll(tile, HD // 2, 1)
    return tile * cosine + jnp.where(lane % HD < HD // 2, ahead, behind) * sine


def rows_by_head(source_ref, block_rows, target_ref):
    for h in range(4):
        m, g = h // 2, h % 2
        tile = source_ref[block_rows, m * LANES : (m + 1) * LANES]
        target_ref[h * BLK : (h + 1) * BLK, :] = to_half(tile, g, m).astype(BF16)


def rows_by_token(values):
    tiles = []
    for m in range(2):
        first = values[2 * m * BLK : (2 * m + 1) * BLK]
        second = values[(2 * m + 1) * BLK : (2 * m + 2) * BLK]
        tiles.append(to_half(first, m, 0) + to_half(second, m, 1))
    return tiles


def turn_kernel(pre_ref, scale_ref, gain_ref, cos_ref, sin_ref, q_ref, kv_ref):
    for col in range(3):
        lanes = slice(col * LANES, (col + 1) * LANES)
        which = 0 if col < 2 else 1
        hat = pre_ref[:, lanes] * scale_ref[:, which : which + 1]
        turned = turn(hat * gain_ref[:, lanes], cos_ref[...], sin_ref[...]).astype(BF16)
        if which == 0:
            q_ref[:, lanes] = (turned.astype(F32) * HD**-0.5).astype(BF16)
        else:
            kv_ref[:, :LANES] = turned
    kv_ref[:, LANES:] = pre_ref[:, 3 * LANES :].astype(BF16)


def attend_kernel(
    total, half, tile_blocks, table, own, q_in, kv, o_ref, lse_ref, kv_s, q_ref, acc, peak, sem
):
    gather_blocks(
        table,
        total,
        [
            (
                rows_of(kv, 4 * BLK),
                lambda to: kv_s.at[pl.ds(to, BLK), pl.ds(0, 2 * LANES)],
                sem.at[0],
            )
        ],
    )
    kv_s[:, 2 * LANES :] = jnp.ones((total * BLK, LANES), BF16)
    wait_all(kv_s.at[:, pl.ds(0, 2 * LANES)], sem.at[0])
    width = tile_blocks * BLK

    def query_block(i, carry):
        block = own[i]
        n_a, base, n_b = key_ranges(block, half, tile_blocks)
        rows = pl.ds(pl.multiple_of(i * BLK, BLK), BLK)
        lanes = pl.ds(pl.multiple_of(i % 2 * BLK, BLK), BLK)
        rows_by_head(q_in, rows, q_ref)

        def first_key(j):
            return pl.multiple_of(jnp.where(j < n_a, j * width, base + (j - n_a) * width), BLK)

        def tile(start, masked):
            scores = dot(q_ref[...], kv_s[pl.ds(start, width), :LANES], NT)
            probs = jnp.exp(scores)
            if masked:
                probs = jnp.where(causal(probs.shape, start, block * BLK, True), probs, 0.0)
            acc[...] += dot(probs.astype(BF16), kv_s[pl.ds(start, width), LANES:], NN)

        def clear_tile(j, carry):
            tile(first_key(j), False)
            return carry

        def store(out, log_sum):
            first, second = rows_by_token(out)
            o_ref[rows, :LANES] = first
            o_ref[rows, LANES:] = second
            for h in range(4):
                lse_ref[i // 2, h : h + 1, lanes] = log_sum[h * BLK : (h + 1) * BLK].T[:1]

        acc[...] = jnp.zeros_like(acc)
        lax.fori_loop(0, n_a + n_b, clear_tile, 0)
        tile(first_key(n_a + n_b), True)
        sums = acc[:, LANES:]
        in_range = (jnp.max(sums) < 2.0**100) & (jnp.min(sums) > 2.0**-40)

        @pl.when(in_range)
        def _():
            store(acc[:, :LANES] / sums, jnp.log(sums))

        @pl.when(jnp.logical_not(in_range))
        def _():
            acc[...] = jnp.zeros_like(acc)
            peak[...] = jnp.full_like(peak, MASK_FLOOR)

            def safe_tile(j, carry):
                start = first_key(j)
                scores = dot(q_ref[...], kv_s[pl.ds(start, width), :LANES], NT)
                seen = causal(scores.shape, start, block * BLK, True)
                scores = jnp.where(seen, scores, MASK_FLOOR)
                old = peak[...]
                new = jnp.maximum(old, jnp.max(scores, axis=1, keepdims=True))
                probs = jnp.where(seen, jnp.exp(scores - new[:, :1]), 0.0)
                keep = jnp.exp(old - new)
                acc[...] = acc[...] * keep[:, :1] + dot(
                    probs.astype(BF16), kv_s[pl.ds(start, width), LANES:], NN
                )
                peak[...] = new
                return carry

            lax.fori_loop(0, n_a + n_b + 1, safe_tile, 0)
            safe_sums = acc[:, LANES:]
            store(acc[:, :LANES] / safe_sums, peak[...] + jnp.log(safe_sums))

        return carry

    lax.fori_loop(0, 4, query_block, 0)


def query_grad_kernel(
    total,
    half,
    tile_blocks,
    table,
    own,
    q_in,
    do_in,
    o_in,
    lse_in,
    cos_ref,
    sin_ref,
    kv,
    dq_ref,
    kv_s,
    q_ref,
    do_ref,
    lse_ref,
    delta_ref,
    acc,
    sem,
):
    gather_blocks(
        table, total, [(rows_of(kv, 4 * BLK), lambda to: kv_s.at[pl.ds(to, BLK)], sem.at[0])]
    )
    wait_all(kv_s, sem.at[0])
    width = tile_blocks * BLK

    def query_block(i, carry):
        block = own[i]
        n_a, base, n_b = key_ranges(block, half, tile_blocks)
        rows = pl.ds(pl.multiple_of(i * BLK, BLK), BLK)
        lanes = pl.ds(pl.multiple_of(i % 2 * BLK, BLK), BLK)
        rows_by_head(q_in, rows, q_ref)
        rows_by_head(do_in, rows, do_ref)
        for h in range(4):
            part = slice(h * BLK, (h + 1) * BLK)
            pair = slice(h // 2 * LANES, (h // 2 + 1) * LANES)
            product = do_in[rows, pair].astype(F32) * o_in[rows, pair]
            own_half = to_half(product, h % 2, h % 2)
            delta = jnp.sum(own_half, axis=1, keepdims=True)
            delta_ref[part, :] = jnp.broadcast_to(delta, (BLK, LANES))
            row = lse_in[i // 2, h : h + 1, lanes]
            lse_ref[part, :] = jnp.broadcast_to(row, (LANES, BLK)).T

        def first_key(j):
            return pl.multiple_of(jnp.where(j < n_a, j * width, base + (j - n_a) * width), BLK)

        def tile(start, masked):
            keys = kv_s[pl.ds(start, width), :LANES]
            scores = dot(q_ref[...], keys, NT)
            prob_grad = dot(do_ref[...], kv_s[pl.ds(start, width), LANES:], NT)
            probs = jnp.exp(scores - lse_ref[:, :1])
            score_grad = probs * (prob_grad - delta_ref[:, :1])
            if masked:
                seen = causal(probs.shape, start, block * BLK, True)
                score_grad = jnp.where(seen, score_grad, 0.0)
            acc[...] += dot(score_grad.astype(BF16), keys, NN)

        def clear_tile(j, carry):
            tile(first_key(j), False)
            return carry

        acc[...] = jnp.zeros_like(acc)
        lax.fori_loop(0, n_a + n_b, clear_tile, 0)
        tile(first_key(n_a + n_b), True)
        for m, gradient in enumerate(rows_by_token(acc[...])):
            back = turn(gradient * HD**-0.5, cos_ref[rows, :], -sin_ref[rows, :])
            dq_ref[rows, m * LANES : (m + 1) * LANES] = back
        return carry

    lax.fori_loop(0, 4, query_block, 0)


def pair_grad_kernel(
    total,
    half,
    tile_blocks,
    do_rows,
    table,
    own,
    kv_in,
    cos_ref,
    sin_ref,
    q_all,
    do_all,
    aux,
    out_ref,
    q_s,
    do_s,
    aux_s,
    k_ref,
    v_ref,
    dk_ref,
    dv_ref,
    sem,
):
    gather_blocks(
        table,
        total,
        [
            (rows_of(q_all, 4 * BLK), lambda to: q_s.at[pl.ds(to, BLK)], sem.at[0]),
            (rows_of(do_all, do_rows), lambda to: do_s.at[pl.ds(to, BLK)], sem.at[1]),
            (
                lambda i: aux.at[i // 4, i // 2 % 2, :, pl.ds(pl.multiple_of(i % 2 * BLK, BLK), BLK)],
                lambda to: aux_s.at[:, pl.ds(to, BLK)],
                sem.at[2],
            ),
        ],
    )

    def place(blk, h):
        return (h * 2 + blk) * BLK if blk < 2 else ((blk * 4) + h) * BLK

    k_ref[...] = jnp.zeros_like(k_ref)
    v_ref[...] = jnp.zeros_like(v_ref)
    dk_ref[...] = jnp.zeros_like(dk_ref)
    dv_ref[...] = jnp.zeros_like(dv_ref)
    for blk in range(4):
        source = slice(blk * BLK, (blk + 1) * BLK)
        for h in range(4):
            m, g = h // 2, h % 2
            target = slice(place(blk, h), place(blk, h) + BLK)
            pair = slice(m * LANES, (m + 1) * LANES)
            k_ref[target, pair] = to_half(kv_in[source, :LANES], m, g).astype(BF16)
            v_ref[target, pair] = to_half(kv_in[source, LANES:], m, g).astype(BF16)
    wait_all(q_s, sem.at[0])
    wait_all(do_s, sem.at[1])
    wait_all(aux_s, sem.at[2])
    width = tile_blocks * BLK

    def tile(first_row, per_head, start, keys_first, masked):
        rows = pl.ds(first_row, 4 * per_head)
        queries = q_s[pl.ds(start, width), :]
        grads = do_s[pl.ds(start, width), :]
        scores = dot(k_ref[rows, :], queries, NT)
        prob_grad = dot(v_ref[rows, :], grads, NT)
        probs_low = []
        score_low = []
        for h in range(4):
            part = slice(h * per_head, (h + 1) * per_head)
            probs = jnp.exp(scores[part] - aux_s[h : h + 1, pl.ds(start, width)])
            if masked:
                seen = [causal((BLK, width), first, start, False) for first in keys_first]
                probs = jnp.where(jnp.concatenate(seen, axis=0), probs, 0.0)
            probs_low.append(probs.astype(BF16))
            shifted = prob_grad[part] - aux_s[4 + h : 5 + h, pl.ds(start, width)]
            score_low.append((probs * shifted).astype(BF16))
        dv_ref[rows, :] += dot(jnp.concatenate(probs_low, axis=0), grads, NN)
        dk_ref[rows, :] += dot(jnp.concatenate(score_low, axis=0), queries, NN)

    low = jnp.minimum(own[0], own[1])
    high = jnp.maximum(own[0], own[1])

    def edge_tile(j, carry):
        firsts = [own[0] * BLK, own[1] * BLK]
        tile(0, 2 * BLK, pl.multiple_of(j * width, width), firsts, True)
        return carry

    def clear_tile(j, carry):
        tile(0, 2 * BLK, pl.multiple_of(j * width, width), None, False)
        return carry

    lax.fori_loop(low // tile_blocks, high // tile_blocks + 1, edge_tile, 0)
    lax.fori_loop(high // tile_blocks + 1, total // tile_blocks, clear_tile, 0)
    for which in range(2):
        block = own[2 + which]
        stop = half + ((block - half) // CONT_BLKS + 1) * CONT_BLKS

        def cont_tile(j, carry, which=which, block=block):
            first_row = (8 + 4 * which) * BLK
            tile(first_row, BLK, pl.multiple_of(j * width, width), [block * BLK], True)
            return carry

        lax.fori_loop(block // tile_blocks, stop // tile_blocks, cont_tile, 0)

    def collect(ref, blk):
        tile_sum = None
        for h in range(4):
            m, g = h // 2, h % 2
            part = ref[place(blk, h) : place(blk, h) + BLK, m * LANES : (m + 1) * LANES]
            moved = to_half(part, g, m)
            tile_sum = moved if tile_sum is None else tile_sum + moved
        return tile_sum

    for blk in range(4):
        rows = slice(blk * BLK, (blk + 1) * BLK)
        out_ref[rows, :LANES] = turn(collect(dk_ref, blk), cos_ref[rows, :], -sin_ref[rows, :])
        out_ref[rows, LANES:] = collect(dv_ref, blk)


def block_of_whole(shape):
    return pl.BlockSpec(shape, lambda i, *_: (0,) * len(shape))


def kernel_call(kernel, name, prefetch, ins, outs, scratch, flops):
    hbm = pl.BlockSpec(memory_space=pl.ANY)
    moved = sum(x.size * x.dtype.itemsize for x, _ in ins)
    return pl.pallas_call(
        kernel,
        out_shape=tuple(outs),
        grid_spec=pltpu.PrefetchScalarGridSpec(
            num_scalar_prefetch=len(prefetch),
            grid=(1,),
            in_specs=[hbm if far else block_of_whole(x.shape) for x, far in ins],
            out_specs=tuple(block_of_whole(out.shape) for out in outs),
            scratch_shapes=scratch,
        ),
        compiler_params=pltpu.CompilerParams(vmem_limit_bytes=48 << 20),
        cost_estimate=pl.CostEstimate(flops=flops, bytes_accessed=moved, transcendentals=0),
        name=name,
    )(*prefetch, *(x for x, _ in ins))


def turn_heads(projected, scales, gain, cosine, sine):
    rows = projected.shape[0]
    out = jax.ShapeDtypeStruct((rows, 2 * LANES), BF16)
    ins = [(x, False) for x in (projected, scales, gain, cosine, sine)]
    return kernel_call(turn_kernel, "turn_heads", (), ins, [out, out], [], 10**6)


def attend(table, own, q, kv_all):
    total = table.shape[0]
    return kernel_call(
        functools.partial(attend_kernel, total, total // 2, 8),
        "attend",
        (table, own),
        [(q, False), (kv_all, True)],
        [
            jax.ShapeDtypeStruct((4 * BLK, 2 * LANES), F32),
            jax.ShapeDtypeStruct((2, 4, 2 * BLK), F32),
        ],
        [
            pltpu.VMEM((total * BLK, 3 * LANES), BF16),
            pltpu.VMEM((4 * BLK, LANES), BF16),
            pltpu.VMEM((4 * BLK, 2 * LANES), F32),
            pltpu.VMEM((4 * BLK, LANES), F32),
            pltpu.SemaphoreType.DMA((1,)),
        ],
        20 * 10**9,
    )


def query_grad(table, own, q, out_grad, heads, lse, cosine, sine, kv_all):
    total = table.shape[0]
    ins = [(x, False) for x in (q, out_grad, heads, lse, cosine, sine)]
    return kernel_call(
        functools.partial(query_grad_kernel, total, total // 2, 4),
        "query_grad",
        (table, own),
        ins + [(kv_all, True)],
        [jax.ShapeDtypeStruct((4 * BLK, 2 * LANES), F32)],
        [
            pltpu.VMEM((total * BLK, 2 * LANES), BF16),
            pltpu.VMEM((4 * BLK, LANES), BF16),
            pltpu.VMEM((4 * BLK, LANES), BF16),
            pltpu.VMEM((4 * BLK, LANES), F32),
            pltpu.VMEM((4 * BLK, LANES), F32),
            pltpu.VMEM((4 * BLK, LANES), F32),
            pltpu.SemaphoreType.DMA((1,)),
        ],
        30 * 10**9,
    )[0]


def pair_grad(table, own, kv, cosine, sine, q_all, do_all, do_rows, aux):
    total = table.shape[0]
    ins = [(x, False) for x in (kv, cosine, sine)] + [(x, True) for x in (q_all, do_all, aux)]
    return kernel_call(
        functools.partial(pair_grad_kernel, total, total // 2, 2, do_rows),
        "pair_grad",
        (table, own),
        ins,
        [jax.ShapeDtypeStruct((4 * BLK, 2 * LANES), F32)],
        [
            pltpu.VMEM((total * BLK, 2 * LANES), BF16),
            pltpu.VMEM((total * BLK, 2 * LANES), BF16),
            pltpu.VMEM((8, total * BLK), F32),
            pltpu.VMEM((16 * BLK, 2 * LANES), BF16),
            pltpu.VMEM((16 * BLK, 2 * LANES), BF16),
            pltpu.VMEM((16 * BLK, 2 * LANES), F32),
            pltpu.VMEM((16 * BLK, 2 * LANES), F32),
            pltpu.SemaphoreType.DMA((3,)),
        ],
        40 * 10**9,
    )[0]


def turn_tables(position):
    half_dim = HD // 2
    frequency = ROPE_BASE ** (-(jnp.arange(half_dim, dtype=F32) * 2.0 / HD))
    angles = position[:, None] * frequency[None, :]
    cosine, sine = jnp.cos(angles), jnp.sin(angles)
    return jnp.concatenate([cosine] * 4, axis=1), jnp.concatenate([-sine, sine] * 2, axis=1)


def norm_back(grad_normed, hat_values, scale_values, gain_values):
    grad_hat = grad_normed * gain_values
    return scale_values * (
        grad_hat - hat_values * jnp.mean(grad_hat * hat_values, axis=-1, keepdims=True)
    )


def pieces(values, count):
    parts = []
    for _ in range(count):
        part = lax.reduce_precision(values, 8, 7)
        parts.append(part.astype(BF16))
        values = values - part
    return parts


def exchange(values, axis):
    return lax.all_to_all(values, axis, split_axis=0, concat_axis=0, tiled=True)


def spread(values, axis, count):
    return exchange(jnp.broadcast_to(values[None], (count,) + values.shape), axis)


def gather_small(values, axis, index, count):
    come = [values]
    for step in range(1, count):
        come.append(lax.ppermute(values, axis, [(i, (i + step) % count) for i in range(count)]))
    twice = jnp.stack(come[::-1] + come[:0:-1], axis=0)
    return lax.dynamic_slice_in_dim(twice, count - 1 - index, count, 0)


def on_device(
    hidden_in,
    teacher,
    valid,
    block_of,
    routes,
    gates,
    w_query,
    w_key,
    w_value,
    w_out,
    gain_attn,
    gain_query,
    gain_key,
    gain_ffn,
    w_gate,
    w_up,
    w_down,
):
    ctx_count = lax.axis_size("ctx")
    exp_count = lax.axis_size("exp")
    ctx_index = lax.axis_index("ctx")
    exp_index = lax.axis_index("exp")
    ctx_rows, model_width = hidden_in.shape
    own_rows = ctx_rows // exp_count
    token_total = block_of.shape[0] * BLK
    head_cols = w_query.shape[1]
    kv_cols = w_key.shape[1]
    kv_total = kv_cols * exp_count
    qkv_cols = head_cols + 2 * kv_cols
    shard_rows = w_query.shape[0]

    own_qkv = jnp.concatenate([w_query, w_key, w_value], axis=1)
    gain_row = jnp.concatenate([gain_attn, gain_query, gain_ffn, gain_key])
    gain_rows = jnp.pad(gain_row, (0, 16 * qkv_cols - gain_row.shape[0])).reshape(16, qkv_cols)
    first_parts = spread(jnp.concatenate([own_qkv, gain_rows], axis=0), "ctx", ctx_count)
    full_qkv = first_parts[:, :shard_rows].reshape(model_width, qkv_cols)
    gains = first_parts[:, shard_rows:].reshape(ctx_count, -1).astype(F32)
    attn_gain = gains[:, :shard_rows].reshape(model_width)
    query_gain_all = gains[:, shard_rows : 2 * shard_rows].reshape(model_width)
    ffn_gain = gains[:, 2 * shard_rows : 3 * shard_rows].reshape(model_width)
    key_gain_all = gains[:, 3 * shard_rows : 3 * shard_rows + gain_key.shape[0]].reshape(kv_total)
    query_gain = lax.dynamic_slice_in_dim(query_gain_all, exp_index * head_cols, head_cols)
    key_gain = lax.dynamic_slice_in_dim(key_gain_all, exp_index * kv_cols, kv_cols)

    out_strip = gather_small(w_out, "exp", exp_index, exp_count)
    width = w_gate.shape[2]
    own_expert = jnp.concatenate([w_gate[0], w_up[0], w_down[0].T], axis=1)
    expert = lax.all_gather(own_expert, "exp", axis=0, tiled=False)

    hidden_f = hidden_in.astype(F32)
    attn_scale = lax.rsqrt(jnp.mean(hidden_f * hidden_f, axis=-1, keepdims=True) + NORM_EPSILON)
    attn_hat = hidden_f * attn_scale
    normed = (attn_hat * attn_gain).astype(BF16)
    projected = dot(normed, full_qkv, NN)
    query_pre = projected[:, :head_cols]
    key_pre = projected[:, head_cols : head_cols + kv_cols]
    query_square, key_square = lax.psum(
        jnp.stack([jnp.sum(query_pre * query_pre, axis=1), jnp.sum(key_pre * key_pre, axis=1)]),
        "exp",
    )
    query_scale = lax.rsqrt(query_square / model_width + NORM_EPSILON)[:, None]
    key_scale = lax.rsqrt(key_square / kv_total + NORM_EPSILON)[:, None]
    query_hat = query_pre * query_scale
    key_hat = key_pre * key_scale
    own_blocks = lax.dynamic_slice_in_dim(block_of, ctx_index * 4, 4)
    token_ids = (own_blocks[:, None] * BLK + jnp.arange(BLK, dtype=jnp.int32)[None]).reshape(-1)
    prompt_len = token_total // 2
    position = jnp.where(
        token_ids >= prompt_len, prompt_len + (token_ids - prompt_len) % CONT_LEN, token_ids
    ).astype(F32)
    cosine, sine = turn_tables(position)
    queries_rot, own_kv = turn_heads(
        projected,
        jnp.concatenate([query_scale, key_scale], axis=1),
        jnp.concatenate([query_gain, key_gain])[None],
        cosine,
        sine,
    )
    own_kv, expert = lax.optimization_barrier((own_kv, expert))
    gate_strips = [expert[u, :, :width] for u in range(exp_count)]
    up_strips = [expert[u, :, width : 2 * width] for u in range(exp_count)]
    wide_gate_up = jnp.concatenate(gate_strips + up_strips, axis=1)
    wide_down = jnp.concatenate([expert[u, :, 2 * width :] for u in range(exp_count)], axis=1)
    kv_all = lax.all_gather(own_kv, "ctx", axis=0, tiled=True)
    kv_all, out_strip = lax.optimization_barrier((kv_all, out_strip))
    full_out = lax.all_gather(out_strip, "ctx", axis=1, tiled=True)
    heads_f, lse = attend(block_of, own_blocks, queries_rot, kv_all)
    heads_low = heads_f.astype(BF16)

    own_heads = exchange(heads_low.reshape(exp_count, own_rows, head_cols), "exp")
    own_heads, full_out, later_q = lax.optimization_barrier((own_heads, full_out, queries_rot))
    q_all = lax.all_gather(later_q, "ctx", axis=0, tiled=True)
    attn_rows = jnp.einsum("erk,eok->ro", own_heads, full_out, preferred_element_type=F32)
    hidden_rows = lax.dynamic_slice_in_dim(hidden_f, exp_index * own_rows, own_rows, 0)
    resid = hidden_rows + attn_rows
    ffn_scale = lax.rsqrt(jnp.mean(resid * resid, axis=-1, keepdims=True) + NORM_EPSILON)
    ffn_hat = resid * ffn_scale
    normed_ffn = (ffn_hat * ffn_gain).astype(BF16)

    expert_total = ctx_count
    capacity = max(2, own_rows * routes.shape[1] * 5 // (expert_total * 4))
    slots = expert_total * capacity
    names = routes[:, :, None] == jnp.arange(expert_total, dtype=jnp.int32)[None, None, :]
    named = jnp.any(names, axis=1)
    gate_of = jnp.sum(jnp.where(names, gates[:, :, None], 0.0), axis=1)
    before = jnp.tril(jnp.ones((own_rows, own_rows), BF16), -1)
    rank = dot(before, named.astype(BF16), NN).astype(jnp.int32)
    slot_rank = jnp.where(named, rank, -1).T[:, None, :]
    holds = slot_rank == jnp.arange(capacity, dtype=jnp.int32)[None, :, None]
    pick = holds.astype(BF16).reshape(slots, own_rows)
    weigh = jnp.where(holds, gate_of.T[:, None, :], 0.0).reshape(slots, own_rows)
    slot_gate = jnp.sum(weigh, axis=1, keepdims=True)

    def send(rows):
        return exchange(rows.reshape(ctx_count, capacity, model_width), "ctx").reshape(
            slots, model_width
        )

    expert_in = send(dot(pick, normed_ffn, NN).astype(BF16))
    pre = dot(expert_in, wide_gate_up, NN)
    gate_pre = pre[:, : exp_count * width]
    up_pre = pre[:, exp_count * width :]
    gate_sig = jax.nn.sigmoid(gate_pre)
    gate_act = gate_pre * gate_sig
    hidden_act = (gate_act * up_pre).astype(BF16)
    returned = send(dot(hidden_act, wide_down, NT).astype(BF16))
    returned, q_all, later_qkv = lax.optimization_barrier((returned, q_all, full_qkv))
    all_qkv = lax.all_gather(later_qkv, "exp", axis=0, tiled=False)
    moe_rows = sum(dot(part, returned, TN) for part in pieces(weigh, 2))
    block_out = resid + moe_rows

    row_start = (ctx_index * exp_count + exp_index) * own_rows
    row_valid = lax.dynamic_slice_in_dim(valid, row_start, own_rows, 0).astype(F32)
    valid_count = jnp.sum(valid.astype(F32))
    misfit = block_out - teacher.astype(F32)
    local_loss = jnp.sum(row_valid[:, None] * misfit * misfit)
    out_grad_rows = misfit * row_valid[:, None] * (token_total / valid_count)
    copy_grad = sum(dot(pick, part, NN) for part in pieces(out_grad_rows, 2))
    grad_copies = send((slot_gate * copy_grad).astype(BF16))
    act_grad = dot(grad_copies, wide_down, NN)
    gate_grad = (act_grad * up_pre * gate_sig * (1.0 + gate_pre * (1.0 - gate_sig))).astype(BF16)
    up_grad = (act_grad * gate_act).astype(BF16)
    both_grad = jnp.concatenate([gate_grad, up_grad], axis=1)
    arrived_grad = send(dot(both_grad, wide_gate_up, NT).astype(BF16))
    arrived_grad, all_qkv = lax.optimization_barrier((arrived_grad, all_qkv))
    ffn_normed_grad = dot(pick, arrived_grad, TN)

    ffn_gain_part = jnp.sum(ffn_normed_grad * ffn_hat, axis=0)
    resid_grad = out_grad_rows + norm_back(ffn_normed_grad, ffn_hat, ffn_scale, ffn_gain)
    branch_rows = resid_grad.astype(BF16)

    do_rows = jnp.einsum("ro,eok->erk", branch_rows, full_out, preferred_element_type=F32)
    out_grad = exchange(do_rows.astype(BF16), "exp").reshape(ctx_rows, head_cols)
    branch_grad = gather_small(branch_rows, "exp", exp_index, exp_count).reshape(
        ctx_rows, model_width
    )
    grad_out = dot(branch_grad, heads_low, TN)
    head_of = jnp.arange(head_cols, dtype=jnp.int32)[None] // HD
    head_ones = (head_of == jnp.arange(4, dtype=jnp.int32)[:, None]).astype(F32)
    delta = lax.dot_general(
        head_ones,
        out_grad.astype(F32) * heads_f,
        NT,
        precision=lax.Precision.HIGHEST,
        preferred_element_type=F32,
    )
    delta = delta.reshape(4, 2, 2 * BLK).transpose(1, 0, 2)
    row_stats = jnp.concatenate([lse, delta], axis=1)
    stat_parts = jnp.stack(pieces(row_stats, 3), axis=0).reshape(-1, 2 * BLK)
    stat_rows = stat_parts.shape[0]
    do_all = lax.all_gather(
        jnp.concatenate([out_grad, stat_parts], axis=0), "ctx", axis=0, tiled=False
    )
    query_n_grad = query_grad(
        block_of, own_blocks, queries_rot, out_grad, heads_f, lse, cosine, sine, kv_all
    )

    do_all, expert_in, both_grad, hidden_act, grad_copies = lax.optimization_barrier(
        (do_all, expert_in, both_grad, hidden_act, grad_copies)
    )
    gate_up_part = dot(expert_in, both_grad, TN)
    down_part = dot(grad_copies, hidden_act, TN)
    strips = []
    for u in range(exp_count):
        own = slice(u * width, (u + 1) * width)
        of_up = slice((exp_count + u) * width, (exp_count + u + 1) * width)
        strips.append(
            jnp.concatenate(
                [gate_up_part[:, own], gate_up_part[:, of_up], down_part[:, own]], axis=1
            )
        )
    grad_expert = lax.psum_scatter(
        jnp.concatenate(strips, axis=0), "exp", scatter_dimension=0, tiled=True
    )
    grad_w_gate = grad_expert[None, :, :width]
    grad_w_up = grad_expert[None, :, width : 2 * width]
    grad_w_down = grad_expert[:, 2 * width :].T[None]

    aux = jnp.sum(
        do_all[:, ctx_rows:].reshape(ctx_count, 3, 2, 8, 2 * BLK).astype(F32), axis=1
    )
    pair_grads = pair_grad(
        block_of,
        own_blocks,
        own_kv,
        cosine,
        sine,
        q_all,
        do_all.reshape(-1, head_cols),
        ctx_rows + stat_rows,
        aux,
    )
    key_n_grad = pair_grads[:, :kv_cols]
    value_grad = pair_grads[:, kv_cols:].astype(BF16)
    query_gain_part = jnp.sum(query_n_grad * query_hat, axis=0)
    key_gain_part = jnp.sum(key_n_grad * key_hat, axis=0)
    query_hat_grad = query_n_grad * query_gain
    key_hat_grad = key_n_grad * key_gain

    stats = jnp.concatenate(
        [
            jnp.sum(query_hat_grad * query_hat, axis=1),
            jnp.sum(key_hat_grad * key_hat, axis=1),
            lax.dynamic_update_slice_in_dim(
                jnp.zeros((model_width,), F32), query_gain_part, exp_index * head_cols, 0
            ),
            ffn_gain_part,
            lax.dynamic_update_slice_in_dim(
                jnp.zeros((kv_total,), F32), key_gain_part, exp_index * kv_cols, 0
            ),
            jnp.full((kv_total,), local_loss),
        ]
    )
    stats = lax.psum(stats.reshape(-1, LANES), "exp").reshape(-1)
    query_stat = stats[:ctx_rows, None] / model_width
    key_stat = stats[ctx_rows : 2 * ctx_rows, None] / kv_total
    sums = stats[2 * ctx_rows :]
    query_low = (query_scale * (query_hat_grad - query_hat * query_stat)).astype(BF16)
    key_low = (key_scale * (key_hat_grad - key_hat * key_stat)).astype(BF16)
    grad_low = jnp.concatenate([query_low, key_low, value_grad], axis=1)

    grad_qkv = dot(normed, grad_low, TN)
    wide_sums = jnp.stack(
        [
            sums[:model_width].reshape(ctx_count, shard_rows),
            sums[model_width : 2 * model_width].reshape(ctx_count, shard_rows),
            jnp.repeat(
                sums[2 * model_width : 2 * model_width + kv_total].reshape(ctx_count, -1), 2, axis=1
            ),
            jnp.broadcast_to(sums[-1], (ctx_count, shard_rows)),
        ],
        axis=-1,
    )
    sum_parts = jnp.concatenate(pieces(wide_sums, 3), axis=-1)
    sum_parts = jnp.pad(sum_parts, ((0, 0), (0, 0), (0, LANES - sum_parts.shape[-1])))
    shards = exchange(
        jnp.concatenate(
            [
                grad_qkv.astype(BF16).reshape(ctx_count, shard_rows, qkv_cols),
                grad_out.astype(BF16).reshape(ctx_count, shard_rows, head_cols),
                sum_parts,
            ],
            axis=2,
        ),
        "ctx",
    )
    shards = jnp.sum(shards.astype(F32), axis=0)
    own_grad_qkv = shards[:, :qkv_cols]
    own_grad_out = shards[:, qkv_cols : qkv_cols + head_cols]
    tail = shards[:, qkv_cols + head_cols :]
    tail = tail[:, 0:4] + tail[:, 4:8] + tail[:, 8:12]
    loss = tail[0, 3] / (valid_count * model_width)

    gain_part = jnp.sum(own_grad_qkv * own_qkv.astype(F32), axis=1)
    gain_parts = jnp.stack(pieces(gain_part, 3), axis=0)
    gain_parts = jnp.pad(gain_parts, ((0, 13), (0, qkv_cols - shard_rows)))
    carried = jnp.broadcast_to(gain_parts[None], (exp_count, 16, qkv_cols))
    back = exchange(
        jnp.concatenate([grad_low.reshape(exp_count, own_rows, qkv_cols), carried], axis=1), "exp"
    )
    gain_sum = jnp.sum(back[:, own_rows : own_rows + 3, :shard_rows].astype(F32), axis=(0, 1))
    grad_gain_attn = gain_sum / gain_attn.astype(F32)
    normed_rows = jnp.einsum(
        "erk,edk->rd", back[:, :own_rows], all_qkv, preferred_element_type=F32
    )
    own_hat = lax.dynamic_slice_in_dim(attn_hat, exp_index * own_rows, own_rows, 0)
    own_scale = lax.dynamic_slice_in_dim(attn_scale, exp_index * own_rows, own_rows, 0)
    grad_hidden = resid_grad + norm_back(normed_rows, own_hat, own_scale, attn_gain)
    return (
        block_out,
        loss,
        grad_hidden,
        own_grad_qkv[:, :head_cols],
        own_grad_qkv[:, head_cols : head_cols + kv_cols],
        own_grad_qkv[:, head_cols + kv_cols :],
        own_grad_out,
        grad_gain_attn,
        tail[:, 0],
        tail[::2, 2],
        tail[:, 1],
        grad_w_gate,
        grad_w_up,
        grad_w_down,
    )


def solution(mesh):
    return jax.shard_map(
        on_device,
        mesh=mesh,
        in_specs=(
            P("ctx", None),
            P(("ctx", "exp"), None),
            P(),
            P(),
            P(("ctx", "exp"), None),
            P(("ctx", "exp"), None),
            P("ctx", "exp"),
            P("ctx", "exp"),
            P("ctx", "exp"),
            P("ctx", "exp"),
            P("ctx"),
            P("ctx"),
            P("ctx"),
            P("ctx"),
            P("ctx", None, "exp"),
            P("ctx", None, "exp"),
            P("ctx", "exp", None),
        ),
        out_specs=(
            P(("ctx", "exp"), None),
            P(),
            P(("ctx", "exp"), None),
            P("ctx", "exp"),
            P("ctx", "exp"),
            P("ctx", "exp"),
            P("ctx", "exp"),
            P("ctx"),
            P("ctx"),
            P("ctx"),
            P("ctx"),
            P("ctx", None, "exp"),
            P("ctx", None, "exp"),
            P("ctx", "exp", None),
        ),
        check_vma=False,
    )
```

time: 2160 us -> 635 us (0.29)
  blocking collectives: 710 us -> 78 us
  matrix products: 574 us -> 55.6 us
  waiting for transfers between devices: 475 us -> 206 us
  other arithmetic: 242 us -> 39.9 us
  Pallas kernels: 0 us -> 127 us
  local copies, waits for them, and re-layouts: 118 us -> 55.9 us
  starting transfers between devices: 6.48 us -> 43.7 us
    dot_general x49 -> x20, matrix products: 574 us -> 55.6 us  [the longest x16 47.2 us: dot(): return lax.dot_general(left, right, dims, preferred_element_type=F32)]
    all_to_all x3 -> x2, blocking collectives: 383 us -> 50.3 us  [exchange(): return lax.all_to_all(values, axis, split_axis=0, concat_axis=0, tiled=True)]
    reduce_scatter x7 -> x1, waiting for transfers between devices: 302 us -> 0.01 us  [on_device(): lax.psum_scatter(jnp.concatenate(strips, axis=0), 'exp', scatter_dimensio...]
    unnamed x3 -> x0, blocking collectives: 209 us -> none
    pallas_call x0 -> x4, Pallas kernels: none -> 127 us  [kernel_call(): pl.pallas_call(kernel, out_shape=tuple(outs), grid_spec=pltpu.PrefetchSca...]
    convert_element_type x15 -> x13, other arithmetic: 116 us -> 8.31 us  [the longest x1 1.7 us: on_device(): branch_rows = resid_grad.astype(BF16)]
    all_gather x4 -> x0, blocking collectives: 95.6 us -> none  [the longest x1 26.5 us: on_device(): lax.all_gather(w_out, 'ctx', axis=0, tiled=True)]
    reduce_sum x15 -> x9, other arithmetic: 90.8 us -> 1.72 us  [the longest x1 0.62 us: on_device(): valid_count = jnp.sum(valid.astype(F32))]
  transfers between devices with their start and end apart: 11 -> 20, of which waited for: 8 -> 13; matrix products, arithmetic and copies ran while one was open for 3% -> 19% of each run, Pallas kernels for 0% -> 20%
where the time goes in v1:
time: 635 us; the launch traced here: 625 us
  waiting for transfers between devices  206 us (32%)
  Pallas kernels  127 us (20%)
  blocking collectives  78 us (12%)
  local copies, waits for them, and re-layouts  55.9 us (9%)
  matrix products  55.6 us (9%)
  starting transfers between devices  43.7 us (7%)
  other arithmetic  39.9 us (6%)
  between operations  18.8 us (3%)
    all_to_all x7, waiting for transfers between devices, exchange(): return lax.all_to_all(values, axis, split_axis=0, concat_axis=0, tiled=True)  155 us
    pallas_call x4, Pallas kernels, kernel_call(): pl.pallas_call(kernel, out_shape=tuple(outs), grid_spec=pltpu.PrefetchSca...  127 us
    all_to_all x2, blocking collectives, exchange(): return lax.all_to_all(values, axis, split_axis=0, concat_axis=0, tiled=True)  50.3 us
    dot_general x16, matrix products, dot(): return lax.dot_general(left, right, dims, preferred_element_type=F32)  47.2 us
    all_gather x1, waiting for transfers between devices, on_device(): kv_all = lax.all_gather(own_kv, 'ctx', axis=0, tiled=True)  40.2 us
    all_to_all x7, starting transfers between devices, exchange(): return lax.all_to_all(values, axis, split_axis=0, concat_axis=0, tiled=True)  38.3 us
    unnamed x138, local copies, waits for them, and re-layouts  29.6 us
    psum x1, blocking collectives, on_device(): stats = lax.psum(stats.reshape(-1, LANES), 'exp').reshape(-1)  16.9 us
  transfers between devices with their start and end apart: 20, of which 13 were waited for; matrix products, arithmetic and copies ran while one was open for 19% of the time, Pallas kernels for 20%

profile of v1, /device:TPU:0, one launch (start us, length us, event | category | flops | bytes accessed | tf_op | source)
XLA Modules:
  0.0 624.7 jit_solution(10205131379230414698)
XLA Ops:
  13.1 8.5 %all-to-all-start = ((bf16[32,48,512]{2,1,0:T(8,128)(2,1)}), bf16[32,48,512]{2,1,0:T(8,128)(2,1)}, u32[]{:S(2)}, u32[]{:S(2)}) async-start(bf16[32,48,512]{2,1,0:T(8,128)(2,1)} %broadcast_in_dim.58), calls=%async_computation | async-start | bytes 3145728 | tf_op jit(solution)/shard_map/all_to_all | solution.py:511
  23.6 21.9 %all-to-all-done = bf16[32,48,512]{2,1,0:T(8,128)(2,1)} async-done(((bf16[32,48,512]{2,1,0:T(8,128)(2,1)}), bf16[32,48,512]{2,1,0:T(8,128)(2,1)}, u32[]{:S(2)}, u32[]{:S(2)}) %all-to-all-start) | async-done | bytes 1572896 | tf_op jit(solution)/shard_map/all_to_all | solution.py:511
  52.2 10.7 %psum.14 = f32[2,512]{1,0:T(2,128)S(1)} all-reduce(f32[2,512]{1,0:T(2,128)S(1)} %pad_maximum_fusion.14), channel_id=1, replica_groups=mesh['ctx'=32,'exp'=4] {'exp'}, use_global_device_ids=true, to_apply=%region_3.4 | all-reduce | flops 1024 | bytes 8192 | tf_op jit(solution)/shard_map/psum | solution.py:583
  65.0 4.7 copy.106
  77.1 40.2 %all-gather.10.cloned.1.call-done.kv = bf16[16384,256]{1,0:T(8,128)(2,1)} async-done(((bf16[512,256]{1,0:T(8,128)(2,1)}), bf16[16384,256]{1,0:T(8,128)(2,1)}) %all-gather.10.cloned.1.call-update) | async-done | bytes 8388624 | tf_op jit(solution)/shard_map/all_gather | solution.py:610
  117.4 28.8 %attend.1 = (f32[512,256]{1,0:T(8,128)S(1)}, f32[2,4,256]{2,1,0:T(4,128)S(1)}) custom-call(s32[128]{0:T(128)S(1)} %copy-done, s32[4]{0:T(128)S(1)} %get-tuple-element.137.own, bf16[512,256]{1,0:T(8,128)(2,1)} %get-tuple-element.44.q_in, bf16[16384,256]{1,0:T(8,128)(2,1)} %all-gather.10.cloned.1.call-done.kv), custom_call_target="tpu_custom_call" | custom-call | flops 20000000000 | bytes 8650752 | tf_op jit(solution)/shard_map/attend/pallas_call | solution.py:396
  146.9 12.4 %all_to_all.45 = bf16[4,128,256]{2,1,0:T(8,128)(2,1)S(1)} all-to-all(bf16[4,128,256]{2,1,0:T(8,128)(2,1)S(1)} %bitcast.201), channel_id=1, replica_groups=mesh['ctx'=32,'exp'=4] {'exp'}, dimensions={0} | all-to-all | bytes 524288 | tf_op jit(solution)/shard_map/all_to_all | solution.py:511
  159.4 4.3 all-gather.12.cloned.1.call-done
  171.0 5.3 all-to-all-start.2
  192.0 23.2 %all-to-all-done.2 = bf16[32,40,1024]{2,1,0:T(8,128)(2,1)} async-done(((bf16[32,40,1024]{2,1,0:T(8,128)(2,1)}), bf16[32,40,1024]{2,1,0:T(8,128)(2,1)}, u32[]{:S(2)}, u32[]{:S(2)}) %all-to-all-start.2) | async-done | bytes 2621472 | tf_op jit(solution)/shard_map/all_to_all | solution.py:511
  215.2 5.6 fusion.79
  226.2 4.9 all-to-all-start.3
  233.9 37.7 %all-to-all-done.3 = bf16[32,40,1024]{2,1,0:T(8,128)(2,1)} async-done(((bf16[32,40,1024]{2,1,0:T(8,128)(2,1)}), bf16[32,40,1024]{2,1,0:T(8,128)(2,1)}, u32[]{:S(2)}, u32[]{:S(2)}) %all-to-all-start.3) | async-done | bytes 2621472 | tf_op jit(solution)/shard_map/all_to_all | solution.py:511
  279.7 5.0 all-to-all-start.4
  285.3 35.5 %all-to-all-done.4 = bf16[32,40,1024]{2,1,0:T(8,128)(2,1)} async-done(((bf16[32,40,1024]{2,1,0:T(8,128)(2,1)}), bf16[32,40,1024]{2,1,0:T(8,128)(2,1)}, u32[]{:S(2)}, u32[]{:S(2)}) %all-to-all-start.4) | async-done | bytes 2621472 | tf_op jit(solution)/shard_map/all_to_all | solution.py:511
  320.7 6.1 multiply_convert_fusion.2
  326.9 5.8 convolution_convert_fusion.2
  332.7 37.9 %all_to_all.46 = bf16[32,40,1024]{2,1,0:T(8,128)(2,1)} all-to-all(bf16[32,40,1024]{2,1,0:T(8,128)(2,1)S(1)} %bitcast.195), channel_id=1, replica_groups=mesh['ctx'=32,'exp'=4] {'ctx'}, dimensions={0} | all-to-all | bytes 5242880 | tf_op jit(solution)/shard_map/all_to_all | solution.py:511
  377.0 4.2 all-to-all-start.6
  381.2 6.9 %all-to-all-done.6 = bf16[4,128,256]{1,2,0:T(8,128)(2,1)S(1)} async-done(((bf16[4,128,256]{1,2,0:T(8,128)(2,1)}), bf16[4,128,256]{1,2,0:T(8,128)(2,1)S(1)}, u32[]{:S(2)}, u32[]{:S(2)}) %all-to-all-start.6) | async-done | bytes 262176 | tf_op jit(solution)/shard_map/all_to_all | solution.py:511
  389.5 3.5 pad_maximum_fusion
  395.8 39.0 %query_grad.1 = f32[512,256]{1,0:T(8,128)S(1)} custom-call(s32[128]{0:T(128)S(1)} %copy-done, s32[4]{0:T(128)S(1)} %get-tuple-element.137.own, bf16[512,256]{1,0:T(8,128)(2,1)} %get-tuple-element.44.q_in, bf16[512,256]{1,0:T(8,128)(2,1)S(1)} %bitcast.175, f32[512,256]{1,0:T(8,128)S(1)} %get-tuple-element.39.o_in, f32[2,4,256]{2,1,0:T(4,128)S(1)} %get-tuple-element.48.lse_in, ...), custom_call_target="tpu_custom_call" | custom-call | flops 30000001024 | bytes 9969664 | tf_op jit(solution)/shard_map/query_grad/pallas_call | solution.py:396
  440.5 3.7 fusion.82
  445.9 4.6 fusion.81
  450.9 13.2 %maximum_maximum_fusion = f32[4096,384]{0,1:T(8,128)} fusion(f32[1024,128]{0,1:T(8,128)S(1)} %get-tuple-element.153, f32[1024,128]{0,1:T(8,128)S(1)} %get-tuple-element.141, f32[1024,128]{0,1:T(8,128)S(1)} %get-tuple-element.142, f32[1024,128]{0,1:T(8,128)S(1)} %get-tuple-element.154, f32[1024,128]{0,1:T(8,128)S(1)} %get-tuple-element.143, ...), kind=kLoop, calls=%fused_computation | loop fusion | flops 17301504 | bytes 12582912 | tf_op jit(solution)/shard_map/concatenate | solution.py:719
  473.8 57.4 %pair_grad.1 = f32[512,256]{1,0:T(8,128)S(1)} custom-call(s32[128]{0:T(128)S(1)} %copy-done, s32[4]{0:T(128)S(1)} %get-tuple-element.137.own, bf16[512,256]{1,0:T(8,128)(2,1)} %get-tuple-element.37.kv_in, f32[512,128]{1,0:T(8,128)S(1)} %get-tuple-element.193.cos_ref, f32[512,128]{1,0:T(8,128)S(1)} %get-tuple-element.194.sin_ref, ...), custom_call_target="tpu_custom_call" | custom-call | flops 40000000000 | bytes 18874368 | tf_op jit(solution)/shard_map/pair_grad/pallas_call | solution.py:396
  532.4 16.9 %psum.15 = f32[32,128]{1,0:T(8,128)S(1)} all-reduce(f32[32,128]{1,0:T(8,128)S(1)} %bitcast.218), channel_id=1, replica_groups=mesh['ctx'=32,'exp'=4] {'exp'}, use_global_device_ids=true, to_apply=%region_17.18 | all-reduce | flops 4096 | bytes 32768 | tf_op jit(solution)/shard_map/psum | solution.py:760
  557.4 6.8 %all-to-all-start.7 = ((bf16[32,32,896]{2,1,0:T(8,128)(2,1)}), bf16[32,32,896]{2,1,0:T(8,128)(2,1)S(1)}, u32[]{:S(2)}, u32[]{:S(2)}) async-start(bf16[32,32,896]{2,1,0:T(8,128)(2,1)} %fusion.2), calls=%async_computation.7 | async-start | bytes 3670016 | tf_op jit(solution)/shard_map/all_to_all | solution.py:511
  566.6 24.5 %all-to-all-done.7 = bf16[32,32,896]{2,1,0:T(8,128)(2,1)S(1)} async-done(((bf16[32,32,896]{2,1,0:T(8,128)(2,1)}), bf16[32,32,896]{2,1,0:T(8,128)(2,1)S(1)}, u32[]{:S(2)}, u32[]{:S(2)}) %all-to-all-start.7) | async-done | bytes 1835040 | tf_op jit(solution)/shard_map/all_to_all | solution.py:511
  593.2 3.5 all-to-all-start.8
  599.9 5.6 all-to-all-done.8
  605.5 3.9 multiply_reduce_fusion.1
  (293 shorter events, 113.6 us)
Async XLA Ops:
  7.3 57.7 %all-gather.16.cloned.1.call-start = ((), (), s32[]{:S(2)}) async-start(), calls=%async_computation.14 | async-start | bytes 3932160 | tf_op jit(solution)/shard_map/all_gather | solution.py:574
  13.1 32.4 %all-to-all-start = ((bf16[32,48,512]{2,1,0:T(8,128)(2,1)}), bf16[32,48,512]{2,1,0:T(8,128)(2,1)}, u32[]{:S(2)}, u32[]{:S(2)}) async-start(bf16[32,48,512]{2,1,0:T(8,128)(2,1)} %broadcast_in_dim.58), calls=%async_computation | async-start | bytes 3145728 | tf_op jit(solution)/shard_map/all_to_all | solution.py:511
  21.6 95.8 %all-gather.10.cloned.1.call-start = ((), (), s32[]{:S(2)}) async-start(), calls=%async_computation.10 | async-start | bytes 8650752 | tf_op jit(solution)/shard_map/all_gather | solution.py:610
  63.0 371.8 %copy-start.27 = (f32[1,512]{1,0:T(1,128)}, f32[1,512]{1,0:T(1,128)S(1)}, u32[]{:S(2)}) copy-start(f32[1,512]{1,0:T(1,128)S(1)} %get-tuple-element.180) | copy-start | bytes 6148
  63.5 371.3 %copy-start.39 = (f32[256]{0:T(256)}, f32[256]{0:T(256)S(1)}, u32[]{:S(2)}) copy-start(f32[256]{0:T(256)S(1)} %dynamic_slice.27) | copy-start | bytes 3076
  69.7 94.0 %all-gather.12.cloned.1.call-start = ((), (), s32[]{:S(2)}) async-start(), calls=%async_computation.11 | async-start | bytes 2162688 | tf_op jit(solution)/shard_map/all_gather | solution.py:612
  69.8 3.8 collective-permute-start
  69.8 5.3 collective-permute-start.1
  71.4 4.9 collective-permute-start.2
  117.3 154.2 %all-gather.14.cloned.1.call-start = ((), (), s32[]{:S(2)}) async-start(), calls=%async_computation.12 | async-start | bytes 8650752 | tf_op jit(solution)/shard_map/all_gather | solution.py:618
  171.0 44.2 %all-to-all-start.2 = ((bf16[32,40,1024]{2,1,0:T(8,128)(2,1)}), bf16[32,40,1024]{2,1,0:T(8,128)(2,1)}, u32[]{:S(2)}, u32[]{:S(2)}) async-start(bf16[32,40,1024]{2,1,0:T(8,128)(2,1)} %bitcast.186), calls=%async_computation.2 | async-start | bytes 5242880 | tf_op jit(solution)/shard_map/all_to_all | solution.py:511
  192.0 31.1 %copy-start.20 = (bf16[1024,128]{1,0:T(8,128)(2,1)}, bf16[1024,128]{1,0:T(8,128)(2,1)S(1)}, u32[]{:S(2)}) copy-start(bf16[1024,128]{1,0:T(8,128)(2,1)S(1)} %get-tuple-element.148) | copy-start | bytes 786436
  192.0 31.1 %copy-start.21 = (bf16[1024,128]{1,0:T(8,128)(2,1)}, bf16[1024,128]{1,0:T(8,128)(2,1)S(1)}, u32[]{:S(2)}) copy-start(bf16[1024,128]{1,0:T(8,128)(2,1)S(1)} %get-tuple-element.149) | copy-start | bytes 786436
  226.2 45.4 %all-to-all-start.3 = ((bf16[32,40,1024]{2,1,0:T(8,128)(2,1)}), bf16[32,40,1024]{2,1,0:T(8,128)(2,1)}, u32[]{:S(2)}, u32[]{:S(2)}) async-start(bf16[32,40,1024]{2,1,0:T(8,128)(2,1)} %bitcast.194), calls=%async_computation.3 | async-start | bytes 5242880 | tf_op jit(solution)/shard_map/all_to_all | solution.py:511
  276.3 97.5 %copy-start.4 = (f32[128,1024]{1,0:T(8,128)}, f32[128,1024]{1,0:T(8,128)S(1)}, u32[]{:S(2)}) copy-start(f32[128,1024]{1,0:T(8,128)S(1)} %fusion.3) | copy-start | bytes 1572868
  279.7 41.0 %all-to-all-start.4 = ((bf16[32,40,1024]{2,1,0:T(8,128)(2,1)}), bf16[32,40,1024]{2,1,0:T(8,128)(2,1)}, u32[]{:S(2)}, u32[]{:S(2)}) async-start(bf16[32,40,1024]{2,1,0:T(8,128)(2,1)} %bitcast.188), calls=%async_computation.4 | async-start | bytes 5242880 | tf_op jit(solution)/shard_map/all_to_all | solution.py:511
  284.7 85.9 %all-gather.18.cloned.1.call-start = ((), (), s32[]{:S(2)}) async-start(), calls=%async_computation.15 | async-start | bytes 5242880 | tf_op jit(solution)/shard_map/all_gather | solution.py:654
  377.0 11.1 %all-to-all-start.6 = ((bf16[4,128,256]{1,2,0:T(8,128)(2,1)}), bf16[4,128,256]{1,2,0:T(8,128)(2,1)S(1)}, u32[]{:S(2)}, u32[]{:S(2)}) async-start(bf16[4,128,256]{1,2,0:T(8,128)(2,1)} %fusion.6), calls=%async_computation.6 | async-start | bytes 524288 | tf_op jit(solution)/shard_map/all_to_all | solution.py:511
  381.2 59.3 %all-gather.20.cloned.1.call-start = ((), (), s32[]{:S(2)}) async-start(), calls=%async_computation.16 | async-start | bytes 9461760 | tf_op jit(solution)/shard_map/all_gather | solution.py:697
  389.5 222.6 %reduce-scatter.2.cloned.1.call-start = ((), (), s32[]{:S(2)}) async-start(), calls=%async_computation.13 | async-start | bytes 7864320 | tf_op jit(solution)/shard_map/reduce_scatter | solution.py:718
  393.0 43.6 %collective-permute-start.3 = (bf16[128,1024]{1,0:T(8,128)(2,1)S(1)}, bf16[128,1024]{1,0:T(8,128)(2,1)S(1)}, u32[]{:S(2)}, u32[]{:S(2)}) collective-permute-start(bf16[128,1024]{1,0:T(8,128)(2,1)S(1)} %copy-done.10), channel_id=1, source_target_pairs={{0,3},{1,0},{2,1},{3,2},{4,7},{5,4},{6,5},{7,6},{8,11},{9,8},{10,9... | collective-permute-start | bytes 786440 | tf_op jit(solution)/shard_map/ppermute | solution.py:521
  394.2 43.2 %collective-permute-start.4 = (bf16[128,1024]{1,0:T(8,128)(2,1)S(1)}, bf16[128,1024]{1,0:T(8,128)(2,1)}, u32[]{:S(2)}, u32[]{:S(2)}) collective-permute-start(bf16[128,1024]{1,0:T(8,128)(2,1)S(1)} %copy-done.10), channel_id=1, source_target_pairs={{0,2},{1,3},{2,0},{3,1},{4,6},{5,7},{6,4},{7,5},{8,10},{9,11},{10,... | collective-permute-start | bytes 786440 | tf_op jit(solution)/shard_map/ppermute | solution.py:521
  395.6 68.4 %collective-permute-start.5 = (bf16[128,1024]{1,0:T(8,128)(2,1)S(1)}, bf16[128,1024]{1,0:T(8,128)(2,1)}, u32[]{:S(2)}, u32[]{:S(2)}) collective-permute-start(bf16[128,1024]{1,0:T(8,128)(2,1)S(1)} %copy-done.10), channel_id=1, source_target_pairs={{0,1},{1,2},{2,3},{3,0},{4,5},{5,6},{6,7},{7,4},{8,9},{9,10},{10,1... | collective-permute-start | bytes 786440 | tf_op jit(solution)/shard_map/ppermute | solution.py:521
  473.7 57.5 %copy-start.30 = (f32[1,512]{1,0:T(1,128)S(1)}, f32[1,512]{1,0:T(1,128)}, u32[]{:S(2)}) copy-start(f32[1,512]{1,0:T(1,128)} %copy-done.29) | copy-start | bytes 6148
  473.7 57.5 %copy-start.46 = (f32[128]{0:T(128)S(1)}, f32[128]{0:T(128)}, u32[]{:S(2)}) copy-start(f32[128]{0:T(128)} %copy-done.45) | copy-start | bytes 1540
  473.7 58.0 %copy-start.33 = (f32[4096]{0:T(1024)S(1)}, f32[4096]{0:T(1024)}, u32[]{:S(2)}) copy-start(f32[4096]{0:T(1024)} %constant_dynamic-update-slice_fusion.10) | copy-start | bytes 49156
  473.7 58.0 %copy-start.35 = (f32[1024]{0:T(1024)S(1)}, f32[1024]{0:T(1024)}, u32[]{:S(2)}) copy-start(f32[1024]{0:T(1024)} %copy-done.34) | copy-start | bytes 12292
  473.7 58.0 %copy-start.40 = (f32[1024]{0:T(1024)S(1)}, f32[1024]{0:T(1024)}, u32[]{:S(2)}) copy-start(f32[1024]{0:T(1024)} %get-tuple-element.130) | copy-start | bytes 12292
  473.8 79.2 %copy-start.28 = (f32[1,512]{1,0:T(1,128)S(1)}, f32[1,512]{1,0:T(1,128)}, u32[]{:S(2)}) copy-start(f32[1,512]{1,0:T(1,128)} %copy-done.27) | copy-start | bytes 6148
  557.4 33.7 %all-to-all-start.7 = ((bf16[32,32,896]{2,1,0:T(8,128)(2,1)}), bf16[32,32,896]{2,1,0:T(8,128)(2,1)S(1)}, u32[]{:S(2)}, u32[]{:S(2)}) async-start(bf16[32,32,896]{2,1,0:T(8,128)(2,1)} %fusion.2), calls=%async_computation.7 | async-start | bytes 3670016 | tf_op jit(solution)/shard_map/all_to_all | solution.py:511
  564.9 27.2 %copy-start.25 = (bf16[32,512]{1,0:T(8,128)(2,1)S(1)}, bf16[32,512]{1,0:T(8,128)(2,1)}, u32[]{:S(2)}) copy-start(bf16[32,512]{1,0:T(8,128)(2,1)} %copy-done.24) | copy-start | bytes 98308
  593.2 12.3 %all-to-all-start.8 = ((bf16[4,144,512]{2,1,0:T(8,128)(2,1)}), bf16[4,144,512]{2,1,0:T(8,128)(2,1)S(1)}, u32[]{:S(2)}, u32[]{:S(2)}) async-start(bf16[4,144,512]{2,1,0:T(8,128)(2,1)} %pad_maximum_fusion.3), calls=%async_computation.8 | async-start | bytes 1179648 | tf_op jit(solution)/shard_map/all_to_all | solution.py:511
  (41 other events, 259.1 us)
Sparse Core Ops, SparseCore 0:
  11.6 42.0 all-gather.15
  69.8 47.4 all-gather.9
  120.2 43.4 all-gather.11
  166.4 94.9 all-gather.13
  286.9 49.6 all-gather.17
  389.6 50.8 all-gather.19
  464.2 65.4 reduce-scatter.1

commit v2 on v1

--- a/solution.py
+++ b/solution.py
@@ -386,6 +386,52 @@
         out_ref[rows, LANES:] = collect(dv_ref, blk)
 
 
+def down_strips(w_ref, pair, width):
+    strips = [w_ref[u, :, 2 * width : 3 * width] for u in (2 * pair, 2 * pair + 1)]
+    return jnp.concatenate(strips, axis=1)
+
+
+def expert_kernel(quarters, width, x_ref, w_ref, out_ref, gate_ref, up_ref):
+    acts = []
+    for u in range(quarters):
+        cols = slice(u * width, (u + 1) * width)
+        pre = dot(x_ref[...], w_ref[u, :, : 2 * width], NN)
+        gate, up = pre[:, :width], pre[:, width:]
+        gate_ref[:, cols] = gate
+        up_ref[:, cols] = up
+        acts.append((gate * jax.nn.sigmoid(gate) * up).astype(BF16))
+    out = None
+    for pair in range(quarters // 2):
+        act = jnp.concatenate(acts[2 * pair : 2 * pair + 2], axis=1)
+        part = dot(act, down_strips(w_ref, pair, width), NT)
+        out = part if out is None else out + part
+    out_ref[...] = out.astype(BF16)
+
+
+def expert_grad_kernel(
+    quarters, width, dy_ref, gate_ref, up_ref, w_ref, dx_ref, dgate_ref, dup_ref, act_ref
+):
+    total = None
+    for pair in range(quarters // 2):
+        both = dot(dy_ref[...], down_strips(w_ref, pair, width), NN)
+        for side in range(2):
+            u = 2 * pair + side
+            cols = slice(u * width, (u + 1) * width)
+            act_grad = both[:, side * width : (side + 1) * width]
+            gate, up = gate_ref[:, cols], up_ref[:, cols]
+            sig = jax.nn.sigmoid(gate)
+            gate_act = gate * sig
+            act_ref[:, cols] = (gate_act * up).astype(BF16)
+            gate_grad = (act_grad * up * sig * (1.0 + gate * (1.0 - sig))).astype(BF16)
+            up_grad = (act_grad * gate_act).astype(BF16)
+            dgate_ref[:, cols] = gate_grad
+            dup_ref[:, cols] = up_grad
+            grads = jnp.concatenate([gate_grad, up_grad], axis=1)
+            part = dot(grads, w_ref[u, :, : 2 * width], NT)
+            total = part if total is None else total + part
+    dx_ref[...] = total.astype(BF16)
+
+
 def block_of_whole(shape):
     return pl.BlockSpec(shape, lambda i, *_: (0,) * len(shape))
 
@@ -407,6 +453,54 @@
         cost_estimate=pl.CostEstimate(flops=flops, bytes_accessed=moved, transcendentals=0),
         name=name,
     )(*prefetch, *(x for x, _ in ins))
+
+
+def by_rows(kernel, name, rows, ins, outs, flops):
+    def spec(shape):
+        if len(shape) == 3:
+            return pl.BlockSpec(shape, lambda i: (0, 0, 0))
+        return pl.BlockSpec((rows, shape[1]), lambda i: (i, 0))
+
+    return pl.pallas_call(
+        kernel,
+        out_shape=tuple(outs),
+        grid=(outs[0].shape[0] // rows,),
+        in_specs=[spec(x.shape) for x in ins],
+        out_specs=tuple(spec(out.shape) for out in outs),
+        compiler_params=pltpu.CompilerParams(vmem_limit_bytes=40 << 20),
+        cost_estimate=pl.CostEstimate(flops=flops, bytes_accessed=10**7, transcendentals=0),
+        name=name,
+    )(*ins)
+
+
+def expert_forward(rows_in, weights):
+    slots, model_width = rows_in.shape
+    quarters, _, cols = weights.shape
+    width = cols // 3
+    hidden = jax.ShapeDtypeStruct((slots, quarters * width), F32)
+    return by_rows(
+        functools.partial(expert_kernel, quarters, width),
+        "expert",
+        slots // 5,
+        [rows_in, weights],
+        [jax.ShapeDtypeStruct((slots, model_width), BF16), hidden, hidden],
+        6 * slots * model_width * quarters * width,
+    )
+
+
+def expert_backward(rows_grad, gate_pre, up_pre, weights):
+    slots, model_width = rows_grad.shape
+    quarters, _, cols = weights.shape
+    width = cols // 3
+    hidden = jax.ShapeDtypeStruct((slots, quarters * width), BF16)
+    return by_rows(
+        functools.partial(expert_grad_kernel, quarters, width),
+        "expert_grad",
+        slots // 5,
+        [rows_grad, gate_pre, up_pre, weights],
+        [jax.ShapeDtypeStruct((slots, model_width), BF16), hidden, hidden, hidden],
+        6 * slots * model_width * quarters * width,
+    )
 
 
 def turn_heads(projected, scales, gain, cosine, sine):
@@ -515,12 +609,32 @@
     return exchange(jnp.broadcast_to(values[None], (count,) + values.shape), axis)
 
 
-def gather_small(values, axis, index, count):
-    come = [values]
+def shifted(values, axis, count):
+    parts = [values]
     for step in range(1, count):
-        come.append(lax.ppermute(values, axis, [(i, (i + step) % count) for i in range(count)]))
-    twice = jnp.stack(come[::-1] + come[:0:-1], axis=0)
-    return lax.dynamic_slice_in_dim(twice, count - 1 - index, count, 0)
+        parts.append(lax.ppermute(values, axis, [(i, (i + step) % count) for i in range(count)]))
+    return parts
+
+
+def gather_short(values, axis, index, count):
+    parts = shifted(values, axis, count)
+    ordered = []
+    for place in range(count):
+        back = (index - place) % count
+        part = parts[0]
+        for step in range(1, count):
+            part = jnp.where(back == step, parts[step], part)
+        ordered.append(part)
+    return jnp.stack(ordered, axis=0)
+
+
+def ride_along(values):
+    parts = jnp.concatenate(pieces(values, 3), axis=-1)
+    return jnp.pad(parts, ((0, 0), (0, 0), (0, LANES - parts.shape[-1])))
+
+
+def parted(sums, count):
+    return sum(sums[:, i * count : (i + 1) * count] for i in range(3))
 
 
 def on_device(
@@ -556,11 +670,10 @@
     shard_rows = w_query.shape[0]
 
     own_qkv = jnp.concatenate([w_query, w_key, w_value], axis=1)
+    full_qkv = spread(own_qkv, "ctx", ctx_count).reshape(model_width, qkv_cols)
     gain_row = jnp.concatenate([gain_attn, gain_query, gain_ffn, gain_key])
-    gain_rows = jnp.pad(gain_row, (0, 16 * qkv_cols - gain_row.shape[0])).reshape(16, qkv_cols)
-    first_parts = spread(jnp.concatenate([own_qkv, gain_rows], axis=0), "ctx", ctx_count)
-    full_qkv = first_parts[:, :shard_rows].reshape(model_width, qkv_cols)
-    gains = first_parts[:, shard_rows:].reshape(ctx_count, -1).astype(F32)
+    gain_row = jnp.pad(gain_row, (0, -gain_row.shape[0] % LANES)).reshape(-1, LANES)
+    gains = spread(gain_row, "ctx", ctx_count).reshape(ctx_count, -1).astype(F32)
     attn_gain = gains[:, :shard_rows].reshape(model_width)
     query_gain_all = gains[:, shard_rows : 2 * shard_rows].reshape(model_width)
     ffn_gain = gains[:, 2 * shard_rows : 3 * shard_rows].reshape(model_width)
@@ -568,7 +681,6 @@
     query_gain = lax.dynamic_slice_in_dim(query_gain_all, exp_index * head_cols, head_cols)
     key_gain = lax.dynamic_slice_in_dim(key_gain_all, exp_index * kv_cols, kv_cols)
 
-    out_strip = gather_small(w_out, "exp", exp_index, exp_count)
     width = w_gate.shape[2]
     own_expert = jnp.concatenate([w_gate[0], w_up[0], w_down[0].T], axis=1)
     expert = lax.all_gather(own_expert, "exp", axis=0, tiled=False)
@@ -603,18 +715,19 @@
         sine,
     )
     own_kv, expert = lax.optimization_barrier((own_kv, expert))
-    gate_strips = [expert[u, :, :width] for u in range(exp_count)]
-    up_strips = [expert[u, :, width : 2 * width] for u in range(exp_count)]
-    wide_gate_up = jnp.concatenate(gate_strips + up_strips, axis=1)
-    wide_down = jnp.concatenate([expert[u, :, 2 * width :] for u in range(exp_count)], axis=1)
     kv_all = lax.all_gather(own_kv, "ctx", axis=0, tiled=True)
-    kv_all, out_strip = lax.optimization_barrier((kv_all, out_strip))
-    full_out = lax.all_gather(out_strip, "ctx", axis=1, tiled=True)
+    own_out, _ = lax.optimization_barrier((w_out, own_kv))
+    full_out = gather_short(
+        spread(own_out, "ctx", ctx_count).reshape(model_width, head_cols),
+        "exp",
+        exp_index,
+        exp_count,
+    )
     heads_f, lse = attend(block_of, own_blocks, queries_rot, kv_all)
     heads_low = heads_f.astype(BF16)
 
     own_heads = exchange(heads_low.reshape(exp_count, own_rows, head_cols), "exp")
-    own_heads, full_out, later_q = lax.optimization_barrier((own_heads, full_out, queries_rot))
+    own_heads, later_q = lax.optimization_barrier((own_heads, queries_rot))
     q_all = lax.all_gather(later_q, "ctx", axis=0, tiled=True)
     attn_rows = jnp.einsum("erk,eok->ro", own_heads, full_out, preferred_element_type=F32)
     hidden_rows = lax.dynamic_slice_in_dim(hidden_f, exp_index * own_rows, own_rows, 0)
@@ -643,16 +756,12 @@
         )
 
     expert_in = send(dot(pick, normed_ffn, NN).astype(BF16))
-    pre = dot(expert_in, wide_gate_up, NN)
-    gate_pre = pre[:, : exp_count * width]
-    up_pre = pre[:, exp_count * width :]
-    gate_sig = jax.nn.sigmoid(gate_pre)
-    gate_act = gate_pre * gate_sig
-    hidden_act = (gate_act * up_pre).astype(BF16)
-    returned = send(dot(hidden_act, wide_down, NT).astype(BF16))
+    expert_out, gate_pre, up_pre = expert_forward(expert_in, expert)
+    returned = send(expert_out)
     returned, q_all, later_qkv = lax.optimization_barrier((returned, q_all, full_qkv))
     all_qkv = lax.all_gather(later_qkv, "exp", axis=0, tiled=False)
-    moe_rows = sum(dot(part, returned, TN) for part in pieces(weigh, 2))
+    moe_parts = dot(jnp.concatenate(pieces(weigh, 2), axis=1), returned, TN)
+    moe_rows = moe_parts[:own_rows] + moe_parts[own_rows:]
     block_out = resid + moe_rows
 
     row_start = (ctx_index * exp_count + exp_index) * own_rows
@@ -661,13 +770,16 @@
     misfit = block_out - teacher.astype(F32)
     local_loss = jnp.sum(row_valid[:, None] * misfit * misfit)
     out_grad_rows = misfit * row_valid[:, None] * (token_total / valid_count)
-    copy_grad = sum(dot(pick, part, NN) for part in pieces(out_grad_rows, 2))
+    copy_grad = dot(
+        jnp.concatenate([pick, pick], axis=1),
+        jnp.concatenate(pieces(out_grad_rows, 2), axis=0),
+        NN,
+    )
     grad_copies = send((slot_gate * copy_grad).astype(BF16))
-    act_grad = dot(grad_copies, wide_down, NN)
-    gate_grad = (act_grad * up_pre * gate_sig * (1.0 + gate_pre * (1.0 - gate_sig))).astype(BF16)
-    up_grad = (act_grad * gate_act).astype(BF16)
-    both_grad = jnp.concatenate([gate_grad, up_grad], axis=1)
-    arrived_grad = send(dot(both_grad, wide_gate_up, NT).astype(BF16))
+    input_grad, gate_grad, up_grad, hidden_act = expert_backward(
+        grad_copies, gate_pre, up_pre, expert
+    )
+    arrived_grad = send(input_grad)
     arrived_grad, all_qkv = lax.optimization_barrier((arrived_grad, all_qkv))
     ffn_normed_grad = dot(pick, arrived_grad, TN)
 
@@ -677,10 +789,7 @@
 
     do_rows = jnp.einsum("ro,eok->erk", branch_rows, full_out, preferred_element_type=F32)
     out_grad = exchange(do_rows.astype(BF16), "exp").reshape(ctx_rows, head_cols)
-    branch_grad = gather_small(branch_rows, "exp", exp_index, exp_count).reshape(
-        ctx_rows, model_width
-    )
-    grad_out = dot(branch_grad, heads_low, TN)
+    branch_parts = shifted(branch_rows, "exp", exp_count)
     head_of = jnp.arange(head_cols, dtype=jnp.int32)[None] // HD
     head_ones = (head_of == jnp.arange(4, dtype=jnp.int32)[:, None]).astype(F32)
     delta = lax.dot_general(
@@ -701,26 +810,62 @@
         block_of, own_blocks, queries_rot, out_grad, heads_f, lse, cosine, sine, kv_all
     )
 
-    do_all, expert_in, both_grad, hidden_act, grad_copies = lax.optimization_barrier(
-        (do_all, expert_in, both_grad, hidden_act, grad_copies)
-    )
-    gate_up_part = dot(expert_in, both_grad, TN)
-    down_part = dot(grad_copies, hidden_act, TN)
-    strips = []
-    for u in range(exp_count):
-        own = slice(u * width, (u + 1) * width)
-        of_up = slice((exp_count + u) * width, (exp_count + u + 1) * width)
-        strips.append(
-            jnp.concatenate(
-                [gate_up_part[:, own], gate_up_part[:, of_up], down_part[:, own]], axis=1
-            )
-        )
-    grad_expert = lax.psum_scatter(
-        jnp.concatenate(strips, axis=0), "exp", scatter_dimension=0, tiled=True
-    )
-    grad_w_gate = grad_expert[None, :, :width]
-    grad_w_up = grad_expert[None, :, width : 2 * width]
-    grad_w_down = grad_expert[:, 2 * width :].T[None]
+    grad_out = None
+    for step, part in enumerate(branch_parts):
+        first = (exp_index - step) % exp_count * own_rows
+        term = dot(part, lax.dynamic_slice_in_dim(heads_low, first, own_rows, 0), TN)
+        grad_out = term if grad_out is None else grad_out + term
+
+    gate_part = dot(expert_in, gate_grad, TN)
+    up_part = dot(expert_in, up_grad, TN)
+    down_part = dot(hidden_act, grad_copies, TN)
+    gate_part = gate_part.reshape(model_width, exp_count, width).transpose(1, 0, 2)
+    up_part = up_part.reshape(model_width, exp_count, width).transpose(1, 0, 2)
+    do_all, gate_part, up_part, down_part = lax.optimization_barrier(
+        (do_all, gate_part, up_part, down_part)
+    )
+    grad_w_gate = lax.psum_scatter(gate_part, "exp", scatter_dimension=0, tiled=True)
+    grad_w_up = lax.psum_scatter(up_part, "exp", scatter_dimension=0, tiled=True)
+    grad_w_down = lax.psum_scatter(down_part, "exp", scatter_dimension=0, tiled=True)[None]
+
+    query_gain_part = jnp.sum(query_n_grad * query_hat, axis=0)
+    query_hat_grad = query_n_grad * query_gain
+    early = jnp.concatenate(
+        [
+            jnp.sum(query_hat_grad * query_hat, axis=1),
+            lax.dynamic_update_slice_in_dim(
+                jnp.zeros((model_width,), F32), query_gain_part, exp_index * head_cols, 0
+            ),
+            ffn_gain_part,
+            jnp.full((4 * LANES,), local_loss),
+        ]
+    )
+    early = lax.psum(early.reshape(-1, LANES), "exp").reshape(-1)
+    do_all, early = lax.optimization_barrier((do_all, early))
+    query_stat = early[:ctx_rows, None] / model_width
+    query_low = (query_scale * (query_hat_grad - query_hat * query_stat)).astype(BF16)
+    early_sums = jnp.stack(
+        [
+            early[ctx_rows : ctx_rows + model_width].reshape(ctx_count, shard_rows),
+            early[ctx_rows + model_width : ctx_rows + 2 * model_width].reshape(
+                ctx_count, shard_rows
+            ),
+            jnp.broadcast_to(early[-1], (ctx_count, shard_rows)),
+        ],
+        axis=-1,
+    )
+    early_shards = exchange(
+        jnp.concatenate(
+            [
+                dot(normed, query_low, TN).astype(BF16).reshape(ctx_count, shard_rows, head_cols),
+                grad_out.astype(BF16).reshape(ctx_count, shard_rows, head_cols),
+                ride_along(early_sums),
+            ],
+            axis=2,
+        ),
+        "ctx",
+    )
+    early_back = exchange(query_low.reshape(exp_count, own_rows, head_cols), "exp")
 
     aux = jnp.sum(
         do_all[:, ctx_rows:].reshape(ctx_count, 3, 2, 8, 2 * BLK).astype(F32), axis=1
@@ -738,76 +883,51 @@
     )
     key_n_grad = pair_grads[:, :kv_cols]
     value_grad = pair_grads[:, kv_cols:].astype(BF16)
-    query_gain_part = jnp.sum(query_n_grad * query_hat, axis=0)
     key_gain_part = jnp.sum(key_n_grad * key_hat, axis=0)
-    query_hat_grad = query_n_grad * query_gain
     key_hat_grad = key_n_grad * key_gain
-
-    stats = jnp.concatenate(
+    late = jnp.concatenate(
         [
-            jnp.sum(query_hat_grad * query_hat, axis=1),
             jnp.sum(key_hat_grad * key_hat, axis=1),
-            lax.dynamic_update_slice_in_dim(
-                jnp.zeros((model_width,), F32), query_gain_part, exp_index * head_cols, 0
-            ),
-            ffn_gain_part,
             lax.dynamic_update_slice_in_dim(
                 jnp.zeros((kv_total,), F32), key_gain_part, exp_index * kv_cols, 0
             ),
-            jnp.full((kv_total,), local_loss),
         ]
     )
-    stats = lax.psum(stats.reshape(-1, LANES), "exp").reshape(-1)
-    query_stat = stats[:ctx_rows, None] / model_width
-    key_stat = stats[ctx_rows : 2 * ctx_rows, None] / kv_total
-    sums = stats[2 * ctx_rows :]
-    query_low = (query_scale * (query_hat_grad - query_hat * query_stat)).astype(BF16)
+    late = lax.psum(late.reshape(-1, LANES), "exp").reshape(-1)
+    key_stat = late[:ctx_rows, None] / kv_total
     key_low = (key_scale * (key_hat_grad - key_hat * key_stat)).astype(BF16)
-    grad_low = jnp.concatenate([query_low, key_low, value_grad], axis=1)
-
-    grad_qkv = dot(normed, grad_low, TN)
-    wide_sums = jnp.stack(
-        [
-            sums[:model_width].reshape(ctx_count, shard_rows),
-            sums[model_width : 2 * model_width].reshape(ctx_count, shard_rows),
-            jnp.repeat(
-                sums[2 * model_width : 2 * model_width + kv_total].reshape(ctx_count, -1), 2, axis=1
-            ),
-            jnp.broadcast_to(sums[-1], (ctx_count, shard_rows)),
-        ],
-        axis=-1,
-    )
-    sum_parts = jnp.concatenate(pieces(wide_sums, 3), axis=-1)
-    sum_parts = jnp.pad(sum_parts, ((0, 0), (0, 0), (0, LANES - sum_parts.shape[-1])))
-    shards = exchange(
+    pair_low = jnp.concatenate([key_low, value_grad], axis=1)
+    key_sums = jnp.repeat(late[ctx_rows:].reshape(ctx_count, -1), 2, axis=1)[:, :, None]
+    late_shards = exchange(
         jnp.concatenate(
             [
-                grad_qkv.astype(BF16).reshape(ctx_count, shard_rows, qkv_cols),
-                grad_out.astype(BF16).reshape(ctx_count, shard_rows, head_cols),
-                sum_parts,
+                dot(normed, pair_low, TN).astype(BF16).reshape(ctx_count, shard_rows, 2 * kv_cols),
+                ride_along(key_sums),
             ],
             axis=2,
         ),
         "ctx",
     )
-    shards = jnp.sum(shards.astype(F32), axis=0)
-    own_grad_qkv = shards[:, :qkv_cols]
-    own_grad_out = shards[:, qkv_cols : qkv_cols + head_cols]
-    tail = shards[:, qkv_cols + head_cols :]
-    tail = tail[:, 0:4] + tail[:, 4:8] + tail[:, 8:12]
-    loss = tail[0, 3] / (valid_count * model_width)
-
-    gain_part = jnp.sum(own_grad_qkv * own_qkv.astype(F32), axis=1)
-    gain_parts = jnp.stack(pieces(gain_part, 3), axis=0)
-    gain_parts = jnp.pad(gain_parts, ((0, 13), (0, qkv_cols - shard_rows)))
-    carried = jnp.broadcast_to(gain_parts[None], (exp_count, 16, qkv_cols))
-    back = exchange(
-        jnp.concatenate([grad_low.reshape(exp_count, own_rows, qkv_cols), carried], axis=1), "exp"
-    )
-    gain_sum = jnp.sum(back[:, own_rows : own_rows + 3, :shard_rows].astype(F32), axis=(0, 1))
-    grad_gain_attn = gain_sum / gain_attn.astype(F32)
+    late_back = exchange(pair_low.reshape(exp_count, own_rows, 2 * kv_cols), "exp")
+    early_shards = jnp.sum(early_shards.astype(F32), axis=0)
+    late_shards = jnp.sum(late_shards.astype(F32), axis=0)
+    grad_w_query = early_shards[:, :head_cols]
+    grad_w_out = early_shards[:, head_cols : 2 * head_cols]
+    early_tail = parted(early_shards[:, 2 * head_cols :], 3)
+    loss = early_tail[0, 2] / (valid_count * model_width)
+    grad_w_key = late_shards[:, :kv_cols]
+    grad_w_value = late_shards[:, kv_cols : 2 * kv_cols]
+    key_tail = parted(late_shards[:, 2 * kv_cols :], 1)
+
+    gain_part = jnp.sum(grad_w_query * w_query.astype(F32), axis=1)
+    gain_part += jnp.sum(grad_w_key * w_key.astype(F32), axis=1)
+    gain_part += jnp.sum(grad_w_value * w_value.astype(F32), axis=1)
+    grad_gain_attn = lax.psum(gain_part, "exp") / gain_attn.astype(F32)
     normed_rows = jnp.einsum(
-        "erk,edk->rd", back[:, :own_rows], all_qkv, preferred_element_type=F32
+        "erk,edk->rd",
+        jnp.concatenate([early_back, late_back], axis=2),
+        all_qkv,
+        preferred_element_type=F32,
     )
     own_hat = lax.dynamic_slice_in_dim(attn_hat, exp_index * own_rows, own_rows, 0)
     own_scale = lax.dynamic_slice_in_dim(attn_scale, exp_index * own_rows, own_rows, 0)
@@ -816,14 +936,14 @@
         block_out,
         loss,
         grad_hidden,
-        own_grad_qkv[:, :head_cols],
-        own_grad_qkv[:, head_cols : head_cols + kv_cols],
-        own_grad_qkv[:, head_cols + kv_cols :],
-        own_grad_out,
+        grad_w_query,
+        grad_w_key,
+        grad_w_value,
+        grad_w_out,
         grad_gain_attn,
-        tail[:, 0],
-        tail[::2, 2],
-        tail[:, 1],
+        early_tail[:, 0],
+        key_tail[::2, 0],
+        early_tail[:, 1],
         grad_w_gate,
         grad_w_up,
         grad_w_down,

time: 635 us -> 700 us (1.10)
  blocking collectives: 78 us -> 191 us
  local copies, waits for them, and re-layouts: 55.9 us -> 29.9 us
  Pallas kernels: 127 us -> 143 us
  other arithmetic: 39.9 us -> 25.4 us
  matrix products: 55.6 us -> 42.2 us
  waiting for transfers between devices: 206 us -> 199 us
    all_to_all x2 -> x5, blocking collectives: 50.3 us -> 147 us  [exchange(): return lax.all_to_all(values, axis, split_axis=0, concat_axis=0, tiled=True)]
    all_to_all x7 -> x8, waiting for transfers between devices: 155 us -> 103 us  [exchange(): return lax.all_to_all(values, axis, split_axis=0, concat_axis=0, tiled=True)]
    all_gather x1, waiting for transfers between devices: 1.52 us -> 25.3 us  [on_device(): lax.all_gather(jnp.concatenate([out_grad, stat_parts], axis=0), 'ctx', ax...]
    ppermute x6, waiting for transfers between devices: 4.27 us -> 22.3 us  [shifted(): lax.ppermute(values, axis, [(i, (i + step) % count) for i in range(count)])]
    unnamed x138 -> x114, local copies, waits for them, and re-layouts: 29.6 us -> 12.2 us
    pallas_call x0 -> x2, Pallas kernels: none -> 16.7 us  [by_rows(): pl.pallas_call(kernel, out_shape=tuple(outs), grid=(outs[0].shape[0] // r...]
    psum x1 -> x3, blocking collectives: 16.9 us -> 33.5 us  [the longest x1 16.8 us: on_device(): early = lax.psum(early.reshape(-1, LANES), 'exp').reshape(-1)]
    concatenate x7 -> x8, other arithmetic: 19 us -> 2.94 us  [the longest x1 1.18 us: on_device(): jnp.concatenate([dot(normed, query_low, TN).astype(BF16).reshape(ctx_coun...]
  transfers between devices with their start and end apart: 20 -> 22, of which waited for: 13 -> 13; matrix products, arithmetic and copies ran while one was open for 19% -> 10% of each run, Pallas kernels for 20% -> 16%
where the time goes in v2:
time: 700 us; the launch traced here: 691 us
  waiting for transfers between devices  199 us (28%)
  blocking collectives  191 us (27%)
  Pallas kernels  143 us (20%)
  matrix products  42.2 us (6%)
  starting transfers between devices  41.9 us (6%)
  local copies, waits for them, and re-layouts  29.9 us (4%)
  other arithmetic  25.4 us (4%)
  between operations  18.9 us (3%)
    all_to_all x5, blocking collectives, exchange(): return lax.all_to_all(values, axis, split_axis=0, concat_axis=0, tiled=True)  147 us
    pallas_call x4, Pallas kernels, kernel_call(): pl.pallas_call(kernel, out_shape=tuple(outs), grid_spec=pltpu.PrefetchSca...  126 us
    all_to_all x8, waiting for transfers between devices, exchange(): return lax.all_to_all(values, axis, split_axis=0, concat_axis=0, tiled=True)  103 us
    all_gather x1, waiting for transfers between devices, on_device(): kv_all = lax.all_gather(own_kv, 'ctx', axis=0, tiled=True)  48.5 us
    all_to_all x8, starting transfers between devices, exchange(): return lax.all_to_all(values, axis, split_axis=0, concat_axis=0, tiled=True)  36 us
    dot_general x15, matrix products, dot(): return lax.dot_general(left, right, dims, preferred_element_type=F32)  33.9 us
    all_gather x1, waiting for transfers between devices, on_device(): lax.all_gather(jnp.concatenate([out_grad, stat_parts], axis=0), 'ctx', ax...  25.3 us
    ppermute x6, waiting for transfers between devices, shifted(): lax.ppermute(values, axis, [(i, (i + step) % count) for i in range(count)])  22.3 us
  transfers between devices with their start and end apart: 22, of which 13 were waited for; matrix products, arithmetic and copies ran while one was open for 10% of the time, Pallas kernels for 16%

profile of v2, /device:TPU:0, one launch (start us, length us, event | category | flops | bytes accessed | tf_op | source)
XLA Modules:
  0.0 690.6 jit_solution(14287841694149716882)
XLA Ops:
  12.2 8.2 %all-to-all-start = ((bf16[32,1,128]{2,1,0:T(2,128)(2,1)}), bf16[32,1,128]{2,1,0:T(2,128)(2,1)S(1)}, u32[]{:S(2)}, u32[]{:S(2)}) async-start(bf16[32,1,128]{2,1,0:T(2,128)(2,1)} %broadcast_in_dim.56), calls=%async_computation | async-start | bytes 32768 | tf_op jit(solution)/shard_map/all_to_all | solution.py:605
  20.6 7.1 %all-to-all-done = bf16[32,1,128]{2,1,0:T(2,128)(2,1)S(1)} async-done(((bf16[32,1,128]{2,1,0:T(2,128)(2,1)}), bf16[32,1,128]{2,1,0:T(2,128)(2,1)S(1)}, u32[]{:S(2)}, u32[]{:S(2)}) %all-to-all-start) | async-done | bytes 8224 | tf_op jit(solution)/shard_map/all_to_all | solution.py:605
  35.3 14.9 %all-to-all-done.1 = bf16[32,32,512]{2,1,0:T(8,128)(2,1)S(1)} async-done(((bf16[32,32,512]{2,1,0:T(8,128)(2,1)}), bf16[32,32,512]{2,1,0:T(8,128)(2,1)S(1)}, u32[]{:S(2)}, u32[]{:S(2)}) %all-to-all-start.1) | async-done | bytes 1048608 | tf_op jit(solution)/shard_map/all_to_all | solution.py:605
  53.5 10.8 %psum.28 = f32[2,512]{1,0:T(2,128)S(1)} all-reduce(f32[2,512]{1,0:T(2,128)S(1)} %pad_maximum_fusion.14), channel_id=1, replica_groups=mesh['ctx'=32,'exp'=4] {'exp'}, use_global_device_ids=true, to_apply=%region_3.4 | all-reduce | flops 1024 | bytes 8192 | tf_op jit(solution)/shard_map/psum | solution.py:695
  65.8 4.7 copy.82
  70.6 48.5 %all-gather.9.cloned.1.call-done.kv = bf16[16384,256]{1,0:T(8,128)(2,1)} async-done(((bf16[512,256]{1,0:T(8,128)(2,1)}), bf16[16384,256]{1,0:T(8,128)(2,1)}) %all-gather.9.cloned.1.call-update) | async-done | bytes 8388624 | tf_op jit(solution)/shard_map/all_gather | solution.py:718
  119.1 28.7 %attend.1 = (f32[512,256]{1,0:T(8,128)S(1)}, f32[2,4,256]{2,1,0:T(4,128)S(1)}) custom-call(s32[128]{0:T(128)S(1)} %copy-done.8, s32[4]{0:T(128)S(1)} %get-tuple-element.87.own, bf16[512,256]{1,0:T(8,128)(2,1)} %get-tuple-element.49.q_in, bf16[16384,256]{1,0:T(8,128)(2,1)} %all-gather.9.cloned.1.call-done.kv), custom_call_target="tpu_custom_call" | custom-call | flops 20000000000 | bytes 8650752 | tf_op jit(solution)/shard_map/attend/pallas_call | solution.py:442
  147.8 12.1 %all_to_all.65 = bf16[4,128,256]{2,1,0:T(8,128)(2,1)} all-to-all(bf16[4,128,256]{2,1,0:T(8,128)(2,1)S(1)} %bitcast.148), channel_id=1, replica_groups=mesh['ctx'=32,'exp'=4] {'exp'}, dimensions={0} | all-to-all | bytes 524288 | tf_op jit(solution)/shard_map/all_to_all | solution.py:605
  160.0 20.6 %all_to_all.66 = bf16[32,32,256]{2,1,0:T(8,128)(2,1)} all-to-all(bf16[32,32,256]{2,1,0:T(8,128)(2,1)S(1)} %broadcast_in_dim.59), channel_id=1, replica_groups=mesh['ctx'=32,'exp'=4] {'ctx'}, dimensions={0} | all-to-all | bytes 1048576 | tf_op jit(solution)/shard_map/all_to_all | solution.py:605
  185.2 10.6 %collective-permute-done = bf16[1024,256]{1,0:T(8,128)(2,1)} collective-permute-done((bf16[1024,256]{1,0:T(8,128)(2,1)}, bf16[1024,256]{1,0:T(8,128)(2,1)}, u32[]{:S(2)}, u32[]{:S(2)}) %collective-permute-start) | collective-permute-done | bytes 524320 | tf_op jit(solution)/shard_map/ppermute | solution.py:615
  197.5 10.0 %collective-permute-done.2 = bf16[1024,256]{1,0:T(8,128)(2,1)} collective-permute-done((bf16[1024,256]{1,0:T(8,128)(2,1)}, bf16[1024,256]{1,0:T(8,128)(2,1)}, u32[]{:S(2)}, u32[]{:S(2)}) %collective-permute-start.2) | collective-permute-done | bytes 524320 | tf_op jit(solution)/shard_map/ppermute | solution.py:615
  212.8 38.2 %all_to_all.67 = bf16[32,40,1024]{2,1,0:T(8,128)(2,1)S(1)} all-to-all(bf16[32,40,1024]{2,1,0:T(8,128)(2,1)S(1)} %bitcast.142), channel_id=1, replica_groups=mesh['ctx'=32,'exp'=4] {'ctx'}, dimensions={0} | all-to-all | bytes 5242880 | tf_op jit(solution)/shard_map/all_to_all | solution.py:605
  251.0 5.4 expert.1
  260.9 4.9 all-to-all-start.5
  268.7 33.2 %all-to-all-done.5 = bf16[32,40,1024]{2,1,0:T(8,128)(2,1)} async-done(((bf16[32,40,1024]{2,1,0:T(8,128)(2,1)}), bf16[32,40,1024]{2,1,0:T(8,128)(2,1)}, u32[]{:S(2)}, u32[]{:S(2)}) %all-to-all-start.5) | async-done | bytes 2621472 | tf_op jit(solution)/shard_map/all_to_all | solution.py:605
  306.6 37.6 %all_to_all.68 = bf16[32,40,1024]{2,1,0:T(8,128)(2,1)S(1)} all-to-all(bf16[32,40,1024]{2,1,0:T(8,128)(2,1)S(1)} %bitcast.147), channel_id=1, replica_groups=mesh['ctx'=32,'exp'=4] {'ctx'}, dimensions={0} | all-to-all | bytes 5242880 | tf_op jit(solution)/shard_map/all_to_all | solution.py:605
  344.3 11.3 %expert_grad.1 = (bf16[1280,1024]{1,0:T(8,128)(2,1)S(1)}, bf16[1280,512]{1,0:T(8,128)(2,1)S(1)}, bf16[1280,512]{1,0:T(8,128)(2,1)S(1)}, bf16[1280,512]{1,0:T(8,128)(2,1)S(1)}) custom-call(bf16[1280,1024]{1,0:T(8,128)(2,1)S(1)} %bitcast.126, f32[1280,512]{1,0:T(8,128)S(1)} %copy-done.10, f32[1280,512]{1,0:T(8,128)S(1)} %copy-done.12, ...), custom_call_target="tpu_custom_call" | custom-call | flops 4026531840 | bytes 10000000 | tf_op jit(solution)/shard_map/expert_grad/pallas_call | solution.py:464
  357.7 37.9 %all_to_all.69 = bf16[32,40,1024]{2,1,0:T(8,128)(2,1)} all-to-all(bf16[32,40,1024]{2,1,0:T(8,128)(2,1)S(1)} %bitcast.134), channel_id=1, replica_groups=mesh['ctx'=32,'exp'=4] {'ctx'}, dimensions={0} | all-to-all | bytes 5242880 | tf_op jit(solution)/shard_map/all_to_all | solution.py:605
  405.7 7.2 %all-to-all-done.8 = bf16[4,128,256]{1,2,0:T(8,128)(2,1)} async-done(((bf16[4,128,256]{1,2,0:T(8,128)(2,1)}), bf16[4,128,256]{1,2,0:T(8,128)(2,1)}, u32[]{:S(2)}, u32[]{:S(2)}) %all-to-all-start.8) | async-done | bytes 262176 | tf_op jit(solution)/shard_map/all_to_all | solution.py:605
  422.9 5.0 fusion.80
  427.9 5.1 convolution_bitcast_fusion
  433.0 4.7 convolution_bitcast_fusion.1
  440.9 25.3 %all-gather.17.cloned.1.call-done = bf16[17920,256]{1,0:T(8,128)(2,1)} async-done(((bf16[560,256]{1,0:T(8,128)(2,1)}), bf16[17920,256]{1,0:T(8,128)(2,1)}) %all-gather.17.cloned.1.call-update) | async-done | bytes 9175056 | tf_op jit(solution)/shard_map/all_gather | solution.py:806
  467.6 36.7 %query_grad.1 = f32[512,256]{1,0:T(8,128)S(1)} custom-call(s32[128]{0:T(128)S(1)} %copy-done.8, s32[4]{0:T(128)S(1)} %get-tuple-element.87.own, bf16[512,256]{1,0:T(8,128)(2,1)} %get-tuple-element.49.q_in, bf16[512,256]{1,0:T(8,128)(2,1)S(1)} %bitcast.137, f32[512,256]{1,0:T(8,128)S(1)} %get-tuple-element.44.o_in, ...), custom_call_target="tpu_custom_call" | custom-call | flops 30000001024 | bytes 9969664 | tf_op jit(solution)/shard_map/query_grad/pallas_call | solution.py:442
  505.5 16.8 %psum.29 = f32[3072]{0:T(1024)S(1)} all-reduce(f32[3072]{0:T(1024)S(1)} %pad_maximum_fusion.13), channel_id=1, replica_groups=mesh['ctx'=32,'exp'=4] {'exp'}, use_global_device_ids=true, to_apply=%region_14.15 | all-reduce | flops 3072 | bytes 24576 | tf_op jit(solution)/shard_map/psum | solution.py:843
  528.7 59.2 %pair_grad.1 = f32[512,256]{1,0:T(8,128)S(1)} custom-call(s32[128]{0:T(128)S(1)} %copy-done.8, s32[4]{0:T(128)S(1)} %get-tuple-element.87.own, bf16[512,256]{1,0:T(8,128)(2,1)} %get-tuple-element.43.kv_in, f32[512,128]{1,0:T(8,128)S(1)} %get-tuple-element.125.cos_ref, f32[512,128]{1,0:T(8,128)S(1)} %copy-done.7, ...), custom_call_target="tpu_custom_call" | custom-call | flops 40000000000 | bytes 18874368 | tf_op jit(solution)/shard_map/pair_grad/pallas_call | solution.py:442
  588.4 7.7 %psum.30 = f32[8,128]{1,0:T(8,128)S(1)} all-reduce(f32[8,128]{1,0:T(8,128)S(1)} %pad_maximum_fusion.16), channel_id=1, replica_groups=mesh['ctx'=32,'exp'=4] {'exp'}, use_global_device_ids=true, to_apply=%region_19.20 | all-reduce | flops 1024 | bytes 8192 | tf_op jit(solution)/shard_map/psum | solution.py:896
  603.6 9.2 %all-to-all-done.11 = bf16[4,128,256]{2,1,0:T(8,128)(2,1)S(1)} async-done(((bf16[4,128,256]{2,1,0:T(8,128)(2,1)}), bf16[4,128,256]{2,1,0:T(8,128)(2,1)S(1)}, u32[]{:S(2)}, u32[]{:S(2)}) %all-to-all-start.11) | async-done | bytes 262176 | tf_op jit(solution)/shard_map/all_to_all | solution.py:605
  617.8 8.1 %all-to-all-done.10 = bf16[4,128,256]{2,1,0:T(8,128)(2,1)S(1)} async-done(((bf16[4,128,256]{2,1,0:T(8,128)(2,1)}), bf16[4,128,256]{2,1,0:T(8,128)(2,1)S(1)}, u32[]{:S(2)}, u32[]{:S(2)}) %all-to-all-start.10) | async-done | bytes 262176 | tf_op jit(solution)/shard_map/all_to_all | solution.py:605
  635.2 9.8 %all-to-all-done.12 = bf16[32,32,384]{2,1,0:T(8,128)(2,1)S(1)} async-done(((bf16[32,32,384]{2,1,0:T(8,128)(2,1)}), bf16[32,32,384]{2,1,0:T(8,128)(2,1)S(1)}, u32[]{:S(2)}, u32[]{:S(2)}) %all-to-all-start.12) | async-done | bytes 786464 | tf_op jit(solution)/shard_map/all_to_all | solution.py:605
  656.6 13.1 %all-to-all-done.9 = bf16[32,32,640]{2,1,0:T(8,128)(2,1)S(1)} async-done(((bf16[32,32,640]{2,1,0:T(8,128)(2,1)}), bf16[32,32,640]{2,1,0:T(8,128)(2,1)S(1)}, u32[]{:S(2)}, u32[]{:S(2)}) %all-to-all-start.9) | async-done | bytes 1310752 | tf_op jit(solution)/shard_map/all_to_all | solution.py:605
  672.0 8.9 %psum.31 = f32[32]{0:T(128)S(1)} all-reduce(f32[32]{0:T(128)S(1)} %add_add_fusion), channel_id=1, replica_groups=mesh['ctx'=32,'exp'=4] {'exp'}, use_global_device_ids=true, to_apply=%region_25.26 | all-reduce | flops 32 | bytes 256 | tf_op jit(solution)/shard_map/psum | solution.py:925
  (272 shorter events, 110.0 us)
Async XLA Ops:
  7.3 58.6 %all-gather.13.cloned.1.call-start = ((), (), s32[]{:S(2)}) async-start(), calls=%async_computation.21 | async-start | bytes 3932160 | tf_op jit(solution)/shard_map/all_gather | solution.py:686
  12.2 15.5 %all-to-all-start = ((bf16[32,1,128]{2,1,0:T(2,128)(2,1)}), bf16[32,1,128]{2,1,0:T(2,128)(2,1)S(1)}, u32[]{:S(2)}, u32[]{:S(2)}) async-start(bf16[32,1,128]{2,1,0:T(2,128)(2,1)} %broadcast_in_dim.56), calls=%async_computation | async-start | bytes 32768 | tf_op jit(solution)/shard_map/all_to_all | solution.py:605
  28.8 21.4 %all-to-all-start.1 = ((bf16[32,32,512]{2,1,0:T(8,128)(2,1)}), bf16[32,32,512]{2,1,0:T(8,128)(2,1)S(1)}, u32[]{:S(2)}, u32[]{:S(2)}) async-start(bf16[32,32,512]{2,1,0:T(8,128)(2,1)} %broadcast_in_dim.57), calls=%async_computation.1 | async-start | bytes 2097152 | tf_op jit(solution)/shard_map/all_to_all | solution.py:605
  32.9 86.2 %all-gather.9.cloned.1.call-start = ((), (), s32[]{:S(2)}) async-start(), calls=%async_computation.16 | async-start | bytes 8650752 | tf_op jit(solution)/shard_map/all_gather | solution.py:718
  34.4 30.0 %copy-start.6 = (f32[512,128]{1,0:T(8,128)}, f32[512,128]{1,0:T(8,128)S(1)}, u32[]{:S(2)}) copy-start(f32[512,128]{1,0:T(8,128)S(1)} %get-tuple-element.126.sin_ref) | copy-start | bytes 786436
  70.5 231.4 %all-gather.11.cloned.1.call-start = ((), (), s32[]{:S(2)}) async-start(), calls=%async_computation.17 | async-start | bytes 8650752 | tf_op jit(solution)/shard_map/all_gather | solution.py:731
  119.1 40.9 %copy-start.47 = (bf16[32,256]{1,0:T(8,128)(2,1)S(1)}, bf16[32,256]{1,0:T(8,128)(2,1)}, u32[]{:S(2)}) copy-start(bf16[32,256]{1,0:T(8,128)(2,1)} %param.26) | copy-start | bytes 49156
  147.8 36.7 %copy-start.22 = (bf16[512,256]{1,0:T(8,128)(2,1)}, bf16[512,256]{1,0:T(8,128)(2,1)S(1)}, u32[]{:S(2)}) copy-start(bf16[512,256]{1,0:T(8,128)(2,1)S(1)} %convert_element_type.195) | copy-start | bytes 786436
  180.7 15.1 %collective-permute-start = (bf16[1024,256]{1,0:T(8,128)(2,1)}, bf16[1024,256]{1,0:T(8,128)(2,1)}, u32[]{:S(2)}, u32[]{:S(2)}) collective-permute-start(bf16[1024,256]{1,0:T(8,128)(2,1)} %bitcast.13), channel_id=1, source_target_pairs={{0,3},{1,0},{2,1},{3,2},{4,7},{5,4},{6,5},{7,6},{8,11},{9,8},{10,9... | collective-permute-start | bytes 1572872 | tf_op jit(solution)/shard_map/ppermute | solution.py:615
  180.8 16.7 %collective-permute-start.1 = (bf16[1024,256]{1,0:T(8,128)(2,1)}, bf16[1024,256]{1,0:T(8,128)(2,1)}, u32[]{:S(2)}, u32[]{:S(2)}) collective-permute-start(bf16[1024,256]{1,0:T(8,128)(2,1)} %bitcast.13), channel_id=1, source_target_pairs={{0,2},{1,3},{2,0},{3,1},{4,6},{5,7},{6,4},{7,5},{8,10},{9,11},{10,... | collective-permute-start | bytes 1572872 | tf_op jit(solution)/shard_map/ppermute | solution.py:615
  182.7 24.8 %collective-permute-start.2 = (bf16[1024,256]{1,0:T(8,128)(2,1)}, bf16[1024,256]{1,0:T(8,128)(2,1)}, u32[]{:S(2)}, u32[]{:S(2)}) collective-permute-start(bf16[1024,256]{1,0:T(8,128)(2,1)} %bitcast.13), channel_id=1, source_target_pairs={{0,1},{1,2},{2,3},{3,0},{4,5},{5,6},{6,7},{7,4},{8,9},{9,10},{10,1... | collective-permute-start | bytes 1572872 | tf_op jit(solution)/shard_map/ppermute | solution.py:615
  185.2 120.5 %copy-start.26 = (pred[1280,128]{1,0:T(32,128)(4,1)}, pred[1280,128]{1,0:T(32,128)(4,1)S(1)}, u32[]{:S(2)}) copy-start(pred[1280,128]{1,0:T(32,128)(4,1)S(1)} %bitcast_compare_fusion) | copy-start | bytes 491524
  211.8 92.9 %copy-start.15 = (f32[128,1024]{1,0:T(8,128)}, f32[128,1024]{1,0:T(8,128)S(1)}, u32[]{:S(2)}) copy-start(f32[128,1024]{1,0:T(8,128)S(1)} %get-tuple-element.121) | copy-start | bytes 1572868
  212.7 38.2 %copy-start.1 = (bf16[4096,384]{1,0:T(8,128)(2,1)S(1)}, bf16[4096,384]{1,0:T(8,128)(2,1)}, u32[]{:S(2)}) copy-start(bf16[4096,384]{1,0:T(8,128)(2,1)} %copy.82) | copy-start | bytes 9437188
  260.9 41.0 %all-to-all-start.5 = ((bf16[32,40,1024]{2,1,0:T(8,128)(2,1)}), bf16[32,40,1024]{2,1,0:T(8,128)(2,1)}, u32[]{:S(2)}, u32[]{:S(2)}) async-start(bf16[32,40,1024]{2,1,0:T(8,128)(2,1)} %bitcast.133), calls=%async_computation.5 | async-start | bytes 5242880 | tf_op jit(solution)/shard_map/all_to_all | solution.py:605
  265.8 129.8 %all-gather.15.cloned.1.call-start = ((), (), s32[]{:S(2)}) async-start(), calls=%async_computation.22 | async-start | bytes 5242880 | tf_op jit(solution)/shard_map/all_gather | solution.py:762
  306.6 37.7 %copy-start.10 = (f32[1280,512]{1,0:T(8,128)S(1)}, f32[1280,512]{1,0:T(8,128)}, u32[]{:S(2)}) copy-start(f32[1280,512]{1,0:T(8,128)} %copy-done.9) | copy-start | bytes 7864324
  306.6 37.7 %copy-start.12 = (f32[1280,512]{1,0:T(8,128)S(1)}, f32[1280,512]{1,0:T(8,128)}, u32[]{:S(2)}) copy-start(f32[1280,512]{1,0:T(8,128)} %copy-done.11) | copy-start | bytes 7864324
  401.6 11.3 %all-to-all-start.8 = ((bf16[4,128,256]{1,2,0:T(8,128)(2,1)}), bf16[4,128,256]{1,2,0:T(8,128)(2,1)}, u32[]{:S(2)}, u32[]{:S(2)}) async-start(bf16[4,128,256]{1,2,0:T(8,128)(2,1)} %fusion.10), calls=%async_computation.8 | async-start | bytes 524288 | tf_op jit(solution)/shard_map/all_to_all | solution.py:605
  405.7 60.6 %all-gather.17.cloned.1.call-start = ((), (), s32[]{:S(2)}) async-start(), calls=%async_computation.23 | async-start | bytes 9461760 | tf_op jit(solution)/shard_map/all_gather | solution.py:806
  415.2 267.0 %reduce-scatter.8.cloned.1.call-start = ((), (), s32[]{:S(2)}) async-start(), calls=%async_computation.20 | async-start | bytes 2621440 | tf_op jit(solution)/shard_map/reduce_scatter | solution.py:829
  437.7 28.6 %copy-start.29 = (bf16[128,1024]{1,0:T(8,128)(2,1)S(1)}, bf16[128,1024]{1,0:T(8,128)(2,1)}, u32[]{:S(2)}) copy-start(bf16[128,1024]{1,0:T(8,128)(2,1)} %copy-done.28) | copy-start | bytes 786436
  437.7 29.9 %copy-start.7 = (f32[512,128]{1,0:T(8,128)S(1)}, f32[512,128]{1,0:T(8,128)}, u32[]{:S(2)}) copy-start(f32[512,128]{1,0:T(8,128)} %copy-done.6) | copy-start | bytes 786436
  437.7 84.7 %collective-permute-start.3 = (bf16[128,1024]{1,0:T(8,128)(2,1)}, bf16[128,1024]{1,0:T(8,128)(2,1)}, u32[]{:S(2)}, u32[]{:S(2)}) collective-permute-start(bf16[128,1024]{1,0:T(8,128)(2,1)} %copy-done.28), channel_id=1, source_target_pairs={{0,1},{1,2},{2,3},{3,0},{4,5},{5,6},{6,7},{7,4},{8,9},{9,10},{10,1... | collective-permute-start | bytes 786440 | tf_op jit(solution)/shard_map/ppermute | solution.py:615
  438.3 85.7 %collective-permute-start.5 = (bf16[128,1024]{1,0:T(8,128)(2,1)}, bf16[128,1024]{1,0:T(8,128)(2,1)}, u32[]{:S(2)}, u32[]{:S(2)}) collective-permute-start(bf16[128,1024]{1,0:T(8,128)(2,1)} %copy-done.28), channel_id=1, source_target_pairs={{0,3},{1,0},{2,1},{3,2},{4,7},{5,4},{6,5},{7,6},{8,11},{9,8},{10,9... | collective-permute-start | bytes 786440 | tf_op jit(solution)/shard_map/ppermute | solution.py:615
  440.9 84.4 %collective-permute-start.4 = (bf16[128,1024]{1,0:T(8,128)(2,1)}, bf16[128,1024]{1,0:T(8,128)(2,1)}, u32[]{:S(2)}, u32[]{:S(2)}) collective-permute-start(bf16[128,1024]{1,0:T(8,128)(2,1)} %copy-done.28), channel_id=1, source_target_pairs={{0,2},{1,3},{2,0},{3,1},{4,6},{5,7},{6,4},{7,5},{8,10},{9,11},{10,... | collective-permute-start | bytes 786440 | tf_op jit(solution)/shard_map/ppermute | solution.py:615
  466.2 215.9 %reduce-scatter.4.cloned.1.call-start = ((), (), s32[]{:S(2)}) async-start(), calls=%async_computation.18 | async-start | bytes 2621440 | tf_op jit(solution)/shard_map/reduce_scatter | solution.py:827
  528.7 153.5 %reduce-scatter.6.cloned.1.call-start = ((), (), s32[]{:S(2)}) async-start(), calls=%async_computation.19 | async-start | bytes 2621440 | tf_op jit(solution)/shard_map/reduce_scatter | solution.py:828
  600.1 12.7 %all-to-all-start.11 = ((bf16[4,128,256]{2,1,0:T(8,128)(2,1)}), bf16[4,128,256]{2,1,0:T(8,128)(2,1)S(1)}, u32[]{:S(2)}, u32[]{:S(2)}) async-start(bf16[4,128,256]{2,1,0:T(8,128)(2,1)} %bitcast.61), calls=%async_computation.11 | async-start | bytes 524288 | tf_op jit(solution)/shard_map/all_to_all | solution.py:605
  612.8 13.0 %all-to-all-start.10 = ((bf16[4,128,256]{2,1,0:T(8,128)(2,1)}), bf16[4,128,256]{2,1,0:T(8,128)(2,1)S(1)}, u32[]{:S(2)}, u32[]{:S(2)}) async-start(bf16[4,128,256]{2,1,0:T(8,128)(2,1)} %bitcast.54), calls=%async_computation.10 | async-start | bytes 524288 | tf_op jit(solution)/shard_map/all_to_all | solution.py:605
  626.5 18.5 %all-to-all-start.12 = ((bf16[32,32,384]{2,1,0:T(8,128)(2,1)}), bf16[32,32,384]{2,1,0:T(8,128)(2,1)S(1)}, u32[]{:S(2)}, u32[]{:S(2)}) async-start(bf16[32,32,384]{2,1,0:T(8,128)(2,1)} %fusion.12), calls=%async_computation.12 | async-start | bytes 1572864 | tf_op jit(solution)/shard_map/all_to_all | solution.py:605
  645.0 24.8 %all-to-all-start.9 = ((bf16[32,32,640]{2,1,0:T(8,128)(2,1)}), bf16[32,32,640]{2,1,0:T(8,128)(2,1)S(1)}, u32[]{:S(2)}, u32[]{:S(2)}) async-start(bf16[32,32,640]{2,1,0:T(8,128)(2,1)} %fusion.3), calls=%async_computation.9 | async-start | bytes 2621440 | tf_op jit(solution)/shard_map/all_to_all | solution.py:605
  (45 other events, 300.7 us)
Sparse Core Ops, SparseCore 0:
  11.6 42.0 all-gather.12
  70.6 48.3 all-gather.8
  160.1 53.3 all-gather.10
  302.0 43.5 all-gather.14
  415.3 50.8 all-gather.16
  469.1 29.1 reduce-scatter.7
  528.8 31.5 reduce-scatter.3
  599.5 29.5 reduce-scatter.5

commit v3 on v2

--- a/solution.py
+++ b/solution.py
@@ -496,7 +496,7 @@
     return by_rows(
         functools.partial(expert_grad_kernel, quarters, width),
         "expert_grad",
-        slots // 5,
+        slots // 2,
         [rows_grad, gate_pre, up_pre, weights],
         [jax.ShapeDtypeStruct((slots, model_width), BF16), hidden, hidden, hidden],
         6 * slots * model_width * quarters * width,
@@ -670,20 +670,24 @@
     shard_rows = w_query.shape[0]
 
     own_qkv = jnp.concatenate([w_query, w_key, w_value], axis=1)
-    full_qkv = spread(own_qkv, "ctx", ctx_count).reshape(model_width, qkv_cols)
-    gain_row = jnp.concatenate([gain_attn, gain_query, gain_ffn, gain_key])
-    gain_row = jnp.pad(gain_row, (0, -gain_row.shape[0] % LANES)).reshape(-1, LANES)
-    gains = spread(gain_row, "ctx", ctx_count).reshape(ctx_count, -1).astype(F32)
-    attn_gain = gains[:, :shard_rows].reshape(model_width)
-    query_gain_all = gains[:, shard_rows : 2 * shard_rows].reshape(model_width)
-    ffn_gain = gains[:, 2 * shard_rows : 3 * shard_rows].reshape(model_width)
-    key_gain_all = gains[:, 3 * shard_rows : 3 * shard_rows + gain_key.shape[0]].reshape(kv_total)
+    mine = jnp.arange(model_width, dtype=jnp.int32) // shard_rows == ctx_index
+    places = [
+        jnp.where(mine, jnp.tile(gain, ctx_count), 0).astype(BF16)
+        for gain in (gain_attn, gain_query, gain_ffn)
+    ]
+    mine_key = jnp.arange(kv_total, dtype=jnp.int32) // gain_key.shape[0] == ctx_index
+    places.append(jnp.where(mine_key, jnp.tile(gain_key, ctx_count), 0).astype(BF16))
+    gain_rows = jnp.concatenate(places)
+    gain_rows = jnp.pad(gain_rows, (0, 8 * qkv_cols - gain_rows.shape[0])).reshape(8, qkv_cols)
+    first_parts = spread(jnp.concatenate([own_qkv, gain_rows], axis=0), "ctx", ctx_count)
+    full_qkv = first_parts[:, :shard_rows].reshape(model_width, qkv_cols)
+    gains = jnp.sum(first_parts[:, shard_rows:].astype(F32), axis=0).reshape(-1)
+    attn_gain = gains[:model_width]
+    query_gain_all = gains[model_width : 2 * model_width]
+    ffn_gain = gains[2 * model_width : 3 * model_width]
+    key_gain_all = gains[3 * model_width : 3 * model_width + kv_total]
     query_gain = lax.dynamic_slice_in_dim(query_gain_all, exp_index * head_cols, head_cols)
     key_gain = lax.dynamic_slice_in_dim(key_gain_all, exp_index * kv_cols, kv_cols)
-
-    width = w_gate.shape[2]
-    own_expert = jnp.concatenate([w_gate[0], w_up[0], w_down[0].T], axis=1)
-    expert = lax.all_gather(own_expert, "exp", axis=0, tiled=False)
 
     hidden_f = hidden_in.astype(F32)
     attn_scale = lax.rsqrt(jnp.mean(hidden_f * hidden_f, axis=-1, keepdims=True) + NORM_EPSILON)
@@ -714,28 +718,19 @@
         cosine,
         sine,
     )
-    own_kv, expert = lax.optimization_barrier((own_kv, expert))
     kv_all = lax.all_gather(own_kv, "ctx", axis=0, tiled=True)
-    own_out, _ = lax.optimization_barrier((w_out, own_kv))
+    own_out, own_gate, own_up, own_down, _ = lax.optimization_barrier(
+        (w_out, w_gate[0], w_up[0], w_down[0], own_kv)
+    )
+    width = w_gate.shape[2]
+    own_expert = jnp.concatenate([own_gate, own_up, own_down.T], axis=1)
+    expert = lax.all_gather(own_expert, "exp", axis=0, tiled=False)
     full_out = gather_short(
         spread(own_out, "ctx", ctx_count).reshape(model_width, head_cols),
         "exp",
         exp_index,
         exp_count,
     )
-    heads_f, lse = attend(block_of, own_blocks, queries_rot, kv_all)
-    heads_low = heads_f.astype(BF16)
-
-    own_heads = exchange(heads_low.reshape(exp_count, own_rows, head_cols), "exp")
-    own_heads, later_q = lax.optimization_barrier((own_heads, queries_rot))
-    q_all = lax.all_gather(later_q, "ctx", axis=0, tiled=True)
-    attn_rows = jnp.einsum("erk,eok->ro", own_heads, full_out, preferred_element_type=F32)
-    hidden_rows = lax.dynamic_slice_in_dim(hidden_f, exp_index * own_rows, own_rows, 0)
-    resid = hidden_rows + attn_rows
-    ffn_scale = lax.rsqrt(jnp.mean(resid * resid, axis=-1, keepdims=True) + NORM_EPSILON)
-    ffn_hat = resid * ffn_scale
-    normed_ffn = (ffn_hat * ffn_gain).astype(BF16)
-
     expert_total = ctx_count
     capacity = max(2, own_rows * routes.shape[1] * 5 // (expert_total * 4))
     slots = expert_total * capacity
@@ -750,6 +745,23 @@
     weigh = jnp.where(holds, gate_of.T[:, None, :], 0.0).reshape(slots, own_rows)
     slot_gate = jnp.sum(weigh, axis=1, keepdims=True)
 
+    kv_all, full_out, pick, weigh, slot_gate = lax.optimization_barrier(
+        (kv_all, full_out, pick, weigh, slot_gate)
+    )
+    heads_f, lse = attend(block_of, own_blocks, queries_rot, kv_all)
+    heads_low = heads_f.astype(BF16)
+
+    own_heads = exchange(heads_low.reshape(exp_count, own_rows, head_cols), "exp")
+    own_heads, later_q = lax.optimization_barrier((own_heads, queries_rot))
+    q_all = lax.all_gather(later_q, "ctx", axis=0, tiled=True)
+    attn_rows = jnp.einsum("erk,eok->ro", own_heads, full_out, preferred_element_type=F32)
+    hidden_rows = lax.dynamic_slice_in_dim(hidden_in, exp_index * own_rows, own_rows, 0)
+    hidden_rows = hidden_rows.astype(F32)
+    resid = hidden_rows + attn_rows
+    ffn_scale = lax.rsqrt(jnp.mean(resid * resid, axis=-1, keepdims=True) + NORM_EPSILON)
+    ffn_hat = resid * ffn_scale
+    normed_ffn = (ffn_hat * ffn_gain).astype(BF16)
+
     def send(rows):
         return exchange(rows.reshape(ctx_count, capacity, model_width), "ctx").reshape(
             slots, model_width
@@ -821,8 +833,8 @@
     down_part = dot(hidden_act, grad_copies, TN)
     gate_part = gate_part.reshape(model_width, exp_count, width).transpose(1, 0, 2)
     up_part = up_part.reshape(model_width, exp_count, width).transpose(1, 0, 2)
-    do_all, gate_part, up_part, down_part = lax.optimization_barrier(
-        (do_all, gate_part, up_part, down_part)
+    do_all, query_n_grad, grad_out, gate_part, up_part, down_part = lax.optimization_barrier(
+        (do_all, query_n_grad, grad_out, gate_part, up_part, down_part)
     )
     grad_w_gate = lax.psum_scatter(gate_part, "exp", scatter_dimension=0, tiled=True)
     grad_w_up = lax.psum_scatter(up_part, "exp", scatter_dimension=0, tiled=True)
@@ -880,6 +892,9 @@
         do_all.reshape(-1, head_cols),
         ctx_rows + stat_rows,
         aux,
+    )
+    pair_grads, early_shards, early_back = lax.optimization_barrier(
+        (pair_grads, early_shards, early_back)
     )
     key_n_grad = pair_grads[:, :kv_cols]
     value_grad = pair_grads[:, kv_cols:].astype(BF16)
@@ -929,8 +944,8 @@
         all_qkv,
         preferred_element_type=F32,
     )
-    own_hat = lax.dynamic_slice_in_dim(attn_hat, exp_index * own_rows, own_rows, 0)
     own_scale = lax.dynamic_slice_in_dim(attn_scale, exp_index * own_rows, own_rows, 0)
+    own_hat = hidden_rows * own_scale
     grad_hidden = resid_grad + norm_back(normed_rows, own_hat, own_scale, attn_gain)
     return (
         block_out,

time: 700 us -> 607 us (0.87)
  blocking collectives: 191 us -> 135 us
  waiting for transfers between devices: 199 us -> 148 us
  starting transfers between devices: 41.9 us -> 65.4 us
  Pallas kernels: 143 us -> 136 us
    all_to_all x5 -> x3, blocking collectives: 147 us -> 89.9 us  [exchange(): return lax.all_to_all(values, axis, split_axis=0, concat_axis=0, tiled=True)]
    all_gather x1, waiting for transfers between devices: 48.5 us -> 0.98 us  [on_device(): kv_all = lax.all_gather(own_kv, 'ctx', axis=0, tiled=True)]
    all_gather x1, waiting for transfers between devices: 25.3 us -> 0.02 us  [on_device(): lax.all_gather(jnp.concatenate([out_grad, stat_parts], axis=0), 'ctx', ax...]
    all_to_all x8 -> x9, starting transfers between devices: 36 us -> 58.5 us  [exchange(): return lax.all_to_all(values, axis, split_axis=0, concat_axis=0, tiled=True)]
    all_to_all x8 -> x9, waiting for transfers between devices: 103 us -> 125 us  [exchange(): return lax.all_to_all(values, axis, split_axis=0, concat_axis=0, tiled=True)]
  transfers between devices with their start and end apart: 22 -> 23, of which waited for: 13 -> 12; matrix products, arithmetic and copies ran while one was open for 10% -> 12% of each run, Pallas kernels for 16% -> 23%
where the time goes in v3:
time: 607 us; the launch traced here: 600 us
  waiting for transfers between devices  148 us (24%)
  Pallas kernels  136 us (22%)
  blocking collectives  135 us (22%)
  starting transfers between devices  65.4 us (11%)
  matrix products  39.1 us (6%)
  local copies, waits for them, and re-layouts  33 us (5%)
  other arithmetic  24.7 us (4%)
  between operations  18.4 us (3%)
    all_to_all x9, waiting for transfers between devices, exchange(): return lax.all_to_all(values, axis, split_axis=0, concat_axis=0, tiled=True)  125 us
    pallas_call x4, Pallas kernels, kernel_call(): pl.pallas_call(kernel, out_shape=tuple(outs), grid_spec=pltpu.PrefetchSca...  119 us
    all_to_all x3, blocking collectives, exchange(): return lax.all_to_all(values, axis, split_axis=0, concat_axis=0, tiled=True)  89.9 us
    all_to_all x9, starting transfers between devices, exchange(): return lax.all_to_all(values, axis, split_axis=0, concat_axis=0, tiled=True)  58.5 us
    dot_general x15, matrix products, dot(): return lax.dot_general(left, right, dims, preferred_element_type=F32)  31 us
    ppermute x6, waiting for transfers between devices, shifted(): lax.ppermute(values, axis, [(i, (i + step) % count) for i in range(count)])  21.1 us
    pallas_call x2, Pallas kernels, by_rows(): pl.pallas_call(kernel, out_shape=tuple(outs), grid=(outs[0].shape[0] // r...  17 us
    psum x1, blocking collectives, on_device(): early = lax.psum(early.reshape(-1, LANES), 'exp').reshape(-1)  15.3 us
  transfers between devices with their start and end apart: 23, of which 12 were waited for; matrix products, arithmetic and copies ran while one was open for 12% of the time, Pallas kernels for 23%

profile of v3, /device:TPU:0, one launch (start us, length us, event | category | flops | bytes accessed | tf_op | source)
XLA Modules:
  0.0 599.7 jit_solution(16485777927490026332)
XLA Ops:
  12.2 8.4 %all-to-all-start = ((bf16[32,40,512]{2,1,0:T(8,128)(2,1)}), bf16[32,40,512]{2,1,0:T(8,128)(2,1)S(1)}, u32[]{:S(2)}, u32[]{:S(2)}) async-start(bf16[32,40,512]{2,1,0:T(8,128)(2,1)} %broadcast_in_dim.112), calls=%async_computation | async-start | bytes 2621440 | tf_op jit(solution)/shard_map/all_to_all | solution.py:605
  22.6 18.8 %all-to-all-done = bf16[32,40,512]{2,1,0:T(8,128)(2,1)S(1)} async-done(((bf16[32,40,512]{2,1,0:T(8,128)(2,1)}), bf16[32,40,512]{2,1,0:T(8,128)(2,1)S(1)}, u32[]{:S(2)}, u32[]{:S(2)}) %all-to-all-start) | async-done | bytes 1310752 | tf_op jit(solution)/shard_map/all_to_all | solution.py:605
  45.2 10.8 %psum.28 = f32[2,512]{1,0:T(2,128)S(1)} all-reduce(f32[2,512]{1,0:T(2,128)S(1)} %pad_maximum_fusion.12), channel_id=1, replica_groups=mesh['ctx'=32,'exp'=4] {'exp'}, use_global_device_ids=true, to_apply=%region_4.5 | all-reduce | flops 1024 | bytes 8192 | tf_op jit(solution)/shard_map/psum | solution.py:699
  60.0 3.9 all-to-all-start.1
  64.0 13.7 %all-to-all-done.1 = bf16[32,32,256]{2,1,0:T(8,128)(2,1)S(1)} async-done(((bf16[32,32,256]{2,1,0:T(8,128)(2,1)}), bf16[32,32,256]{2,1,0:T(8,128)(2,1)S(1)}, u32[]{:S(2)}, u32[]{:S(2)}) %all-to-all-start.1) | async-done | bytes 524320 | tf_op jit(solution)/shard_map/all_to_all | solution.py:605
  83.0 9.4 %collective-permute-done = bf16[1024,256]{1,0:T(8,128)(2,1)S(1)} collective-permute-done((bf16[1024,256]{1,0:T(8,128)(2,1)S(1)}, bf16[1024,256]{1,0:T(8,128)(2,1)S(1)}, u32[]{:S(2)}, u32[]{:S(2)}) %collective-permute-start) | collective-permute-done | bytes 524320 | tf_op jit(solution)/shard_map/ppermute | solution.py:615
  94.9 10.0 %collective-permute-done.2 = bf16[1024,256]{1,0:T(8,128)(2,1)} collective-permute-done((bf16[1024,256]{1,0:T(8,128)(2,1)S(1)}, bf16[1024,256]{1,0:T(8,128)(2,1)}, u32[]{:S(2)}, u32[]{:S(2)}) %collective-permute-start.2) | collective-permute-done | bytes 524320 | tf_op jit(solution)/shard_map/ppermute | solution.py:615
  109.2 29.5 %attend.1 = (f32[512,256]{1,0:T(8,128)S(1)}, f32[2,4,256]{2,1,0:T(4,128)S(1)}) custom-call(s32[128]{0:T(128)S(1)} %copy-done.7, s32[4]{0:T(128)S(1)} %get-tuple-element.109.own, bf16[512,256]{1,0:T(8,128)(2,1)} %get-tuple-element.65.q_in, bf16[16384,256]{1,0:T(8,128)(2,1)} %all-gather.9.cloned.1.call-done.kv), custom_call_target="tpu_custom_call" | custom-call | flops 20000000000 | bytes 8650752 | tf_op jit(solution)/shard_map/attend/pallas_call | solution.py:442
  138.8 13.9 %all_to_all.60 = bf16[4,128,256]{2,1,0:T(8,128)(2,1)S(1)} all-to-all(bf16[4,128,256]{2,1,0:T(8,128)(2,1)S(1)} %bitcast.152), channel_id=1, replica_groups=mesh['ctx'=32,'exp'=4] {'exp'}, dimensions={0} | all-to-all | bytes 524288 | tf_op jit(solution)/shard_map/all_to_all | solution.py:605
  157.7 7.2 %all-to-all-start.3 = ((bf16[32,40,1024]{2,1,0:T(8,128)(2,1)}), bf16[32,40,1024]{2,1,0:T(8,128)(2,1)}, u32[]{:S(2)}, u32[]{:S(2)}) async-start(bf16[32,40,1024]{2,1,0:T(8,128)(2,1)} %bitcast.145), calls=%async_computation.3 | async-start | bytes 5242880 | tf_op jit(solution)/shard_map/all_to_all | solution.py:605
  164.8 4.7 copy.83
  169.5 34.4 %all-to-all-done.3 = bf16[32,40,1024]{2,1,0:T(8,128)(2,1)} async-done(((bf16[32,40,1024]{2,1,0:T(8,128)(2,1)}), bf16[32,40,1024]{2,1,0:T(8,128)(2,1)}, u32[]{:S(2)}, u32[]{:S(2)}) %all-to-all-start.3) | async-done | bytes 2621472 | tf_op jit(solution)/shard_map/all_to_all | solution.py:605
  205.8 6.6 %expert.1 = (bf16[1280,1024]{1,0:T(8,128)(2,1)S(1)}, f32[1280,512]{1,0:T(8,128)S(1)}, f32[1280,512]{1,0:T(8,128)S(1)}) custom-call(bf16[1280,1024]{1,0:T(8,128)(2,1)} %bitcast.22.x_ref, bf16[4,1024,384]{2,1,0:T(8,128)(2,1)S(1)} %bitcast.136), custom_call_target="tpu_custom_call" | custom-call | flops 4026531840 | bytes 10000000 | tf_op jit(solution)/shard_map/expert/pallas_call | solution.py:464
  216.9 4.9 all-to-all-start.4
  225.2 34.3 %all-to-all-done.4 = bf16[32,40,1024]{2,1,0:T(8,128)(2,1)} async-done(((bf16[32,40,1024]{2,1,0:T(8,128)(2,1)}), bf16[32,40,1024]{2,1,0:T(8,128)(2,1)}, u32[]{:S(2)}, u32[]{:S(2)}) %all-to-all-start.4) | async-done | bytes 2621472 | tf_op jit(solution)/shard_map/all_to_all | solution.py:605
  264.3 38.1 %all_to_all.61 = bf16[32,40,1024]{2,1,0:T(8,128)(2,1)S(1)} all-to-all(bf16[32,40,1024]{2,1,0:T(8,128)(2,1)S(1)} %bitcast.151), channel_id=1, replica_groups=mesh['ctx'=32,'exp'=4] {'ctx'}, dimensions={0} | all-to-all | bytes 5242880 | tf_op jit(solution)/shard_map/all_to_all | solution.py:605
  302.4 10.4 %expert_grad.1 = (bf16[1280,1024]{1,0:T(8,128)(2,1)S(1)}, bf16[1280,512]{1,0:T(8,128)(2,1)S(1)}, bf16[1280,512]{1,0:T(8,128)(2,1)S(1)}, bf16[1280,512]{1,0:T(8,128)(2,1)S(1)}) custom-call(bf16[1280,1024]{1,0:T(8,128)(2,1)S(1)} %bitcast.133, f32[1280,512]{1,0:T(8,128)S(1)} %copy-done.9, f32[1280,512]{1,0:T(8,128)S(1)} %copy-done.11, ...), custom_call_target="tpu_custom_call" | custom-call | flops 4026531840 | bytes 10000000 | tf_op jit(solution)/shard_map/expert_grad/pallas_call | solution.py:464
  314.9 37.9 %all_to_all.62 = bf16[32,40,1024]{2,1,0:T(8,128)(2,1)} all-to-all(bf16[32,40,1024]{2,1,0:T(8,128)(2,1)S(1)} %bitcast.138), channel_id=1, replica_groups=mesh['ctx'=32,'exp'=4] {'ctx'}, dimensions={0} | all-to-all | bytes 5242880 | tf_op jit(solution)/shard_map/all_to_all | solution.py:605
  358.8 4.3 all-to-all-start.7
  363.1 7.0 %all-to-all-done.7 = bf16[4,128,256]{1,2,0:T(8,128)(2,1)} async-done(((bf16[4,128,256]{1,2,0:T(8,128)(2,1)}), bf16[4,128,256]{1,2,0:T(8,128)(2,1)}, u32[]{:S(2)}, u32[]{:S(2)}) %all-to-all-start.7) | async-done | bytes 262176 | tf_op jit(solution)/shard_map/all_to_all | solution.py:605
  376.4 5.3 fusion.108
  381.6 4.6 convolution_bitcast_fusion
  386.2 5.0 convolution_bitcast_fusion.1
  395.9 40.5 %query_grad.1 = f32[512,256]{1,0:T(8,128)S(1)} custom-call(s32[128]{0:T(128)S(1)} %copy-done.7, s32[4]{0:T(128)S(1)} %get-tuple-element.109.own, bf16[512,256]{1,0:T(8,128)(2,1)} %get-tuple-element.65.q_in, bf16[512,256]{1,0:T(8,128)(2,1)S(1)} %bitcast.141, f32[512,256]{1,0:T(8,128)S(1)} %get-tuple-element.56.o_in, ...), custom_call_target="tpu_custom_call" | custom-call | flops 30000001024 | bytes 9969664 | tf_op jit(solution)/shard_map/query_grad/pallas_call | solution.py:442
  440.1 15.3 %psum.29 = f32[3072]{0:T(1024)S(1)} all-reduce(f32[3072]{0:T(1024)S(1)} %pad_maximum_fusion.11), channel_id=1, replica_groups=mesh['ctx'=32,'exp'=4] {'exp'}, use_global_device_ids=true, to_apply=%region_15.16 | all-reduce | flops 3072 | bytes 24576 | tf_op jit(solution)/shard_map/psum | solution.py:855
  466.1 5.1 all-to-all-done.9
  471.2 8.3 %all-to-all-start.8 = ((bf16[32,32,640]{2,1,0:T(8,128)(2,1)}), bf16[32,32,640]{2,1,0:T(8,128)(2,1)}, u32[]{:S(2)}, u32[]{:S(2)}) async-start(bf16[32,32,640]{2,1,0:T(8,128)(2,1)} %fusion.6), calls=%async_computation.8 | async-start | bytes 2621440 | tf_op jit(solution)/shard_map/all_to_all | solution.py:605
  479.5 48.0 %pair_grad.1 = f32[512,256]{1,0:T(8,128)S(1)} custom-call(s32[128]{0:T(128)S(1)} %copy-done.7, s32[4]{0:T(128)S(1)} %get-tuple-element.109.own, bf16[512,256]{1,0:T(8,128)(2,1)} %get-tuple-element.53.kv_in, f32[512,128]{1,0:T(8,128)S(1)} %get-tuple-element.149.cos_ref, f32[512,128]{1,0:T(8,128)S(1)} %copy-done.6, ...), custom_call_target="tpu_custom_call" | custom-call | flops 40000000000 | bytes 18874368 | tf_op jit(solution)/shard_map/pair_grad/pallas_call | solution.py:442
  528.1 8.8 %psum.30 = f32[8,128]{1,0:T(8,128)S(1)} all-reduce(f32[8,128]{1,0:T(8,128)S(1)} %pad_maximum_fusion.14), channel_id=1, replica_groups=mesh['ctx'=32,'exp'=4] {'exp'}, use_global_device_ids=true, to_apply=%region_20.21 | all-reduce | flops 1024 | bytes 8192 | tf_op jit(solution)/shard_map/psum | solution.py:911
  549.9 14.7 %all-to-all-start.11 = ((bf16[32,32,384]{2,1,0:T(8,128)(2,1)}), bf16[32,32,384]{2,1,0:T(8,128)(2,1)S(1)}, u32[]{:S(2)}, u32[]{:S(2)}) async-start(bf16[32,32,384]{2,1,0:T(8,128)(2,1)} %fusion.11), calls=%async_computation.11 | async-start | bytes 1572864 | tf_op jit(solution)/shard_map/all_to_all | solution.py:605
  569.6 9.6 %all-to-all-done.11 = bf16[32,32,384]{2,1,0:T(8,128)(2,1)S(1)} async-done(((bf16[32,32,384]{2,1,0:T(8,128)(2,1)}), bf16[32,32,384]{2,1,0:T(8,128)(2,1)S(1)}, u32[]{:S(2)}, u32[]{:S(2)}) %all-to-all-start.11) | async-done | bytes 786464 | tf_op jit(solution)/shard_map/all_to_all | solution.py:605
  580.8 10.2 %psum.31 = f32[32]{0:T(128)S(1)} all-reduce(f32[32]{0:T(128)S(1)} %add_add_fusion), channel_id=1, replica_groups=mesh['ctx'=32,'exp'=4] {'exp'}, use_global_device_ids=true, to_apply=%region_26.27 | all-reduce | flops 32 | bytes 256 | tf_op jit(solution)/shard_map/psum | solution.py:940
  (260 shorter events, 97.8 us)
Async XLA Ops:
  12.2 29.2 %all-to-all-start = ((bf16[32,40,512]{2,1,0:T(8,128)(2,1)}), bf16[32,40,512]{2,1,0:T(8,128)(2,1)S(1)}, u32[]{:S(2)}, u32[]{:S(2)}) async-start(bf16[32,40,512]{2,1,0:T(8,128)(2,1)} %broadcast_in_dim.112), calls=%async_computation | async-start | bytes 2621440 | tf_op jit(solution)/shard_map/all_to_all | solution.py:605
  20.6 88.6 %all-gather.9.cloned.1.call-start = ((), (), s32[]{:S(2)}) async-start(), calls=%async_computation.15 | async-start | bytes 8650752 | tf_op jit(solution)/shard_map/all_gather | solution.py:721
  22.3 34.0 %copy-start.5 = (f32[512,128]{1,0:T(8,128)}, f32[512,128]{1,0:T(8,128)S(1)}, u32[]{:S(2)}) copy-start(f32[512,128]{1,0:T(8,128)S(1)} %get-tuple-element.150.sin_ref) | copy-start | bytes 786436
  57.7 107.1 %all-gather.13.cloned.1.call-start = ((), (), s32[]{:S(2)}) async-start(), calls=%async_computation.20 | async-start | bytes 3932160 | tf_op jit(solution)/shard_map/all_gather | solution.py:727
  58.1 23.3 %copy-start.41 = (f32[128,8]{0,1:T(8,128)S(1)}, f32[128,8]{0,1:T(8,128)}, u32[]{:S(2)}) copy-start(f32[128,8]{0,1:T(8,128)} %param.22) | copy-start | bytes 12292
  60.0 17.7 %all-to-all-start.1 = ((bf16[32,32,256]{2,1,0:T(8,128)(2,1)}), bf16[32,32,256]{2,1,0:T(8,128)(2,1)S(1)}, u32[]{:S(2)}, u32[]{:S(2)}) async-start(bf16[32,32,256]{2,1,0:T(8,128)(2,1)} %broadcast_in_dim.114), calls=%async_computation.1 | async-start | bytes 1048576 | tf_op jit(solution)/shard_map/all_to_all | solution.py:605
  63.9 195.7 %all-gather.11.cloned.1.call-start = ((), (), s32[]{:S(2)}) async-start(), calls=%async_computation.16 | async-start | bytes 8650752 | tf_op jit(solution)/shard_map/all_gather | solution.py:756
  77.7 14.7 %collective-permute-start = (bf16[1024,256]{1,0:T(8,128)(2,1)S(1)}, bf16[1024,256]{1,0:T(8,128)(2,1)S(1)}, u32[]{:S(2)}, u32[]{:S(2)}) collective-permute-start(bf16[1024,256]{1,0:T(8,128)(2,1)S(1)} %bitcast.154), channel_id=1, source_target_pairs={{0,3},{1,0},{2,1},{3,2},{4,7},{5,4},{6,5},{7,6},{8,11},{9,8},{10,9... | collective-permute-start | bytes 1572872 | tf_op jit(solution)/shard_map/ppermute | solution.py:615
  77.8 16.3 %collective-permute-start.1 = (bf16[1024,256]{1,0:T(8,128)(2,1)S(1)}, bf16[1024,256]{1,0:T(8,128)(2,1)S(1)}, u32[]{:S(2)}, u32[]{:S(2)}) collective-permute-start(bf16[1024,256]{1,0:T(8,128)(2,1)S(1)} %bitcast.155), channel_id=1, source_target_pairs={{0,2},{1,3},{2,0},{3,1},{4,6},{5,7},{6,4},{7,5},{8,10},{9,11},{10,... | collective-permute-start | bytes 1572872 | tf_op jit(solution)/shard_map/ppermute | solution.py:615
  80.0 24.9 %collective-permute-start.2 = (bf16[1024,256]{1,0:T(8,128)(2,1)S(1)}, bf16[1024,256]{1,0:T(8,128)(2,1)}, u32[]{:S(2)}, u32[]{:S(2)}) collective-permute-start(bf16[1024,256]{1,0:T(8,128)(2,1)S(1)} %bitcast.156), channel_id=1, source_target_pairs={{0,1},{1,2},{2,3},{3,0},{4,5},{5,6},{6,7},{7,4},{8,9},{9,10},{10,1... | collective-permute-start | bytes 1572872 | tf_op jit(solution)/shard_map/ppermute | solution.py:615
  81.5 181.9 %copy-start.19 = (bf16[1280,128]{1,0:T(8,128)(2,1)}, bf16[1280,128]{1,0:T(8,128)(2,1)S(1)}, u32[]{:S(2)}) copy-start(bf16[1280,128]{1,0:T(8,128)(2,1)S(1)} %fusion.21) | copy-start | bytes 983044
  155.2 107.2 %copy-start.13 = (f32[128,1024]{1,0:T(8,128)}, f32[128,1024]{1,0:T(8,128)S(1)}, u32[]{:S(2)}) copy-start(f32[128,1024]{1,0:T(8,128)S(1)} %get-tuple-element.143) | copy-start | bytes 1572868
  157.7 46.2 %all-to-all-start.3 = ((bf16[32,40,1024]{2,1,0:T(8,128)(2,1)}), bf16[32,40,1024]{2,1,0:T(8,128)(2,1)}, u32[]{:S(2)}, u32[]{:S(2)}) async-start(bf16[32,40,1024]{2,1,0:T(8,128)(2,1)} %bitcast.145), calls=%async_computation.3 | async-start | bytes 5242880 | tf_op jit(solution)/shard_map/all_to_all | solution.py:605
  216.9 42.7 %all-to-all-start.4 = ((bf16[32,40,1024]{2,1,0:T(8,128)(2,1)}), bf16[32,40,1024]{2,1,0:T(8,128)(2,1)}, u32[]{:S(2)}, u32[]{:S(2)}) async-start(bf16[32,40,1024]{2,1,0:T(8,128)(2,1)} %bitcast.137), calls=%async_computation.4 | async-start | bytes 5242880 | tf_op jit(solution)/shard_map/all_to_all | solution.py:605
  221.8 131.0 %all-gather.15.cloned.1.call-start = ((), (), s32[]{:S(2)}) async-start(), calls=%async_computation.21 | async-start | bytes 5242880 | tf_op jit(solution)/shard_map/all_gather | solution.py:774
  264.3 38.1 %copy-start.9 = (f32[1280,512]{1,0:T(8,128)S(1)}, f32[1280,512]{1,0:T(8,128)}, u32[]{:S(2)}) copy-start(f32[1280,512]{1,0:T(8,128)} %copy-done.8) | copy-start | bytes 7864324
  264.3 38.1 %copy-start.11 = (f32[1280,512]{1,0:T(8,128)S(1)}, f32[1280,512]{1,0:T(8,128)}, u32[]{:S(2)}) copy-start(f32[1280,512]{1,0:T(8,128)} %copy-done.10) | copy-start | bytes 7864324
  358.8 11.3 %all-to-all-start.7 = ((bf16[4,128,256]{1,2,0:T(8,128)(2,1)}), bf16[4,128,256]{1,2,0:T(8,128)(2,1)}, u32[]{:S(2)}, u32[]{:S(2)}) async-start(bf16[4,128,256]{1,2,0:T(8,128)(2,1)} %fusion.9), calls=%async_computation.7 | async-start | bytes 524288 | tf_op jit(solution)/shard_map/all_to_all | solution.py:605
  363.1 74.3 %all-gather.17.cloned.1.call-start = ((), (), s32[]{:S(2)}) async-start(), calls=%async_computation.22 | async-start | bytes 9461760 | tf_op jit(solution)/shard_map/all_gather | solution.py:818
  372.4 219.2 %reduce-scatter.8.cloned.1.call-start = ((), (), s32[]{:S(2)}) async-start(), calls=%async_computation.19 | async-start | bytes 2621440 | tf_op jit(solution)/shard_map/reduce_scatter | solution.py:841
  391.3 45.1 %collective-permute-start.3 = (bf16[128,1024]{1,0:T(8,128)(2,1)S(1)}, bf16[128,1024]{1,0:T(8,128)(2,1)S(1)}, u32[]{:S(2)}, u32[]{:S(2)}) collective-permute-start(bf16[128,1024]{1,0:T(8,128)(2,1)S(1)} %copy-done.21), channel_id=1, source_target_pairs={{0,1},{1,2},{2,3},{3,0},{4,5},{5,6},{6,7},{7,4},{8,9},{9,10},{10,1... | collective-permute-start | bytes 786440 | tf_op jit(solution)/shard_map/ppermute | solution.py:615
  391.7 45.0 %collective-permute-start.5 = (bf16[128,1024]{1,0:T(8,128)(2,1)S(1)}, bf16[128,1024]{1,0:T(8,128)(2,1)S(1)}, u32[]{:S(2)}, u32[]{:S(2)}) collective-permute-start(bf16[128,1024]{1,0:T(8,128)(2,1)S(1)} %copy-done.21), channel_id=1, source_target_pairs={{0,3},{1,0},{2,1},{3,2},{4,7},{5,4},{6,5},{7,6},{8,11},{9,8},{10,9... | collective-permute-start | bytes 786440 | tf_op jit(solution)/shard_map/ppermute | solution.py:615
  394.5 42.5 %collective-permute-start.4 = (bf16[128,1024]{1,0:T(8,128)(2,1)S(1)}, bf16[128,1024]{1,0:T(8,128)(2,1)S(1)}, u32[]{:S(2)}, u32[]{:S(2)}) collective-permute-start(bf16[128,1024]{1,0:T(8,128)(2,1)S(1)} %copy-done.21), channel_id=1, source_target_pairs={{0,2},{1,3},{2,0},{3,1},{4,6},{5,7},{6,4},{7,5},{8,10},{9,11},{10,... | collective-permute-start | bytes 786440 | tf_op jit(solution)/shard_map/ppermute | solution.py:615
  395.9 40.5 %copy-start.25 = (bf16[512,256]{1,0:T(8,128)(2,1)S(1)}, bf16[512,256]{1,0:T(8,128)(2,1)}, u32[]{:S(2)}) copy-start(bf16[512,256]{1,0:T(8,128)(2,1)} %copy-done.24) | copy-start | bytes 786436
  437.5 154.1 %reduce-scatter.4.cloned.1.call-start = ((), (), s32[]{:S(2)}) async-start(), calls=%async_computation.17 | async-start | bytes 2621440 | tf_op jit(solution)/shard_map/reduce_scatter | solution.py:839
  458.2 13.0 %all-to-all-start.9 = ((bf16[4,128,256]{2,1,0:T(8,128)(2,1)}), bf16[4,128,256]{2,1,0:T(8,128)(2,1)S(1)}, u32[]{:S(2)}, u32[]{:S(2)}) async-start(bf16[4,128,256]{2,1,0:T(8,128)(2,1)} %bitcast.55), calls=%async_computation.9 | async-start | bytes 524288 | tf_op jit(solution)/shard_map/all_to_all | solution.py:605
  461.6 130.0 %reduce-scatter.6.cloned.1.call-start = ((), (), s32[]{:S(2)}) async-start(), calls=%async_computation.18 | async-start | bytes 2621440 | tf_op jit(solution)/shard_map/reduce_scatter | solution.py:840
  471.2 56.3 %copy-start.28 = (bf16[4,128,256]{2,1,0:T(8,128)(2,1)}, bf16[4,128,256]{2,1,0:T(8,128)(2,1)S(1)}, u32[]{:S(2)}) copy-start(bf16[4,128,256]{2,1,0:T(8,128)(2,1)S(1)} %all-to-all-done.9) | copy-start | bytes 786436
  471.2 56.3 %all-to-all-start.8 = ((bf16[32,32,640]{2,1,0:T(8,128)(2,1)}), bf16[32,32,640]{2,1,0:T(8,128)(2,1)}, u32[]{:S(2)}, u32[]{:S(2)}) async-start(bf16[32,32,640]{2,1,0:T(8,128)(2,1)} %fusion.6), calls=%async_computation.8 | async-start | bytes 2621440 | tf_op jit(solution)/shard_map/all_to_all | solution.py:605
  538.6 11.4 %all-to-all-start.10 = ((bf16[4,128,256]{2,1,0:T(8,128)(2,1)}), bf16[4,128,256]{2,1,0:T(8,128)(2,1)S(1)}, u32[]{:S(2)}, u32[]{:S(2)}) async-start(bf16[4,128,256]{2,1,0:T(8,128)(2,1)} %bitcast.61), calls=%async_computation.10 | async-start | bytes 524288 | tf_op jit(solution)/shard_map/all_to_all | solution.py:605
  549.9 29.3 %all-to-all-start.11 = ((bf16[32,32,384]{2,1,0:T(8,128)(2,1)}), bf16[32,32,384]{2,1,0:T(8,128)(2,1)S(1)}, u32[]{:S(2)}, u32[]{:S(2)}) async-start(bf16[32,32,384]{2,1,0:T(8,128)(2,1)} %fusion.11), calls=%async_computation.11 | async-start | bytes 1572864 | tf_op jit(solution)/shard_map/all_to_all | solution.py:605
  568.5 22.5 %copy-start.42 = (bf16[32]{0:T(256)(128)(2,1)S(1)}, bf16[32]{0:T(256)(128)(2,1)}, u32[]{:S(2)}) copy-start(bf16[32]{0:T(256)(128)(2,1)} %param.27) | copy-start | bytes 196
  (34 other events, 214.9 us)
Sparse Core Ops, SparseCore 0:
  57.9 51.2 all-gather.8
  110.9 41.1 all-gather.12
  154.3 90.6 all-gather.10
  259.7 44.8 all-gather.14
  372.5 50.8 all-gather.16
  437.6 36.1 reduce-scatter.7
  476.9 29.3 reduce-scatter.3
  509.3 29.5 reduce-scatter.5

commit v4 on v3

--- a/solution.py
+++ b/solution.py
@@ -111,7 +111,7 @@
 
 
 def attend_kernel(
-    total, half, tile_blocks, table, own, q_in, kv, o_ref, lse_ref, kv_s, q_ref, acc, peak, sem
+    total, half, tile_blocks, table, own, q_in, kv, o_ref, lse_ref, kv_s, q_ref, acc, peak, s_buf, sem
 ):
     gather_blocks(
         table,
@@ -156,9 +156,40 @@
             for h in range(4):
                 lse_ref[i // 2, h : h + 1, lanes] = log_sum[h * BLK : (h + 1) * BLK].T[:1]
 
+        def score(j):
+            return dot(q_ref[...], kv_s[pl.ds(first_key(j), width), :LANES], NT)
+
+        def weigh(scores, j, masked):
+            start = first_key(j)
+            probs = jnp.exp(scores)
+            if masked:
+                probs = jnp.where(causal(probs.shape, start, block * BLK, True), probs, 0.0)
+            acc[...] += dot(probs.astype(BF16), kv_s[pl.ds(start, width), LANES:], NN)
+
         acc[...] = jnp.zeros_like(acc)
-        lax.fori_loop(0, n_a + n_b, clear_tile, 0)
-        tile(first_key(n_a + n_b), True)
+        count = n_a + n_b
+        s_buf[0] = score(0)
+
+        def two_tiles(i2, carry):
+            j = 2 * i2
+            s_buf[1] = score(j + 1)
+            weigh(s_buf[0], j, False)
+            s_buf[0] = score(j + 2)
+            weigh(s_buf[1], j + 1, False)
+            return carry
+
+        lax.fori_loop(0, count // 2, two_tiles, 0)
+
+        @pl.when(count % 2 == 1)
+        def _():
+            s_buf[1] = score(count)
+            weigh(s_buf[0], count - 1, False)
+            weigh(s_buf[1], count, True)
+
+        @pl.when(count % 2 == 0)
+        def _():
+            weigh(s_buf[0], count, True)
+
         sums = acc[:, LANES:]
         in_range = (jnp.max(sums) < 2.0**100) & (jnp.min(sums) > 2.0**-40)
 
@@ -290,6 +321,8 @@
     v_ref,
     dk_ref,
     dv_ref,
+    s_buf,
+    p_buf,
     sem,
 ):
     gather_blocks(
@@ -326,47 +359,60 @@
     wait_all(aux_s, sem.at[2])
     width = tile_blocks * BLK
 
-    def tile(first_row, per_head, start, keys_first, masked):
+    def score(first_row, per_head, j):
         rows = pl.ds(first_row, 4 * per_head)
-        queries = q_s[pl.ds(start, width), :]
-        grads = do_s[pl.ds(start, width), :]
-        scores = dot(k_ref[rows, :], queries, NT)
-        prob_grad = dot(v_ref[rows, :], grads, NT)
+        start = pl.multiple_of(j * width, width)
+        scores = dot(k_ref[rows, :], q_s[pl.ds(start, width), :], NT)
+        return scores, dot(v_ref[rows, :], do_s[pl.ds(start, width), :], NT)
+
+    def add(first_row, per_head, j, scores, prob_grad, keys_first):
+        rows = pl.ds(first_row, 4 * per_head)
+        start = pl.multiple_of(j * width, width)
         probs_low = []
         score_low = []
         for h in range(4):
             part = slice(h * per_head, (h + 1) * per_head)
             probs = jnp.exp(scores[part] - aux_s[h : h + 1, pl.ds(start, width)])
-            if masked:
+            if keys_first is not None:
                 seen = [causal((BLK, width), first, start, False) for first in keys_first]
                 probs = jnp.where(jnp.concatenate(seen, axis=0), probs, 0.0)
             probs_low.append(probs.astype(BF16))
             shifted = prob_grad[part] - aux_s[4 + h : 5 + h, pl.ds(start, width)]
             score_low.append((probs * shifted).astype(BF16))
+        grads = do_s[pl.ds(start, width), :]
         dv_ref[rows, :] += dot(jnp.concatenate(probs_low, axis=0), grads, NN)
+        queries = q_s[pl.ds(start, width), :]
         dk_ref[rows, :] += dot(jnp.concatenate(score_low, axis=0), queries, NN)
 
     low = jnp.minimum(own[0], own[1])
     high = jnp.maximum(own[0], own[1])
-
-    def edge_tile(j, carry):
-        firsts = [own[0] * BLK, own[1] * BLK]
-        tile(0, 2 * BLK, pl.multiple_of(j * width, width), firsts, True)
-        return carry
-
-    def clear_tile(j, carry):
-        tile(0, 2 * BLK, pl.multiple_of(j * width, width), None, False)
-        return carry
-
-    lax.fori_loop(low // tile_blocks, high // tile_blocks + 1, edge_tile, 0)
-    lax.fori_loop(high // tile_blocks + 1, total // tile_blocks, clear_tile, 0)
+    last = total // tile_blocks - 1
+
+    def fill(side, j):
+        s_buf[side], p_buf[side] = score(0, 2 * BLK, jnp.minimum(j, last))
+
+    def two_tiles(keys_first):
+        def step(i, carry):
+            fill(1, 2 * i + 1)
+            add(0, 2 * BLK, 2 * i, s_buf[0], p_buf[0], keys_first)
+            fill(0, 2 * i + 2)
+            add(0, 2 * BLK, 2 * i + 1, s_buf[1], p_buf[1], keys_first)
+            return carry
+
+        return step
+
+    pair = 2 * tile_blocks
+    fill(0, low // pair * 2)
+    edge = [own[0] * BLK, own[1] * BLK]
+    lax.fori_loop(low // pair, high // pair + 1, two_tiles(edge), 0)
+    lax.fori_loop(high // pair + 1, total // pair, two_tiles(None), 0)
     for which in range(2):
         block = own[2 + which]
         stop = half + ((block - half) // CONT_BLKS + 1) * CONT_BLKS
 
         def cont_tile(j, carry, which=which, block=block):
             first_row = (8 + 4 * which) * BLK
-            tile(first_row, BLK, pl.multiple_of(j * width, width), [block * BLK], True)
+            add(first_row, BLK, j, *score(first_row, BLK, j), [block * BLK])
             return carry
 
         lax.fori_loop(block // tile_blocks, stop // tile_blocks, cont_tile, 0)
@@ -526,6 +572,7 @@
             pltpu.VMEM((4 * BLK, LANES), BF16),
             pltpu.VMEM((4 * BLK, 2 * LANES), F32),
             pltpu.VMEM((4 * BLK, LANES), F32),
+            pltpu.VMEM((2, 4 * BLK, 8 * BLK), F32),
             pltpu.SemaphoreType.DMA((1,)),
         ],
         20 * 10**9,
@@ -558,7 +605,7 @@
     total = table.shape[0]
     ins = [(x, False) for x in (kv, cosine, sine)] + [(x, True) for x in (q_all, do_all, aux)]
     return kernel_call(
-        functools.partial(pair_grad_kernel, total, total // 2, 2, do_rows),
+        functools.partial(pair_grad_kernel, total, total // 2, 4, do_rows),
         "pair_grad",
         (table, own),
         ins,
@@ -571,6 +618,8 @@
             pltpu.VMEM((16 * BLK, 2 * LANES), BF16),
             pltpu.VMEM((16 * BLK, 2 * LANES), F32),
             pltpu.VMEM((16 * BLK, 2 * LANES), F32),
+            pltpu.VMEM((2, 8 * BLK, 4 * BLK), F32),
+            pltpu.VMEM((2, 8 * BLK, 4 * BLK), F32),
             pltpu.SemaphoreType.DMA((3,)),
         ],
         40 * 10**9,
@@ -792,7 +841,15 @@
         grad_copies, gate_pre, up_pre, expert
     )
     arrived_grad = send(input_grad)
-    arrived_grad, all_qkv = lax.optimization_barrier((arrived_grad, all_qkv))
+
+    gate_part = dot(expert_in, gate_grad, TN)
+    up_part = dot(expert_in, up_grad, TN)
+    down_part = dot(hidden_act, grad_copies, TN)
+    gate_part = gate_part.reshape(model_width, exp_count, width).transpose(1, 0, 2)
+    up_part = up_part.reshape(model_width, exp_count, width).transpose(1, 0, 2)
+    arrived_grad, all_qkv, gate_part, up_part, down_part = lax.optimization_barrier(
+        (arrived_grad, all_qkv, gate_part, up_part, down_part)
+    )
     ffn_normed_grad = dot(pick, arrived_grad, TN)
 
     ffn_gain_part = jnp.sum(ffn_normed_grad * ffn_hat, axis=0)
@@ -828,56 +885,12 @@
         term = dot(part, lax.dynamic_slice_in_dim(heads_low, first, own_rows, 0), TN)
         grad_out = term if grad_out is None else grad_out + term
 
-    gate_part = dot(expert_in, gate_grad, TN)
-    up_part = dot(expert_in, up_grad, TN)
-    down_part = dot(hidden_act, grad_copies, TN)
-    gate_part = gate_part.reshape(model_width, exp_count, width).transpose(1, 0, 2)
-    up_part = up_part.reshape(model_width, exp_count, width).transpose(1, 0, 2)
     do_all, query_n_grad, grad_out, gate_part, up_part, down_part = lax.optimization_barrier(
         (do_all, query_n_grad, grad_out, gate_part, up_part, down_part)
     )
     grad_w_gate = lax.psum_scatter(gate_part, "exp", scatter_dimension=0, tiled=True)
     grad_w_up = lax.psum_scatter(up_part, "exp", scatter_dimension=0, tiled=True)
     grad_w_down = lax.psum_scatter(down_part, "exp", scatter_dimension=0, tiled=True)[None]
-
-    query_gain_part = jnp.sum(query_n_grad * query_hat, axis=0)
-    query_hat_grad = query_n_grad * query_gain
-    early = jnp.concatenate(
-        [
-            jnp.sum(query_hat_grad * query_hat, axis=1),
-            lax.dynamic_update_slice_in_dim(
-                jnp.zeros((model_width,), F32), query_gain_part, exp_index * head_cols, 0
-            ),
-            ffn_gain_part,
-            jnp.full((4 * LANES,), local_loss),
-        ]
-    )
-    early = lax.psum(early.reshape(-1, LANES), "exp").reshape(-1)
-    do_all, early = lax.optimization_barrier((do_all, early))
-    query_stat = early[:ctx_rows, None] / model_width
-    query_low = (query_scale * (query_hat_grad - query_hat * query_stat)).astype(BF16)
-    early_sums = jnp.stack(
-        [
-            early[ctx_rows : ctx_rows + model_width].reshape(ctx_count, shard_rows),
-            early[ctx_rows + model_width : ctx_rows + 2 * model_width].reshape(
-                ctx_count, shard_rows
-            ),
-            jnp.broadcast_to(early[-1], (ctx_count, shard_rows)),
-        ],
-        axis=-1,
-    )
-    early_shards = exchange(
-        jnp.concatenate(
-            [
-                dot(normed, query_low, TN).astype(BF16).reshape(ctx_count, shard_rows, head_cols),
-                grad_out.astype(BF16).reshape(ctx_count, shard_rows, head_cols),
-                ride_along(early_sums),
-            ],
-            axis=2,
-        ),
-        "ctx",
-    )
-    early_back = exchange(query_low.reshape(exp_count, own_rows, head_cols), "exp")
 
     aux = jnp.sum(
         do_all[:, ctx_rows:].reshape(ctx_count, 3, 2, 8, 2 * BLK).astype(F32), axis=1
@@ -893,57 +906,71 @@
         ctx_rows + stat_rows,
         aux,
     )
-    pair_grads, early_shards, early_back = lax.optimization_barrier(
-        (pair_grads, early_shards, early_back)
-    )
     key_n_grad = pair_grads[:, :kv_cols]
     value_grad = pair_grads[:, kv_cols:].astype(BF16)
+    query_gain_part = jnp.sum(query_n_grad * query_hat, axis=0)
     key_gain_part = jnp.sum(key_n_grad * key_hat, axis=0)
+    query_hat_grad = query_n_grad * query_gain
     key_hat_grad = key_n_grad * key_gain
-    late = jnp.concatenate(
+    stats = jnp.concatenate(
         [
+            jnp.sum(query_hat_grad * query_hat, axis=1),
             jnp.sum(key_hat_grad * key_hat, axis=1),
+            lax.dynamic_update_slice_in_dim(
+                jnp.zeros((model_width,), F32), query_gain_part, exp_index * head_cols, 0
+            ),
+            ffn_gain_part,
             lax.dynamic_update_slice_in_dim(
                 jnp.zeros((kv_total,), F32), key_gain_part, exp_index * kv_cols, 0
             ),
+            jnp.full((kv_total,), local_loss),
         ]
     )
-    late = lax.psum(late.reshape(-1, LANES), "exp").reshape(-1)
-    key_stat = late[:ctx_rows, None] / kv_total
+    stats = lax.psum(stats.reshape(-1, LANES), "exp").reshape(-1)
+    query_stat = stats[:ctx_rows, None] / model_width
+    key_stat = stats[ctx_rows : 2 * ctx_rows, None] / kv_total
+    sums = stats[2 * ctx_rows :]
+    query_low = (query_scale * (query_hat_grad - query_hat * query_stat)).astype(BF16)
     key_low = (key_scale * (key_hat_grad - key_hat * key_stat)).astype(BF16)
-    pair_low = jnp.concatenate([key_low, value_grad], axis=1)
-    key_sums = jnp.repeat(late[ctx_rows:].reshape(ctx_count, -1), 2, axis=1)[:, :, None]
-    late_shards = exchange(
+    grad_low = jnp.concatenate([query_low, key_low, value_grad], axis=1)
+
+    wide_sums = jnp.stack(
+        [
+            sums[:model_width].reshape(ctx_count, shard_rows),
+            sums[model_width : 2 * model_width].reshape(ctx_count, shard_rows),
+            jnp.repeat(
+                sums[2 * model_width : 2 * model_width + kv_total].reshape(ctx_count, -1), 2, axis=1
+            ),
+            jnp.broadcast_to(sums[-1], (ctx_count, shard_rows)),
+        ],
+        axis=-1,
+    )
+    grad_qkv = dot(normed, grad_low, TN)
+    shards = exchange(
         jnp.concatenate(
             [
-                dot(normed, pair_low, TN).astype(BF16).reshape(ctx_count, shard_rows, 2 * kv_cols),
-                ride_along(key_sums),
+                grad_qkv.astype(BF16).reshape(ctx_count, shard_rows, qkv_cols),
+                grad_out.astype(BF16).reshape(ctx_count, shard_rows, head_cols),
+                ride_along(wide_sums),
             ],
             axis=2,
         ),
         "ctx",
     )
-    late_back = exchange(pair_low.reshape(exp_count, own_rows, 2 * kv_cols), "exp")
-    early_shards = jnp.sum(early_shards.astype(F32), axis=0)
-    late_shards = jnp.sum(late_shards.astype(F32), axis=0)
-    grad_w_query = early_shards[:, :head_cols]
-    grad_w_out = early_shards[:, head_cols : 2 * head_cols]
-    early_tail = parted(early_shards[:, 2 * head_cols :], 3)
-    loss = early_tail[0, 2] / (valid_count * model_width)
-    grad_w_key = late_shards[:, :kv_cols]
-    grad_w_value = late_shards[:, kv_cols : 2 * kv_cols]
-    key_tail = parted(late_shards[:, 2 * kv_cols :], 1)
+    back = exchange(grad_low.reshape(exp_count, own_rows, qkv_cols), "exp")
+    shards = jnp.sum(shards.astype(F32), axis=0)
+    grad_w_query = shards[:, :head_cols]
+    grad_w_key = shards[:, head_cols : head_cols + kv_cols]
+    grad_w_value = shards[:, head_cols + kv_cols : qkv_cols]
+    grad_w_out = shards[:, qkv_cols : qkv_cols + head_cols]
+    tail = parted(shards[:, qkv_cols + head_cols :], 4)
+    loss = tail[0, 3] / (valid_count * model_width)
 
     gain_part = jnp.sum(grad_w_query * w_query.astype(F32), axis=1)
     gain_part += jnp.sum(grad_w_key * w_key.astype(F32), axis=1)
     gain_part += jnp.sum(grad_w_value * w_value.astype(F32), axis=1)
     grad_gain_attn = lax.psum(gain_part, "exp") / gain_attn.astype(F32)
-    normed_rows = jnp.einsum(
-        "erk,edk->rd",
-        jnp.concatenate([early_back, late_back], axis=2),
-        all_qkv,
-        preferred_element_type=F32,
-    )
+    normed_rows = jnp.einsum("erk,edk->rd", back, all_qkv, preferred_element_type=F32)
     own_scale = lax.dynamic_slice_in_dim(attn_scale, exp_index * own_rows, own_rows, 0)
     own_hat = hidden_rows * own_scale
     grad_hidden = resid_grad + norm_back(normed_rows, own_hat, own_scale, attn_gain)
@@ -956,9 +983,9 @@
         grad_w_value,
         grad_w_out,
         grad_gain_attn,
-        early_tail[:, 0],
-        key_tail[::2, 0],
-        early_tail[:, 1],
+        tail[:, 0],
+        tail[::2, 2],
+        tail[:, 1],
         grad_w_gate,
         grad_w_up,
         grad_w_down,

time: 607 us -> 577 us (0.951)
  blocking collectives: 135 us -> 89.2 us
  waiting for transfers between devices: 148 us -> 176 us
  Pallas kernels: 136 us -> 128 us
    all_to_all x3 -> x2, blocking collectives: 89.9 us -> 52.2 us  [exchange(): return lax.all_to_all(values, axis, split_axis=0, concat_axis=0, tiled=True)]
    all_to_all x9 -> x8, waiting for transfers between devices: 125 us -> 150 us  [exchange(): return lax.all_to_all(values, axis, split_axis=0, concat_axis=0, tiled=True)]
    pallas_call x4, Pallas kernels: 119 us -> 111 us  [kernel_call(): pl.pallas_call(kernel, out_shape=tuple(outs), grid_spec=pltpu.PrefetchSca...]
    psum x2 -> x1, blocking collectives: 24 us -> 17.4 us  [on_device(): stats = lax.psum(stats.reshape(-1, LANES), 'exp').reshape(-1)]
    all_to_all x9 -> x8, starting transfers between devices: 58.5 us -> 55 us  [exchange(): return lax.all_to_all(values, axis, split_axis=0, concat_axis=0, tiled=True)]
    unnamed x94 -> x108, local copies, waits for them, and re-layouts: 11.3 us -> 12.4 us
    dot_general x15 -> x14, matrix products: 31 us -> 30 us  [dot(): return lax.dot_general(left, right, dims, preferred_element_type=F32)]
  transfers between devices with their start and end apart: 23 -> 22, of which waited for: 12 -> 13; matrix products, arithmetic and copies ran while one was open for 12% -> 12% of each run, Pallas kernels for 23% -> 22%
where the time goes in v4:
time: 577 us; the launch traced here: 571 us
  waiting for transfers between devices  176 us (31%)
  Pallas kernels  128 us (22%)
  blocking collectives  89.2 us (15%)
  starting transfers between devices  62.2 us (11%)
  matrix products  38.4 us (7%)
  local copies, waits for them, and re-layouts  33.8 us (6%)
  other arithmetic  24.1 us (4%)
  between operations  18.5 us (3%)
    all_to_all x8, waiting for transfers between devices, exchange(): return lax.all_to_all(values, axis, split_axis=0, concat_axis=0, tiled=True)  150 us
    pallas_call x4, Pallas kernels, kernel_call(): pl.pallas_call(kernel, out_shape=tuple(outs), grid_spec=pltpu.PrefetchSca...  111 us
    all_to_all x8, starting transfers between devices, exchange(): return lax.all_to_all(values, axis, split_axis=0, concat_axis=0, tiled=True)  55 us
    all_to_all x2, blocking collectives, exchange(): return lax.all_to_all(values, axis, split_axis=0, concat_axis=0, tiled=True)  52.2 us
    dot_general x14, matrix products, dot(): return lax.dot_general(left, right, dims, preferred_element_type=F32)  30 us
    ppermute x6, waiting for transfers between devices, shifted(): lax.ppermute(values, axis, [(i, (i + step) % count) for i in range(count)])  21.8 us
    psum x1, blocking collectives, on_device(): stats = lax.psum(stats.reshape(-1, LANES), 'exp').reshape(-1)  17.4 us
    pallas_call x2, Pallas kernels, by_rows(): pl.pallas_call(kernel, out_shape=tuple(outs), grid=(outs[0].shape[0] // r...  16.9 us
  transfers between devices with their start and end apart: 22, of which 13 were waited for; matrix products, arithmetic and copies ran while one was open for 12% of the time, Pallas kernels for 22%

profile of v4, /device:TPU:0, one launch (start us, length us, event | category | flops | bytes accessed | tf_op | source)
XLA Modules:
  0.0 570.7 jit_solution(4145397083014701477)
XLA Ops:
  12.2 8.4 %all-to-all-start = ((bf16[32,40,512]{2,1,0:T(8,128)(2,1)}), bf16[32,40,512]{2,1,0:T(8,128)(2,1)S(1)}, u32[]{:S(2)}, u32[]{:S(2)}) async-start(bf16[32,40,512]{2,1,0:T(8,128)(2,1)} %broadcast_in_dim.112), calls=%async_computation | async-start | bytes 2621440 | tf_op jit(solution)/shard_map/all_to_all | solution.py:654
  22.6 18.8 %all-to-all-done = bf16[32,40,512]{2,1,0:T(8,128)(2,1)S(1)} async-done(((bf16[32,40,512]{2,1,0:T(8,128)(2,1)}), bf16[32,40,512]{2,1,0:T(8,128)(2,1)S(1)}, u32[]{:S(2)}, u32[]{:S(2)}) %all-to-all-start) | async-done | bytes 1310752 | tf_op jit(solution)/shard_map/all_to_all | solution.py:654
  45.2 10.7 %psum.21 = f32[2,512]{1,0:T(2,128)S(1)} all-reduce(f32[2,512]{1,0:T(2,128)S(1)} %pad_maximum_fusion.10), channel_id=1, replica_groups=mesh['ctx'=32,'exp'=4] {'exp'}, use_global_device_ids=true, to_apply=%region_4.5 | all-reduce | flops 1024 | bytes 8192 | tf_op jit(solution)/shard_map/psum | solution.py:748
  60.0 3.9 all-to-all-start.1
  64.0 13.8 %all-to-all-done.1 = bf16[32,32,256]{2,1,0:T(8,128)(2,1)S(1)} async-done(((bf16[32,32,256]{2,1,0:T(8,128)(2,1)}), bf16[32,32,256]{2,1,0:T(8,128)(2,1)S(1)}, u32[]{:S(2)}, u32[]{:S(2)}) %all-to-all-start.1) | async-done | bytes 524320 | tf_op jit(solution)/shard_map/all_to_all | solution.py:654
  83.0 9.4 %collective-permute-done = bf16[1024,256]{1,0:T(8,128)(2,1)S(1)} collective-permute-done((bf16[1024,256]{1,0:T(8,128)(2,1)S(1)}, bf16[1024,256]{1,0:T(8,128)(2,1)S(1)}, u32[]{:S(2)}, u32[]{:S(2)}) %collective-permute-start) | collective-permute-done | bytes 524320 | tf_op jit(solution)/shard_map/ppermute | solution.py:664
  94.1 10.8 %collective-permute-done.2 = bf16[1024,256]{1,0:T(8,128)(2,1)} collective-permute-done((bf16[1024,256]{1,0:T(8,128)(2,1)S(1)}, bf16[1024,256]{1,0:T(8,128)(2,1)}, u32[]{:S(2)}, u32[]{:S(2)}) %collective-permute-start.2) | collective-permute-done | bytes 524320 | tf_op jit(solution)/shard_map/ppermute | solution.py:664
  109.1 26.1 %attend.1 = (f32[512,256]{1,0:T(8,128)S(1)}, f32[2,4,256]{2,1,0:T(4,128)S(1)}) custom-call(s32[128]{0:T(128)S(1)} %copy-done.6, s32[4]{0:T(128)S(1)} %get-tuple-element.105.own, bf16[512,256]{1,0:T(8,128)(2,1)} %get-tuple-element.63.q_in, bf16[16384,256]{1,0:T(8,128)(2,1)} %all-gather.9.cloned.1.call-done.kv), custom_call_target="tpu_custom_call" | custom-call | flops 20000000000 | bytes 8650752 | tf_op jit(solution)/shard_map/attend/pallas_call | solution.py:488
  135.2 14.5 %all_to_all.50 = bf16[4,128,256]{2,1,0:T(8,128)(2,1)} all-to-all(bf16[4,128,256]{2,1,0:T(8,128)(2,1)S(1)} %bitcast.152), channel_id=1, replica_groups=mesh['ctx'=32,'exp'=4] {'exp'}, dimensions={0} | all-to-all | bytes 524288 | tf_op jit(solution)/shard_map/all_to_all | solution.py:654
  154.8 5.7 all-to-all-start.3
  160.5 4.7 copy.98
  165.2 34.4 %all-to-all-done.3 = bf16[32,40,1024]{2,1,0:T(8,128)(2,1)} async-done(((bf16[32,40,1024]{2,1,0:T(8,128)(2,1)}), bf16[32,40,1024]{2,1,0:T(8,128)(2,1)}, u32[]{:S(2)}, u32[]{:S(2)}) %all-to-all-start.3) | async-done | bytes 2621472 | tf_op jit(solution)/shard_map/all_to_all | solution.py:654
  201.4 6.5 %expert.1 = (bf16[1280,1024]{1,0:T(8,128)(2,1)S(1)}, f32[1280,512]{1,0:T(8,128)S(1)}, f32[1280,512]{1,0:T(8,128)S(1)}) custom-call(bf16[1280,1024]{1,0:T(8,128)(2,1)} %bitcast.22.x_ref, bf16[4,1024,384]{2,1,0:T(8,128)(2,1)S(1)} %bitcast.137), custom_call_target="tpu_custom_call" | custom-call | flops 4026531840 | bytes 10000000 | tf_op jit(solution)/shard_map/expert/pallas_call | solution.py:510
  212.4 4.9 all-to-all-start.4
  220.1 34.3 %all-to-all-done.4 = bf16[32,40,1024]{2,1,0:T(8,128)(2,1)} async-done(((bf16[32,40,1024]{2,1,0:T(8,128)(2,1)}), bf16[32,40,1024]{2,1,0:T(8,128)(2,1)}, u32[]{:S(2)}, u32[]{:S(2)}) %all-to-all-start.4) | async-done | bytes 2621472 | tf_op jit(solution)/shard_map/all_to_all | solution.py:654
  259.2 37.6 %all_to_all.51 = bf16[32,40,1024]{2,1,0:T(8,128)(2,1)S(1)} all-to-all(bf16[32,40,1024]{2,1,0:T(8,128)(2,1)S(1)} %bitcast.151), channel_id=1, replica_groups=mesh['ctx'=32,'exp'=4] {'ctx'}, dimensions={0} | all-to-all | bytes 5242880 | tf_op jit(solution)/shard_map/all_to_all | solution.py:654
  296.9 10.4 %expert_grad.1 = (bf16[1280,1024]{1,0:T(8,128)(2,1)S(1)}, bf16[1280,512]{1,0:T(8,128)(2,1)S(1)}, bf16[1280,512]{1,0:T(8,128)(2,1)S(1)}, bf16[1280,512]{1,0:T(8,128)(2,1)S(1)}) custom-call(bf16[1280,1024]{1,0:T(8,128)(2,1)S(1)} %bitcast.134, f32[1280,512]{1,0:T(8,128)S(1)} %copy-done.8, f32[1280,512]{1,0:T(8,128)S(1)} %copy-done.10, ...), custom_call_target="tpu_custom_call" | custom-call | flops 4026531840 | bytes 10000000 | tf_op jit(solution)/shard_map/expert_grad/pallas_call | solution.py:510
  310.9 5.3 all-to-all-start.6
  320.1 5.1 fusion.100
  325.2 4.6 convolution_bitcast_fusion
  329.9 5.1 convolution_bitcast_fusion.1
  334.9 17.3 %all-to-all-done.6 = bf16[32,40,1024]{2,1,0:T(8,128)(2,1)} async-done(((bf16[32,40,1024]{2,1,0:T(8,128)(2,1)}), bf16[32,40,1024]{2,1,0:T(8,128)(2,1)}, u32[]{:S(2)}, u32[]{:S(2)}) %all-to-all-start.6) | async-done | bytes 2621472 | tf_op jit(solution)/shard_map/all_to_all | solution.py:654
  358.4 4.3 all-to-all-start.7
  362.6 6.7 %all-to-all-done.7 = bf16[4,128,256]{1,2,0:T(8,128)(2,1)S(1)} async-done(((bf16[4,128,256]{1,2,0:T(8,128)(2,1)}), bf16[4,128,256]{1,2,0:T(8,128)(2,1)S(1)}, u32[]{:S(2)}, u32[]{:S(2)}) %all-to-all-start.7) | async-done | bytes 262176 | tf_op jit(solution)/shard_map/all_to_all | solution.py:654
  374.4 41.6 %query_grad.1 = f32[512,256]{1,0:T(8,128)S(1)} custom-call(s32[128]{0:T(128)S(1)} %copy-done.6, s32[4]{0:T(128)S(1)} %get-tuple-element.105.own, bf16[512,256]{1,0:T(8,128)(2,1)} %get-tuple-element.63.q_in, bf16[512,256]{1,0:T(8,128)(2,1)S(1)} %bitcast.142, f32[512,256]{1,0:T(8,128)S(1)} %get-tuple-element.54.o_in, ...), custom_call_target="tpu_custom_call" | custom-call | flops 30000001024 | bytes 9969664 | tf_op jit(solution)/shard_map/query_grad/pallas_call | solution.py:488
  422.5 42.4 %pair_grad.1 = f32[512,256]{1,0:T(8,128)S(1)} custom-call(s32[128]{0:T(128)S(1)} %copy-done.6, s32[4]{0:T(128)S(1)} %get-tuple-element.105.own, bf16[512,256]{1,0:T(8,128)(2,1)} %get-tuple-element.51.kv_in, f32[512,128]{1,0:T(8,128)S(1)} %get-tuple-element.143.cos_ref, f32[512,128]{1,0:T(8,128)S(1)} %get-tuple-element.144.sin_ref, ...), custom_call_target="tpu_custom_call" | custom-call | flops 40000000000 | bytes 18874368 | tf_op jit(solution)/shard_map/pair_grad/pallas_call | solution.py:488
  466.6 17.4 %psum.22 = f32[32,128]{1,0:T(8,128)S(1)} all-reduce(f32[32,128]{1,0:T(8,128)S(1)} %bitcast.178), channel_id=1, replica_groups=mesh['ctx'=32,'exp'=4] {'exp'}, use_global_device_ids=true, to_apply=%region_18.19 | all-reduce | flops 4096 | bytes 32768 | tf_op jit(solution)/shard_map/psum | solution.py:929
  497.2 4.7 all-to-all-done.9
  502.7 19.0 %all-to-all-start.8 = ((bf16[32,32,896]{2,1,0:T(8,128)(2,1)}), bf16[32,32,896]{2,1,0:T(8,128)(2,1)S(1)}, u32[]{:S(2)}, u32[]{:S(2)}) async-start(bf16[32,32,896]{2,1,0:T(8,128)(2,1)} %fusion.4), calls=%async_computation.8 | async-start | bytes 3670016 | tf_op jit(solution)/shard_map/all_to_all | solution.py:654
  523.2 4.0 fusion.22
  528.3 20.4 %all-to-all-done.8 = bf16[32,32,896]{2,1,0:T(8,128)(2,1)S(1)} async-done(((bf16[32,32,896]{2,1,0:T(8,128)(2,1)}), bf16[32,32,896]{2,1,0:T(8,128)(2,1)S(1)}, u32[]{:S(2)}, u32[]{:S(2)}) %all-to-all-start.8) | async-done | bytes 1835040 | tf_op jit(solution)/shard_map/all_to_all | solution.py:654
  552.4 8.9 %psum.23 = f32[32]{0:T(128)S(1)} all-reduce(f32[32]{0:T(128)S(1)} %add_add_fusion), channel_id=1, replica_groups=mesh['ctx'=32,'exp'=4] {'exp'}, use_global_device_ids=true, to_apply=%region_24.25 | all-reduce | flops 32 | bytes 256 | tf_op jit(solution)/shard_map/psum | solution.py:972
  (264 shorter events, 90.7 us)
Async XLA Ops:
  12.2 29.2 %all-to-all-start = ((bf16[32,40,512]{2,1,0:T(8,128)(2,1)}), bf16[32,40,512]{2,1,0:T(8,128)(2,1)S(1)}, u32[]{:S(2)}, u32[]{:S(2)}) async-start(bf16[32,40,512]{2,1,0:T(8,128)(2,1)} %broadcast_in_dim.112), calls=%async_computation | async-start | bytes 2621440 | tf_op jit(solution)/shard_map/all_to_all | solution.py:654
  20.6 88.5 %all-gather.9.cloned.1.call-start = ((), (), s32[]{:S(2)}) async-start(), calls=%async_computation.13 | async-start | bytes 8650752 | tf_op jit(solution)/shard_map/all_gather | solution.py:770
  57.7 102.8 %all-gather.13.cloned.1.call-start = ((), (), s32[]{:S(2)}) async-start(), calls=%async_computation.18 | async-start | bytes 3932160 | tf_op jit(solution)/shard_map/all_gather | solution.py:776
  60.0 17.8 %all-to-all-start.1 = ((bf16[32,32,256]{2,1,0:T(8,128)(2,1)}), bf16[32,32,256]{2,1,0:T(8,128)(2,1)S(1)}, u32[]{:S(2)}, u32[]{:S(2)}) async-start(bf16[32,32,256]{2,1,0:T(8,128)(2,1)} %broadcast_in_dim.114), calls=%async_computation.1 | async-start | bytes 1048576 | tf_op jit(solution)/shard_map/all_to_all | solution.py:654
  63.9 190.5 %all-gather.11.cloned.1.call-start = ((), (), s32[]{:S(2)}) async-start(), calls=%async_computation.14 | async-start | bytes 8650752 | tf_op jit(solution)/shard_map/all_gather | solution.py:805
  77.7 14.7 %collective-permute-start = (bf16[1024,256]{1,0:T(8,128)(2,1)S(1)}, bf16[1024,256]{1,0:T(8,128)(2,1)S(1)}, u32[]{:S(2)}, u32[]{:S(2)}) collective-permute-start(bf16[1024,256]{1,0:T(8,128)(2,1)S(1)} %bitcast.154), channel_id=1, source_target_pairs={{0,3},{1,0},{2,1},{3,2},{4,7},{5,4},{6,5},{7,6},{8,11},{9,8},{10,9... | collective-permute-start | bytes 1572872 | tf_op jit(solution)/shard_map/ppermute | solution.py:664
  77.7 16.4 %collective-permute-start.1 = (bf16[1024,256]{1,0:T(8,128)(2,1)S(1)}, bf16[1024,256]{1,0:T(8,128)(2,1)}, u32[]{:S(2)}, u32[]{:S(2)}) collective-permute-start(bf16[1024,256]{1,0:T(8,128)(2,1)S(1)} %bitcast.155), channel_id=1, source_target_pairs={{0,2},{1,3},{2,0},{3,1},{4,6},{5,7},{6,4},{7,5},{8,10},{9,11},{10,... | collective-permute-start | bytes 1572872 | tf_op jit(solution)/shard_map/ppermute | solution.py:664
  80.0 24.9 %collective-permute-start.2 = (bf16[1024,256]{1,0:T(8,128)(2,1)S(1)}, bf16[1024,256]{1,0:T(8,128)(2,1)}, u32[]{:S(2)}, u32[]{:S(2)}) collective-permute-start(bf16[1024,256]{1,0:T(8,128)(2,1)S(1)} %bitcast.156), channel_id=1, source_target_pairs={{0,1},{1,2},{2,3},{3,0},{4,5},{5,6},{6,7},{7,4},{8,9},{9,10},{10,1... | collective-permute-start | bytes 1572872 | tf_op jit(solution)/shard_map/ppermute | solution.py:664
  81.5 70.9 %copy-start.19 = (bf16[1280,128]{1,0:T(8,128)(2,1)}, bf16[1280,128]{1,0:T(8,128)(2,1)S(1)}, u32[]{:S(2)}) copy-start(bf16[1280,128]{1,0:T(8,128)(2,1)S(1)} %fusion.19) | copy-start | bytes 983044
  152.3 104.9 %copy-start.12 = (f32[128,1024]{1,0:T(8,128)}, f32[128,1024]{1,0:T(8,128)S(1)}, u32[]{:S(2)}) copy-start(f32[128,1024]{1,0:T(8,128)S(1)} %get-tuple-element.137) | copy-start | bytes 1572868
  154.8 44.8 %all-to-all-start.3 = ((bf16[32,40,1024]{2,1,0:T(8,128)(2,1)}), bf16[32,40,1024]{2,1,0:T(8,128)(2,1)}, u32[]{:S(2)}, u32[]{:S(2)}) async-start(bf16[32,40,1024]{2,1,0:T(8,128)(2,1)} %bitcast.146), calls=%async_computation.3 | async-start | bytes 5242880 | tf_op jit(solution)/shard_map/all_to_all | solution.py:654
  212.4 42.0 %all-to-all-start.4 = ((bf16[32,40,1024]{2,1,0:T(8,128)(2,1)}), bf16[32,40,1024]{2,1,0:T(8,128)(2,1)}, u32[]{:S(2)}, u32[]{:S(2)}) async-start(bf16[32,40,1024]{2,1,0:T(8,128)(2,1)} %bitcast.138), calls=%async_computation.4 | async-start | bytes 5242880 | tf_op jit(solution)/shard_map/all_to_all | solution.py:654
  217.4 134.9 %all-gather.15.cloned.1.call-start = ((), (), s32[]{:S(2)}) async-start(), calls=%async_computation.19 | async-start | bytes 5242880 | tf_op jit(solution)/shard_map/all_gather | solution.py:823
  259.2 37.7 %copy-start.8 = (f32[1280,512]{1,0:T(8,128)S(1)}, f32[1280,512]{1,0:T(8,128)}, u32[]{:S(2)}) copy-start(f32[1280,512]{1,0:T(8,128)} %copy-done.7) | copy-start | bytes 7864324
  259.2 37.7 %copy-start.10 = (f32[1280,512]{1,0:T(8,128)S(1)}, f32[1280,512]{1,0:T(8,128)}, u32[]{:S(2)}) copy-start(f32[1280,512]{1,0:T(8,128)} %copy-done.9) | copy-start | bytes 7864324
  310.9 41.3 %all-to-all-start.6 = ((bf16[32,40,1024]{2,1,0:T(8,128)(2,1)}), bf16[32,40,1024]{2,1,0:T(8,128)(2,1)}, u32[]{:S(2)}, u32[]{:S(2)}) async-start(bf16[32,40,1024]{2,1,0:T(8,128)(2,1)} %bitcast.139), calls=%async_computation.6 | async-start | bytes 5242880 | tf_op jit(solution)/shard_map/all_to_all | solution.py:654
  358.4 11.0 %all-to-all-start.7 = ((bf16[4,128,256]{1,2,0:T(8,128)(2,1)}), bf16[4,128,256]{1,2,0:T(8,128)(2,1)S(1)}, u32[]{:S(2)}, u32[]{:S(2)}) async-start(bf16[4,128,256]{1,2,0:T(8,128)(2,1)} %fusion.8), calls=%async_computation.7 | async-start | bytes 524288 | tf_op jit(solution)/shard_map/all_to_all | solution.py:654
  362.6 58.2 %all-gather.17.cloned.1.call-start = ((), (), s32[]{:S(2)}) async-start(), calls=%async_computation.20 | async-start | bytes 9461760 | tf_op jit(solution)/shard_map/all_gather | solution.py:875
  370.6 191.9 %reduce-scatter.8.cloned.1.call-start = ((), (), s32[]{:S(2)}) async-start(), calls=%async_computation.17 | async-start | bytes 2621440 | tf_op jit(solution)/shard_map/reduce_scatter | solution.py:893
  370.7 45.3 %collective-permute-start.3 = (bf16[128,1024]{1,0:T(8,128)(2,1)S(1)}, bf16[128,1024]{1,0:T(8,128)(2,1)S(1)}, u32[]{:S(2)}, u32[]{:S(2)}) collective-permute-start(bf16[128,1024]{1,0:T(8,128)(2,1)S(1)} %get-tuple-element.102), channel_id=1, source_target_pairs={{0,1},{1,2},{2,3},{3,0},{4,5},{5,6},{6,7},{7,4},{8,9},{9,10},{10,1... | collective-permute-start | bytes 786440 | tf_op jit(solution)/shard_map/ppermute | solution.py:664
  371.4 45.0 %collective-permute-start.5 = (bf16[128,1024]{1,0:T(8,128)(2,1)S(1)}, bf16[128,1024]{1,0:T(8,128)(2,1)S(1)}, u32[]{:S(2)}, u32[]{:S(2)}) collective-permute-start(bf16[128,1024]{1,0:T(8,128)(2,1)S(1)} %get-tuple-element.102), channel_id=1, source_target_pairs={{0,3},{1,0},{2,1},{3,2},{4,7},{5,4},{6,5},{7,6},{8,11},{9,8},{10,9... | collective-permute-start | bytes 786440 | tf_op jit(solution)/shard_map/ppermute | solution.py:664
  374.0 42.6 %collective-permute-start.4 = (bf16[128,1024]{1,0:T(8,128)(2,1)S(1)}, bf16[128,1024]{1,0:T(8,128)(2,1)S(1)}, u32[]{:S(2)}, u32[]{:S(2)}) collective-permute-start(bf16[128,1024]{1,0:T(8,128)(2,1)S(1)} %get-tuple-element.102), channel_id=1, source_target_pairs={{0,2},{1,3},{2,0},{3,1},{4,6},{5,7},{6,4},{7,5},{8,10},{9,11},{10,... | collective-permute-start | bytes 786440 | tf_op jit(solution)/shard_map/ppermute | solution.py:664
  420.9 141.7 %reduce-scatter.4.cloned.1.call-start = ((), (), s32[]{:S(2)}) async-start(), calls=%async_computation.15 | async-start | bytes 2621440 | tf_op jit(solution)/shard_map/reduce_scatter | solution.py:891
  422.3 140.3 %reduce-scatter.6.cloned.1.call-start = ((), (), s32[]{:S(2)}) async-start(), calls=%async_computation.16 | async-start | bytes 2621440 | tf_op jit(solution)/shard_map/reduce_scatter | solution.py:892
  422.5 42.9 %copy-start.44 = (f32[128]{0:T(128)S(1)}, f32[128]{0:T(128)}, u32[]{:S(2)}) copy-start(f32[128]{0:T(128)} %copy-done.43) | copy-start | bytes 1540
  490.3 11.5 %all-to-all-start.9 = ((bf16[4,128,512]{2,1,0:T(8,128)(2,1)}), bf16[4,128,512]{2,1,0:T(8,128)(2,1)S(1)}, u32[]{:S(2)}, u32[]{:S(2)}) async-start(bf16[4,128,512]{2,1,0:T(8,128)(2,1)} %bitcast.62), calls=%async_computation.9 | async-start | bytes 1048576 | tf_op jit(solution)/shard_map/all_to_all | solution.py:654
  497.2 26.0 %copy-start.18 = (bf16[512,1024]{1,0:T(8,128)(2,1)S(1)}, bf16[512,1024]{1,0:T(8,128)(2,1)}, u32[]{:S(2)}) copy-start(bf16[512,1024]{1,0:T(8,128)(2,1)} %param.17) | copy-start | bytes 3145732
  502.7 46.0 %all-to-all-start.8 = ((bf16[32,32,896]{2,1,0:T(8,128)(2,1)}), bf16[32,32,896]{2,1,0:T(8,128)(2,1)S(1)}, u32[]{:S(2)}, u32[]{:S(2)}) async-start(bf16[32,32,896]{2,1,0:T(8,128)(2,1)} %fusion.4), calls=%async_computation.8 | async-start | bytes 3670016 | tf_op jit(solution)/shard_map/all_to_all | solution.py:654
  527.1 23.8 %copy-start.37 = (bf16[32,128]{1,0:T(8,128)(2,1)S(1)}, bf16[32,128]{1,0:T(8,128)(2,1)}, u32[]{:S(2)}) copy-start(bf16[32,128]{1,0:T(8,128)(2,1)} %param.25) | copy-start | bytes 24580
  527.1 23.8 %copy-start.38 = (bf16[32,128]{1,0:T(8,128)(2,1)S(1)}, bf16[32,128]{1,0:T(8,128)(2,1)}, u32[]{:S(2)}) copy-start(bf16[32,128]{1,0:T(8,128)(2,1)} %param.24) | copy-start | bytes 24580
  527.2 24.5 %copy-start.35 = (bf16[32,256]{1,0:T(8,128)(2,1)S(1)}, bf16[32,256]{1,0:T(8,128)(2,1)}, u32[]{:S(2)}) copy-start(bf16[32,256]{1,0:T(8,128)(2,1)} %param.23) | copy-start | bytes 49156
  527.2 34.9 %copy-start.47 = (bf16[32]{0:T(256)(128)(2,1)S(1)}, bf16[32]{0:T(256)(128)(2,1)}, u32[]{:S(2)}) copy-start(bf16[32]{0:T(256)(128)(2,1)} %param.27) | copy-start | bytes 196
  (38 other events, 270.6 us)
Sparse Core Ops, SparseCore 0:
  57.9 51.1 all-gather.8
  110.8 41.8 all-gather.12
  154.9 77.1 all-gather.10
  254.5 44.7 all-gather.14
  370.8 50.0 all-gather.16
  423.7 29.1 reduce-scatter.7
  456.0 29.6 reduce-scatter.3
  488.7 33.4 reduce-scatter.5

commit v5 on v4

--- a/solution.py
+++ b/solution.py
@@ -455,7 +455,7 @@
 
 
 def expert_grad_kernel(
-    quarters, width, dy_ref, gate_ref, up_ref, w_ref, dx_ref, dgate_ref, dup_ref, act_ref
+    quarters, width, dy_ref, gate_ref, up_ref, w_ref, wt_ref, dx_ref, dgate_ref, dup_ref, act_ref
 ):
     total = None
     for pair in range(quarters // 2):
@@ -473,7 +473,7 @@
             dgate_ref[:, cols] = gate_grad
             dup_ref[:, cols] = up_grad
             grads = jnp.concatenate([gate_grad, up_grad], axis=1)
-            part = dot(grads, w_ref[u, :, : 2 * width], NT)
+            part = dot(grads, wt_ref[u], NN)
             total = part if total is None else total + part
     dx_ref[...] = total.astype(BF16)
 
@@ -509,7 +509,7 @@
 
     return pl.pallas_call(
         kernel,
-        out_shape=tuple(outs),
+        out_shape=tuple(pltpu.HBM(out.shape, out.dtype) for out in outs),
         grid=(outs[0].shape[0] // rows,),
         in_specs=[spec(x.shape) for x in ins],
         out_specs=tuple(spec(out.shape) for out in outs),
@@ -534,7 +534,7 @@
     )
 
 
-def expert_backward(rows_grad, gate_pre, up_pre, weights):
+def expert_backward(rows_grad, gate_pre, up_pre, weights, turned):
     slots, model_width = rows_grad.shape
     quarters, _, cols = weights.shape
     width = cols // 3
@@ -543,7 +543,7 @@
         functools.partial(expert_grad_kernel, quarters, width),
         "expert_grad",
         slots // 2,
-        [rows_grad, gate_pre, up_pre, weights],
+        [rows_grad, gate_pre, up_pre, weights, turned],
         [jax.ShapeDtypeStruct((slots, model_width), BF16), hidden, hidden, hidden],
         6 * slots * model_width * quarters * width,
     )
@@ -665,8 +665,19 @@
     return parts
 
 
-def gather_short(values, axis, index, count):
-    parts = shifted(values, axis, count)
+def exchange_short(values, axis, index, count):
+    rows = values.shape[0] // count
+    come = []
+    for step in range(count):
+        to = (index + step) % count
+        part = lax.dynamic_slice_in_dim(values, to * rows, rows, 0)
+        if step > 0:
+            part = lax.ppermute(part, axis, [(i, (i + step) % count) for i in range(count)])
+        come.append(part)
+    return jnp.concatenate(come, axis=1)
+
+
+def in_order(parts, index, count):
     ordered = []
     for place in range(count):
         back = (index - place) % count
@@ -774,12 +785,11 @@
     width = w_gate.shape[2]
     own_expert = jnp.concatenate([own_gate, own_up, own_down.T], axis=1)
     expert = lax.all_gather(own_expert, "exp", axis=0, tiled=False)
-    full_out = gather_short(
-        spread(own_out, "ctx", ctx_count).reshape(model_width, head_cols),
-        "exp",
-        exp_index,
-        exp_count,
-    )
+    out_parts = shifted(
+        spread(own_out, "ctx", ctx_count).reshape(model_width, head_cols), "exp", exp_count
+    )
+    wide_out = jnp.concatenate(out_parts, axis=1)
+    full_out = in_order(out_parts, exp_index, exp_count)
     expert_total = ctx_count
     capacity = max(2, own_rows * routes.shape[1] * 5 // (expert_total * 4))
     slots = expert_total * capacity
@@ -794,16 +804,16 @@
     weigh = jnp.where(holds, gate_of.T[:, None, :], 0.0).reshape(slots, own_rows)
     slot_gate = jnp.sum(weigh, axis=1, keepdims=True)
 
-    kv_all, full_out, pick, weigh, slot_gate = lax.optimization_barrier(
-        (kv_all, full_out, pick, weigh, slot_gate)
+    kv_all, wide_out, full_out, pick, weigh, slot_gate = lax.optimization_barrier(
+        (kv_all, wide_out, full_out, pick, weigh, slot_gate)
     )
     heads_f, lse = attend(block_of, own_blocks, queries_rot, kv_all)
     heads_low = heads_f.astype(BF16)
 
-    own_heads = exchange(heads_low.reshape(exp_count, own_rows, head_cols), "exp")
+    own_heads = exchange_short(heads_low, "exp", exp_index, exp_count)
     own_heads, later_q = lax.optimization_barrier((own_heads, queries_rot))
     q_all = lax.all_gather(later_q, "ctx", axis=0, tiled=True)
-    attn_rows = jnp.einsum("erk,eok->ro", own_heads, full_out, preferred_element_type=F32)
+    attn_rows = dot(own_heads, wide_out, NT)
     hidden_rows = lax.dynamic_slice_in_dim(hidden_in, exp_index * own_rows, own_rows, 0)
     hidden_rows = hidden_rows.astype(F32)
     resid = hidden_rows + attn_rows
@@ -819,8 +829,11 @@
     expert_in = send(dot(pick, normed_ffn, NN).astype(BF16))
     expert_out, gate_pre, up_pre = expert_forward(expert_in, expert)
     returned = send(expert_out)
-    returned, q_all, later_qkv = lax.optimization_barrier((returned, q_all, full_qkv))
-    all_qkv = lax.all_gather(later_qkv, "exp", axis=0, tiled=False)
+    turned = expert[:, :, : 2 * width].transpose(0, 2, 1)
+    returned, q_all, later_qkv, turned = lax.optimization_barrier(
+        (returned, q_all, full_qkv, turned)
+    )
+    wide_qkv = jnp.concatenate(shifted(later_qkv, "exp", exp_count), axis=1)
     moe_parts = dot(jnp.concatenate(pieces(weigh, 2), axis=1), returned, TN)
     moe_rows = moe_parts[:own_rows] + moe_parts[own_rows:]
     block_out = resid + moe_rows
@@ -838,7 +851,7 @@
     )
     grad_copies = send((slot_gate * copy_grad).astype(BF16))
     input_grad, gate_grad, up_grad, hidden_act = expert_backward(
-        grad_copies, gate_pre, up_pre, expert
+        grad_copies, gate_pre, up_pre, expert, turned
     )
     arrived_grad = send(input_grad)
 
@@ -847,8 +860,8 @@
     down_part = dot(hidden_act, grad_copies, TN)
     gate_part = gate_part.reshape(model_width, exp_count, width).transpose(1, 0, 2)
     up_part = up_part.reshape(model_width, exp_count, width).transpose(1, 0, 2)
-    arrived_grad, all_qkv, gate_part, up_part, down_part = lax.optimization_barrier(
-        (arrived_grad, all_qkv, gate_part, up_part, down_part)
+    arrived_grad, wide_qkv, gate_part, up_part, down_part = lax.optimization_barrier(
+        (arrived_grad, wide_qkv, gate_part, up_part, down_part)
     )
     ffn_normed_grad = dot(pick, arrived_grad, TN)
 
@@ -957,7 +970,7 @@
         ),
         "ctx",
     )
-    back = exchange(grad_low.reshape(exp_count, own_rows, qkv_cols), "exp")
+    back = exchange_short(grad_low, "exp", exp_index, exp_count)
     shards = jnp.sum(shards.astype(F32), axis=0)
     grad_w_query = shards[:, :head_cols]
     grad_w_key = shards[:, head_cols : head_cols + kv_cols]
@@ -970,7 +983,7 @@
     gain_part += jnp.sum(grad_w_key * w_key.astype(F32), axis=1)
     gain_part += jnp.sum(grad_w_value * w_value.astype(F32), axis=1)
     grad_gain_attn = lax.psum(gain_part, "exp") / gain_attn.astype(F32)
-    normed_rows = jnp.einsum("erk,edk->rd", back, all_qkv, preferred_element_type=F32)
+    normed_rows = dot(back, wide_qkv, NT)
     own_scale = lax.dynamic_slice_in_dim(attn_scale, exp_index * own_rows, own_rows, 0)
     own_hat = hidden_rows * own_scale
     grad_hidden = resid_grad + norm_back(normed_rows, own_hat, own_scale, attn_gain)

time: 577 us -> 569 us (0.986)
  blocking collectives: 89.2 us -> 35.4 us
  waiting for transfers between devices: 176 us -> 197 us
  other arithmetic: 24.1 us -> 32.5 us
  Pallas kernels: 128 us -> 135 us
    all_to_all x2 -> x0, blocking collectives: 52.2 us -> none  [exchange(): return lax.all_to_all(values, axis, split_axis=0, concat_axis=0, tiled=True)]
    ppermute x0 -> x6, waiting for transfers between devices: none -> 19.6 us  [exchange_short(): lax.ppermute(part, axis, [(i, (i + step) % count) for i in range(count)])]
    all_to_all x8, starting transfers between devices: 55 us -> 44.2 us  [exchange(): return lax.all_to_all(values, axis, split_axis=0, concat_axis=0, tiled=True)]
    dot_general x14 -> x16, matrix products: 30 us -> 39.1 us  [dot(): return lax.dot_general(left, right, dims, preferred_element_type=F32)]
    ppermute x0 -> x6, starting transfers between devices: none -> 7.69 us  [exchange_short(): lax.ppermute(part, axis, [(i, (i + step) % count) for i in range(count)])]
    ppermute x6 -> x9, starting transfers between devices: 6.49 us -> 13.6 us  [shifted(): lax.ppermute(values, axis, [(i, (i + step) % count) for i in range(count)])]
    concatenate x0 -> x3, other arithmetic: none -> 6.59 us  [the longest x1 3.85 us: on_device(): wide_qkv = jnp.concatenate(shifted(later_qkv, 'exp', exp_count), axis=1)]
    dot_general x2 -> x0, matrix products: 6.53 us -> none  [the longest x1 3.97 us: on_device(): jnp.einsum('erk,edk->rd', back, all_qkv, preferred_element_type=F32)]
  transfers between devices with their start and end apart: 22 -> 30, of which waited for: 13 -> 16; matrix products, arithmetic and copies ran while one was open for 12% -> 14% of each run, Pallas kernels for 22% -> 24%
where the time goes in v5:
time: 569 us; the launch traced here: 563 us
  waiting for transfers between devices  197 us (35%)
  Pallas kernels  135 us (24%)
  starting transfers between devices  66 us (12%)
  matrix products  41 us (7%)
  local copies, waits for them, and re-layouts  37 us (7%)
  blocking collectives  35.4 us (6%)
  other arithmetic  32.5 us (6%)
  between operations  18.7 us (3%)
    all_to_all x8, waiting for transfers between devices, exchange(): return lax.all_to_all(values, axis, split_axis=0, concat_axis=0, tiled=True)  152 us
    pallas_call x4, Pallas kernels, kernel_call(): pl.pallas_call(kernel, out_shape=tuple(outs), grid_spec=pltpu.PrefetchSca...  117 us
    all_to_all x8, starting transfers between devices, exchange(): return lax.all_to_all(values, axis, split_axis=0, concat_axis=0, tiled=True)  44.2 us
    dot_general x16, matrix products, dot(): return lax.dot_general(left, right, dims, preferred_element_type=F32)  39.1 us
    ppermute x9, waiting for transfers between devices, shifted(): lax.ppermute(values, axis, [(i, (i + step) % count) for i in range(count)])  20.7 us
    ppermute x6, waiting for transfers between devices, exchange_short(): lax.ppermute(part, axis, [(i, (i + step) % count) for i in range(count)])  19.6 us
    pallas_call x2, Pallas kernels, by_rows(): pl.pallas_call(kernel, out_shape=tuple((pltpu.HBM(out.shape, out.dtype) f...  18 us
    psum x1, blocking collectives, on_device(): stats = lax.psum(stats.reshape(-1, LANES), 'exp').reshape(-1)  16.9 us
  transfers between devices with their start and end apart: 30, of which 16 were waited for; matrix products, arithmetic and copies ran while one was open for 14% of the time, Pallas kernels for 24%

profile of v5, /device:TPU:0, one launch (start us, length us, event | category | flops | bytes accessed | tf_op | source)
XLA Modules:
  0.0 562.7 jit_solution(8062232090408458206)
XLA Ops:
  12.2 8.4 %all-to-all-start = ((bf16[32,40,512]{2,1,0:T(8,128)(2,1)}), bf16[32,40,512]{2,1,0:T(8,128)(2,1)S(1)}, u32[]{:S(2)}, u32[]{:S(2)}) async-start(bf16[32,40,512]{2,1,0:T(8,128)(2,1)} %broadcast_in_dim.112), calls=%async_computation | async-start | bytes 2621440 | tf_op jit(solution)/shard_map/all_to_all | solution.py:654
  22.6 18.8 %all-to-all-done = bf16[32,40,512]{2,1,0:T(8,128)(2,1)S(1)} async-done(((bf16[32,40,512]{2,1,0:T(8,128)(2,1)}), bf16[32,40,512]{2,1,0:T(8,128)(2,1)S(1)}, u32[]{:S(2)}, u32[]{:S(2)}) %all-to-all-start) | async-done | bytes 1310752 | tf_op jit(solution)/shard_map/all_to_all | solution.py:654
  44.9 10.8 %psum.21 = f32[2,512]{1,0:T(2,128)S(1)} all-reduce(f32[2,512]{1,0:T(2,128)S(1)} %pad_maximum_fusion.13), channel_id=1, replica_groups=mesh['ctx'=32,'exp'=4] {'exp'}, use_global_device_ids=true, to_apply=%region_4.5 | all-reduce | flops 1024 | bytes 8192 | tf_op jit(solution)/shard_map/psum | solution.py:759
  60.8 3.9 all-to-all-start.1
  64.8 13.9 %all-to-all-done.1 = bf16[32,32,256]{2,1,0:T(8,128)(2,1)S(1)} async-done(((bf16[32,32,256]{2,1,0:T(8,128)(2,1)}), bf16[32,32,256]{2,1,0:T(8,128)(2,1)S(1)}, u32[]{:S(2)}, u32[]{:S(2)}) %all-to-all-start.1) | async-done | bytes 524320 | tf_op jit(solution)/shard_map/all_to_all | solution.py:654
  85.3 19.9 %collective-permute-done = bf16[1024,256]{1,0:T(8,128)(2,1)S(1)} collective-permute-done((bf16[1024,256]{1,0:T(8,128)(2,1)S(1)}, bf16[1024,256]{1,0:T(8,128)(2,1)S(1)}, u32[]{:S(2)}, u32[]{:S(2)}) %collective-permute-start) | collective-permute-done | bytes 524320 | tf_op jit(solution)/shard_map/ppermute | solution.py:664
  111.8 25.4 %attend.1 = (f32[512,256]{1,0:T(8,128)S(1)}, f32[2,4,256]{2,1,0:T(4,128)S(1)}) custom-call(s32[128]{0:T(128)S(1)} %copy-done.3, s32[4]{0:T(128)S(1)} %get-tuple-element.109.own, bf16[512,256]{1,0:T(8,128)(2,1)} %get-tuple-element.65.q_in, bf16[16384,256]{1,0:T(8,128)(2,1)} %all-gather.7.cloned.1.call-done.kv), custom_call_target="tpu_custom_call" | custom-call | flops 20000000000 | bytes 8650752 | tf_op jit(solution)/shard_map/attend/pallas_call | solution.py:488
  153.6 4.8 all-to-all-start.2
  158.5 39.4 %all-to-all-done.2 = bf16[32,40,1024]{2,1,0:T(8,128)(2,1)} async-done(((bf16[32,40,1024]{2,1,0:T(8,128)(2,1)}), bf16[32,40,1024]{2,1,0:T(8,128)(2,1)}, u32[]{:S(2)}, u32[]{:S(2)}) %all-to-all-start.2) | async-done | bytes 2621472 | tf_op jit(solution)/shard_map/all_to_all | solution.py:654
  199.8 7.9 %expert.1 = (bf16[1280,1024]{1,0:T(8,128)(2,1)}, f32[1280,512]{1,0:T(8,128)}, f32[1280,512]{1,0:T(8,128)}) custom-call(bf16[1280,1024]{1,0:T(8,128)(2,1)} %bitcast.20.x_ref, bf16[4,1024,384]{2,1,0:T(8,128)(2,1)S(1)} %bitcast.129), custom_call_target="tpu_custom_call" | custom-call | flops 4026531840 | bytes 10000000 | tf_op jit(solution)/shard_map/expert/pallas_call | solution.py:510
  207.6 5.1 all-to-all-start.3
  217.9 4.0 copy.106
  224.4 29.2 %all-to-all-done.3 = bf16[32,40,1024]{2,1,0:T(8,128)(2,1)} async-done(((bf16[32,40,1024]{2,1,0:T(8,128)(2,1)}), bf16[32,40,1024]{2,1,0:T(8,128)(2,1)}, u32[]{:S(2)}, u32[]{:S(2)}) %all-to-all-start.3) | async-done | bytes 2621472 | tf_op jit(solution)/shard_map/all_to_all | solution.py:654
  259.8 4.8 all-to-all-start.4
  270.4 30.3 %all-to-all-done.4 = bf16[32,40,1024]{2,1,0:T(8,128)(2,1)} async-done(((bf16[32,40,1024]{2,1,0:T(8,128)(2,1)}), bf16[32,40,1024]{2,1,0:T(8,128)(2,1)}, u32[]{:S(2)}, u32[]{:S(2)}) %all-to-all-start.4) | async-done | bytes 2621472 | tf_op jit(solution)/shard_map/all_to_all | solution.py:654
  307.7 10.2 %expert_grad.1 = (bf16[1280,1024]{1,0:T(8,128)(2,1)}, bf16[1280,512]{1,0:T(8,128)(2,1)}, bf16[1280,512]{1,0:T(8,128)(2,1)}, bf16[1280,512]{1,0:T(8,128)(2,1)}) custom-call(bf16[1280,1024]{1,0:T(8,128)(2,1)} %bitcast.28.dy_ref, f32[1280,512]{1,0:T(8,128)S(1)} %copy-done.4, f32[1280,512]{1,0:T(8,128)S(1)} %copy-done.5, bf16[4,1024,384]{2,1,0:T(8,128)(2,1)S(1)} %bitcast.130, ...), custom_call_target="tpu_custom_call" | custom-call | flops 4026531840 | bytes 10000000 | tf_op jit(solution)/shard_map/expert_grad/pallas_call | solution.py:510
  317.8 5.0 all-to-all-start.5
  322.9 3.9 pad_maximum_fusion
  331.6 5.0 fusion.103
  336.7 5.0 convolution_bitcast_fusion
  341.6 5.0 convolution_bitcast_fusion.1
  346.6 12.3 %all-to-all-done.5 = bf16[32,40,1024]{2,1,0:T(8,128)(2,1)} async-done(((bf16[32,40,1024]{2,1,0:T(8,128)(2,1)}), bf16[32,40,1024]{2,1,0:T(8,128)(2,1)}, u32[]{:S(2)}, u32[]{:S(2)}) %all-to-all-start.5) | async-done | bytes 2621472 | tf_op jit(solution)/shard_map/all_to_all | solution.py:654
  365.3 4.3 all-to-all-start.6
  369.6 6.7 %all-to-all-done.6 = bf16[4,128,256]{1,2,0:T(8,128)(2,1)S(1)} async-done(((bf16[4,128,256]{1,2,0:T(8,128)(2,1)}), bf16[4,128,256]{1,2,0:T(8,128)(2,1)S(1)}, u32[]{:S(2)}, u32[]{:S(2)}) %all-to-all-start.6) | async-done | bytes 262176 | tf_op jit(solution)/shard_map/all_to_all | solution.py:654
  381.3 39.7 %query_grad.1 = f32[512,256]{1,0:T(8,128)S(1)} custom-call(s32[128]{0:T(128)S(1)} %copy-done.3, s32[4]{0:T(128)S(1)} %get-tuple-element.109.own, bf16[512,256]{1,0:T(8,128)(2,1)} %get-tuple-element.65.q_in, bf16[512,256]{1,0:T(8,128)(2,1)S(1)} %bitcast.126, f32[512,256]{1,0:T(8,128)S(1)} %get-tuple-element.56.o_in, ...), custom_call_target="tpu_custom_call" | custom-call | flops 30000001024 | bytes 9969664 | tf_op jit(solution)/shard_map/query_grad/pallas_call | solution.py:488
  422.8 4.9 all-gather.13.cloned.1.call-done
  432.2 50.1 %pair_grad.1 = f32[512,256]{1,0:T(8,128)S(1)} custom-call(s32[128]{0:T(128)S(1)} %copy-done.3, s32[4]{0:T(128)S(1)} %get-tuple-element.109.own, bf16[512,256]{1,0:T(8,128)(2,1)} %get-tuple-element.53.kv_in, f32[512,128]{1,0:T(8,128)S(1)} %get-tuple-element.155.cos_ref, f32[512,128]{1,0:T(8,128)S(1)} %get-tuple-element.156.sin_ref, ...), custom_call_target="tpu_custom_call" | custom-call | flops 40000000000 | bytes 18874368 | tf_op jit(solution)/shard_map/pair_grad/pallas_call | solution.py:488
  483.5 16.9 %psum.22 = f32[32,128]{1,0:T(8,128)S(1)} all-reduce(f32[32,128]{1,0:T(8,128)S(1)} %bitcast.170), channel_id=1, replica_groups=mesh['ctx'=32,'exp'=4] {'exp'}, use_global_device_ids=true, to_apply=%region_18.19 | all-reduce | flops 4096 | bytes 32768 | tf_op jit(solution)/shard_map/psum | solution.py:942
  506.7 7.8 %all-to-all-start.7 = ((bf16[32,32,896]{2,1,0:T(8,128)(2,1)}), bf16[32,32,896]{2,1,0:T(8,128)(2,1)S(1)}, u32[]{:S(2)}, u32[]{:S(2)}) async-start(bf16[32,32,896]{2,1,0:T(8,128)(2,1)} %fusion.4), calls=%async_computation.7 | async-start | bytes 3670016 | tf_op jit(solution)/shard_map/all_to_all | solution.py:654
  520.7 8.5 %collective-permute-done.12 = bf16[128,512]{1,0:T(8,128)(2,1)S(1)} collective-permute-done((bf16[128,512]{1,0:T(8,128)(2,1)}, bf16[128,512]{1,0:T(8,128)(2,1)S(1)}, u32[]{:S(2)}, u32[]{:S(2)}) %collective-permute-start.12) | collective-permute-done | bytes 131104 | tf_op jit(solution)/shard_map/ppermute | solution.py:675
  534.0 4.1 fusion.20
  545.3 7.7 %psum.23 = f32[32]{0:T(128)S(1)} all-reduce(f32[32]{0:T(128)S(1)} %add_add_fusion), channel_id=1, replica_groups=mesh['ctx'=32,'exp'=4] {'exp'}, use_global_device_ids=true, to_apply=%region_24.25 | all-reduce | flops 32 | bytes 256 | tf_op jit(solution)/shard_map/psum | solution.py:985
  (290 shorter events, 120.4 us)
Async XLA Ops:
  12.2 29.2 %all-to-all-start = ((bf16[32,40,512]{2,1,0:T(8,128)(2,1)}), bf16[32,40,512]{2,1,0:T(8,128)(2,1)S(1)}, u32[]{:S(2)}, u32[]{:S(2)}) async-start(bf16[32,40,512]{2,1,0:T(8,128)(2,1)} %broadcast_in_dim.112), calls=%async_computation | async-start | bytes 2621440 | tf_op jit(solution)/shard_map/all_to_all | solution.py:654
  20.6 91.2 %all-gather.7.cloned.1.call-start = ((), (), s32[]{:S(2)}) async-start(), calls=%async_computation.11 | async-start | bytes 8650752 | tf_op jit(solution)/shard_map/all_gather | solution.py:781
  58.6 99.9 %all-gather.11.cloned.1.call-start = ((), (), s32[]{:S(2)}) async-start(), calls=%async_computation.16 | async-start | bytes 3932160 | tf_op jit(solution)/shard_map/all_gather | solution.py:787
  60.8 17.9 %all-to-all-start.1 = ((bf16[32,32,256]{2,1,0:T(8,128)(2,1)}), bf16[32,32,256]{2,1,0:T(8,128)(2,1)S(1)}, u32[]{:S(2)}, u32[]{:S(2)}) async-start(bf16[32,32,256]{2,1,0:T(8,128)(2,1)} %broadcast_in_dim.114), calls=%async_computation.1 | async-start | bytes 1048576 | tf_op jit(solution)/shard_map/all_to_all | solution.py:654
  64.7 188.9 %all-gather.9.cloned.1.call-start = ((), (), s32[]{:S(2)}) async-start(), calls=%async_computation.12 | async-start | bytes 8650752 | tf_op jit(solution)/shard_map/all_gather | solution.py:815
  78.6 26.6 %collective-permute-start = (bf16[1024,256]{1,0:T(8,128)(2,1)S(1)}, bf16[1024,256]{1,0:T(8,128)(2,1)S(1)}, u32[]{:S(2)}, u32[]{:S(2)}) collective-permute-start(bf16[1024,256]{1,0:T(8,128)(2,1)S(1)} %bitcast.133), channel_id=1, source_target_pairs={{0,1},{1,2},{2,3},{3,0},{4,5},{5,6},{6,7},{7,4},{8,9},{9,10},{10,1... | collective-permute-start | bytes 1572872 | tf_op jit(solution)/shard_map/ppermute | solution.py:664
  78.7 26.5 %collective-permute-start.1 = (bf16[1024,256]{1,0:T(8,128)(2,1)S(1)}, bf16[1024,256]{1,0:T(8,128)(2,1)S(1)}, u32[]{:S(2)}, u32[]{:S(2)}) collective-permute-start(bf16[1024,256]{1,0:T(8,128)(2,1)S(1)} %bitcast.134), channel_id=1, source_target_pairs={{0,2},{1,3},{2,0},{3,1},{4,6},{5,7},{6,4},{7,5},{8,10},{9,11},{10,... | collective-permute-start | bytes 1572872 | tf_op jit(solution)/shard_map/ppermute | solution.py:664
  80.1 25.8 %collective-permute-start.2 = (bf16[1024,256]{1,0:T(8,128)(2,1)S(1)}, bf16[1024,256]{1,0:T(8,128)(2,1)}, u32[]{:S(2)}, u32[]{:S(2)}) collective-permute-start(bf16[1024,256]{1,0:T(8,128)(2,1)S(1)} %bitcast.135), channel_id=1, source_target_pairs={{0,3},{1,0},{2,1},{3,2},{4,7},{5,4},{6,5},{7,6},{8,11},{9,8},{10,9... | collective-permute-start | bytes 1572872 | tf_op jit(solution)/shard_map/ppermute | solution.py:664
  137.3 7.4 %collective-permute-start.3 = (bf16[128,256]{1,0:T(8,128)(2,1)S(1)}, bf16[128,256]{1,0:T(8,128)(2,1)S(1)}, u32[]{:S(2)}, u32[]{:S(2)}) collective-permute-start(bf16[128,256]{1,0:T(8,128)(2,1)S(1)} %get-tuple-element.125), channel_id=1, source_target_pairs={{0,1},{1,2},{2,3},{3,0},{4,5},{5,6},{6,7},{7,4},{8,9},{9,10},{10,1... | collective-permute-start | bytes 196616 | tf_op jit(solution)/shard_map/ppermute | solution.py:675
  137.7 10.8 %collective-permute-start.4 = (bf16[128,256]{1,0:T(8,128)(2,1)S(1)}, bf16[128,256]{1,0:T(8,128)(2,1)S(1)}, u32[]{:S(2)}, u32[]{:S(2)}) collective-permute-start(bf16[128,256]{1,0:T(8,128)(2,1)S(1)} %get-tuple-element.124), channel_id=1, source_target_pairs={{0,2},{1,3},{2,0},{3,1},{4,6},{5,7},{6,4},{7,5},{8,10},{9,11},{10,... | collective-permute-start | bytes 196616 | tf_op jit(solution)/shard_map/ppermute | solution.py:675
  141.5 7.0 %collective-permute-start.5 = (bf16[128,256]{1,0:T(8,128)(2,1)S(1)}, bf16[128,256]{1,0:T(8,128)(2,1)S(1)}, u32[]{:S(2)}, u32[]{:S(2)}) collective-permute-start(bf16[128,256]{1,0:T(8,128)(2,1)S(1)} %get-tuple-element.123), channel_id=1, source_target_pairs={{0,3},{1,0},{2,1},{3,2},{4,7},{5,4},{6,5},{7,6},{8,11},{9,8},{10,9... | collective-permute-start | bytes 196616 | tf_op jit(solution)/shard_map/ppermute | solution.py:675
  153.6 44.3 %all-to-all-start.2 = ((bf16[32,40,1024]{2,1,0:T(8,128)(2,1)}), bf16[32,40,1024]{2,1,0:T(8,128)(2,1)}, u32[]{:S(2)}, u32[]{:S(2)}) async-start(bf16[32,40,1024]{2,1,0:T(8,128)(2,1)} %bitcast.132), calls=%async_computation.2 | async-start | bytes 5242880 | tf_op jit(solution)/shard_map/all_to_all | solution.py:654
  207.6 45.9 %all-to-all-start.3 = ((bf16[32,40,1024]{2,1,0:T(8,128)(2,1)}), bf16[32,40,1024]{2,1,0:T(8,128)(2,1)}, u32[]{:S(2)}, u32[]{:S(2)}) async-start(bf16[32,40,1024]{2,1,0:T(8,128)(2,1)} %bitcast.144), calls=%async_computation.3 | async-start | bytes 5242880 | tf_op jit(solution)/shard_map/all_to_all | solution.py:654
  257.3 104.7 %copy-start.7 = (f32[128,1024]{1,0:T(8,128)}, f32[128,1024]{1,0:T(8,128)S(1)}, u32[]{:S(2)}) copy-start(f32[128,1024]{1,0:T(8,128)S(1)} %get-tuple-element.105) | copy-start | bytes 1572868
  259.8 40.9 %all-to-all-start.4 = ((bf16[32,40,1024]{2,1,0:T(8,128)(2,1)}), bf16[32,40,1024]{2,1,0:T(8,128)(2,1)}, u32[]{:S(2)}, u32[]{:S(2)}) async-start(bf16[32,40,1024]{2,1,0:T(8,128)(2,1)} %bitcast.145), calls=%async_computation.4 | async-start | bytes 5242880 | tf_op jit(solution)/shard_map/all_to_all | solution.py:654
  264.6 58.2 %collective-permute-start.6 = (bf16[1024,512]{1,0:T(8,128)(2,1)}, bf16[1024,512]{1,0:T(8,128)(2,1)}, u32[]{:S(2)}, u32[]{:S(2)}) collective-permute-start(bf16[1024,512]{1,0:T(8,128)(2,1)} %bitcast.138), channel_id=1, source_target_pairs={{0,1},{1,2},{2,3},{3,0},{4,5},{5,6},{6,7},{7,4},{8,9},{9,10},{10,1... | collective-permute-start | bytes 3145736 | tf_op jit(solution)/shard_map/ppermute | solution.py:664
  266.1 56.7 %collective-permute-start.7 = (bf16[1024,512]{1,0:T(8,128)(2,1)}, bf16[1024,512]{1,0:T(8,128)(2,1)}, u32[]{:S(2)}, u32[]{:S(2)}) collective-permute-start(bf16[1024,512]{1,0:T(8,128)(2,1)} %bitcast.139), channel_id=1, source_target_pairs={{0,2},{1,3},{2,0},{3,1},{4,6},{5,7},{6,4},{7,5},{8,10},{9,11},{10,... | collective-permute-start | bytes 3145736 | tf_op jit(solution)/shard_map/ppermute | solution.py:664
  268.9 54.0 %collective-permute-start.8 = (bf16[1024,512]{1,0:T(8,128)(2,1)}, bf16[1024,512]{1,0:T(8,128)(2,1)}, u32[]{:S(2)}, u32[]{:S(2)}) collective-permute-start(bf16[1024,512]{1,0:T(8,128)(2,1)} %bitcast.140), channel_id=1, source_target_pairs={{0,3},{1,0},{2,1},{3,2},{4,7},{5,4},{6,5},{7,6},{8,11},{9,8},{10,9... | collective-permute-start | bytes 3145736 | tf_op jit(solution)/shard_map/ppermute | solution.py:664
  317.8 41.1 %all-to-all-start.5 = ((bf16[32,40,1024]{2,1,0:T(8,128)(2,1)}), bf16[32,40,1024]{2,1,0:T(8,128)(2,1)}, u32[]{:S(2)}, u32[]{:S(2)}) async-start(bf16[32,40,1024]{2,1,0:T(8,128)(2,1)} %bitcast.143), calls=%async_computation.5 | async-start | bytes 5242880 | tf_op jit(solution)/shard_map/all_to_all | solution.py:654
  365.3 11.0 %all-to-all-start.6 = ((bf16[4,128,256]{1,2,0:T(8,128)(2,1)}), bf16[4,128,256]{1,2,0:T(8,128)(2,1)S(1)}, u32[]{:S(2)}, u32[]{:S(2)}) async-start(bf16[4,128,256]{1,2,0:T(8,128)(2,1)} %fusion.6), calls=%async_computation.6 | async-start | bytes 524288 | tf_op jit(solution)/shard_map/all_to_all | solution.py:654
  369.6 58.2 %all-gather.13.cloned.1.call-start = ((), (), s32[]{:S(2)}) async-start(), calls=%async_computation.17 | async-start | bytes 9461760 | tf_op jit(solution)/shard_map/all_gather | solution.py:888
  377.6 176.7 %reduce-scatter.8.cloned.1.call-start = ((), (), s32[]{:S(2)}) async-start(), calls=%async_computation.15 | async-start | bytes 2621440 | tf_op jit(solution)/shard_map/reduce_scatter | solution.py:906
  377.7 43.3 %collective-permute-start.9 = (bf16[128,1024]{1,0:T(8,128)(2,1)S(1)}, bf16[128,1024]{1,0:T(8,128)(2,1)S(1)}, u32[]{:S(2)}, u32[]{:S(2)}) collective-permute-start(bf16[128,1024]{1,0:T(8,128)(2,1)S(1)} %get-tuple-element.106), channel_id=1, source_target_pairs={{0,1},{1,2},{2,3},{3,0},{4,5},{5,6},{6,7},{7,4},{8,9},{9,10},{10,1... | collective-permute-start | bytes 786440 | tf_op jit(solution)/shard_map/ppermute | solution.py:664
  378.3 43.0 %collective-permute-start.11 = (bf16[128,1024]{1,0:T(8,128)(2,1)S(1)}, bf16[128,1024]{1,0:T(8,128)(2,1)S(1)}, u32[]{:S(2)}, u32[]{:S(2)}) collective-permute-start(bf16[128,1024]{1,0:T(8,128)(2,1)S(1)} %get-tuple-element.106), channel_id=1, source_target_pairs={{0,3},{1,0},{2,1},{3,2},{4,7},{5,4},{6,5},{7,6},{8,11},{9,8},{10,9... | collective-permute-start | bytes 786440 | tf_op jit(solution)/shard_map/ppermute | solution.py:664
  381.0 40.7 %collective-permute-start.10 = (bf16[128,1024]{1,0:T(8,128)(2,1)S(1)}, bf16[128,1024]{1,0:T(8,128)(2,1)S(1)}, u32[]{:S(2)}, u32[]{:S(2)}) collective-permute-start(bf16[128,1024]{1,0:T(8,128)(2,1)S(1)} %get-tuple-element.106), channel_id=1, source_target_pairs={{0,2},{1,3},{2,0},{3,1},{4,6},{5,7},{6,4},{7,5},{8,10},{9,11},{10,... | collective-permute-start | bytes 786440 | tf_op jit(solution)/shard_map/ppermute | solution.py:664
  427.8 126.5 %reduce-scatter.4.cloned.1.call-start = ((), (), s32[]{:S(2)}) async-start(), calls=%async_computation.13 | async-start | bytes 2621440 | tf_op jit(solution)/shard_map/reduce_scatter | solution.py:904
  431.8 122.4 %reduce-scatter.6.cloned.1.call-start = ((), (), s32[]{:S(2)}) async-start(), calls=%async_computation.14 | async-start | bytes 2621440 | tf_op jit(solution)/shard_map/reduce_scatter | solution.py:905
  432.2 50.6 %copy-start.31 = (f32[1024]{0:T(1024)S(1)}, f32[1024]{0:T(1024)}, u32[]{:S(2)}) copy-start(f32[1024]{0:T(1024)} %get-tuple-element.94) | copy-start | bytes 12292
  506.7 34.8 %all-to-all-start.7 = ((bf16[32,32,896]{2,1,0:T(8,128)(2,1)}), bf16[32,32,896]{2,1,0:T(8,128)(2,1)S(1)}, u32[]{:S(2)}, u32[]{:S(2)}) async-start(bf16[32,32,896]{2,1,0:T(8,128)(2,1)} %fusion.4), calls=%async_computation.7 | async-start | bytes 3670016 | tf_op jit(solution)/shard_map/all_to_all | solution.py:654
  516.5 12.7 %collective-permute-start.12 = (bf16[128,512]{1,0:T(8,128)(2,1)}, bf16[128,512]{1,0:T(8,128)(2,1)S(1)}, u32[]{:S(2)}, u32[]{:S(2)}) collective-permute-start(bf16[128,512]{1,0:T(8,128)(2,1)} %get-tuple-element.120), channel_id=1, source_target_pairs={{0,1},{1,2},{2,3},{3,0},{4,5},{5,6},{6,7},{7,4},{8,9},{9,10},{10,1... | collective-permute-start | bytes 393224 | tf_op jit(solution)/shard_map/ppermute | solution.py:675
  516.5 13.9 %collective-permute-start.13 = (bf16[128,512]{1,0:T(8,128)(2,1)}, bf16[128,512]{1,0:T(8,128)(2,1)S(1)}, u32[]{:S(2)}, u32[]{:S(2)}) collective-permute-start(bf16[128,512]{1,0:T(8,128)(2,1)} %get-tuple-element.119), channel_id=1, source_target_pairs={{0,2},{1,3},{2,0},{3,1},{4,6},{5,7},{6,4},{7,5},{8,10},{9,11},{10,... | collective-permute-start | bytes 393224 | tf_op jit(solution)/shard_map/ppermute | solution.py:675
  517.7 15.6 %collective-permute-start.14 = (bf16[128,512]{1,0:T(8,128)(2,1)}, bf16[128,512]{1,0:T(8,128)(2,1)S(1)}, u32[]{:S(2)}, u32[]{:S(2)}) collective-permute-start(bf16[128,512]{1,0:T(8,128)(2,1)} %get-tuple-element.121), channel_id=1, source_target_pairs={{0,3},{1,0},{2,1},{3,2},{4,7},{5,4},{6,5},{7,6},{8,11},{9,8},{10,9... | collective-permute-start | bytes 393224 | tf_op jit(solution)/shard_map/ppermute | solution.py:675
  (50 other events, 433.6 us)
Sparse Core Ops, SparseCore 0:
  58.7 51.0 all-gather.6
  111.5 41.8 all-gather.10
  156.2 87.1 all-gather.8
  377.7 50.0 all-gather.12
  430.6 29.1 reduce-scatter.7
  462.8 29.6 reduce-scatter.3
  502.2 34.8 reduce-scatter.5

commit v6 on v5

--- a/solution.py
+++ b/solution.py
@@ -56,6 +56,10 @@
         return ref.at[pl.ds(pl.multiple_of(first, 16), BLK)]
 
     return place
+
+
+def stats_of(ref):
+    return lambda i: ref.at[i // 4, i // 2 % 2, :, pl.ds(pl.multiple_of(i % 2 * BLK, BLK), BLK)]
 
 
 def causal(shape, key_first, query_first, rows_are_queries):
@@ -300,10 +304,98 @@
     lax.fori_loop(0, 4, query_block, 0)
 
 
+def place(blk, h):
+    return (h * 2 + blk) * BLK if blk < 2 else ((blk * 4) + h) * BLK
+
+
+def spread_heads(source_ref, lanes, target_ref):
+    target_ref[...] = jnp.zeros_like(target_ref)
+    for blk in range(4):
+        for h in range(4):
+            m, g = h // 2, h % 2
+            rows = slice(place(blk, h), place(blk, h) + BLK)
+            tile = source_ref[blk * BLK : (blk + 1) * BLK, lanes]
+            target_ref[rows, m * LANES : (m + 1) * LANES] = to_half(tile, m, g).astype(BF16)
+
+
+def cont_tiles(own, which, half, tile_blocks):
+    block = own[2 + which]
+    base = half + (block - half) // CONT_BLKS * CONT_BLKS
+    return block, block // tile_blocks, (base + CONT_BLKS) // tile_blocks, base // tile_blocks
+
+
+def pair_probs_kernel(
+    total, half, tile_blocks, q_rows, table, own, kv_in, q_all, lse_all, p_ref, pc_ref, q_s, lse_s, k_ref, sem
+):
+    step = pl.program_id(0)
+    width = tile_blocks * BLK
+    pair = 2 * tile_blocks
+
+    @pl.when(step == 0)
+    def _():
+        gather_blocks(
+            table,
+            total,
+            [
+                (rows_of(q_all, q_rows), lambda to: q_s.at[pl.ds(to, BLK)], sem.at[0]),
+                (stats_of(lse_all), lambda to: lse_s.at[:, pl.ds(to, BLK)], sem.at[1]),
+            ],
+        )
+        spread_heads(kv_in, slice(0, LANES), k_ref)
+        wait_all(q_s, sem.at[0])
+        wait_all(lse_s, sem.at[1])
+
+    def probs_of(first_row, per_head, j, keys_first, store):
+        start = pl.multiple_of(j * width, width)
+        keys = k_ref[first_row : first_row + 4 * per_head, :]
+        scores = dot(keys, q_s[pl.ds(start, width), :], NT)
+        for h in range(4):
+            part = slice(h * per_head, (h + 1) * per_head)
+            probs = jnp.exp(scores[part] - lse_s[h : h + 1, pl.ds(start, width)])
+            if keys_first is not None:
+                seen = [causal((BLK, width), first, start, False) for first in keys_first]
+                probs = jnp.where(jnp.concatenate(seen, axis=0), probs, 0.0)
+            store(part, probs.astype(BF16))
+
+    low = jnp.minimum(own[0], own[1])
+    high = jnp.maximum(own[0], own[1])
+
+    def prompt(keys_first):
+        for side in range(2):
+
+            def store(part, probs, side=side):
+                p_ref[0, part, side * width : (side + 1) * width] = probs
+
+            probs_of(0, 2 * BLK, 2 * step + side, keys_first, store)
+
+    @pl.when((step >= low // pair) & (step <= high // pair))
+    def _():
+        prompt([own[0] * BLK, own[1] * BLK])
+
+    @pl.when(step > high // pair)
+    def _():
+        prompt(None)
+
+    @pl.when(step == pl.num_programs(0) - 1)
+    def _():
+        for which in range(2):
+            block, first, stop, base = cont_tiles(own, which, half, tile_blocks)
+
+            def cont_tile(j, carry, which=which, block=block, base=base):
+                def store(part, probs):
+                    pc_ref[which, j - base, part, :] = probs
+
+                probs_of((8 + 4 * which) * BLK, BLK, j, [block * BLK], store)
+                return carry
+
+            lax.fori_loop(first, stop, cont_tile, 0)
+
+
 def pair_grad_kernel(
     total,
     half,
     tile_blocks,
+    q_rows,
     do_rows,
     table,
     own,
@@ -312,110 +404,71 @@
     sin_ref,
     q_all,
     do_all,
-    aux,
+    delta_all,
+    p_ref,
+    pc_ref,
     out_ref,
     q_s,
     do_s,
-    aux_s,
-    k_ref,
+    delta_s,
     v_ref,
     dk_ref,
     dv_ref,
-    s_buf,
-    p_buf,
+    d_buf,
     sem,
 ):
-    gather_blocks(
-        table,
-        total,
-        [
-            (rows_of(q_all, 4 * BLK), lambda to: q_s.at[pl.ds(to, BLK)], sem.at[0]),
-            (rows_of(do_all, do_rows), lambda to: do_s.at[pl.ds(to, BLK)], sem.at[1]),
-            (
-                lambda i: aux.at[i // 4, i // 2 % 2, :, pl.ds(pl.multiple_of(i % 2 * BLK, BLK), BLK)],
-                lambda to: aux_s.at[:, pl.ds(to, BLK)],
-                sem.at[2],
-            ),
-        ],
-    )
-
-    def place(blk, h):
-        return (h * 2 + blk) * BLK if blk < 2 else ((blk * 4) + h) * BLK
-
-    k_ref[...] = jnp.zeros_like(k_ref)
-    v_ref[...] = jnp.zeros_like(v_ref)
-    dk_ref[...] = jnp.zeros_like(dk_ref)
-    dv_ref[...] = jnp.zeros_like(dv_ref)
-    for blk in range(4):
-        source = slice(blk * BLK, (blk + 1) * BLK)
-        for h in range(4):
-            m, g = h // 2, h % 2
-            target = slice(place(blk, h), place(blk, h) + BLK)
-            pair = slice(m * LANES, (m + 1) * LANES)
-            k_ref[target, pair] = to_half(kv_in[source, :LANES], m, g).astype(BF16)
-            v_ref[target, pair] = to_half(kv_in[source, LANES:], m, g).astype(BF16)
-    wait_all(q_s, sem.at[0])
-    wait_all(do_s, sem.at[1])
-    wait_all(aux_s, sem.at[2])
+    step = pl.program_id(0)
     width = tile_blocks * BLK
-
-    def score(first_row, per_head, j):
+    pair = 2 * tile_blocks
+
+    @pl.when(step == 0)
+    def _():
+        gather_blocks(
+            table,
+            total,
+            [
+                (rows_of(q_all, q_rows), lambda to: q_s.at[pl.ds(to, BLK)], sem.at[0]),
+                (rows_of(do_all, do_rows), lambda to: do_s.at[pl.ds(to, BLK)], sem.at[1]),
+                (stats_of(delta_all), lambda to: delta_s.at[:, pl.ds(to, BLK)], sem.at[2]),
+            ],
+        )
+        dk_ref[...] = jnp.zeros_like(dk_ref)
+        dv_ref[...] = jnp.zeros_like(dv_ref)
+        spread_heads(kv_in, slice(LANES, 2 * LANES), v_ref)
+        wait_all(q_s, sem.at[0])
+        wait_all(do_s, sem.at[1])
+        wait_all(delta_s, sem.at[2])
+
+    def prob_grad(first_row, per_head, j):
+        start = pl.multiple_of(j * width, width)
+        values = v_ref[first_row : first_row + 4 * per_head, :]
+        return dot(values, do_s[pl.ds(start, width), :], NT)
+
+    def add(first_row, per_head, j, probs, grads_in):
         rows = pl.ds(first_row, 4 * per_head)
         start = pl.multiple_of(j * width, width)
-        scores = dot(k_ref[rows, :], q_s[pl.ds(start, width), :], NT)
-        return scores, dot(v_ref[rows, :], do_s[pl.ds(start, width), :], NT)
-
-    def add(first_row, per_head, j, scores, prob_grad, keys_first):
-        rows = pl.ds(first_row, 4 * per_head)
-        start = pl.multiple_of(j * width, width)
-        probs_low = []
         score_low = []
         for h in range(4):
             part = slice(h * per_head, (h + 1) * per_head)
-            probs = jnp.exp(scores[part] - aux_s[h : h + 1, pl.ds(start, width)])
-            if keys_first is not None:
-                seen = [causal((BLK, width), first, start, False) for first in keys_first]
-                probs = jnp.where(jnp.concatenate(seen, axis=0), probs, 0.0)
-            probs_low.append(probs.astype(BF16))
-            shifted = prob_grad[part] - aux_s[4 + h : 5 + h, pl.ds(start, width)]
-            score_low.append((probs * shifted).astype(BF16))
-        grads = do_s[pl.ds(start, width), :]
-        dv_ref[rows, :] += dot(jnp.concatenate(probs_low, axis=0), grads, NN)
+            shifted_grad = grads_in[part] - delta_s[h : h + 1, pl.ds(start, width)]
+            score_low.append((probs[part].astype(F32) * shifted_grad).astype(BF16))
+        dv_ref[rows, :] += dot(probs, do_s[pl.ds(start, width), :], NN)
         queries = q_s[pl.ds(start, width), :]
         dk_ref[rows, :] += dot(jnp.concatenate(score_low, axis=0), queries, NN)
 
     low = jnp.minimum(own[0], own[1])
-    high = jnp.maximum(own[0], own[1])
     last = total // tile_blocks - 1
 
-    def fill(side, j):
-        s_buf[side], p_buf[side] = score(0, 2 * BLK, jnp.minimum(j, last))
-
-    def two_tiles(keys_first):
-        def step(i, carry):
-            fill(1, 2 * i + 1)
-            add(0, 2 * BLK, 2 * i, s_buf[0], p_buf[0], keys_first)
-            fill(0, 2 * i + 2)
-            add(0, 2 * BLK, 2 * i + 1, s_buf[1], p_buf[1], keys_first)
-            return carry
-
-        return step
-
-    pair = 2 * tile_blocks
-    fill(0, low // pair * 2)
-    edge = [own[0] * BLK, own[1] * BLK]
-    lax.fori_loop(low // pair, high // pair + 1, two_tiles(edge), 0)
-    lax.fori_loop(high // pair + 1, total // pair, two_tiles(None), 0)
-    for which in range(2):
-        block = own[2 + which]
-        stop = half + ((block - half) // CONT_BLKS + 1) * CONT_BLKS
-
-        def cont_tile(j, carry, which=which, block=block):
-            first_row = (8 + 4 * which) * BLK
-            add(first_row, BLK, j, *score(first_row, BLK, j), [block * BLK])
-            return carry
-
-        lax.fori_loop(block // tile_blocks, stop // tile_blocks, cont_tile, 0)
+    @pl.when(step == low // pair)
+    def _():
+        d_buf[0] = prob_grad(0, 2 * BLK, 2 * step)
+
+    @pl.when(step >= low // pair)
+    def _():
+        d_buf[1] = prob_grad(0, 2 * BLK, 2 * step + 1)
+        add(0, 2 * BLK, 2 * step, p_ref[0, :, :width], d_buf[0])
+        d_buf[0] = prob_grad(0, 2 * BLK, jnp.minimum(2 * step + 2, last))
+        add(0, 2 * BLK, 2 * step + 1, p_ref[0, :, width:], d_buf[1])
 
     def collect(ref, blk):
         tile_sum = None
@@ -426,10 +479,22 @@
             tile_sum = moved if tile_sum is None else tile_sum + moved
         return tile_sum
 
-    for blk in range(4):
-        rows = slice(blk * BLK, (blk + 1) * BLK)
-        out_ref[rows, :LANES] = turn(collect(dk_ref, blk), cos_ref[rows, :], -sin_ref[rows, :])
-        out_ref[rows, LANES:] = collect(dv_ref, blk)
+    @pl.when(step == pl.num_programs(0) - 1)
+    def _():
+        for which in range(2):
+            _, first, stop, base = cont_tiles(own, which, half, tile_blocks)
+
+            def cont_tile(j, carry, which=which, base=base):
+                first_row = (8 + 4 * which) * BLK
+                grads_in = prob_grad(first_row, BLK, j)
+                add(first_row, BLK, j, pc_ref[which, j - base], grads_in)
+                return carry
+
+            lax.fori_loop(first, stop, cont_tile, 0)
+        for blk in range(4):
+            rows = slice(blk * BLK, (blk + 1) * BLK)
+            out_ref[rows, :LANES] = turn(collect(dk_ref, blk), cos_ref[rows, :], -sin_ref[rows, :])
+            out_ref[rows, LANES:] = collect(dv_ref, blk)
 
 
 def down_strips(w_ref, pair, width):
@@ -516,7 +581,7 @@
         compiler_params=pltpu.CompilerParams(vmem_limit_bytes=40 << 20),
         cost_estimate=pl.CostEstimate(flops=flops, bytes_accessed=10**7, transcendentals=0),
         name=name,
-    )(*ins)
+    )(*(pltpu.with_memory_space_constraint(x, pltpu.HBM) for x in ins))
 
 
 def expert_forward(rows_in, weights):
@@ -601,28 +666,85 @@
     )[0]
 
 
-def pair_grad(table, own, kv, cosine, sine, q_all, do_all, do_rows, aux):
+def pair_call(kernel, name, table, own, ins, blocks, outs, out_blocks, scratch, flops):
+    steps = table.shape[0] // 8
+
+    def tile_place(step, table_ref, own_ref):
+        return (jnp.maximum(step, jnp.minimum(own_ref[0], own_ref[1]) // 8), 0, 0)
+
+    def spec(shape, block):
+        if block is None:
+            return pl.BlockSpec(memory_space=pl.ANY)
+        if block == shape:
+            return pl.BlockSpec(shape, lambda *_: (0,) * len(shape))
+        return pl.BlockSpec(block, tile_place)
+
+    return pl.pallas_call(
+        kernel,
+        out_shape=tuple(outs),
+        grid_spec=pltpu.PrefetchScalarGridSpec(
+            num_scalar_prefetch=2,
+            grid=(steps,),
+            in_specs=[spec(x.shape, block) for x, block in zip(ins, blocks)],
+            out_specs=tuple(spec(x.shape, block) for x, block in zip(outs, out_blocks)),
+            scratch_shapes=scratch,
+        ),
+        compiler_params=pltpu.CompilerParams(vmem_limit_bytes=48 << 20),
+        cost_estimate=pl.CostEstimate(flops=flops, bytes_accessed=4 * 10**7, transcendentals=0),
+        name=name,
+    )(table, own, *ins)
+
+
+PROB_BLOCK = (1, 8 * BLK, 8 * BLK)
+CONT_SHAPE = (2, CONT_BLKS // 4, 4 * BLK, 4 * BLK)
+
+
+def pair_probs(table, own, kv, q_all, q_rows, lse_all):
     total = table.shape[0]
-    ins = [(x, False) for x in (kv, cosine, sine)] + [(x, True) for x in (q_all, do_all, aux)]
-    return kernel_call(
-        functools.partial(pair_grad_kernel, total, total // 2, 4, do_rows),
+    return pair_call(
+        functools.partial(pair_probs_kernel, total, total // 2, 4, q_rows),
+        "pair_probs",
+        table,
+        own,
+        [kv, q_all, lse_all],
+        [kv.shape, None, None],
+        [
+            jax.ShapeDtypeStruct((total // 8,) + PROB_BLOCK[1:], BF16),
+            jax.ShapeDtypeStruct(CONT_SHAPE, BF16),
+        ],
+        [PROB_BLOCK, CONT_SHAPE],
+        [
+            pltpu.VMEM((total * BLK, 2 * LANES), BF16),
+            pltpu.VMEM((4, total * BLK), F32),
+            pltpu.VMEM((16 * BLK, 2 * LANES), BF16),
+            pltpu.SemaphoreType.DMA((2,)),
+        ],
+        20 * 10**9,
+    )
+
+
+def pair_grad(table, own, kv, cosine, sine, q_all, q_rows, do_all, do_rows, delta_all, probs):
+    total = table.shape[0]
+    return pair_call(
+        functools.partial(pair_grad_kernel, total, total // 2, 4, q_rows, do_rows),
         "pair_grad",
-        (table, own),
-        ins,
+        table,
+        own,
+        [kv, cosine, sine, q_all, do_all, delta_all, *probs],
+        [kv.shape, cosine.shape, sine.shape, None, None, None, PROB_BLOCK, CONT_SHAPE],
         [jax.ShapeDtypeStruct((4 * BLK, 2 * LANES), F32)],
+        [(4 * BLK, 2 * LANES)],
         [
             pltpu.VMEM((total * BLK, 2 * LANES), BF16),
             pltpu.VMEM((total * BLK, 2 * LANES), BF16),
-            pltpu.VMEM((8, total * BLK), F32),
-            pltpu.VMEM((16 * BLK, 2 * LANES), BF16),
+            pltpu.VMEM((4, total * BLK), F32),
             pltpu.VMEM((16 * BLK, 2 * LANES), BF16),
             pltpu.VMEM((16 * BLK, 2 * LANES), F32),
             pltpu.VMEM((16 * BLK, 2 * LANES), F32),
             pltpu.VMEM((2, 8 * BLK, 4 * BLK), F32),
-            pltpu.VMEM((2, 8 * BLK, 4 * BLK), F32),
             pltpu.SemaphoreType.DMA((3,)),
         ],
-        40 * 10**9,
+        30 * 10**9,
     )[0]
 
 
@@ -686,6 +808,16 @@
             part = jnp.where(back == step, parts[step], part)
         ordered.append(part)
     return jnp.stack(ordered, axis=0)
+
+
+def with_stats(rows, stats):
+    parts = jnp.stack(pieces(stats, 3), axis=0).reshape(-1, rows.shape[1])
+    return jnp.concatenate([rows, jnp.pad(parts, ((0, -parts.shape[0] % 16), (0, 0)))], axis=0)
+
+
+def stats_in(gathered, first):
+    parts = gathered[:, first : first + 24].reshape(-1, 3, 2, 4, gathered.shape[2])
+    return jnp.sum(parts.astype(F32), axis=1)
 
 
 def ride_along(values):
@@ -729,23 +861,19 @@
     qkv_cols = head_cols + 2 * kv_cols
     shard_rows = w_query.shape[0]
 
-    own_qkv = jnp.concatenate([w_query, w_key, w_value], axis=1)
-    mine = jnp.arange(model_width, dtype=jnp.int32) // shard_rows == ctx_index
-    places = [
-        jnp.where(mine, jnp.tile(gain, ctx_count), 0).astype(BF16)
-        for gain in (gain_attn, gain_query, gain_ffn)
-    ]
-    mine_key = jnp.arange(kv_total, dtype=jnp.int32) // gain_key.shape[0] == ctx_index
-    places.append(jnp.where(mine_key, jnp.tile(gain_key, ctx_count), 0).astype(BF16))
-    gain_rows = jnp.concatenate(places)
-    gain_rows = jnp.pad(gain_rows, (0, 8 * qkv_cols - gain_rows.shape[0])).reshape(8, qkv_cols)
-    first_parts = spread(jnp.concatenate([own_qkv, gain_rows], axis=0), "ctx", ctx_count)
-    full_qkv = first_parts[:, :shard_rows].reshape(model_width, qkv_cols)
-    gains = jnp.sum(first_parts[:, shard_rows:].astype(F32), axis=0).reshape(-1)
-    attn_gain = gains[:model_width]
-    query_gain_all = gains[model_width : 2 * model_width]
-    ffn_gain = gains[2 * model_width : 3 * model_width]
-    key_gain_all = gains[3 * model_width : 3 * model_width + kv_total]
+    own_weights = jnp.concatenate([w_query, w_key, w_value, w_out], axis=1)
+    gain_row = jnp.concatenate([gain_attn, gain_query, gain_ffn, gain_key])
+    gain_rows = jnp.pad(
+        gain_row, (0, 8 * own_weights.shape[1] - gain_row.shape[0])
+    ).reshape(8, -1)
+    first_parts = spread(jnp.concatenate([own_weights, gain_rows], axis=0), "ctx", ctx_count)
+    full_weights = first_parts[:, :shard_rows].reshape(model_width, -1)
+    full_qkv = full_weights[:, :qkv_cols]
+    gains = first_parts[:, shard_rows:].reshape(ctx_count, -1)[:, : gain_row.shape[0]].astype(F32)
+    attn_gain = gains[:, :shard_rows].reshape(model_width)
+    query_gain_all = gains[:, shard_rows : 2 * shard_rows].reshape(model_width)
+    ffn_gain = gains[:, 2 * shard_rows : 3 * shard_rows].reshape(model_width)
+    key_gain_all = gains[:, 3 * shard_rows :].reshape(kv_total)
     query_gain = lax.dynamic_slice_in_dim(query_gain_all, exp_index * head_cols, head_cols)
     key_gain = lax.dynamic_slice_in_dim(key_gain_all, exp_index * kv_cols, kv_cols)
 
@@ -780,14 +908,12 @@
     )
     kv_all = lax.all_gather(own_kv, "ctx", axis=0, tiled=True)
     own_out, own_gate, own_up, own_down, _ = lax.optimization_barrier(
-        (w_out, w_gate[0], w_up[0], w_down[0], own_kv)
+        (full_weights[:, qkv_cols:], w_gate[0], w_up[0], w_down[0], own_kv)
     )
     width = w_gate.shape[2]
     own_expert = jnp.concatenate([own_gate, own_up, own_down.T], axis=1)
     expert = lax.all_gather(own_expert, "exp", axis=0, tiled=False)
-    out_parts = shifted(
-        spread(own_out, "ctx", ctx_count).reshape(model_width, head_cols), "exp", exp_count
-    )
+    out_parts = shifted(own_out, "exp", exp_count)
     wide_out = jnp.concatenate(out_parts, axis=1)
     full_out = in_order(out_parts, exp_index, exp_count)
     expert_total = ctx_count
@@ -811,8 +937,8 @@
     heads_low = heads_f.astype(BF16)
 
     own_heads = exchange_short(heads_low, "exp", exp_index, exp_count)
-    own_heads, later_q = lax.optimization_barrier((own_heads, queries_rot))
-    q_all = lax.all_gather(later_q, "ctx", axis=0, tiled=True)
+    own_heads, later_q, lse = lax.optimization_barrier((own_heads, queries_rot, lse))
+    q_all = lax.all_gather(with_stats(later_q, lse), "ctx", axis=0, tiled=False)
     attn_rows = dot(own_heads, wide_out, NT)
     hidden_rows = lax.dynamic_slice_in_dim(hidden_in, exp_index * own_rows, own_rows, 0)
     hidden_rows = hidden_rows.astype(F32)
@@ -832,6 +958,14 @@
     turned = expert[:, :, : 2 * width].transpose(0, 2, 1)
     returned, q_all, later_qkv, turned = lax.optimization_barrier(
         (returned, q_all, full_qkv, turned)
+    )
+    probs = pair_probs(
+        block_of,
+        own_blocks,
+        own_kv,
+        q_all.reshape(-1, head_cols),
+        q_all.shape[1],
+        stats_in(q_all, ctx_rows),
     )
     wide_qkv = jnp.concatenate(shifted(later_qkv, "exp", exp_count), axis=1)
     moe_parts = dot(jnp.concatenate(pieces(weigh, 2), axis=1), returned, TN)
@@ -850,6 +984,7 @@
         NN,
     )
     grad_copies = send((slot_gate * copy_grad).astype(BF16))
+    grad_copies, probs = lax.optimization_barrier((grad_copies, probs))
     input_grad, gate_grad, up_grad, hidden_act = expert_backward(
         grad_copies, gate_pre, up_pre, expert, turned
     )
@@ -882,12 +1017,7 @@
         preferred_element_type=F32,
     )
     delta = delta.reshape(4, 2, 2 * BLK).transpose(1, 0, 2)
-    row_stats = jnp.concatenate([lse, delta], axis=1)
-    stat_parts = jnp.stack(pieces(row_stats, 3), axis=0).reshape(-1, 2 * BLK)
-    stat_rows = stat_parts.shape[0]
-    do_all = lax.all_gather(
-        jnp.concatenate([out_grad, stat_parts], axis=0), "ctx", axis=0, tiled=False
-    )
+    do_all = lax.all_gather(with_stats(out_grad, delta), "ctx", axis=0, tiled=False)
     query_n_grad = query_grad(
         block_of, own_blocks, queries_rot, out_grad, heads_f, lse, cosine, sine, kv_all
     )
@@ -905,19 +1035,18 @@
     grad_w_up = lax.psum_scatter(up_part, "exp", scatter_dimension=0, tiled=True)
     grad_w_down = lax.psum_scatter(down_part, "exp", scatter_dimension=0, tiled=True)[None]
 
-    aux = jnp.sum(
-        do_all[:, ctx_rows:].reshape(ctx_count, 3, 2, 8, 2 * BLK).astype(F32), axis=1
-    )
     pair_grads = pair_grad(
         block_of,
         own_blocks,
         own_kv,
         cosine,
         sine,
-        q_all,
+        q_all.reshape(-1, head_cols),
+        q_all.shape[1],
         do_all.reshape(-1, head_cols),
-        ctx_rows + stat_rows,
-        aux,
+        do_all.shape[1],
+        stats_in(do_all, ctx_rows),
+        probs,
     )
     key_n_grad = pair_grads[:, :kv_cols]
     value_grad = pair_grads[:, kv_cols:].astype(BF16)

time: 569 us -> 569 us (level)
  waiting for transfers between devices: 197 us -> 176 us
  Pallas kernels: 135 us -> 146 us
  starting transfers between devices: 66 us -> 73.4 us
    pallas_call x0 -> x2, Pallas kernels: none -> 60.4 us  [pair_call(): pl.pallas_call(kernel, out_shape=tuple(outs), grid_spec=pltpu.PrefetchSca...]
    pallas_call x4 -> x3, Pallas kernels: 117 us -> 63.7 us  [kernel_call(): pl.pallas_call(kernel, out_shape=tuple(outs), grid_spec=pltpu.PrefetchSca...]
    all_to_all x8 -> x7, waiting for transfers between devices: 152 us -> 120 us  [exchange(): return lax.all_to_all(values, axis, split_axis=0, concat_axis=0, tiled=True)]
    all_gather x1, waiting for transfers between devices: 0.01 us -> 15.9 us  [on_device(): kv_all = lax.all_gather(own_kv, 'ctx', axis=0, tiled=True)]
    all_to_all x8 -> x7, starting transfers between devices: 44.2 us -> 50.6 us  [exchange(): return lax.all_to_all(values, axis, split_axis=0, concat_axis=0, tiled=True)]
    unnamed x116 -> x117, local copies, waits for them, and re-layouts: 15.9 us -> 10.6 us
  transfers between devices with their start and end apart: 30 -> 29, of which waited for: 16 -> 16; matrix products, arithmetic and copies ran while one was open for 14% -> 15% of each run, Pallas kernels for 24% -> 26%
where the time goes in v6:
time: 569 us; the launch traced here: 563 us
  waiting for transfers between devices  176 us (31%)
  Pallas kernels  146 us (26%)
  starting transfers between devices  73.4 us (13%)
  matrix products  38 us (7%)
  local copies, waits for them, and re-layouts  37.8 us (7%)
  other arithmetic  37 us (7%)
  blocking collectives  35.8 us (6%)
  between operations  18.8 us (3%)
    all_to_all x7, waiting for transfers between devices, exchange(): return lax.all_to_all(values, axis, split_axis=0, concat_axis=0, tiled=True)  120 us
    pallas_call x3, Pallas kernels, kernel_call(): pl.pallas_call(kernel, out_shape=tuple(outs), grid_spec=pltpu.PrefetchSca...  63.7 us
    pallas_call x2, Pallas kernels, pair_call(): pl.pallas_call(kernel, out_shape=tuple(outs), grid_spec=pltpu.PrefetchSca...  60.4 us
    all_to_all x7, starting transfers between devices, exchange(): return lax.all_to_all(values, axis, split_axis=0, concat_axis=0, tiled=True)  50.6 us
    dot_general x16, matrix products, dot(): return lax.dot_general(left, right, dims, preferred_element_type=F32)  36.2 us
    pallas_call x2, Pallas kernels, by_rows(): pl.pallas_call(kernel, out_shape=tuple((pltpu.HBM(out.shape, out.dtype) f...  21.6 us
    psum x1, blocking collectives, on_device(): stats = lax.psum(stats.reshape(-1, LANES), 'exp').reshape(-1)  17.3 us
    ppermute x6, waiting for transfers between devices, exchange_short(): lax.ppermute(part, axis, [(i, (i + step) % count) for i in range(count)])  16.8 us
  transfers between devices with their start and end apart: 29, of which 16 were waited for; matrix products, arithmetic and copies ran while one was open for 15% of the time, Pallas kernels for 26%

profile of v6, /device:TPU:0, one launch (start us, length us, event | category | flops | bytes accessed | tf_op | source)
XLA Modules:
  0.0 562.6 jit_solution(12761478672461342591)
XLA Ops:
  10.2 8.5 %all-to-all-start = ((bf16[32,40,768]{2,1,0:T(8,128)(2,1)}), bf16[32,40,768]{2,1,0:T(8,128)(2,1)}, u32[]{:S(2)}, u32[]{:S(2)}) async-start(bf16[32,40,768]{2,1,0:T(8,128)(2,1)} %broadcast_in_dim.54), calls=%async_computation | async-start | bytes 3932160 | tf_op jit(solution)/shard_map/all_to_all | solution.py:776
  20.7 26.4 %all-to-all-done = bf16[32,40,768]{2,1,0:T(8,128)(2,1)} async-done(((bf16[32,40,768]{2,1,0:T(8,128)(2,1)}), bf16[32,40,768]{2,1,0:T(8,128)(2,1)}, u32[]{:S(2)}, u32[]{:S(2)}) %all-to-all-start) | async-done | bytes 1966112 | tf_op jit(solution)/shard_map/all_to_all | solution.py:776
  52.9 10.8 %psum.21 = f32[2,512]{1,0:T(2,128)S(1)} all-reduce(f32[2,512]{1,0:T(2,128)S(1)} %pad_maximum_fusion.12), channel_id=1, replica_groups=mesh['ctx'=32,'exp'=4] {'exp'}, use_global_device_ids=true, to_apply=%region_3.4 | all-reduce | flops 1024 | bytes 8192 | tf_op jit(solution)/shard_map/psum | solution.py:887
  74.9 15.8 %collective-permute-done = bf16[1024,256]{1,0:T(8,128)(2,1)S(1)} collective-permute-done((bf16[1024,256]{1,0:T(8,128)(2,1)S(1)}, bf16[1024,256]{1,0:T(8,128)(2,1)S(1)}, u32[]{:S(2)}, u32[]{:S(2)}) %collective-permute-start) | collective-permute-done | bytes 524320 | tf_op jit(solution)/shard_map/ppermute | solution.py:786
  97.4 15.9 %all-gather.8.cloned.1.call-done.kv = bf16[16384,256]{1,0:T(8,128)(2,1)} async-done(((bf16[512,256]{1,0:T(8,128)(2,1)}), bf16[16384,256]{1,0:T(8,128)(2,1)}) %all-gather.8.cloned.1.call-update) | async-done | bytes 8388624 | tf_op jit(solution)/shard_map/all_gather | solution.py:909
  113.3 24.0 %attend.1 = (f32[512,256]{1,0:T(8,128)S(1)}, f32[2,4,256]{2,1,0:T(4,128)S(1)}) custom-call(s32[128]{0:T(128)S(1)} %copy-done, s32[4]{0:T(128)S(1)} %get-tuple-element.121.own, bf16[512,256]{1,0:T(8,128)(2,1)S(1)} %get-tuple-element.72.q_in, bf16[16384,256]{1,0:T(8,128)(2,1)} %all-gather.8.cloned.1.call-done.kv), custom_call_target="tpu_custom_call" | custom-call | flops 20000000000 | bytes 8650752 | tf_op jit(solution)/shard_map/attend/pallas_call | solution.py:553
  153.8 8.5 %all-to-all-start.1 = ((bf16[32,40,1024]{2,1,0:T(8,128)(2,1)}), bf16[32,40,1024]{2,1,0:T(8,128)(2,1)}, u32[]{:S(2)}, u32[]{:S(2)}) async-start(bf16[32,40,1024]{2,1,0:T(8,128)(2,1)} %bitcast.120), calls=%async_computation.1 | async-start | bytes 5242880 | tf_op jit(solution)/shard_map/all_to_all | solution.py:776
  162.3 39.5 %all-to-all-done.1 = bf16[32,40,1024]{2,1,0:T(8,128)(2,1)} async-done(((bf16[32,40,1024]{2,1,0:T(8,128)(2,1)}), bf16[32,40,1024]{2,1,0:T(8,128)(2,1)}, u32[]{:S(2)}, u32[]{:S(2)}) %all-to-all-start.1) | async-done | bytes 2621472 | tf_op jit(solution)/shard_map/all_to_all | solution.py:776
  201.8 8.8 %expert.1 = (bf16[1280,1024]{1,0:T(8,128)(2,1)}, f32[1280,512]{1,0:T(8,128)}, f32[1280,512]{1,0:T(8,128)}) custom-call(bf16[1280,1024]{1,0:T(8,128)(2,1)} %bitcast.18.x_ref, bf16[4,1024,384]{2,1,0:T(8,128)(2,1)} %bitcast.130), custom_call_target="tpu_custom_call" | custom-call | flops 4026531840 | bytes 10000000 | tf_op jit(solution)/shard_map/expert/pallas_call | solution.py:575
  210.6 5.1 all-to-all-start.2
  222.7 4.0 copy.111
  229.4 30.0 %all-to-all-done.2 = bf16[32,40,1024]{2,1,0:T(8,128)(2,1)} async-done(((bf16[32,40,1024]{2,1,0:T(8,128)(2,1)}), bf16[32,40,1024]{2,1,0:T(8,128)(2,1)}, u32[]{:S(2)}, u32[]{:S(2)}) %all-to-all-start.2) | async-done | bytes 2621472 | tf_op jit(solution)/shard_map/all_to_all | solution.py:776
  267.2 4.8 all-to-all-start.3
  283.2 22.8 %pair_probs.1 = (bf16[16,1024,1024]{2,1,0:T(8,128)(2,1)}, bf16[2,2,512,512]{3,2,1,0:T(8,128)(2,1)S(1)}) custom-call(s32[128]{0:T(128)S(1)} %copy-done, s32[4]{0:T(128)S(1)} %get-tuple-element.121.own, bf16[512,256]{1,0:T(8,128)(2,1)} %get-tuple-element.59.kv_in, bf16[17408,256]{1,0:T(8,128)(2,1)} %all-gather.12.cloned.1.call-done, ...), custom_call_target="tpu_custom_call" | custom-call | flops 20000000000 | bytes 40000000 | tf_op jit(solution)/shard_map/pair_probs/pallas_call | solution.py:682
  308.0 12.8 %expert_grad.1 = (bf16[1280,1024]{1,0:T(8,128)(2,1)}, bf16[1280,512]{1,0:T(8,128)(2,1)}, bf16[1280,512]{1,0:T(8,128)(2,1)}, bf16[1280,512]{1,0:T(8,128)(2,1)}) custom-call(bf16[1280,1024]{1,0:T(8,128)(2,1)} %bitcast.30.dy_ref, f32[1280,512]{1,0:T(8,128)} %get-tuple-element.81.gate_ref, f32[1280,512]{1,0:T(8,128)} %get-tuple-element.82.up_ref, ...), custom_call_target="tpu_custom_call" | custom-call | flops 4026531840 | bytes 10000000 | tf_op jit(solution)/shard_map/expert_grad/pallas_call | solution.py:575
  320.8 10.1 %all-to-all-start.4 = ((bf16[32,40,1024]{2,1,0:T(8,128)(2,1)}), bf16[32,40,1024]{2,1,0:T(8,128)(2,1)}, u32[]{:S(2)}, u32[]{:S(2)}) async-start(bf16[32,40,1024]{2,1,0:T(8,128)(2,1)} %bitcast.124), calls=%async_computation.4 | async-start | bytes 5242880 | tf_op jit(solution)/shard_map/all_to_all | solution.py:776
  330.9 3.9 pad_maximum_fusion
  339.7 5.0 fusion.104
  344.7 5.1 convolution_bitcast_fusion
  349.7 5.0 convolution_bitcast_fusion.1
  354.8 12.1 %all-to-all-done.4 = bf16[32,40,1024]{2,1,0:T(8,128)(2,1)} async-done(((bf16[32,40,1024]{2,1,0:T(8,128)(2,1)}), bf16[32,40,1024]{2,1,0:T(8,128)(2,1)}, u32[]{:S(2)}, u32[]{:S(2)}) %all-to-all-start.4) | async-done | bytes 2621472 | tf_op jit(solution)/shard_map/all_to_all | solution.py:776
  372.7 3.5 all-to-all-start.5
  376.3 6.6 %all-to-all-done.5 = bf16[4,128,256]{1,2,0:T(8,128)(2,1)S(1)} async-done(((bf16[4,128,256]{1,2,0:T(8,128)(2,1)}), bf16[4,128,256]{1,2,0:T(8,128)(2,1)S(1)}, u32[]{:S(2)}, u32[]{:S(2)}) %all-to-all-start.5) | async-done | bytes 262176 | tf_op jit(solution)/shard_map/all_to_all | solution.py:776
  388.0 38.3 %query_grad.1 = f32[512,256]{1,0:T(8,128)S(1)} custom-call(s32[128]{0:T(128)S(1)} %copy-done, s32[4]{0:T(128)S(1)} %get-tuple-element.121.own, bf16[512,256]{1,0:T(8,128)(2,1)S(1)} %get-tuple-element.72.q_in, bf16[512,256]{1,0:T(8,128)(2,1)S(1)} %bitcast.119, f32[512,256]{1,0:T(8,128)S(1)} %get-tuple-element.62.o_in, ...), custom_call_target="tpu_custom_call" | custom-call | flops 30000001024 | bytes 9969664 | tf_op jit(solution)/shard_map/query_grad/pallas_call | solution.py:553
  427.3 6.6 %all-gather.14.cloned.1.call-done = bf16[17408,256]{1,0:T(8,128)(2,1)} async-done(((bf16[544,256]{1,0:T(8,128)(2,1)}), bf16[17408,256]{1,0:T(8,128)(2,1)}) %all-gather.14.cloned.1.call-update) | async-done | bytes 8912912 | tf_op jit(solution)/shard_map/all_gather | solution.py:1020
  442.0 37.7 %pair_grad.1 = f32[512,256]{1,0:T(8,128)S(1)} custom-call(s32[128]{0:T(128)S(1)} %copy-done, s32[4]{0:T(128)S(1)} %get-tuple-element.121.own, bf16[512,256]{1,0:T(8,128)(2,1)} %get-tuple-element.59.kv_in, f32[512,128]{1,0:T(8,128)S(1)} %get-tuple-element.168.cos_ref, f32[512,128]{1,0:T(8,128)S(1)} %get-tuple-element.169.sin_ref, ...), custom_call_target="tpu_custom_call" | custom-call | flops 30000001024 | bytes 40000000 | tf_op jit(solution)/shard_map/pair_grad/pallas_call | solution.py:682
  480.9 17.3 %psum.22 = f32[32,128]{1,0:T(8,128)S(1)} all-reduce(f32[32,128]{1,0:T(8,128)S(1)} %bitcast.154), channel_id=1, replica_groups=mesh['ctx'=32,'exp'=4] {'exp'}, use_global_device_ids=true, to_apply=%region_18.19 | all-reduce | flops 4096 | bytes 32768 | tf_op jit(solution)/shard_map/psum | solution.py:1071
  504.4 10.1 %all-to-all-start.6 = ((bf16[32,32,896]{2,1,0:T(8,128)(2,1)}), bf16[32,32,896]{2,1,0:T(8,128)(2,1)S(1)}, u32[]{:S(2)}, u32[]{:S(2)}) async-start(bf16[32,32,896]{2,1,0:T(8,128)(2,1)} %fusion.4), calls=%async_computation.6 | async-start | bytes 3670016 | tf_op jit(solution)/shard_map/all_to_all | solution.py:776
  518.9 8.2 %collective-permute-done.12 = bf16[128,512]{1,0:T(8,128)(2,1)S(1)} collective-permute-done((bf16[128,512]{1,0:T(8,128)(2,1)S(1)}, bf16[128,512]{1,0:T(8,128)(2,1)S(1)}, u32[]{:S(2)}, u32[]{:S(2)}) %collective-permute-start.12) | collective-permute-done | bytes 131104 | tf_op jit(solution)/shard_map/ppermute | solution.py:797
  531.4 4.0 fusion.22
  536.6 4.9 all-to-all-done.6
  545.2 7.7 %psum.23 = f32[32]{0:T(128)S(1)} all-reduce(f32[32]{0:T(128)S(1)} %add_add_fusion), channel_id=1, replica_groups=mesh['ctx'=32,'exp'=4] {'exp'}, use_global_device_ids=true, to_apply=%region_24.25 | all-reduce | flops 32 | bytes 256 | tf_op jit(solution)/shard_map/psum | solution.py:1114
  (295 shorter events, 120.3 us)
Async XLA Ops:
  10.2 36.9 %all-to-all-start = ((bf16[32,40,768]{2,1,0:T(8,128)(2,1)}), bf16[32,40,768]{2,1,0:T(8,128)(2,1)}, u32[]{:S(2)}, u32[]{:S(2)}) async-start(bf16[32,40,768]{2,1,0:T(8,128)(2,1)} %broadcast_in_dim.54), calls=%async_computation | async-start | bytes 3932160 | tf_op jit(solution)/shard_map/all_to_all | solution.py:776
  18.7 94.6 %all-gather.8.cloned.1.call-start = ((), (), s32[]{:S(2)}) async-start(), calls=%async_computation.10 | async-start | bytes 8650752 | tf_op jit(solution)/shard_map/all_gather | solution.py:909
  65.7 96.6 %all-gather.10.cloned.1.call-start = ((), (), s32[]{:S(2)}) async-start(), calls=%async_computation.14 | async-start | bytes 3932160 | tf_op jit(solution)/shard_map/all_gather | solution.py:915
  68.1 191.3 %all-gather.12.cloned.1.call-start = ((), (), s32[]{:S(2)}) async-start(), calls=%async_computation.15 | async-start | bytes 9191424 | tf_op jit(solution)/shard_map/all_gather | solution.py:941
  68.2 22.5 %collective-permute-start = (bf16[1024,256]{1,0:T(8,128)(2,1)S(1)}, bf16[1024,256]{1,0:T(8,128)(2,1)S(1)}, u32[]{:S(2)}, u32[]{:S(2)}) collective-permute-start(bf16[1024,256]{1,0:T(8,128)(2,1)S(1)} %slice.170), channel_id=1, source_target_pairs={{0,1},{1,2},{2,3},{3,0},{4,5},{5,6},{6,7},{7,4},{8,9},{9,10},{10,1... | collective-permute-start | bytes 1572872 | tf_op jit(solution)/shard_map/ppermute | solution.py:786
  68.3 22.4 %collective-permute-start.1 = (bf16[1024,256]{1,0:T(8,128)(2,1)S(1)}, bf16[1024,256]{1,0:T(8,128)(2,1)}, u32[]{:S(2)}, u32[]{:S(2)}) collective-permute-start(bf16[1024,256]{1,0:T(8,128)(2,1)S(1)} %slice.170), channel_id=1, source_target_pairs={{0,2},{1,3},{2,0},{3,1},{4,6},{5,7},{6,4},{7,5},{8,10},{9,11},{10,... | collective-permute-start | bytes 1572872 | tf_op jit(solution)/shard_map/ppermute | solution.py:786
  69.5 22.0 %collective-permute-start.2 = (bf16[1024,256]{1,0:T(8,128)(2,1)S(1)}, bf16[1024,256]{1,0:T(8,128)(2,1)}, u32[]{:S(2)}, u32[]{:S(2)}) collective-permute-start(bf16[1024,256]{1,0:T(8,128)(2,1)S(1)} %slice.170), channel_id=1, source_target_pairs={{0,3},{1,0},{2,1},{3,2},{4,7},{5,4},{6,5},{7,6},{8,11},{9,8},{10,9... | collective-permute-start | bytes 1572872 | tf_op jit(solution)/shard_map/ppermute | solution.py:786
  72.8 192.0 %copy-start.7 = (bf16[1280,128]{1,0:T(8,128)(2,1)}, bf16[1280,128]{1,0:T(8,128)(2,1)S(1)}, u32[]{:S(2)}) copy-start(bf16[1280,128]{1,0:T(8,128)(2,1)S(1)} %fusion.17) | copy-start | bytes 983044
  137.3 6.9 %collective-permute-start.3 = (bf16[128,256]{1,0:T(8,128)(2,1)S(1)}, bf16[128,256]{1,0:T(8,128)(2,1)S(1)}, u32[]{:S(2)}, u32[]{:S(2)}) collective-permute-start(bf16[128,256]{1,0:T(8,128)(2,1)S(1)} %get-tuple-element.137), channel_id=1, source_target_pairs={{0,1},{1,2},{2,3},{3,0},{4,5},{5,6},{6,7},{7,4},{8,9},{9,10},{10,1... | collective-permute-start | bytes 196616 | tf_op jit(solution)/shard_map/ppermute | solution.py:797
  138.9 8.4 %collective-permute-start.4 = (bf16[128,256]{1,0:T(8,128)(2,1)S(1)}, bf16[128,256]{1,0:T(8,128)(2,1)S(1)}, u32[]{:S(2)}, u32[]{:S(2)}) collective-permute-start(bf16[128,256]{1,0:T(8,128)(2,1)S(1)} %get-tuple-element.136), channel_id=1, source_target_pairs={{0,2},{1,3},{2,0},{3,1},{4,6},{5,7},{6,4},{7,5},{8,10},{9,11},{10,... | collective-permute-start | bytes 196616 | tf_op jit(solution)/shard_map/ppermute | solution.py:797
  141.6 5.7 %collective-permute-start.5 = (bf16[128,256]{1,0:T(8,128)(2,1)S(1)}, bf16[128,256]{1,0:T(8,128)(2,1)S(1)}, u32[]{:S(2)}, u32[]{:S(2)}) collective-permute-start(bf16[128,256]{1,0:T(8,128)(2,1)S(1)} %get-tuple-element.135), channel_id=1, source_target_pairs={{0,3},{1,0},{2,1},{3,2},{4,7},{5,4},{6,5},{7,6},{8,11},{9,8},{10,9... | collective-permute-start | bytes 196616 | tf_op jit(solution)/shard_map/ppermute | solution.py:797
  153.8 48.0 %all-to-all-start.1 = ((bf16[32,40,1024]{2,1,0:T(8,128)(2,1)}), bf16[32,40,1024]{2,1,0:T(8,128)(2,1)}, u32[]{:S(2)}, u32[]{:S(2)}) async-start(bf16[32,40,1024]{2,1,0:T(8,128)(2,1)} %bitcast.120), calls=%async_computation.1 | async-start | bytes 5242880 | tf_op jit(solution)/shard_map/all_to_all | solution.py:776
  210.6 48.8 %all-to-all-start.2 = ((bf16[32,40,1024]{2,1,0:T(8,128)(2,1)}), bf16[32,40,1024]{2,1,0:T(8,128)(2,1)}, u32[]{:S(2)}, u32[]{:S(2)}) async-start(bf16[32,40,1024]{2,1,0:T(8,128)(2,1)} %bitcast.125), calls=%async_computation.2 | async-start | bytes 5242880 | tf_op jit(solution)/shard_map/all_to_all | solution.py:776
  217.2 45.1 %copy-start.46 = (f32[128]{0:T(128)}, f32[128]{0:T(128)S(1)}, u32[]{:S(2)}) copy-start(f32[128]{0:T(128)S(1)} %dynamic-slice_convert_fusion) | copy-start | bytes 1540
  267.2 40.9 %all-to-all-start.3 = ((bf16[32,40,1024]{2,1,0:T(8,128)(2,1)}), bf16[32,40,1024]{2,1,0:T(8,128)(2,1)}, u32[]{:S(2)}, u32[]{:S(2)}) async-start(bf16[32,40,1024]{2,1,0:T(8,128)(2,1)} %bitcast.126), calls=%async_computation.3 | async-start | bytes 5242880 | tf_op jit(solution)/shard_map/all_to_all | solution.py:776
  272.0 58.9 %collective-permute-start.6 = (bf16[1024,512]{1,0:T(8,128)(2,1)}, bf16[1024,512]{1,0:T(8,128)(2,1)}, u32[]{:S(2)}, u32[]{:S(2)}) collective-permute-start(bf16[1024,512]{1,0:T(8,128)(2,1)} %slice.165), channel_id=1, source_target_pairs={{0,1},{1,2},{2,3},{3,0},{4,5},{5,6},{6,7},{7,4},{8,9},{9,10},{10,1... | collective-permute-start | bytes 3145736 | tf_op jit(solution)/shard_map/ppermute | solution.py:786
  273.6 57.3 %collective-permute-start.7 = (bf16[1024,512]{1,0:T(8,128)(2,1)}, bf16[1024,512]{1,0:T(8,128)(2,1)}, u32[]{:S(2)}, u32[]{:S(2)}) collective-permute-start(bf16[1024,512]{1,0:T(8,128)(2,1)} %slice.165), channel_id=1, source_target_pairs={{0,2},{1,3},{2,0},{3,1},{4,6},{5,7},{6,4},{7,5},{8,10},{9,11},{10,... | collective-permute-start | bytes 3145736 | tf_op jit(solution)/shard_map/ppermute | solution.py:786
  276.3 54.6 %collective-permute-start.8 = (bf16[1024,512]{1,0:T(8,128)(2,1)}, bf16[1024,512]{1,0:T(8,128)(2,1)}, u32[]{:S(2)}, u32[]{:S(2)}) collective-permute-start(bf16[1024,512]{1,0:T(8,128)(2,1)} %slice.165), channel_id=1, source_target_pairs={{0,3},{1,0},{2,1},{3,2},{4,7},{5,4},{6,5},{7,6},{8,11},{9,8},{10,9... | collective-permute-start | bytes 3145736 | tf_op jit(solution)/shard_map/ppermute | solution.py:786
  320.8 46.1 %all-to-all-start.4 = ((bf16[32,40,1024]{2,1,0:T(8,128)(2,1)}), bf16[32,40,1024]{2,1,0:T(8,128)(2,1)}, u32[]{:S(2)}, u32[]{:S(2)}) async-start(bf16[32,40,1024]{2,1,0:T(8,128)(2,1)} %bitcast.124), calls=%async_computation.4 | async-start | bytes 5242880 | tf_op jit(solution)/shard_map/all_to_all | solution.py:776
  372.7 10.2 %all-to-all-start.5 = ((bf16[4,128,256]{1,2,0:T(8,128)(2,1)}), bf16[4,128,256]{1,2,0:T(8,128)(2,1)S(1)}, u32[]{:S(2)}, u32[]{:S(2)}) async-start(bf16[4,128,256]{1,2,0:T(8,128)(2,1)} %fusion.6), calls=%async_computation.5 | async-start | bytes 524288 | tf_op jit(solution)/shard_map/all_to_all | solution.py:776
  376.2 57.6 %all-gather.14.cloned.1.call-start = ((), (), s32[]{:S(2)}) async-start(), calls=%async_computation.16 | async-start | bytes 9191424 | tf_op jit(solution)/shard_map/all_gather | solution.py:1020
  384.2 170.0 %reduce-scatter.8.cloned.1.call-start = ((), (), s32[]{:S(2)}) async-start(), calls=%async_computation.13 | async-start | bytes 2621440 | tf_op jit(solution)/shard_map/reduce_scatter | solution.py:1036
  384.3 41.9 %collective-permute-start.9 = (bf16[128,1024]{1,0:T(8,128)(2,1)S(1)}, bf16[128,1024]{1,0:T(8,128)(2,1)S(1)}, u32[]{:S(2)}, u32[]{:S(2)}) collective-permute-start(bf16[128,1024]{1,0:T(8,128)(2,1)S(1)} %copy-done.11), channel_id=1, source_target_pairs={{0,1},{1,2},{2,3},{3,0},{4,5},{5,6},{6,7},{7,4},{8,9},{9,10},{10,1... | collective-permute-start | bytes 786440 | tf_op jit(solution)/shard_map/ppermute | solution.py:786
  385.0 41.6 %collective-permute-start.11 = (bf16[128,1024]{1,0:T(8,128)(2,1)S(1)}, bf16[128,1024]{1,0:T(8,128)(2,1)S(1)}, u32[]{:S(2)}, u32[]{:S(2)}) collective-permute-start(bf16[128,1024]{1,0:T(8,128)(2,1)S(1)} %copy-done.11), channel_id=1, source_target_pairs={{0,3},{1,0},{2,1},{3,2},{4,7},{5,4},{6,5},{7,6},{8,11},{9,8},{10,9... | collective-permute-start | bytes 786440 | tf_op jit(solution)/shard_map/ppermute | solution.py:786
  387.6 39.3 %collective-permute-start.10 = (bf16[128,1024]{1,0:T(8,128)(2,1)S(1)}, bf16[128,1024]{1,0:T(8,128)(2,1)S(1)}, u32[]{:S(2)}, u32[]{:S(2)}) collective-permute-start(bf16[128,1024]{1,0:T(8,128)(2,1)S(1)} %copy-done.11), channel_id=1, source_target_pairs={{0,2},{1,3},{2,0},{3,1},{4,6},{5,7},{6,4},{7,5},{8,10},{9,11},{10,... | collective-permute-start | bytes 786440 | tf_op jit(solution)/shard_map/ppermute | solution.py:786
  388.0 38.3 %copy-start.16 = (bf16[512,256]{1,0:T(8,128)(2,1)S(1)}, bf16[512,256]{1,0:T(8,128)(2,1)}, u32[]{:S(2)}) copy-start(bf16[512,256]{1,0:T(8,128)(2,1)} %copy-done.15) | copy-start | bytes 786436
  433.9 120.3 %reduce-scatter.4.cloned.1.call-start = ((), (), s32[]{:S(2)}) async-start(), calls=%async_computation.11 | async-start | bytes 2621440 | tf_op jit(solution)/shard_map/reduce_scatter | solution.py:1034
  440.1 114.1 %reduce-scatter.6.cloned.1.call-start = ((), (), s32[]{:S(2)}) async-start(), calls=%async_computation.12 | async-start | bytes 2621440 | tf_op jit(solution)/shard_map/reduce_scatter | solution.py:1035
  504.4 37.0 %all-to-all-start.6 = ((bf16[32,32,896]{2,1,0:T(8,128)(2,1)}), bf16[32,32,896]{2,1,0:T(8,128)(2,1)S(1)}, u32[]{:S(2)}, u32[]{:S(2)}) async-start(bf16[32,32,896]{2,1,0:T(8,128)(2,1)} %fusion.4), calls=%async_computation.6 | async-start | bytes 3670016 | tf_op jit(solution)/shard_map/all_to_all | solution.py:776
  514.6 12.4 %collective-permute-start.12 = (bf16[128,512]{1,0:T(8,128)(2,1)S(1)}, bf16[128,512]{1,0:T(8,128)(2,1)S(1)}, u32[]{:S(2)}, u32[]{:S(2)}) collective-permute-start(bf16[128,512]{1,0:T(8,128)(2,1)S(1)} %get-tuple-element.132), channel_id=1, source_target_pairs={{0,1},{1,2},{2,3},{3,0},{4,5},{5,6},{6,7},{7,4},{8,9},{9,10},{10,1... | collective-permute-start | bytes 393224 | tf_op jit(solution)/shard_map/ppermute | solution.py:797
  514.7 13.8 %collective-permute-start.13 = (bf16[128,512]{1,0:T(8,128)(2,1)S(1)}, bf16[128,512]{1,0:T(8,128)(2,1)}, u32[]{:S(2)}, u32[]{:S(2)}) collective-permute-start(bf16[128,512]{1,0:T(8,128)(2,1)S(1)} %get-tuple-element.131), channel_id=1, source_target_pairs={{0,2},{1,3},{2,0},{3,1},{4,6},{5,7},{6,4},{7,5},{8,10},{9,11},{10,... | collective-permute-start | bytes 393224 | tf_op jit(solution)/shard_map/ppermute | solution.py:797
  515.9 15.5 %collective-permute-start.14 = (bf16[128,512]{1,0:T(8,128)(2,1)S(1)}, bf16[128,512]{1,0:T(8,128)(2,1)}, u32[]{:S(2)}, u32[]{:S(2)}) collective-permute-start(bf16[128,512]{1,0:T(8,128)(2,1)S(1)} %get-tuple-element.133), channel_id=1, source_target_pairs={{0,3},{1,0},{2,1},{3,2},{4,7},{5,4},{6,5},{7,6},{8,11},{9,8},{10,9... | collective-permute-start | bytes 393224 | tf_op jit(solution)/shard_map/ppermute | solution.py:797
  (51 other events, 463.5 us)
Sparse Core Ops, SparseCore 0:
  65.9 47.3 all-gather.7
  114.9 41.8 all-gather.9
  159.7 96.7 all-gather.11
  384.4 49.4 all-gather.13
  436.7 29.1 reduce-scatter.7
  468.8 29.6 reduce-scatter.3
  501.5 35.6 reduce-scatter.5

commit v7 on v6

--- a/solution.py
+++ b/solution.py
@@ -681,7 +681,9 @@
 
     return pl.pallas_call(
         kernel,
-        out_shape=tuple(outs),
+        out_shape=tuple(
+            out if out.dtype == F32 else pltpu.HBM(out.shape, out.dtype) for out in outs
+        ),
         grid_spec=pltpu.PrefetchScalarGridSpec(
             num_scalar_prefetch=2,
             grid=(steps,),
@@ -715,7 +717,7 @@
         [PROB_BLOCK, CONT_SHAPE],
         [
             pltpu.VMEM((total * BLK, 2 * LANES), BF16),
-            pltpu.VMEM((4, total * BLK), F32),
+            pltpu.VMEM((8, total * BLK), F32),
             pltpu.VMEM((16 * BLK, 2 * LANES), BF16),
             pltpu.SemaphoreType.DMA((2,)),
         ],
@@ -737,7 +739,7 @@
         [
             pltpu.VMEM((total * BLK, 2 * LANES), BF16),
             pltpu.VMEM((total * BLK, 2 * LANES), BF16),
-            pltpu.VMEM((4, total * BLK), F32),
+            pltpu.VMEM((8, total * BLK), F32),
             pltpu.VMEM((16 * BLK, 2 * LANES), BF16),
             pltpu.VMEM((16 * BLK, 2 * LANES), F32),
             pltpu.VMEM((16 * BLK, 2 * LANES), F32),
@@ -811,12 +813,13 @@
 
 
 def with_stats(rows, stats):
+    stats = jnp.pad(stats, ((0, 0), (0, 4), (0, 0)))
     parts = jnp.stack(pieces(stats, 3), axis=0).reshape(-1, rows.shape[1])
-    return jnp.concatenate([rows, jnp.pad(parts, ((0, -parts.shape[0] % 16), (0, 0)))], axis=0)
+    return jnp.concatenate([rows, parts], axis=0)
 
 
 def stats_in(gathered, first):
-    parts = gathered[:, first : first + 24].reshape(-1, 3, 2, 4, gathered.shape[2])
+    parts = gathered[:, first:].reshape(-1, 3, 2, 8, gathered.shape[2])
     return jnp.sum(parts.astype(F32), axis=1)
 
 
@@ -861,14 +864,13 @@
     qkv_cols = head_cols + 2 * kv_cols
     shard_rows = w_query.shape[0]
 
-    own_weights = jnp.concatenate([w_query, w_key, w_value, w_out], axis=1)
+    own_weights = jnp.concatenate([w_query, w_key, w_value], axis=1)
     gain_row = jnp.concatenate([gain_attn, gain_query, gain_ffn, gain_key])
     gain_rows = jnp.pad(
         gain_row, (0, 8 * own_weights.shape[1] - gain_row.shape[0])
     ).reshape(8, -1)
     first_parts = spread(jnp.concatenate([own_weights, gain_rows], axis=0), "ctx", ctx_count)
-    full_weights = first_parts[:, :shard_rows].reshape(model_width, -1)
-    full_qkv = full_weights[:, :qkv_cols]
+    full_qkv = first_parts[:, :shard_rows].reshape(model_width, qkv_cols)
     gains = first_parts[:, shard_rows:].reshape(ctx_count, -1)[:, : gain_row.shape[0]].astype(F32)
     attn_gain = gains[:, :shard_rows].reshape(model_width)
     query_gain_all = gains[:, shard_rows : 2 * shard_rows].reshape(model_width)
@@ -876,6 +878,10 @@
     key_gain_all = gains[:, 3 * shard_rows :].reshape(kv_total)
     query_gain = lax.dynamic_slice_in_dim(query_gain_all, exp_index * head_cols, head_cols)
     key_gain = lax.dynamic_slice_in_dim(key_gain_all, exp_index * kv_cols, kv_cols)
+
+    width = w_gate.shape[2]
+    own_expert = jnp.concatenate([w_gate[0], w_up[0], w_down[0].T], axis=1)
+    expert = lax.all_gather(own_expert, "exp", axis=0, tiled=False)
 
     hidden_f = hidden_in.astype(F32)
     attn_scale = lax.rsqrt(jnp.mean(hidden_f * hidden_f, axis=-1, keepdims=True) + NORM_EPSILON)
@@ -906,16 +912,16 @@
         cosine,
         sine,
     )
+    own_kv, expert = lax.optimization_barrier((own_kv, expert))
     kv_all = lax.all_gather(own_kv, "ctx", axis=0, tiled=True)
-    own_out, own_gate, own_up, own_down, _ = lax.optimization_barrier(
-        (full_weights[:, qkv_cols:], w_gate[0], w_up[0], w_down[0], own_kv)
-    )
-    width = w_gate.shape[2]
-    own_expert = jnp.concatenate([own_gate, own_up, own_down.T], axis=1)
-    expert = lax.all_gather(own_expert, "exp", axis=0, tiled=False)
-    out_parts = shifted(own_out, "exp", exp_count)
+    own_out, _ = lax.optimization_barrier((w_out, own_kv))
+    out_parts = shifted(
+        spread(own_out, "ctx", ctx_count).reshape(model_width, head_cols), "exp", exp_count
+    )
     wide_out = jnp.concatenate(out_parts, axis=1)
     full_out = in_order(out_parts, exp_index, exp_count)
+    full_out, later_q = lax.optimization_barrier((full_out, queries_rot))
+    q_all = lax.all_gather(later_q, "ctx", axis=0, tiled=True)
     expert_total = ctx_count
     capacity = max(2, own_rows * routes.shape[1] * 5 // (expert_total * 4))
     slots = expert_total * capacity
@@ -937,8 +943,8 @@
     heads_low = heads_f.astype(BF16)
 
     own_heads = exchange_short(heads_low, "exp", exp_index, exp_count)
-    own_heads, later_q, lse = lax.optimization_barrier((own_heads, queries_rot, lse))
-    q_all = lax.all_gather(with_stats(later_q, lse), "ctx", axis=0, tiled=False)
+    stat_rows = jnp.pad(lse, ((0, 0), (0, 28), (0, 0)))
+    lse_all = lax.all_gather(stat_rows, "ctx", axis=0, tiled=False)
     attn_rows = dot(own_heads, wide_out, NT)
     hidden_rows = lax.dynamic_slice_in_dim(hidden_in, exp_index * own_rows, own_rows, 0)
     hidden_rows = hidden_rows.astype(F32)
@@ -953,19 +959,20 @@
         )
 
     expert_in = send(dot(pick, normed_ffn, NN).astype(BF16))
+    expert_in, q_all = lax.optimization_barrier((expert_in, q_all))
     expert_out, gate_pre, up_pre = expert_forward(expert_in, expert)
     returned = send(expert_out)
     turned = expert[:, :, : 2 * width].transpose(0, 2, 1)
-    returned, q_all, later_qkv, turned = lax.optimization_barrier(
-        (returned, q_all, full_qkv, turned)
+    returned, q_all, lse_all, later_qkv, turned = lax.optimization_barrier(
+        (returned, q_all, lse_all[:, :, :8], full_qkv, turned)
     )
     probs = pair_probs(
         block_of,
         own_blocks,
         own_kv,
-        q_all.reshape(-1, head_cols),
-        q_all.shape[1],
-        stats_in(q_all, ctx_rows),
+        q_all,
+        ctx_rows,
+        lse_all,
     )
     wide_qkv = jnp.concatenate(shifted(later_qkv, "exp", exp_count), axis=1)
     moe_parts = dot(jnp.concatenate(pieces(weigh, 2), axis=1), returned, TN)
@@ -1041,8 +1048,8 @@
         own_kv,
         cosine,
         sine,
-        q_all.reshape(-1, head_cols),
-        q_all.shape[1],
+        q_all,
+        ctx_rows,
         do_all.reshape(-1, head_cols),
         do_all.shape[1],
         stats_in(do_all, ctx_rows),

time: 569 us -> 551 us (0.968)
  waiting for transfers between devices: 176 us -> 155 us
  blocking collectives: 35.8 us -> 51.9 us
  local copies, waits for them, and re-layouts: 37.8 us -> 31.3 us
  starting transfers between devices: 73.4 us -> 67.5 us
    all_to_all x7, waiting for transfers between devices: 120 us -> 59.9 us  [exchange(): return lax.all_to_all(values, axis, split_axis=0, concat_axis=0, tiled=True)]
    all_gather x1 -> x2, waiting for transfers between devices: 0.01 us -> 52.6 us  [the longest x1 27.7 us: on_device(): lse_all = lax.all_gather(stat_rows, 'ctx', axis=0, tiled=False)]
    all_to_all x0 -> x1, blocking collectives: none -> 16.2 us  [exchange(): return lax.all_to_all(values, axis, split_axis=0, concat_axis=0, tiled=True)]
    all_gather x1, waiting for transfers between devices: 15.9 us -> 0.01 us  [on_device(): kv_all = lax.all_gather(own_kv, 'ctx', axis=0, tiled=True)]
    ppermute x9, waiting for transfers between devices: 16.6 us -> 23.3 us  [shifted(): lax.ppermute(values, axis, [(i, (i + step) % count) for i in range(count)])]
    pallas_call x3, Pallas kernels: 63.7 us -> 69.8 us  [kernel_call(): pl.pallas_call(kernel, out_shape=tuple(outs), grid_spec=pltpu.PrefetchSca...]
    reshape x2, local copies, waits for them, and re-layouts: 0.02 us -> 5.85 us  [the longest x1 2.93 us: on_device(): up_part = up_part.reshape(model_width, exp_count, width).transpose(1, 0, 2)]
  transfers between devices with their start and end apart: 29 -> 30, of which waited for: 16 -> 17; matrix products, arithmetic and copies ran while one was open for 15% -> 15% of each run, Pallas kernels for 26% -> 27%
where the time goes in v7:
time: 551 us; the launch traced here: 545 us
  waiting for transfers between devices  155 us (28%)
  Pallas kernels  147 us (27%)
  starting transfers between devices  67.5 us (12%)
  blocking collectives  51.9 us (9%)
  matrix products  40.6 us (7%)
  other arithmetic  32.9 us (6%)
  local copies, waits for them, and re-layouts  31.3 us (6%)
  between operations  18.8 us (3%)
    pallas_call x3, Pallas kernels, kernel_call(): pl.pallas_call(kernel, out_shape=tuple(outs), grid_spec=pltpu.PrefetchSca...  69.8 us
    all_to_all x7, waiting for transfers between devices, exchange(): return lax.all_to_all(values, axis, split_axis=0, concat_axis=0, tiled=True)  59.9 us
    pallas_call x2, Pallas kernels, pair_call(): pl.pallas_call(kernel, out_shape=tuple((out if out.dtype == F32 else pltp...  55.5 us
    all_to_all x7, starting transfers between devices, exchange(): return lax.all_to_all(values, axis, split_axis=0, concat_axis=0, tiled=True)  46.2 us
    dot_general x16, matrix products, dot(): return lax.dot_general(left, right, dims, preferred_element_type=F32)  38.8 us
    all_gather x1, waiting for transfers between devices, on_device(): lse_all = lax.all_gather(stat_rows, 'ctx', axis=0, tiled=False)  27.7 us
    all_gather x1, waiting for transfers between devices, on_device(): q_all = lax.all_gather(later_q, 'ctx', axis=0, tiled=True)  24.9 us
    ppermute x9, waiting for transfers between devices, shifted(): lax.ppermute(values, axis, [(i, (i + step) % count) for i in range(count)])  23.3 us
  transfers between devices with their start and end apart: 30, of which 17 were waited for; matrix products, arithmetic and copies ran while one was open for 15% of the time, Pallas kernels for 27%

profile of v7, /device:TPU:0, one launch (start us, length us, event | category | flops | bytes accessed | tf_op | source)
XLA Modules:
  0.0 545.3 jit_solution(1371565026305984798)
XLA Ops:
  11.9 8.4 %all-to-all-start = ((bf16[32,40,512]{2,1,0:T(8,128)(2,1)}), bf16[32,40,512]{2,1,0:T(8,128)(2,1)S(1)}, u32[]{:S(2)}, u32[]{:S(2)}) async-start(bf16[32,40,512]{2,1,0:T(8,128)(2,1)} %broadcast_in_dim.56), calls=%async_computation | async-start | bytes 2621440 | tf_op jit(solution)/shard_map/all_to_all | solution.py:778
  22.3 18.8 %all-to-all-done = bf16[32,40,512]{2,1,0:T(8,128)(2,1)S(1)} async-done(((bf16[32,40,512]{2,1,0:T(8,128)(2,1)}), bf16[32,40,512]{2,1,0:T(8,128)(2,1)S(1)}, u32[]{:S(2)}, u32[]{:S(2)}) %all-to-all-start) | async-done | bytes 1310752 | tf_op jit(solution)/shard_map/all_to_all | solution.py:778
  45.5 10.7 %psum.21 = f32[2,512]{1,0:T(2,128)S(1)} all-reduce(f32[2,512]{1,0:T(2,128)S(1)} %pad_maximum_fusion.11), channel_id=1, replica_groups=mesh['ctx'=32,'exp'=4] {'exp'}, use_global_device_ids=true, to_apply=%region_3.4 | all-reduce | flops 1024 | bytes 8192 | tf_op jit(solution)/shard_map/psum | solution.py:893
  58.6 16.2 %all_to_all.40 = bf16[32,32,256]{2,1,0:T(8,128)(2,1)S(1)} all-to-all(bf16[32,32,256]{2,1,0:T(8,128)(2,1)S(1)} %broadcast_in_dim.58), channel_id=1, replica_groups=mesh['ctx'=32,'exp'=4] {'ctx'}, dimensions={0} | all-to-all | bytes 1048576 | tf_op jit(solution)/shard_map/all_to_all | solution.py:778
  78.5 22.5 %collective-permute-done = bf16[1024,256]{1,0:T(8,128)(2,1)S(1)} collective-permute-done((bf16[1024,256]{1,0:T(8,128)(2,1)S(1)}, bf16[1024,256]{1,0:T(8,128)(2,1)S(1)}, u32[]{:S(2)}, u32[]{:S(2)}) %collective-permute-start) | collective-permute-done | bytes 524320 | tf_op jit(solution)/shard_map/ppermute | solution.py:788
  109.8 26.9 %attend.1 = (f32[512,256]{1,0:T(8,128)S(1)}, f32[2,4,256]{2,1,0:T(4,128)S(1)}) custom-call(s32[128]{0:T(128)S(1)} %copy-done, s32[4]{0:T(128)S(1)} %get-tuple-element.123.own, bf16[512,256]{1,0:T(8,128)(2,1)} %get-tuple-element.69.q_in, bf16[16384,256]{1,0:T(8,128)(2,1)} %all-gather.9.cloned.1.call-done.kv), custom_call_target="tpu_custom_call" | custom-call | flops 20000000000 | bytes 8650752 | tf_op jit(solution)/shard_map/attend/pallas_call | solution.py:553
  150.1 5.0 all-to-all-start.2
  155.8 24.9 %all-gather.11.cloned.1.call-done.q_all = bf16[16384,256]{1,0:T(8,128)(2,1)} async-done(((bf16[512,256]{1,0:T(8,128)(2,1)}), bf16[16384,256]{1,0:T(8,128)(2,1)}) %all-gather.11.cloned.1.call-update) | async-done | bytes 8388624 | tf_op jit(solution)/shard_map/all_gather | solution.py:924
  180.7 12.6 %all-to-all-done.2 = bf16[32,40,1024]{2,1,0:T(8,128)(2,1)} async-done(((bf16[32,40,1024]{2,1,0:T(8,128)(2,1)}), bf16[32,40,1024]{2,1,0:T(8,128)(2,1)}, u32[]{:S(2)}, u32[]{:S(2)}) %all-to-all-start.2) | async-done | bytes 2621472 | tf_op jit(solution)/shard_map/all_to_all | solution.py:778
  193.3 8.6 %expert.1 = (bf16[1280,1024]{1,0:T(8,128)(2,1)}, f32[1280,512]{1,0:T(8,128)}, f32[1280,512]{1,0:T(8,128)}) custom-call(bf16[1280,1024]{1,0:T(8,128)(2,1)} %bitcast.21.x_ref, bf16[4,1024,384]{2,1,0:T(8,128)(2,1)} %bitcast.129), custom_call_target="tpu_custom_call" | custom-call | flops 4026531840 | bytes 10000000 | tf_op jit(solution)/shard_map/expert/pallas_call | solution.py:575
  201.9 5.1 all-to-all-start.3
  209.0 4.7 copy.98
  219.4 27.7 %all-gather.15.cloned.1.call-done = f32[64,32,256]{2,1,0:T(8,128)} async-done(((f32[2,32,256]{2,1,0:T(8,128)}), f32[64,32,256]{2,1,0:T(8,128)}) %all-gather.15.cloned.1.call-update) | async-done | bytes 2097168 | tf_op jit(solution)/shard_map/all_gather | solution.py:947
  255.3 5.4 all-to-all-start.4
  266.6 21.6 %pair_probs.1 = (bf16[16,1024,1024]{2,1,0:T(8,128)(2,1)}, bf16[2,2,512,512]{3,2,1,0:T(8,128)(2,1)}) custom-call(s32[128]{0:T(128)S(1)} %copy-done, s32[4]{0:T(128)S(1)} %get-tuple-element.123.own, bf16[512,256]{1,0:T(8,128)(2,1)} %get-tuple-element.61.kv_in, bf16[16384,256]{1,0:T(8,128)(2,1)} %all-gather.11.cloned.1.call-done.q_all, ...), custom_call_target="tpu_custom_call" | custom-call | flops 20000000000 | bytes 40000000 | tf_op jit(solution)/shard_map/pair_probs/pallas_call | solution.py:682
  288.2 8.6 %all-to-all-done.4 = bf16[32,40,1024]{2,1,0:T(8,128)(2,1)} async-done(((bf16[32,40,1024]{2,1,0:T(8,128)(2,1)}), bf16[32,40,1024]{2,1,0:T(8,128)(2,1)}, u32[]{:S(2)}, u32[]{:S(2)}) %all-to-all-start.4) | async-done | bytes 2621472 | tf_op jit(solution)/shard_map/all_to_all | solution.py:778
  296.8 12.8 %expert_grad.1 = (bf16[1280,1024]{1,0:T(8,128)(2,1)}, bf16[1280,512]{1,0:T(8,128)(2,1)}, bf16[1280,512]{1,0:T(8,128)(2,1)}, bf16[1280,512]{1,0:T(8,128)(2,1)}) custom-call(bf16[1280,1024]{1,0:T(8,128)(2,1)} %bitcast.28.dy_ref, f32[1280,512]{1,0:T(8,128)} %get-tuple-element.83.gate_ref, f32[1280,512]{1,0:T(8,128)} %get-tuple-element.84.up_ref, ...), custom_call_target="tpu_custom_call" | custom-call | flops 4026531840 | bytes 10000000 | tf_op jit(solution)/shard_map/expert_grad/pallas_call | solution.py:575
  309.6 5.0 all-to-all-start.5
  314.7 4.0 pad_maximum_fusion
  318.6 4.7 fusion.103
  326.2 5.0 fusion.102
  334.2 5.0 fusion.104
  339.2 11.4 %all-to-all-done.5 = bf16[32,40,1024]{2,1,0:T(8,128)(2,1)} async-done(((bf16[32,40,1024]{2,1,0:T(8,128)(2,1)}), bf16[32,40,1024]{2,1,0:T(8,128)(2,1)}, u32[]{:S(2)}, u32[]{:S(2)}) %all-to-all-start.5) | async-done | bytes 2621472 | tf_op jit(solution)/shard_map/all_to_all | solution.py:778
  357.1 4.4 all-to-all-start.6
  361.5 6.7 %all-to-all-done.6 = bf16[4,128,256]{1,2,0:T(8,128)(2,1)S(1)} async-done(((bf16[4,128,256]{1,2,0:T(8,128)(2,1)}), bf16[4,128,256]{1,2,0:T(8,128)(2,1)S(1)}, u32[]{:S(2)}, u32[]{:S(2)}) %all-to-all-start.6) | async-done | bytes 262176 | tf_op jit(solution)/shard_map/all_to_all | solution.py:778
  373.2 41.5 %query_grad.1 = f32[512,256]{1,0:T(8,128)S(1)} custom-call(s32[128]{0:T(128)S(1)} %copy-done, s32[4]{0:T(128)S(1)} %get-tuple-element.123.own, bf16[512,256]{1,0:T(8,128)(2,1)} %get-tuple-element.69.q_in, bf16[512,256]{1,0:T(8,128)(2,1)S(1)} %bitcast.116, f32[512,256]{1,0:T(8,128)S(1)} %get-tuple-element.65.o_in, f32[2,4,256]{2,1,0:T(4,128)S(1)} %get-tuple-element.74.lse_in, ...), custom_call_target="tpu_custom_call" | custom-call | flops 30000001024 | bytes 9969664 | tf_op jit(solution)/shard_map/query_grad/pallas_call | solution.py:553
  425.6 33.9 %pair_grad.1 = f32[512,256]{1,0:T(8,128)S(1)} custom-call(s32[128]{0:T(128)S(1)} %copy-done, s32[4]{0:T(128)S(1)} %get-tuple-element.123.own, bf16[512,256]{1,0:T(8,128)(2,1)} %get-tuple-element.61.kv_in, f32[512,128]{1,0:T(8,128)S(1)} %get-tuple-element.167.cos_ref, f32[512,128]{1,0:T(8,128)S(1)} %get-tuple-element.168.sin_ref, ...), custom_call_target="tpu_custom_call" | custom-call | flops 30000001024 | bytes 40000000 | tf_op jit(solution)/shard_map/pair_grad/pallas_call | solution.py:682
  460.8 17.3 %psum.22 = f32[32,128]{1,0:T(8,128)S(1)} all-reduce(f32[32,128]{1,0:T(8,128)S(1)} %bitcast.158), channel_id=1, replica_groups=mesh['ctx'=32,'exp'=4] {'exp'}, use_global_device_ids=true, to_apply=%region_17.18 | all-reduce | flops 4096 | bytes 32768 | tf_op jit(solution)/shard_map/psum | solution.py:1078
  484.4 12.8 %all-to-all-start.7 = ((bf16[32,32,896]{2,1,0:T(8,128)(2,1)}), bf16[32,32,896]{2,1,0:T(8,128)(2,1)S(1)}, u32[]{:S(2)}, u32[]{:S(2)}) async-start(bf16[32,32,896]{2,1,0:T(8,128)(2,1)} %fusion.4), calls=%async_computation.7 | async-start | bytes 3670016 | tf_op jit(solution)/shard_map/all_to_all | solution.py:778
  503.3 8.3 %collective-permute-done.12 = bf16[128,512]{1,0:T(8,128)(2,1)S(1)} collective-permute-done((bf16[128,512]{1,0:T(8,128)(2,1)}, bf16[128,512]{1,0:T(8,128)(2,1)S(1)}, u32[]{:S(2)}, u32[]{:S(2)}) %collective-permute-start.12) | collective-permute-done | bytes 131104 | tf_op jit(solution)/shard_map/ppermute | solution.py:799
  516.5 4.1 fusion.20
  527.9 7.7 %psum.23 = f32[32]{0:T(128)S(1)} all-reduce(f32[32]{0:T(128)S(1)} %add_add_fusion), channel_id=1, replica_groups=mesh['ctx'=32,'exp'=4] {'exp'}, use_global_device_ids=true, to_apply=%region_23.24 | all-reduce | flops 32 | bytes 256 | tf_op jit(solution)/shard_map/psum | solution.py:1121
  (290 shorter events, 114.1 us)
Async XLA Ops:
  7.3 51.2 %all-gather.13.cloned.1.call-start = ((), (), s32[]{:S(2)}) async-start(), calls=%async_computation.16 | async-start | bytes 3932160 | tf_op jit(solution)/shard_map/all_gather | solution.py:884
  11.9 29.2 %all-to-all-start = ((bf16[32,40,512]{2,1,0:T(8,128)(2,1)}), bf16[32,40,512]{2,1,0:T(8,128)(2,1)S(1)}, u32[]{:S(2)}, u32[]{:S(2)}) async-start(bf16[32,40,512]{2,1,0:T(8,128)(2,1)} %broadcast_in_dim.56), calls=%async_computation | async-start | bytes 2621440 | tf_op jit(solution)/shard_map/all_to_all | solution.py:778
  20.3 89.5 %all-gather.9.cloned.1.call-start = ((), (), s32[]{:S(2)}) async-start(), calls=%async_computation.11 | async-start | bytes 8650752 | tf_op jit(solution)/shard_map/all_gather | solution.py:916
  58.5 122.1 %all-gather.11.cloned.1.call-start = ((), (), s32[]{:S(2)}) async-start(), calls=%async_computation.12 | async-start | bytes 8650752 | tf_op jit(solution)/shard_map/all_gather | solution.py:924
  74.8 26.2 %collective-permute-start = (bf16[1024,256]{1,0:T(8,128)(2,1)S(1)}, bf16[1024,256]{1,0:T(8,128)(2,1)S(1)}, u32[]{:S(2)}, u32[]{:S(2)}) collective-permute-start(bf16[1024,256]{1,0:T(8,128)(2,1)S(1)} %bitcast.120), channel_id=1, source_target_pairs={{0,1},{1,2},{2,3},{3,0},{4,5},{5,6},{6,7},{7,4},{8,9},{9,10},{10,1... | collective-permute-start | bytes 1572872 | tf_op jit(solution)/shard_map/ppermute | solution.py:788
  74.8 26.2 %collective-permute-start.1 = (bf16[1024,256]{1,0:T(8,128)(2,1)S(1)}, bf16[1024,256]{1,0:T(8,128)(2,1)S(1)}, u32[]{:S(2)}, u32[]{:S(2)}) collective-permute-start(bf16[1024,256]{1,0:T(8,128)(2,1)S(1)} %bitcast.121), channel_id=1, source_target_pairs={{0,2},{1,3},{2,0},{3,1},{4,6},{5,7},{6,4},{7,5},{8,10},{9,11},{10,... | collective-permute-start | bytes 1572872 | tf_op jit(solution)/shard_map/ppermute | solution.py:788
  74.8 26.9 %collective-permute-start.2 = (bf16[1024,256]{1,0:T(8,128)(2,1)S(1)}, bf16[1024,256]{1,0:T(8,128)(2,1)}, u32[]{:S(2)}, u32[]{:S(2)}) collective-permute-start(bf16[1024,256]{1,0:T(8,128)(2,1)S(1)} %bitcast.122), channel_id=1, source_target_pairs={{0,3},{1,0},{2,1},{3,2},{4,7},{5,4},{6,5},{7,6},{8,11},{9,8},{10,9... | collective-permute-start | bytes 1572872 | tf_op jit(solution)/shard_map/ppermute | solution.py:788
  136.7 5.5 %collective-permute-start.3 = (bf16[128,256]{1,0:T(8,128)(2,1)S(1)}, bf16[128,256]{1,0:T(8,128)(2,1)S(1)}, u32[]{:S(2)}, u32[]{:S(2)}) collective-permute-start(bf16[128,256]{1,0:T(8,128)(2,1)S(1)} %get-tuple-element.139), channel_id=1, source_target_pairs={{0,1},{1,2},{2,3},{3,0},{4,5},{5,6},{6,7},{7,4},{8,9},{9,10},{10,1... | collective-permute-start | bytes 196616 | tf_op jit(solution)/shard_map/ppermute | solution.py:799
  137.0 6.8 %collective-permute-start.4 = (bf16[128,256]{1,0:T(8,128)(2,1)S(1)}, bf16[128,256]{1,0:T(8,128)(2,1)S(1)}, u32[]{:S(2)}, u32[]{:S(2)}) collective-permute-start(bf16[128,256]{1,0:T(8,128)(2,1)S(1)} %get-tuple-element.138), channel_id=1, source_target_pairs={{0,2},{1,3},{2,0},{3,1},{4,6},{5,7},{6,4},{7,5},{8,10},{9,11},{10,... | collective-permute-start | bytes 196616 | tf_op jit(solution)/shard_map/ppermute | solution.py:799
  140.9 4.3 collective-permute-start.5
  150.1 43.2 %all-to-all-start.2 = ((bf16[32,40,1024]{2,1,0:T(8,128)(2,1)}), bf16[32,40,1024]{2,1,0:T(8,128)(2,1)}, u32[]{:S(2)}, u32[]{:S(2)}) async-start(bf16[32,40,1024]{2,1,0:T(8,128)(2,1)} %bitcast.117), calls=%async_computation.2 | async-start | bytes 5242880 | tf_op jit(solution)/shard_map/all_to_all | solution.py:778
  155.1 92.1 %all-gather.15.cloned.1.call-start = ((), (), s32[]{:S(2)}) async-start(), calls=%async_computation.17 | async-start | bytes 2162688 | tf_op jit(solution)/shard_map/all_gather | solution.py:947
  201.9 46.3 %all-to-all-start.3 = ((bf16[32,40,1024]{2,1,0:T(8,128)(2,1)}), bf16[32,40,1024]{2,1,0:T(8,128)(2,1)}, u32[]{:S(2)}, u32[]{:S(2)}) async-start(bf16[32,40,1024]{2,1,0:T(8,128)(2,1)} %bitcast.133), calls=%async_computation.3 | async-start | bytes 5242880 | tf_op jit(solution)/shard_map/all_to_all | solution.py:778
  255.3 41.5 %all-to-all-start.4 = ((bf16[32,40,1024]{2,1,0:T(8,128)(2,1)}), bf16[32,40,1024]{2,1,0:T(8,128)(2,1)}, u32[]{:S(2)}, u32[]{:S(2)}) async-start(bf16[32,40,1024]{2,1,0:T(8,128)(2,1)} %bitcast.135), calls=%async_computation.4 | async-start | bytes 5242880 | tf_op jit(solution)/shard_map/all_to_all | solution.py:778
  260.8 53.9 %collective-permute-start.6 = (bf16[1024,512]{1,0:T(8,128)(2,1)}, bf16[1024,512]{1,0:T(8,128)(2,1)}, u32[]{:S(2)}, u32[]{:S(2)}) collective-permute-start(bf16[1024,512]{1,0:T(8,128)(2,1)} %bitcast.125), channel_id=1, source_target_pairs={{0,1},{1,2},{2,3},{3,0},{4,5},{5,6},{6,7},{7,4},{8,9},{9,10},{10,1... | collective-permute-start | bytes 3145736 | tf_op jit(solution)/shard_map/ppermute | solution.py:788
  262.5 52.2 %collective-permute-start.7 = (bf16[1024,512]{1,0:T(8,128)(2,1)}, bf16[1024,512]{1,0:T(8,128)(2,1)}, u32[]{:S(2)}, u32[]{:S(2)}) collective-permute-start(bf16[1024,512]{1,0:T(8,128)(2,1)} %bitcast.126), channel_id=1, source_target_pairs={{0,2},{1,3},{2,0},{3,1},{4,6},{5,7},{6,4},{7,5},{8,10},{9,11},{10,... | collective-permute-start | bytes 3145736 | tf_op jit(solution)/shard_map/ppermute | solution.py:788
  265.2 49.5 %collective-permute-start.8 = (bf16[1024,512]{1,0:T(8,128)(2,1)}, bf16[1024,512]{1,0:T(8,128)(2,1)}, u32[]{:S(2)}, u32[]{:S(2)}) collective-permute-start(bf16[1024,512]{1,0:T(8,128)(2,1)} %bitcast.127), channel_id=1, source_target_pairs={{0,3},{1,0},{2,1},{3,2},{4,7},{5,4},{6,5},{7,6},{8,11},{9,8},{10,9... | collective-permute-start | bytes 3145736 | tf_op jit(solution)/shard_map/ppermute | solution.py:788
  309.6 41.1 %all-to-all-start.5 = ((bf16[32,40,1024]{2,1,0:T(8,128)(2,1)}), bf16[32,40,1024]{2,1,0:T(8,128)(2,1)}, u32[]{:S(2)}, u32[]{:S(2)}) async-start(bf16[32,40,1024]{2,1,0:T(8,128)(2,1)} %bitcast.134), calls=%async_computation.5 | async-start | bytes 5242880 | tf_op jit(solution)/shard_map/all_to_all | solution.py:778
  357.1 11.1 %all-to-all-start.6 = ((bf16[4,128,256]{1,2,0:T(8,128)(2,1)}), bf16[4,128,256]{1,2,0:T(8,128)(2,1)S(1)}, u32[]{:S(2)}, u32[]{:S(2)}) async-start(bf16[4,128,256]{1,2,0:T(8,128)(2,1)} %fusion.6), calls=%async_computation.6 | async-start | bytes 524288 | tf_op jit(solution)/shard_map/all_to_all | solution.py:778
  361.5 58.2 %all-gather.17.cloned.1.call-start = ((), (), s32[]{:S(2)}) async-start(), calls=%async_computation.18 | async-start | bytes 9461760 | tf_op jit(solution)/shard_map/all_gather | solution.py:1027
  369.5 167.4 %reduce-scatter.8.cloned.1.call-start = ((), (), s32[]{:S(2)}) async-start(), calls=%async_computation.15 | async-start | bytes 2621440 | tf_op jit(solution)/shard_map/reduce_scatter | solution.py:1043
  369.6 45.1 %collective-permute-start.9 = (bf16[128,1024]{1,0:T(8,128)(2,1)S(1)}, bf16[128,1024]{1,0:T(8,128)(2,1)S(1)}, u32[]{:S(2)}, u32[]{:S(2)}) collective-permute-start(bf16[128,1024]{1,0:T(8,128)(2,1)S(1)} %get-tuple-element.120), channel_id=1, source_target_pairs={{0,1},{1,2},{2,3},{3,0},{4,5},{5,6},{6,7},{7,4},{8,9},{9,10},{10,1... | collective-permute-start | bytes 786440 | tf_op jit(solution)/shard_map/ppermute | solution.py:788
  370.2 44.8 %collective-permute-start.11 = (bf16[128,1024]{1,0:T(8,128)(2,1)S(1)}, bf16[128,1024]{1,0:T(8,128)(2,1)S(1)}, u32[]{:S(2)}, u32[]{:S(2)}) collective-permute-start(bf16[128,1024]{1,0:T(8,128)(2,1)S(1)} %get-tuple-element.120), channel_id=1, source_target_pairs={{0,3},{1,0},{2,1},{3,2},{4,7},{5,4},{6,5},{7,6},{8,11},{9,8},{10,9... | collective-permute-start | bytes 786440 | tf_op jit(solution)/shard_map/ppermute | solution.py:788
  372.9 42.5 %collective-permute-start.10 = (bf16[128,1024]{1,0:T(8,128)(2,1)S(1)}, bf16[128,1024]{1,0:T(8,128)(2,1)S(1)}, u32[]{:S(2)}, u32[]{:S(2)}) collective-permute-start(bf16[128,1024]{1,0:T(8,128)(2,1)S(1)} %get-tuple-element.120), channel_id=1, source_target_pairs={{0,2},{1,3},{2,0},{3,1},{4,6},{5,7},{6,4},{7,5},{8,10},{9,11},{10,... | collective-permute-start | bytes 786440 | tf_op jit(solution)/shard_map/ppermute | solution.py:788
  373.2 41.5 %copy-start.11 = (bf16[512,256]{1,0:T(8,128)(2,1)S(1)}, bf16[512,256]{1,0:T(8,128)(2,1)}, u32[]{:S(2)}) copy-start(bf16[512,256]{1,0:T(8,128)(2,1)} %copy-done.10) | copy-start | bytes 786436
  419.7 117.2 %reduce-scatter.4.cloned.1.call-start = ((), (), s32[]{:S(2)}) async-start(), calls=%async_computation.13 | async-start | bytes 2621440 | tf_op jit(solution)/shard_map/reduce_scatter | solution.py:1041
  423.7 113.2 %reduce-scatter.6.cloned.1.call-start = ((), (), s32[]{:S(2)}) async-start(), calls=%async_computation.14 | async-start | bytes 2621440 | tf_op jit(solution)/shard_map/reduce_scatter | solution.py:1042
  425.6 34.5 %copy-start.29 = (f32[1024]{0:T(1024)S(1)}, f32[1024]{0:T(1024)}, u32[]{:S(2)}) copy-start(f32[1024]{0:T(1024)} %get-tuple-element.108) | copy-start | bytes 12292
  484.4 39.8 %all-to-all-start.7 = ((bf16[32,32,896]{2,1,0:T(8,128)(2,1)}), bf16[32,32,896]{2,1,0:T(8,128)(2,1)S(1)}, u32[]{:S(2)}, u32[]{:S(2)}) async-start(bf16[32,32,896]{2,1,0:T(8,128)(2,1)} %fusion.4), calls=%async_computation.7 | async-start | bytes 3670016 | tf_op jit(solution)/shard_map/all_to_all | solution.py:778
  499.1 12.6 %collective-permute-start.12 = (bf16[128,512]{1,0:T(8,128)(2,1)}, bf16[128,512]{1,0:T(8,128)(2,1)S(1)}, u32[]{:S(2)}, u32[]{:S(2)}) collective-permute-start(bf16[128,512]{1,0:T(8,128)(2,1)} %get-tuple-element.134), channel_id=1, source_target_pairs={{0,1},{1,2},{2,3},{3,0},{4,5},{5,6},{6,7},{7,4},{8,9},{9,10},{10,1... | collective-permute-start | bytes 393224 | tf_op jit(solution)/shard_map/ppermute | solution.py:799
  499.1 13.9 %collective-permute-start.13 = (bf16[128,512]{1,0:T(8,128)(2,1)}, bf16[128,512]{1,0:T(8,128)(2,1)S(1)}, u32[]{:S(2)}, u32[]{:S(2)}) collective-permute-start(bf16[128,512]{1,0:T(8,128)(2,1)} %get-tuple-element.133), channel_id=1, source_target_pairs={{0,2},{1,3},{2,0},{3,1},{4,6},{5,7},{6,4},{7,5},{8,10},{9,11},{10,... | collective-permute-start | bytes 393224 | tf_op jit(solution)/shard_map/ppermute | solution.py:799
  500.3 15.6 %collective-permute-start.14 = (bf16[128,512]{1,0:T(8,128)(2,1)}, bf16[128,512]{1,0:T(8,128)(2,1)S(1)}, u32[]{:S(2)}, u32[]{:S(2)}) collective-permute-start(bf16[128,512]{1,0:T(8,128)(2,1)} %get-tuple-element.135), channel_id=1, source_target_pairs={{0,3},{1,0},{2,1},{3,2},{4,7},{5,4},{6,5},{7,6},{8,11},{9,8},{10,9... | collective-permute-start | bytes 393224 | tf_op jit(solution)/shard_map/ppermute | solution.py:799
  (52 other events, 360.3 us)
Sparse Core Ops, SparseCore 0:
  10.6 42.1 all-gather.12
  58.7 49.7 all-gather.8
  111.3 69.2 all-gather.10
  183.4 63.7 all-gather.14
  369.6 50.0 all-gather.16
  422.5 29.1 reduce-scatter.7
  454.8 29.7 reduce-scatter.3
  487.6 34.8 reduce-scatter.5

commit v8 on v7

--- a/solution.py
+++ b/solution.py
@@ -123,14 +123,14 @@
         [
             (
                 rows_of(kv, 4 * BLK),
-                lambda to: kv_s.at[pl.ds(to, BLK), pl.ds(0, 2 * LANES)],
+                lambda to: kv_s.at[pl.ds(to, BLK)],
                 sem.at[0],
             )
         ],
     )
-    kv_s[:, 2 * LANES :] = jnp.ones((total * BLK, LANES), BF16)
-    wait_all(kv_s.at[:, pl.ds(0, 2 * LANES)], sem.at[0])
+    wait_all(kv_s, sem.at[0])
     width = tile_blocks * BLK
+    ones = jnp.ones((width, LANES), BF16)
 
     def query_block(i, carry):
         block = own[i]
@@ -147,7 +147,7 @@
             probs = jnp.exp(scores)
             if masked:
                 probs = jnp.where(causal(probs.shape, start, block * BLK, True), probs, 0.0)
-            acc[...] += dot(probs.astype(BF16), kv_s[pl.ds(start, width), LANES:], NN)
+            acc[...] += dot(probs.astype(BF16), values_at(start), NN)
 
         def clear_tile(j, carry):
             tile(first_key(j), False)
@@ -160,6 +160,9 @@
             for h in range(4):
                 lse_ref[i // 2, h : h + 1, lanes] = log_sum[h * BLK : (h + 1) * BLK].T[:1]
 
+        def values_at(start):
+            return jnp.concatenate([kv_s[pl.ds(start, width), LANES:], ones], axis=1)
+
         def score(j):
             return dot(q_ref[...], kv_s[pl.ds(first_key(j), width), :LANES], NT)
 
@@ -168,7 +171,7 @@
             probs = jnp.exp(scores)
             if masked:
                 probs = jnp.where(causal(probs.shape, start, block * BLK, True), probs, 0.0)
-            acc[...] += dot(probs.astype(BF16), kv_s[pl.ds(start, width), LANES:], NN)
+            acc[...] += dot(probs.astype(BF16), values_at(start), NN)
 
         acc[...] = jnp.zeros_like(acc)
         count = n_a + n_b
@@ -216,7 +219,7 @@
                 probs = jnp.where(seen, jnp.exp(scores - new[:, :1]), 0.0)
                 keep = jnp.exp(old - new)
                 acc[...] = acc[...] * keep[:, :1] + dot(
-                    probs.astype(BF16), kv_s[pl.ds(start, width), LANES:], NN
+                    probs.astype(BF16), values_at(start), NN
                 )
                 peak[...] = new
                 return carry
@@ -396,7 +399,6 @@
     half,
     tile_blocks,
     q_rows,
-    do_rows,
     table,
     own,
     kv_in,
@@ -404,12 +406,12 @@
     sin_ref,
     q_all,
     do_all,
-    delta_all,
     p_ref,
     pc_ref,
     out_ref,
     q_s,
     do_s,
+    parts_s,
     delta_s,
     v_ref,
     dk_ref,
@@ -428,16 +430,32 @@
             total,
             [
                 (rows_of(q_all, q_rows), lambda to: q_s.at[pl.ds(to, BLK)], sem.at[0]),
-                (rows_of(do_all, do_rows), lambda to: do_s.at[pl.ds(to, BLK)], sem.at[1]),
-                (stats_of(delta_all), lambda to: delta_s.at[:, pl.ds(to, BLK)], sem.at[2]),
+                (
+                    lambda i: do_all.at[i // 4, pl.ds(pl.multiple_of(i % 4 * BLK, BLK), BLK)],
+                    lambda to: do_s.at[pl.ds(to, BLK)],
+                    sem.at[1],
+                ),
             ],
         )
+        stats = pltpu.make_async_copy(do_all.at[:, pl.ds(4 * BLK, 48)], parts_s, sem.at[2])
+        stats.start()
         dk_ref[...] = jnp.zeros_like(dk_ref)
         dv_ref[...] = jnp.zeros_like(dv_ref)
         spread_heads(kv_in, slice(LANES, 2 * LANES), v_ref)
         wait_all(q_s, sem.at[0])
         wait_all(do_s, sem.at[1])
-        wait_all(delta_s, sem.at[2])
+        stats.wait()
+
+        def place_stats(c, carry):
+            parts = parts_s[c].astype(F32)
+            sums = parts[:16] + parts[16:32] + parts[32:]
+            for blk in range(4):
+                to = pl.multiple_of(table[4 * c + blk] * BLK, BLK)
+                first, lane = blk // 2 * 8, blk % 2 * BLK
+                delta_s[:, pl.ds(to, BLK)] = sums[first : first + 8, lane : lane + BLK]
+            return carry
+
+        lax.fori_loop(0, total // 4, place_stats, 0)
 
     def prob_grad(first_row, per_head, j):
         start = pl.multiple_of(j * width, width)
@@ -543,6 +561,10 @@
     dx_ref[...] = total.astype(BF16)
 
 
+def in_hbm(values):
+    return pltpu.with_memory_space_constraint(values, pltpu.HBM)
+
+
 def block_of_whole(shape):
     return pl.BlockSpec(shape, lambda i, *_: (0,) * len(shape))
 
@@ -581,7 +603,7 @@
         compiler_params=pltpu.CompilerParams(vmem_limit_bytes=40 << 20),
         cost_estimate=pl.CostEstimate(flops=flops, bytes_accessed=10**7, transcendentals=0),
         name=name,
-    )(*(pltpu.with_memory_space_constraint(x, pltpu.HBM) for x in ins))
+    )(*(in_hbm(x) for x in ins))
 
 
 def expert_forward(rows_in, weights):
@@ -633,7 +655,7 @@
             jax.ShapeDtypeStruct((2, 4, 2 * BLK), F32),
         ],
         [
-            pltpu.VMEM((total * BLK, 3 * LANES), BF16),
+            pltpu.VMEM((total * BLK, 2 * LANES), BF16),
             pltpu.VMEM((4 * BLK, LANES), BF16),
             pltpu.VMEM((4 * BLK, 2 * LANES), F32),
             pltpu.VMEM((4 * BLK, LANES), F32),
@@ -725,20 +747,21 @@
     )
 
 
-def pair_grad(table, own, kv, cosine, sine, q_all, q_rows, do_all, do_rows, delta_all, probs):
+def pair_grad(table, own, kv, cosine, sine, q_all, q_rows, do_all, probs):
     total = table.shape[0]
     return pair_call(
-        functools.partial(pair_grad_kernel, total, total // 2, 4, q_rows, do_rows),
+        functools.partial(pair_grad_kernel, total, total // 2, 4, q_rows),
         "pair_grad",
         table,
         own,
-        [kv, cosine, sine, q_all, do_all, delta_all, *probs],
-        [kv.shape, cosine.shape, sine.shape, None, None, None, PROB_BLOCK, CONT_SHAPE],
+        [kv, cosine, sine, q_all, do_all, *(in_hbm(x) for x in probs)],
+        [kv.shape, cosine.shape, sine.shape, None, None, PROB_BLOCK, CONT_SHAPE],
         [jax.ShapeDtypeStruct((4 * BLK, 2 * LANES), F32)],
         [(4 * BLK, 2 * LANES)],
         [
             pltpu.VMEM((total * BLK, 2 * LANES), BF16),
             pltpu.VMEM((total * BLK, 2 * LANES), BF16),
+            pltpu.VMEM((total // 4, 48, 2 * LANES), BF16),
             pltpu.VMEM((8, total * BLK), F32),
             pltpu.VMEM((16 * BLK, 2 * LANES), BF16),
             pltpu.VMEM((16 * BLK, 2 * LANES), F32),
@@ -787,6 +810,14 @@
     for step in range(1, count):
         parts.append(lax.ppermute(values, axis, [(i, (i + step) % count) for i in range(count)]))
     return parts
+
+
+def sum_short(values, axis, count):
+    parts = shifted(values, axis, count)
+    while len(parts) > 1:
+        half = len(parts) // 2
+        parts = [parts[i] + parts[i + half] for i in range(half)]
+    return parts[0]
 
 
 def exchange_short(values, axis, index, count):
@@ -816,11 +847,6 @@
     stats = jnp.pad(stats, ((0, 0), (0, 4), (0, 0)))
     parts = jnp.stack(pieces(stats, 3), axis=0).reshape(-1, rows.shape[1])
     return jnp.concatenate([rows, parts], axis=0)
-
-
-def stats_in(gathered, first):
-    parts = gathered[:, first:].reshape(-1, 3, 2, 8, gathered.shape[2])
-    return jnp.sum(parts.astype(F32), axis=1)
 
 
 def ride_along(values):
@@ -890,10 +916,10 @@
     projected = dot(normed, full_qkv, NN)
     query_pre = projected[:, :head_cols]
     key_pre = projected[:, head_cols : head_cols + kv_cols]
-    query_square, key_square = lax.psum(
-        jnp.stack([jnp.sum(query_pre * query_pre, axis=1), jnp.sum(key_pre * key_pre, axis=1)]),
-        "exp",
-    )
+    squares = jnp.stack(
+        [jnp.sum(query_pre * query_pre, axis=1), jnp.sum(key_pre * key_pre, axis=1)]
+    )
+    query_square, key_square = sum_short(squares, "exp", exp_count)
     query_scale = lax.rsqrt(query_square / model_width + NORM_EPSILON)[:, None]
     key_scale = lax.rsqrt(key_square / kv_total + NORM_EPSILON)[:, None]
     query_hat = query_pre * query_scale
@@ -963,8 +989,8 @@
     expert_out, gate_pre, up_pre = expert_forward(expert_in, expert)
     returned = send(expert_out)
     turned = expert[:, :, : 2 * width].transpose(0, 2, 1)
-    returned, q_all, lse_all, later_qkv, turned = lax.optimization_barrier(
-        (returned, q_all, lse_all[:, :, :8], full_qkv, turned)
+    returned, q_all, later_qkv, turned = lax.optimization_barrier(
+        (returned, q_all, full_qkv, turned)
     )
     probs = pair_probs(
         block_of,
@@ -972,7 +998,7 @@
         own_kv,
         q_all,
         ctx_rows,
-        lse_all,
+        lse_all[:, :, :8],
     )
     wide_qkv = jnp.concatenate(shifted(later_qkv, "exp", exp_count), axis=1)
     moe_parts = dot(jnp.concatenate(pieces(weigh, 2), axis=1), returned, TN)
@@ -1050,9 +1076,7 @@
         sine,
         q_all,
         ctx_rows,
-        do_all.reshape(-1, head_cols),
-        do_all.shape[1],
-        stats_in(do_all, ctx_rows),
+        do_all,
         probs,
     )
     key_n_grad = pair_grads[:, :kv_cols]
@@ -1075,7 +1099,7 @@
             jnp.full((kv_total,), local_loss),
         ]
     )
-    stats = lax.psum(stats.reshape(-1, LANES), "exp").reshape(-1)
+    stats = sum_short(stats.reshape(-1, LANES), "exp", exp_count).reshape(-1)
     query_stat = stats[:ctx_rows, None] / model_width
     key_stat = stats[ctx_rows : 2 * ctx_rows, None] / kv_total
     sums = stats[2 * ctx_rows :]
@@ -1118,7 +1142,7 @@
     gain_part = jnp.sum(grad_w_query * w_query.astype(F32), axis=1)
     gain_part += jnp.sum(grad_w_key * w_key.astype(F32), axis=1)
     gain_part += jnp.sum(grad_w_value * w_value.astype(F32), axis=1)
-    grad_gain_attn = lax.psum(gain_part, "exp") / gain_attn.astype(F32)
+    grad_gain_attn = sum_short(gain_part, "exp", exp_count) / gain_attn.astype(F32)
     normed_rows = dot(back, wide_qkv, NT)
     own_scale = lax.dynamic_slice_in_dim(attn_scale, exp_index * own_rows, own_rows, 0)
     own_hat = hidden_rows * own_scale

time: 551 us -> 556 us (level)
  blocking collectives: 51.9 us -> 16.5 us
  waiting for transfers between devices: 155 us -> 180 us
  starting transfers between devices: 67.5 us -> 90.5 us
    psum x3 -> x0, blocking collectives: 35.8 us -> none  [the longest x1 17.3 us: on_device(): stats = lax.psum(stats.reshape(-1, LANES), 'exp').reshape(-1)]
    all_to_all x7, waiting for transfers between devices: 59.9 us -> 78.3 us  [exchange(): return lax.all_to_all(values, axis, split_axis=0, concat_axis=0, tiled=True)]
    ppermute x9 -> x18, starting transfers between devices: 12.8 us -> 31 us  [shifted(): lax.ppermute(values, axis, [(i, (i + step) % count) for i in range(count)])]
    pallas_call x3, Pallas kernels: 69.8 us -> 57.5 us  [kernel_call(): pl.pallas_call(kernel, out_shape=tuple(outs), grid_spec=pltpu.PrefetchSca...]
    pallas_call x2, Pallas kernels: 55.5 us -> 65.6 us  [pair_call(): pl.pallas_call(kernel, out_shape=tuple((out if out.dtype == F32 else pltp...]
    all_gather x1, waiting for transfers between devices: 3.14 us -> 11.8 us  [on_device(): lax.all_gather(with_stats(out_grad, delta), 'ctx', axis=0, tiled=False)]
    ppermute x6, waiting for transfers between devices: 16.5 us -> 9.11 us  [exchange_short(): lax.ppermute(part, axis, [(i, (i + step) % count) for i in range(count)])]
    ppermute x9 -> x18, waiting for transfers between devices: 23.3 us -> 25.3 us  [shifted(): lax.ppermute(values, axis, [(i, (i + step) % count) for i in range(count)])]
  transfers between devices with their start and end apart: 30 -> 39, of which waited for: 17 -> 20; matrix products, arithmetic and copies ran while one was open for 15% -> 16% of each run, Pallas kernels for 27% -> 25%
where the time goes in v8:
time: 556 us; the launch traced here: 549 us
  waiting for transfers between devices  180 us (32%)
  Pallas kernels  145 us (26%)
  starting transfers between devices  90.5 us (16%)
  matrix products  39.8 us (7%)
  other arithmetic  30.8 us (6%)
  local copies, waits for them, and re-layouts  27.2 us (5%)
  between operations  18.9 us (3%)
  blocking collectives  16.5 us (3%)
    all_to_all x7, waiting for transfers between devices, exchange(): return lax.all_to_all(values, axis, split_axis=0, concat_axis=0, tiled=True)  78.3 us
    pallas_call x2, Pallas kernels, pair_call(): pl.pallas_call(kernel, out_shape=tuple((out if out.dtype == F32 else pltp...  65.6 us
    pallas_call x3, Pallas kernels, kernel_call(): pl.pallas_call(kernel, out_shape=tuple(outs), grid_spec=pltpu.PrefetchSca...  57.5 us
    all_to_all x7, starting transfers between devices, exchange(): return lax.all_to_all(values, axis, split_axis=0, concat_axis=0, tiled=True)  48.5 us
    dot_general x16, matrix products, dot(): return lax.dot_general(left, right, dims, preferred_element_type=F32)  38 us
    ppermute x18, starting transfers between devices, shifted(): lax.ppermute(values, axis, [(i, (i + step) % count) for i in range(count)])  31 us
    all_gather x1, waiting for transfers between devices, on_device(): q_all = lax.all_gather(later_q, 'ctx', axis=0, tiled=True)  28.8 us
    ppermute x18, waiting for transfers between devices, shifted(): lax.ppermute(values, axis, [(i, (i + step) % count) for i in range(count)])  25.3 us
  transfers between devices with their start and end apart: 39, of which 20 were waited for; matrix products, arithmetic and copies ran while one was open for 16% of the time, Pallas kernels for 25%

profile of v8, /device:TPU:0, one launch (start us, length us, event | category | flops | bytes accessed | tf_op | source)
XLA Modules:
  0.0 548.8 jit_solution(1719517885652005877)
XLA Ops:
  11.9 8.4 %all-to-all-start = ((bf16[32,40,512]{2,1,0:T(8,128)(2,1)}), bf16[32,40,512]{2,1,0:T(8,128)(2,1)S(1)}, u32[]{:S(2)}, u32[]{:S(2)}) async-start(bf16[32,40,512]{2,1,0:T(8,128)(2,1)} %broadcast_in_dim.56), calls=%async_computation | async-start | bytes 2621440 | tf_op jit(solution)/shard_map/all_to_all | solution.py:801
  22.3 18.8 %all-to-all-done = bf16[32,40,512]{2,1,0:T(8,128)(2,1)S(1)} async-done(((bf16[32,40,512]{2,1,0:T(8,128)(2,1)}), bf16[32,40,512]{2,1,0:T(8,128)(2,1)S(1)}, u32[]{:S(2)}, u32[]{:S(2)}) %all-to-all-start) | async-done | bytes 1310752 | tf_op jit(solution)/shard_map/all_to_all | solution.py:801
  55.3 16.5 %all_to_all.40 = bf16[32,32,256]{2,1,0:T(8,128)(2,1)S(1)} all-to-all(bf16[32,32,256]{2,1,0:T(8,128)(2,1)S(1)} %broadcast_in_dim.58), channel_id=1, replica_groups=mesh['ctx'=32,'exp'=4] {'ctx'}, dimensions={0} | all-to-all | bytes 1048576 | tf_op jit(solution)/shard_map/all_to_all | solution.py:801
  76.8 21.3 %collective-permute-done.3 = bf16[1024,256]{1,0:T(8,128)(2,1)S(1)} collective-permute-done((bf16[1024,256]{1,0:T(8,128)(2,1)S(1)}, bf16[1024,256]{1,0:T(8,128)(2,1)S(1)}, u32[]{:S(2)}, u32[]{:S(2)}) %collective-permute-start.3) | collective-permute-done | bytes 524320 | tf_op jit(solution)/shard_map/ppermute | solution.py:811
  108.9 22.3 %attend.1 = (f32[512,256]{1,0:T(8,128)S(1)}, f32[2,4,256]{2,1,0:T(4,128)S(1)}) custom-call(s32[128]{0:T(128)S(1)} %copy-done, s32[4]{0:T(128)S(1)} %get-tuple-element.121.own, bf16[512,256]{1,0:T(8,128)(2,1)} %get-tuple-element.68.q_in, bf16[16384,256]{1,0:T(8,128)(2,1)} %all-gather.9.cloned.1.call-done.kv), custom_call_target="tpu_custom_call" | custom-call | flops 20000000000 | bytes 8650752 | tf_op jit(solution)/shard_map/attend/pallas_call | solution.py:575
  145.4 9.1 %all-to-all-start.2 = ((bf16[32,40,1024]{2,1,0:T(8,128)(2,1)}), bf16[32,40,1024]{2,1,0:T(8,128)(2,1)}, u32[]{:S(2)}, u32[]{:S(2)}) async-start(bf16[32,40,1024]{2,1,0:T(8,128)(2,1)} %bitcast.115), calls=%async_computation.2 | async-start | bytes 5242880 | tf_op jit(solution)/shard_map/all_to_all | solution.py:801
  154.5 28.8 %all-gather.11.cloned.1.call-done.q_all = bf16[16384,256]{1,0:T(8,128)(2,1)} async-done(((bf16[512,256]{1,0:T(8,128)(2,1)}), bf16[16384,256]{1,0:T(8,128)(2,1)}) %all-gather.11.cloned.1.call-update) | async-done | bytes 8388624 | tf_op jit(solution)/shard_map/all_gather | solution.py:950
  183.3 10.3 %all-to-all-done.2 = bf16[32,40,1024]{2,1,0:T(8,128)(2,1)} async-done(((bf16[32,40,1024]{2,1,0:T(8,128)(2,1)}), bf16[32,40,1024]{2,1,0:T(8,128)(2,1)}, u32[]{:S(2)}, u32[]{:S(2)}) %all-to-all-start.2) | async-done | bytes 2621472 | tf_op jit(solution)/shard_map/all_to_all | solution.py:801
  193.7 8.6 %expert.1 = (bf16[1280,1024]{1,0:T(8,128)(2,1)}, f32[1280,512]{1,0:T(8,128)}, f32[1280,512]{1,0:T(8,128)}) custom-call(bf16[1280,1024]{1,0:T(8,128)(2,1)} %bitcast.21.x_ref, bf16[4,1024,384]{2,1,0:T(8,128)(2,1)} %bitcast.127), custom_call_target="tpu_custom_call" | custom-call | flops 4026531840 | bytes 10000000 | tf_op jit(solution)/shard_map/expert/pallas_call | solution.py:597
  202.3 4.9 all-to-all-start.3
  210.0 4.7 copy.98
  220.3 23.8 %all-to-all-done.3 = bf16[32,40,1024]{2,1,0:T(8,128)(2,1)} async-done(((bf16[32,40,1024]{2,1,0:T(8,128)(2,1)}), bf16[32,40,1024]{2,1,0:T(8,128)(2,1)}, u32[]{:S(2)}, u32[]{:S(2)}) %all-to-all-start.3) | async-done | bytes 2621472 | tf_op jit(solution)/shard_map/all_to_all | solution.py:801
  250.3 4.8 all-to-all-start.4
  255.1 24.1 %all-gather.15.cloned.1.call-done = f32[64,32,256]{2,1,0:T(8,128)} async-done(((f32[2,32,256]{2,1,0:T(8,128)}), f32[64,32,256]{2,1,0:T(8,128)}) %all-gather.15.cloned.1.call-update) | async-done | bytes 2097168 | tf_op jit(solution)/shard_map/all_gather | solution.py:973
  285.5 24.8 %pair_probs.1 = (bf16[16,1024,1024]{2,1,0:T(8,128)(2,1)}, bf16[2,2,512,512]{3,2,1,0:T(8,128)(2,1)}) custom-call(s32[128]{0:T(128)S(1)} %copy-done, s32[4]{0:T(128)S(1)} %get-tuple-element.121.own, bf16[512,256]{1,0:T(8,128)(2,1)} %get-tuple-element.60.kv_in, bf16[16384,256]{1,0:T(8,128)(2,1)} %all-gather.11.cloned.1.call-done.q_all, ...), custom_call_target="tpu_custom_call" | custom-call | flops 20000000000 | bytes 40000000 | tf_op jit(solution)/shard_map/pair_probs/pallas_call | solution.py:704
  310.4 12.9 %expert_grad.1 = (bf16[1280,1024]{1,0:T(8,128)(2,1)}, bf16[1280,512]{1,0:T(8,128)(2,1)}, bf16[1280,512]{1,0:T(8,128)(2,1)}, bf16[1280,512]{1,0:T(8,128)(2,1)}) custom-call(bf16[1280,1024]{1,0:T(8,128)(2,1)} %bitcast.27.dy_ref, f32[1280,512]{1,0:T(8,128)} %get-tuple-element.81.gate_ref, f32[1280,512]{1,0:T(8,128)} %get-tuple-element.82.up_ref, ...), custom_call_target="tpu_custom_call" | custom-call | flops 4026531840 | bytes 10000000 | tf_op jit(solution)/shard_map/expert_grad/pallas_call | solution.py:597
  323.2 9.7 %all-to-all-start.5 = ((bf16[32,40,1024]{2,1,0:T(8,128)(2,1)}), bf16[32,40,1024]{2,1,0:T(8,128)(2,1)}, u32[]{:S(2)}, u32[]{:S(2)}) async-start(bf16[32,40,1024]{2,1,0:T(8,128)(2,1)} %bitcast.131), calls=%async_computation.5 | async-start | bytes 5242880 | tf_op jit(solution)/shard_map/all_to_all | solution.py:801
  332.9 3.9 pad_maximum_fusion
  336.8 4.7 fusion.103
  344.4 5.0 fusion.102
  352.3 5.0 fusion.104
  357.3 11.6 %all-to-all-done.5 = bf16[32,40,1024]{2,1,0:T(8,128)(2,1)} async-done(((bf16[32,40,1024]{2,1,0:T(8,128)(2,1)}), bf16[32,40,1024]{2,1,0:T(8,128)(2,1)}, u32[]{:S(2)}, u32[]{:S(2)}) %all-to-all-start.5) | async-done | bytes 2621472 | tf_op jit(solution)/shard_map/all_to_all | solution.py:801
  375.3 3.6 all-to-all-start.6
  379.0 6.7 %all-to-all-done.6 = bf16[4,128,256]{1,2,0:T(8,128)(2,1)S(1)} async-done(((bf16[4,128,256]{1,2,0:T(8,128)(2,1)}), bf16[4,128,256]{1,2,0:T(8,128)(2,1)S(1)}, u32[]{:S(2)}, u32[]{:S(2)}) %all-to-all-start.6) | async-done | bytes 262176 | tf_op jit(solution)/shard_map/all_to_all | solution.py:801
  390.7 33.7 %query_grad.1 = f32[512,256]{1,0:T(8,128)S(1)} custom-call(s32[128]{0:T(128)S(1)} %copy-done, s32[4]{0:T(128)S(1)} %get-tuple-element.121.own, bf16[512,256]{1,0:T(8,128)(2,1)} %get-tuple-element.68.q_in, bf16[512,256]{1,0:T(8,128)(2,1)S(1)} %bitcast.114, f32[512,256]{1,0:T(8,128)S(1)} %get-tuple-element.64.o_in, f32[2,4,256]{2,1,0:T(4,128)S(1)} %get-tuple-element.77.lse_in, ...), custom_call_target="tpu_custom_call" | custom-call | flops 30000001024 | bytes 9969664 | tf_op jit(solution)/shard_map/query_grad/pallas_call | solution.py:575
  425.4 11.8 %all-gather.17.cloned.1.call-done = bf16[17920,256]{1,0:T(8,128)(2,1)} async-done(((bf16[560,256]{1,0:T(8,128)(2,1)}), bf16[17920,256]{1,0:T(8,128)(2,1)}) %all-gather.17.cloned.1.call-update) | async-done | bytes 9175056 | tf_op jit(solution)/shard_map/all_gather | solution.py:1053
  438.9 40.8 %pair_grad.1 = f32[512,256]{1,0:T(8,128)S(1)} custom-call(s32[128]{0:T(128)S(1)} %copy-done, s32[4]{0:T(128)S(1)} %get-tuple-element.121.own, bf16[512,256]{1,0:T(8,128)(2,1)} %get-tuple-element.60.kv_in, f32[512,128]{1,0:T(8,128)S(1)} %get-tuple-element.165.cos_ref, f32[512,128]{1,0:T(8,128)S(1)} %get-tuple-element.166.sin_ref, ...), custom_call_target="tpu_custom_call" | custom-call | flops 30000001024 | bytes 40000000 | tf_op jit(solution)/shard_map/pair_grad/pallas_call | solution.py:704
  495.6 8.0 %all-to-all-start.7 = ((bf16[32,32,896]{2,1,0:T(8,128)(2,1)}), bf16[32,32,896]{2,1,0:T(8,128)(2,1)S(1)}, u32[]{:S(2)}, u32[]{:S(2)}) async-start(bf16[32,32,896]{2,1,0:T(8,128)(2,1)} %fusion.4), calls=%async_computation.7 | async-start | bytes 3670016 | tf_op jit(solution)/shard_map/all_to_all | solution.py:801
  505.4 4.6 collective-permute-start.19
  512.7 4.0 collective-permute-done.19
  518.0 4.1 fusion.20
  523.2 7.2 %all-to-all-done.7 = bf16[32,32,896]{2,1,0:T(8,128)(2,1)S(1)} async-done(((bf16[32,32,896]{2,1,0:T(8,128)(2,1)}), bf16[32,32,896]{2,1,0:T(8,128)(2,1)S(1)}, u32[]{:S(2)}, u32[]{:S(2)}) %all-to-all-start.7) | async-done | bytes 1835040 | tf_op jit(solution)/shard_map/all_to_all | solution.py:801
  (295 shorter events, 121.4 us)
Async XLA Ops:
  7.3 47.9 %all-gather.13.cloned.1.call-start = ((), (), s32[]{:S(2)}) async-start(), calls=%async_computation.16 | async-start | bytes 3932160 | tf_op jit(solution)/shard_map/all_gather | solution.py:910
  11.9 29.2 %all-to-all-start = ((bf16[32,40,512]{2,1,0:T(8,128)(2,1)}), bf16[32,40,512]{2,1,0:T(8,128)(2,1)S(1)}, u32[]{:S(2)}, u32[]{:S(2)}) async-start(bf16[32,40,512]{2,1,0:T(8,128)(2,1)} %broadcast_in_dim.56), calls=%async_computation | async-start | bytes 2621440 | tf_op jit(solution)/shard_map/all_to_all | solution.py:801
  20.3 88.7 %all-gather.9.cloned.1.call-start = ((), (), s32[]{:S(2)}) async-start(), calls=%async_computation.11 | async-start | bytes 8650752 | tf_op jit(solution)/shard_map/all_gather | solution.py:942
  44.8 6.9 %collective-permute-start = (f32[2,512]{1,0:T(2,128)S(1)}, f32[2,512]{1,0:T(2,128)S(1)}, u32[]{:S(2)}, u32[]{:S(2)}) collective-permute-start(f32[2,512]{1,0:T(2,128)S(1)} %pad_maximum_fusion.11), channel_id=1, source_target_pairs={{0,2},{1,3},{2,0},{3,1},{4,6},{5,7},{6,4},{7,5},{8,10},{9,11},{10,... | collective-permute-start | bytes 12296 | tf_op jit(solution)/shard_map/ppermute | solution.py:811
  55.2 128.1 %all-gather.11.cloned.1.call-start = ((), (), s32[]{:S(2)}) async-start(), calls=%async_computation.12 | async-start | bytes 8650752 | tf_op jit(solution)/shard_map/all_gather | solution.py:950
  71.8 26.3 %collective-permute-start.3 = (bf16[1024,256]{1,0:T(8,128)(2,1)S(1)}, bf16[1024,256]{1,0:T(8,128)(2,1)S(1)}, u32[]{:S(2)}, u32[]{:S(2)}) collective-permute-start(bf16[1024,256]{1,0:T(8,128)(2,1)S(1)} %bitcast.118), channel_id=1, source_target_pairs={{0,1},{1,2},{2,3},{3,0},{4,5},{5,6},{6,7},{7,4},{8,9},{9,10},{10,1... | collective-permute-start | bytes 1572872 | tf_op jit(solution)/shard_map/ppermute | solution.py:811
  72.5 25.7 %collective-permute-start.4 = (bf16[1024,256]{1,0:T(8,128)(2,1)S(1)}, bf16[1024,256]{1,0:T(8,128)(2,1)S(1)}, u32[]{:S(2)}, u32[]{:S(2)}) collective-permute-start(bf16[1024,256]{1,0:T(8,128)(2,1)S(1)} %bitcast.119), channel_id=1, source_target_pairs={{0,2},{1,3},{2,0},{3,1},{4,6},{5,7},{6,4},{7,5},{8,10},{9,11},{10,... | collective-permute-start | bytes 1572872 | tf_op jit(solution)/shard_map/ppermute | solution.py:811
  74.8 24.1 %collective-permute-start.5 = (bf16[1024,256]{1,0:T(8,128)(2,1)S(1)}, bf16[1024,256]{1,0:T(8,128)(2,1)}, u32[]{:S(2)}, u32[]{:S(2)}) collective-permute-start(bf16[1024,256]{1,0:T(8,128)(2,1)S(1)} %bitcast.120), channel_id=1, source_target_pairs={{0,3},{1,0},{2,1},{3,2},{4,7},{5,4},{6,5},{7,6},{8,11},{9,8},{10,9... | collective-permute-start | bytes 1572872 | tf_op jit(solution)/shard_map/ppermute | solution.py:811
  131.3 5.8 %collective-permute-start.6 = (bf16[128,256]{1,0:T(8,128)(2,1)S(1)}, bf16[128,256]{1,0:T(8,128)(2,1)S(1)}, u32[]{:S(2)}, u32[]{:S(2)}) collective-permute-start(bf16[128,256]{1,0:T(8,128)(2,1)S(1)} %get-tuple-element.137), channel_id=1, source_target_pairs={{0,1},{1,2},{2,3},{3,0},{4,5},{5,6},{6,7},{7,4},{8,9},{9,10},{10,1... | collective-permute-start | bytes 196616 | tf_op jit(solution)/shard_map/ppermute | solution.py:830
  145.4 48.2 %all-to-all-start.2 = ((bf16[32,40,1024]{2,1,0:T(8,128)(2,1)}), bf16[32,40,1024]{2,1,0:T(8,128)(2,1)}, u32[]{:S(2)}, u32[]{:S(2)}) async-start(bf16[32,40,1024]{2,1,0:T(8,128)(2,1)} %bitcast.115), calls=%async_computation.2 | async-start | bytes 5242880 | tf_op jit(solution)/shard_map/all_to_all | solution.py:801
  202.3 41.8 %all-to-all-start.3 = ((bf16[32,40,1024]{2,1,0:T(8,128)(2,1)}), bf16[32,40,1024]{2,1,0:T(8,128)(2,1)}, u32[]{:S(2)}, u32[]{:S(2)}) async-start(bf16[32,40,1024]{2,1,0:T(8,128)(2,1)} %bitcast.130), calls=%async_computation.3 | async-start | bytes 5242880 | tf_op jit(solution)/shard_map/all_to_all | solution.py:801
  207.2 72.1 %all-gather.15.cloned.1.call-start = ((), (), s32[]{:S(2)}) async-start(), calls=%async_computation.17 | async-start | bytes 2162688 | tf_op jit(solution)/shard_map/all_gather | solution.py:973
  250.3 60.0 %all-to-all-start.4 = ((bf16[32,40,1024]{2,1,0:T(8,128)(2,1)}), bf16[32,40,1024]{2,1,0:T(8,128)(2,1)}, u32[]{:S(2)}, u32[]{:S(2)}) async-start(bf16[32,40,1024]{2,1,0:T(8,128)(2,1)} %bitcast.132), calls=%async_computation.4 | async-start | bytes 5242880 | tf_op jit(solution)/shard_map/all_to_all | solution.py:801
  280.4 52.5 %collective-permute-start.10 = (bf16[1024,512]{1,0:T(8,128)(2,1)}, bf16[1024,512]{1,0:T(8,128)(2,1)}, u32[]{:S(2)}, u32[]{:S(2)}) collective-permute-start(bf16[1024,512]{1,0:T(8,128)(2,1)} %bitcast.123), channel_id=1, source_target_pairs={{0,2},{1,3},{2,0},{3,1},{4,6},{5,7},{6,4},{7,5},{8,10},{9,11},{10,... | collective-permute-start | bytes 3145736 | tf_op jit(solution)/shard_map/ppermute | solution.py:811
  283.5 49.4 %collective-permute-start.11 = (bf16[1024,512]{1,0:T(8,128)(2,1)}, bf16[1024,512]{1,0:T(8,128)(2,1)}, u32[]{:S(2)}, u32[]{:S(2)}) collective-permute-start(bf16[1024,512]{1,0:T(8,128)(2,1)} %bitcast.124), channel_id=1, source_target_pairs={{0,3},{1,0},{2,1},{3,2},{4,7},{5,4},{6,5},{7,6},{8,11},{9,8},{10,9... | collective-permute-start | bytes 3145736 | tf_op jit(solution)/shard_map/ppermute | solution.py:811
  283.5 49.5 %collective-permute-start.9 = (bf16[1024,512]{1,0:T(8,128)(2,1)}, bf16[1024,512]{1,0:T(8,128)(2,1)}, u32[]{:S(2)}, u32[]{:S(2)}) collective-permute-start(bf16[1024,512]{1,0:T(8,128)(2,1)} %bitcast.125), channel_id=1, source_target_pairs={{0,1},{1,2},{2,3},{3,0},{4,5},{5,6},{6,7},{7,4},{8,9},{9,10},{10,1... | collective-permute-start | bytes 3145736 | tf_op jit(solution)/shard_map/ppermute | solution.py:811
  323.2 45.7 %all-to-all-start.5 = ((bf16[32,40,1024]{2,1,0:T(8,128)(2,1)}), bf16[32,40,1024]{2,1,0:T(8,128)(2,1)}, u32[]{:S(2)}, u32[]{:S(2)}) async-start(bf16[32,40,1024]{2,1,0:T(8,128)(2,1)} %bitcast.131), calls=%async_computation.5 | async-start | bytes 5242880 | tf_op jit(solution)/shard_map/all_to_all | solution.py:801
  375.3 10.3 %all-to-all-start.6 = ((bf16[4,128,256]{1,2,0:T(8,128)(2,1)}), bf16[4,128,256]{1,2,0:T(8,128)(2,1)S(1)}, u32[]{:S(2)}, u32[]{:S(2)}) async-start(bf16[4,128,256]{1,2,0:T(8,128)(2,1)} %fusion.6), calls=%async_computation.6 | async-start | bytes 524288 | tf_op jit(solution)/shard_map/all_to_all | solution.py:801
  379.0 58.3 %all-gather.17.cloned.1.call-start = ((), (), s32[]{:S(2)}) async-start(), calls=%async_computation.18 | async-start | bytes 9461760 | tf_op jit(solution)/shard_map/all_gather | solution.py:1053
  387.0 153.4 %reduce-scatter.8.cloned.1.call-start = ((), (), s32[]{:S(2)}) async-start(), calls=%async_computation.15 | async-start | bytes 2621440 | tf_op jit(solution)/shard_map/reduce_scatter | solution.py:1069
  387.1 37.4 %collective-permute-start.12 = (bf16[128,1024]{1,0:T(8,128)(2,1)S(1)}, bf16[128,1024]{1,0:T(8,128)(2,1)S(1)}, u32[]{:S(2)}, u32[]{:S(2)}) collective-permute-start(bf16[128,1024]{1,0:T(8,128)(2,1)S(1)} %get-tuple-element.118), channel_id=1, source_target_pairs={{0,1},{1,2},{2,3},{3,0},{4,5},{5,6},{6,7},{7,4},{8,9},{9,10},{10,1... | collective-permute-start | bytes 786440 | tf_op jit(solution)/shard_map/ppermute | solution.py:811
  387.7 37.1 %collective-permute-start.14 = (bf16[128,1024]{1,0:T(8,128)(2,1)S(1)}, bf16[128,1024]{1,0:T(8,128)(2,1)S(1)}, u32[]{:S(2)}, u32[]{:S(2)}) collective-permute-start(bf16[128,1024]{1,0:T(8,128)(2,1)S(1)} %get-tuple-element.118), channel_id=1, source_target_pairs={{0,3},{1,0},{2,1},{3,2},{4,7},{5,4},{6,5},{7,6},{8,11},{9,8},{10,9... | collective-permute-start | bytes 786440 | tf_op jit(solution)/shard_map/ppermute | solution.py:811
  390.4 34.7 %collective-permute-start.13 = (bf16[128,1024]{1,0:T(8,128)(2,1)S(1)}, bf16[128,1024]{1,0:T(8,128)(2,1)S(1)}, u32[]{:S(2)}, u32[]{:S(2)}) collective-permute-start(bf16[128,1024]{1,0:T(8,128)(2,1)S(1)} %get-tuple-element.118), channel_id=1, source_target_pairs={{0,2},{1,3},{2,0},{3,1},{4,6},{5,7},{6,4},{7,5},{8,10},{9,11},{10,... | collective-permute-start | bytes 786440 | tf_op jit(solution)/shard_map/ppermute | solution.py:811
  437.3 103.0 %reduce-scatter.4.cloned.1.call-start = ((), (), s32[]{:S(2)}) async-start(), calls=%async_computation.13 | async-start | bytes 2621440 | tf_op jit(solution)/shard_map/reduce_scatter | solution.py:1067
  438.1 102.3 %reduce-scatter.6.cloned.1.call-start = ((), (), s32[]{:S(2)}) async-start(), calls=%async_computation.14 | async-start | bytes 2621440 | tf_op jit(solution)/shard_map/reduce_scatter | solution.py:1068
  480.9 6.4 %collective-permute-start.15 = (f32[32,128]{1,0:T(8,128)S(1)}, f32[32,128]{1,0:T(8,128)S(1)}, u32[]{:S(2)}, u32[]{:S(2)}) collective-permute-start(f32[32,128]{1,0:T(8,128)S(1)} %bitcast.158), channel_id=1, source_target_pairs={{0,2},{1,3},{2,0},{3,1},{4,6},{5,7},{6,4},{7,5},{8,10},{9,11},{10,... | collective-permute-start | bytes 49160 | tf_op jit(solution)/shard_map/ppermute | solution.py:811
  495.6 34.9 %all-to-all-start.7 = ((bf16[32,32,896]{2,1,0:T(8,128)(2,1)}), bf16[32,32,896]{2,1,0:T(8,128)(2,1)S(1)}, u32[]{:S(2)}, u32[]{:S(2)}) async-start(bf16[32,32,896]{2,1,0:T(8,128)(2,1)} %fusion.4), calls=%async_computation.7 | async-start | bytes 3670016 | tf_op jit(solution)/shard_map/all_to_all | solution.py:801
  505.4 7.3 %collective-permute-start.18 = (bf16[128,512]{1,0:T(8,128)(2,1)}, bf16[128,512]{1,0:T(8,128)(2,1)S(1)}, u32[]{:S(2)}, u32[]{:S(2)}) collective-permute-start(bf16[128,512]{1,0:T(8,128)(2,1)} %get-tuple-element.132), channel_id=1, source_target_pairs={{0,1},{1,2},{2,3},{3,0},{4,5},{5,6},{6,7},{7,4},{8,9},{9,10},{10,1... | collective-permute-start | bytes 393224 | tf_op jit(solution)/shard_map/ppermute | solution.py:830
  505.4 11.3 %collective-permute-start.19 = (bf16[128,512]{1,0:T(8,128)(2,1)}, bf16[128,512]{1,0:T(8,128)(2,1)S(1)}, u32[]{:S(2)}, u32[]{:S(2)}) collective-permute-start(bf16[128,512]{1,0:T(8,128)(2,1)} %get-tuple-element.131), channel_id=1, source_target_pairs={{0,2},{1,3},{2,0},{3,1},{4,6},{5,7},{6,4},{7,5},{8,10},{9,11},{10,... | collective-permute-start | bytes 393224 | tf_op jit(solution)/shard_map/ppermute | solution.py:830
  510.0 7.2 %collective-permute-start.20 = (bf16[128,512]{1,0:T(8,128)(2,1)}, bf16[128,512]{1,0:T(8,128)(2,1)S(1)}, u32[]{:S(2)}, u32[]{:S(2)}) collective-permute-start(bf16[128,512]{1,0:T(8,128)(2,1)} %get-tuple-element.133), channel_id=1, source_target_pairs={{0,3},{1,0},{2,1},{3,2},{4,7},{5,4},{6,5},{7,6},{8,11},{9,8},{10,9... | collective-permute-start | bytes 393224 | tf_op jit(solution)/shard_map/ppermute | solution.py:830
  532.2 7.5 %collective-permute-start.21 = (f32[32]{0:T(128)S(1)}, f32[32]{0:T(128)S(1)}, u32[]{:S(2)}, u32[]{:S(2)}) collective-permute-start(f32[32]{0:T(128)S(1)} %add_add_fusion.2), channel_id=1, source_target_pairs={{0,2},{1,3},{2,0},{3,1},{4,6},{5,7},{6,4},{7,5},{8,10},{9,11},{10,... | collective-permute-start | bytes 392 | tf_op jit(solution)/shard_map/ppermute | solution.py:811
  533.7 6.0 %collective-permute-start.22 = (f32[32]{0:T(128)S(1)}, f32[32]{0:T(128)S(1)}, u32[]{:S(2)}, u32[]{:S(2)}) collective-permute-start(f32[32]{0:T(128)S(1)} %add_add_fusion.2), channel_id=1, source_target_pairs={{0,1},{1,2},{2,3},{3,0},{4,5},{5,6},{6,7},{7,4},{8,9},{9,10},{10,1... | collective-permute-start | bytes 392 | tf_op jit(solution)/shard_map/ppermute | solution.py:811
  (56 other events, 578.6 us)
Sparse Core Ops, SparseCore 0:
  10.6 42.2 all-gather.12
  55.7 53.1 all-gather.8
  111.8 71.5 all-gather.10
  210.6 68.6 all-gather.14
  387.1 50.1 all-gather.16
  440.1 29.1 reduce-scatter.7
  472.4 30.0 reduce-scatter.3
  505.5 29.0 reduce-scatter.5

commit v9 on v8

--- a/solution.py
+++ b/solution.py
@@ -267,11 +267,13 @@
         rows = pl.ds(pl.multiple_of(i * BLK, BLK), BLK)
         lanes = pl.ds(pl.multiple_of(i % 2 * BLK, BLK), BLK)
         rows_by_head(q_in, rows, q_ref)
-        rows_by_head(do_in, rows, do_ref)
+        do_block = (i + 4 - own[4]) % 4
+        do_rows = pl.ds(pl.multiple_of(do_block * BLK, BLK), BLK)
+        rows_by_head(do_in, do_rows, do_ref)
         for h in range(4):
             part = slice(h * BLK, (h + 1) * BLK)
             pair = slice(h // 2 * LANES, (h // 2 + 1) * LANES)
-            product = do_in[rows, pair].astype(F32) * o_in[rows, pair]
+            product = do_in[do_rows, pair].astype(F32) * o_in[rows, pair]
             own_half = to_half(product, h % 2, h % 2)
             delta = jnp.sum(own_half, axis=1, keepdims=True)
             delta_ref[part, :] = jnp.broadcast_to(delta, (BLK, LANES))
@@ -431,7 +433,9 @@
             [
                 (rows_of(q_all, q_rows), lambda to: q_s.at[pl.ds(to, BLK)], sem.at[0]),
                 (
-                    lambda i: do_all.at[i // 4, pl.ds(pl.multiple_of(i % 4 * BLK, BLK), BLK)],
+                    lambda i: do_all.at[
+                        i // 4, pl.ds(pl.multiple_of((i + 4 - own[4]) % 4 * BLK, BLK), BLK)
+                    ],
                     lambda to: do_s.at[pl.ds(to, BLK)],
                     sem.at[1],
                 ),
@@ -450,7 +454,7 @@
             parts = parts_s[c].astype(F32)
             sums = parts[:16] + parts[16:32] + parts[32:]
             for blk in range(4):
-                to = pl.multiple_of(table[4 * c + blk] * BLK, BLK)
+                to = pl.multiple_of(table[4 * c + (blk + own[4]) % 4] * BLK, BLK)
                 first, lane = blk // 2 * 8, blk % 2 * BLK
                 delta_s[:, pl.ds(to, BLK)] = sums[first : first + 8, lane : lane + BLK]
             return carry
@@ -830,17 +834,6 @@
             part = lax.ppermute(part, axis, [(i, (i + step) % count) for i in range(count)])
         come.append(part)
     return jnp.concatenate(come, axis=1)
-
-
-def in_order(parts, index, count):
-    ordered = []
-    for place in range(count):
-        back = (index - place) % count
-        part = parts[0]
-        for step in range(1, count):
-            part = jnp.where(back == step, parts[step], part)
-        ordered.append(part)
-    return jnp.stack(ordered, axis=0)
 
 
 def with_stats(rows, stats):
@@ -925,6 +918,7 @@
     query_hat = query_pre * query_scale
     key_hat = key_pre * key_scale
     own_blocks = lax.dynamic_slice_in_dim(block_of, ctx_index * 4, 4)
+    own = jnp.concatenate([own_blocks, jnp.full((1,), exp_index, jnp.int32)])
     token_ids = (own_blocks[:, None] * BLK + jnp.arange(BLK, dtype=jnp.int32)[None]).reshape(-1)
     prompt_len = token_total // 2
     position = jnp.where(
@@ -945,8 +939,7 @@
         spread(own_out, "ctx", ctx_count).reshape(model_width, head_cols), "exp", exp_count
     )
     wide_out = jnp.concatenate(out_parts, axis=1)
-    full_out = in_order(out_parts, exp_index, exp_count)
-    full_out, later_q = lax.optimization_barrier((full_out, queries_rot))
+    wide_out, later_q = lax.optimization_barrier((wide_out, queries_rot))
     q_all = lax.all_gather(later_q, "ctx", axis=0, tiled=True)
     expert_total = ctx_count
     capacity = max(2, own_rows * routes.shape[1] * 5 // (expert_total * 4))
@@ -962,10 +955,10 @@
     weigh = jnp.where(holds, gate_of.T[:, None, :], 0.0).reshape(slots, own_rows)
     slot_gate = jnp.sum(weigh, axis=1, keepdims=True)
 
-    kv_all, wide_out, full_out, pick, weigh, slot_gate = lax.optimization_barrier(
-        (kv_all, wide_out, full_out, pick, weigh, slot_gate)
-    )
-    heads_f, lse = attend(block_of, own_blocks, queries_rot, kv_all)
+    kv_all, wide_out, pick, weigh, slot_gate = lax.optimization_barrier(
+        (kv_all, wide_out, pick, weigh, slot_gate)
+    )
+    heads_f, lse = attend(block_of, own, queries_rot, kv_all)
     heads_low = heads_f.astype(BF16)
 
     own_heads = exchange_short(heads_low, "exp", exp_index, exp_count)
@@ -992,15 +985,6 @@
     returned, q_all, later_qkv, turned = lax.optimization_barrier(
         (returned, q_all, full_qkv, turned)
     )
-    probs = pair_probs(
-        block_of,
-        own_blocks,
-        own_kv,
-        q_all,
-        ctx_rows,
-        lse_all[:, :, :8],
-    )
-    wide_qkv = jnp.concatenate(shifted(later_qkv, "exp", exp_count), axis=1)
     moe_parts = dot(jnp.concatenate(pieces(weigh, 2), axis=1), returned, TN)
     moe_rows = moe_parts[:own_rows] + moe_parts[own_rows:]
     block_out = resid + moe_rows
@@ -1016,7 +1000,18 @@
         jnp.concatenate(pieces(out_grad_rows, 2), axis=0),
         NN,
     )
-    grad_copies = send((slot_gate * copy_grad).astype(BF16))
+    copy_grad = (slot_gate * copy_grad).astype(BF16)
+    copy_grad, lse_all = lax.optimization_barrier((copy_grad, lse_all))
+    grad_copies = send(copy_grad)
+    probs = pair_probs(
+        block_of,
+        own,
+        own_kv,
+        q_all,
+        ctx_rows,
+        lse_all[:, :, :8],
+    )
+    wide_qkv = jnp.concatenate(shifted(later_qkv, "exp", exp_count), axis=1)
     grad_copies, probs = lax.optimization_barrier((grad_copies, probs))
     input_grad, gate_grad, up_grad, hidden_act = expert_backward(
         grad_copies, gate_pre, up_pre, expert, turned
@@ -1037,14 +1032,22 @@
     resid_grad = out_grad_rows + norm_back(ffn_normed_grad, ffn_hat, ffn_scale, ffn_gain)
     branch_rows = resid_grad.astype(BF16)
 
-    do_rows = jnp.einsum("ro,eok->erk", branch_rows, full_out, preferred_element_type=F32)
-    out_grad = exchange(do_rows.astype(BF16), "exp").reshape(ctx_rows, head_cols)
+    do_parts = dot(branch_rows, wide_out, NN).astype(BF16)
+    come = [do_parts[:, :head_cols]]
+    for step in range(1, exp_count):
+        part = do_parts[:, step * head_cols : (step + 1) * head_cols]
+        turns = [(i, (i - step) % exp_count) for i in range(exp_count)]
+        come.append(lax.ppermute(part, "exp", turns))
+    out_grad = jnp.concatenate(come, axis=0)
+    heads_turned = lax.dynamic_slice_in_dim(
+        jnp.concatenate([heads_f, heads_f], axis=0), exp_index * own_rows, ctx_rows, 0
+    )
     branch_parts = shifted(branch_rows, "exp", exp_count)
     head_of = jnp.arange(head_cols, dtype=jnp.int32)[None] // HD
     head_ones = (head_of == jnp.arange(4, dtype=jnp.int32)[:, None]).astype(F32)
     delta = lax.dot_general(
         head_ones,
-        out_grad.astype(F32) * heads_f,
+        out_grad.astype(F32) * heads_turned,
         NT,
         precision=lax.Precision.HIGHEST,
         preferred_element_type=F32,
@@ -1052,7 +1055,7 @@
     delta = delta.reshape(4, 2, 2 * BLK).transpose(1, 0, 2)
     do_all = lax.all_gather(with_stats(out_grad, delta), "ctx", axis=0, tiled=False)
     query_n_grad = query_grad(
-        block_of, own_blocks, queries_rot, out_grad, heads_f, lse, cosine, sine, kv_all
+        block_of, own, queries_rot, out_grad, heads_f, lse, cosine, sine, kv_all
     )
 
     grad_out = None
@@ -1070,7 +1073,7 @@
 
     pair_grads = pair_grad(
         block_of,
-        own_blocks,
+        own,
         own_kv,
         cosine,
         sine,

time: 556 us -> 531 us (0.955)
  waiting for transfers between devices: 180 us -> 158 us
  Pallas kernels: 145 us -> 155 us
  starting transfers between devices: 90.5 us -> 84.1 us
  other arithmetic: 30.8 us -> 24.9 us
    all_gather x1, waiting for transfers between devices: 24.1 us -> 0.01 us  [on_device(): lse_all = lax.all_gather(stat_rows, 'ctx', axis=0, tiled=False)]
    all_gather x1, waiting for transfers between devices: 28.8 us -> 13.8 us  [on_device(): q_all = lax.all_gather(later_q, 'ctx', axis=0, tiled=True)]
    all_to_all x7 -> x6, waiting for transfers between devices: 78.3 us -> 92.5 us  [exchange(): return lax.all_to_all(values, axis, split_axis=0, concat_axis=0, tiled=True)]
    all_to_all x7 -> x6, starting transfers between devices: 48.5 us -> 37 us  [exchange(): return lax.all_to_all(values, axis, split_axis=0, concat_axis=0, tiled=True)]
    pallas_call x3, Pallas kernels: 57.5 us -> 64.1 us  [kernel_call(): pl.pallas_call(kernel, out_shape=tuple(outs), grid_spec=pltpu.PrefetchSca...]
    dot_general x16 -> x17, matrix products: 38 us -> 38.1 us  [dot(): return lax.dot_general(left, right, dims, preferred_element_type=F32)]
  transfers between devices with their start and end apart: 39 -> 41, of which waited for: 20 -> 21; matrix products, arithmetic and copies ran while one was open for 16% -> 15% of each run, Pallas kernels for 25% -> 30%
where the time goes in v9:
time: 531 us; the launch traced here: 523 us
  waiting for transfers between devices  158 us (30%)
  Pallas kernels  155 us (29%)
  starting transfers between devices  84.1 us (16%)
  matrix products  38.6 us (7%)
  local copies, waits for them, and re-layouts  26.4 us (5%)
  other arithmetic  24.9 us (5%)
  between operations  19 us (4%)
  blocking collectives  17.1 us (3%)
    all_to_all x6, waiting for transfers between devices, exchange(): return lax.all_to_all(values, axis, split_axis=0, concat_axis=0, tiled=True)  92.5 us
    pallas_call x2, Pallas kernels, pair_call(): pl.pallas_call(kernel, out_shape=tuple((out if out.dtype == F32 else pltp...  69.8 us
    pallas_call x3, Pallas kernels, kernel_call(): pl.pallas_call(kernel, out_shape=tuple(outs), grid_spec=pltpu.PrefetchSca...  64.1 us
    dot_general x17, matrix products, dot(): return lax.dot_general(left, right, dims, preferred_element_type=F32)  38.1 us
    all_to_all x6, starting transfers between devices, exchange(): return lax.all_to_all(values, axis, split_axis=0, concat_axis=0, tiled=True)  37 us
    ppermute x18, starting transfers between devices, shifted(): lax.ppermute(values, axis, [(i, (i + step) % count) for i in range(count)])  31.3 us
    ppermute x18, waiting for transfers between devices, shifted(): lax.ppermute(values, axis, [(i, (i + step) % count) for i in range(count)])  24.9 us
    pallas_call x2, Pallas kernels, by_rows(): pl.pallas_call(kernel, out_shape=tuple((pltpu.HBM(out.shape, out.dtype) f...  21.4 us
  transfers between devices with their start and end apart: 41, of which 21 were waited for; matrix products, arithmetic and copies ran while one was open for 15% of the time, Pallas kernels for 30%

profile of v9, /device:TPU:0, one launch (start us, length us, event | category | flops | bytes accessed | tf_op | source)
XLA Modules:
  0.0 523.4 jit_solution(2523868159139376656)
XLA Ops:
  11.9 8.4 %all-to-all-start = ((bf16[32,40,512]{2,1,0:T(8,128)(2,1)}), bf16[32,40,512]{2,1,0:T(8,128)(2,1)S(1)}, u32[]{:S(2)}, u32[]{:S(2)}) async-start(bf16[32,40,512]{2,1,0:T(8,128)(2,1)} %broadcast_in_dim.59), calls=%async_computation | async-start | bytes 2621440 | tf_op jit(solution)/shard_map/all_to_all | solution.py:805
  22.3 18.8 %all-to-all-done = bf16[32,40,512]{2,1,0:T(8,128)(2,1)S(1)} async-done(((bf16[32,40,512]{2,1,0:T(8,128)(2,1)}), bf16[32,40,512]{2,1,0:T(8,128)(2,1)S(1)}, u32[]{:S(2)}, u32[]{:S(2)}) %all-to-all-start) | async-done | bytes 1310752 | tf_op jit(solution)/shard_map/all_to_all | solution.py:805
  44.2 3.3 collective-permute-start
  54.7 17.1 %all_to_all.35 = bf16[32,32,256]{2,1,0:T(8,128)(2,1)S(1)} all-to-all(bf16[32,32,256]{2,1,0:T(8,128)(2,1)S(1)} %broadcast_in_dim.102), channel_id=1, replica_groups=mesh['ctx'=32,'exp'=4] {'ctx'}, dimensions={0} | all-to-all | bytes 1048576 | tf_op jit(solution)/shard_map/all_to_all | solution.py:805
  76.8 21.3 %collective-permute-done.3 = bf16[1024,256]{1,0:T(8,128)(2,1)S(1)} collective-permute-done((bf16[1024,256]{1,0:T(8,128)(2,1)S(1)}, bf16[1024,256]{1,0:T(8,128)(2,1)S(1)}, u32[]{:S(2)}, u32[]{:S(2)}) %collective-permute-start.3) | collective-permute-done | bytes 524320 | tf_op jit(solution)/shard_map/ppermute | solution.py:815
  102.7 6.3 %all-gather.9.cloned.1.call-done.kv = bf16[16384,256]{1,0:T(8,128)(2,1)} async-done(((bf16[512,256]{1,0:T(8,128)(2,1)}), bf16[16384,256]{1,0:T(8,128)(2,1)}) %all-gather.9.cloned.1.call-update) | async-done | bytes 8388624 | tf_op jit(solution)/shard_map/all_gather | solution.py:936
  108.9 24.7 %attend.1 = (f32[512,256]{1,0:T(8,128)S(1)}, f32[2,4,256]{2,1,0:T(4,128)S(1)}) custom-call(s32[128]{0:T(128)S(1)} %copy-done, s32[5]{0:T(128)S(1)} %pad_add_fusion.own, bf16[512,256]{1,0:T(8,128)(2,1)} %get-tuple-element.69.q_in, bf16[16384,256]{1,0:T(8,128)(2,1)} %all-gather.9.cloned.1.call-done.kv), custom_call_target="tpu_custom_call" | custom-call | flops 20000000000 | bytes 8650752 | tf_op jit(solution)/shard_map/attend/pallas_call | solution.py:579
  147.3 9.4 %all-to-all-start.2 = ((bf16[32,40,1024]{2,1,0:T(8,128)(2,1)}), bf16[32,40,1024]{2,1,0:T(8,128)(2,1)}, u32[]{:S(2)}, u32[]{:S(2)}) async-start(bf16[32,40,1024]{2,1,0:T(8,128)(2,1)} %bitcast.96), calls=%async_computation.2 | async-start | bytes 5242880 | tf_op jit(solution)/shard_map/all_to_all | solution.py:805
  157.4 13.8 %all-gather.11.cloned.1.call-done.q_all = bf16[16384,256]{1,0:T(8,128)(2,1)} async-done(((bf16[512,256]{1,0:T(8,128)(2,1)}), bf16[16384,256]{1,0:T(8,128)(2,1)}) %all-gather.11.cloned.1.call-update) | async-done | bytes 8388624 | tf_op jit(solution)/shard_map/all_gather | solution.py:943
  171.2 22.4 %all-to-all-done.2 = bf16[32,40,1024]{2,1,0:T(8,128)(2,1)} async-done(((bf16[32,40,1024]{2,1,0:T(8,128)(2,1)}), bf16[32,40,1024]{2,1,0:T(8,128)(2,1)}, u32[]{:S(2)}, u32[]{:S(2)}) %all-to-all-start.2) | async-done | bytes 2621472 | tf_op jit(solution)/shard_map/all_to_all | solution.py:805
  193.6 8.6 %expert.1 = (bf16[1280,1024]{1,0:T(8,128)(2,1)}, f32[1280,512]{1,0:T(8,128)}, f32[1280,512]{1,0:T(8,128)}) custom-call(bf16[1280,1024]{1,0:T(8,128)(2,1)} %bitcast.18.x_ref, bf16[4,1024,384]{2,1,0:T(8,128)(2,1)} %bitcast.104), custom_call_target="tpu_custom_call" | custom-call | flops 4026531840 | bytes 10000000 | tf_op jit(solution)/shard_map/expert/pallas_call | solution.py:601
  202.2 5.1 all-to-all-start.3
  209.2 4.7 copy.90
  219.6 26.8 %all-to-all-done.3 = bf16[32,40,1024]{2,1,0:T(8,128)(2,1)} async-done(((bf16[32,40,1024]{2,1,0:T(8,128)(2,1)}), bf16[32,40,1024]{2,1,0:T(8,128)(2,1)}, u32[]{:S(2)}, u32[]{:S(2)}) %all-to-all-start.3) | async-done | bytes 2621472 | tf_op jit(solution)/shard_map/all_to_all | solution.py:805
  252.5 4.8 all-to-all-start.4
  263.6 26.8 %pair_probs.1 = (bf16[16,1024,1024]{2,1,0:T(8,128)(2,1)}, bf16[2,2,512,512]{3,2,1,0:T(8,128)(2,1)}) custom-call(s32[128]{0:T(128)S(1)} %copy-done, s32[5]{0:T(128)S(1)} %pad_add_fusion.own, bf16[512,256]{1,0:T(8,128)(2,1)} %get-tuple-element.61.kv_in, bf16[16384,256]{1,0:T(8,128)(2,1)} %all-gather.11.cloned.1.call-done.q_all, ...), custom_call_target="tpu_custom_call" | custom-call | flops 20000000000 | bytes 40000000 | tf_op jit(solution)/shard_map/pair_probs/pallas_call | solution.py:708
  293.4 12.8 %expert_grad.1 = (bf16[1280,1024]{1,0:T(8,128)(2,1)}, bf16[1280,512]{1,0:T(8,128)(2,1)}, bf16[1280,512]{1,0:T(8,128)(2,1)}, bf16[1280,512]{1,0:T(8,128)(2,1)}) custom-call(bf16[1280,1024]{1,0:T(8,128)(2,1)} %bitcast.25.dy_ref, f32[1280,512]{1,0:T(8,128)} %get-tuple-element.83.gate_ref, f32[1280,512]{1,0:T(8,128)} %get-tuple-element.84.up_ref, ...), custom_call_target="tpu_custom_call" | custom-call | flops 4026531840 | bytes 10000000 | tf_op jit(solution)/shard_map/expert_grad/pallas_call | solution.py:601
  306.1 4.8 all-to-all-start.5
  311.3 3.9 pad_maximum_fusion
  315.2 4.7 fusion.106
  322.8 5.0 fusion.105
  330.7 5.0 fusion.107
  335.7 11.3 %all-to-all-done.5 = bf16[32,40,1024]{2,1,0:T(8,128)(2,1)} async-done(((bf16[32,40,1024]{2,1,0:T(8,128)(2,1)}), bf16[32,40,1024]{2,1,0:T(8,128)(2,1)}, u32[]{:S(2)}, u32[]{:S(2)}) %all-to-all-start.5) | async-done | bytes 2621472 | tf_op jit(solution)/shard_map/all_to_all | solution.py:805
  357.3 3.9 collective-permute-done.13
  367.0 37.9 %query_grad.1 = f32[512,256]{1,0:T(8,128)S(1)} custom-call(s32[128]{0:T(128)S(1)} %copy-done, s32[5]{0:T(128)S(1)} %pad_add_fusion.own, bf16[512,256]{1,0:T(8,128)(2,1)} %get-tuple-element.69.q_in, bf16[512,256]{1,0:T(8,128)(2,1)S(1)} %pad_maximum_fusion.6.do_in, f32[512,256]{1,0:T(8,128)S(1)} %get-tuple-element.65.o_in, ...), custom_call_target="tpu_custom_call" | custom-call | flops 30000001024 | bytes 9969664 | tf_op jit(solution)/shard_map/query_grad/pallas_call | solution.py:579
  406.0 7.0 %all-gather.17.cloned.1.call-done = bf16[17920,256]{1,0:T(8,128)(2,1)} async-done(((bf16[560,256]{1,0:T(8,128)(2,1)}), bf16[17920,256]{1,0:T(8,128)(2,1)}) %all-gather.17.cloned.1.call-update) | async-done | bytes 9175056 | tf_op jit(solution)/shard_map/all_gather | solution.py:1056
  414.7 43.0 %pair_grad.1 = f32[512,256]{1,0:T(8,128)S(1)} custom-call(s32[128]{0:T(128)S(1)} %copy-done, s32[5]{0:T(128)S(1)} %pad_add_fusion.own, bf16[512,256]{1,0:T(8,128)(2,1)} %get-tuple-element.61.kv_in, f32[512,128]{1,0:T(8,128)S(1)} %get-tuple-element.168.cos_ref, f32[512,128]{1,0:T(8,128)S(1)} %get-tuple-element.169.sin_ref, ...), custom_call_target="tpu_custom_call" | custom-call | flops 30000001024 | bytes 40000000 | tf_op jit(solution)/shard_map/pair_grad/pallas_call | solution.py:708
  473.6 4.5 all-to-all-start.6
  478.3 4.6 collective-permute-start.22
  485.4 4.1 collective-permute-done.22
  489.5 4.1 fusion.19
  494.7 10.3 %all-to-all-done.6 = bf16[32,32,896]{2,1,0:T(8,128)(2,1)S(1)} async-done(((bf16[32,32,896]{2,1,0:T(8,128)(2,1)}), bf16[32,32,896]{2,1,0:T(8,128)(2,1)S(1)}, u32[]{:S(2)}, u32[]{:S(2)}) %all-to-all-start.6) | async-done | bytes 1835040 | tf_op jit(solution)/shard_map/all_to_all | solution.py:805
  (298 shorter events, 115.2 us)
Async XLA Ops:
  7.3 47.3 %all-gather.13.cloned.1.call-start = ((), (), s32[]{:S(2)}) async-start(), calls=%async_computation.15 | async-start | bytes 3932160 | tf_op jit(solution)/shard_map/all_gather | solution.py:903
  11.9 29.2 %all-to-all-start = ((bf16[32,40,512]{2,1,0:T(8,128)(2,1)}), bf16[32,40,512]{2,1,0:T(8,128)(2,1)S(1)}, u32[]{:S(2)}, u32[]{:S(2)}) async-start(bf16[32,40,512]{2,1,0:T(8,128)(2,1)} %broadcast_in_dim.59), calls=%async_computation | async-start | bytes 2621440 | tf_op jit(solution)/shard_map/all_to_all | solution.py:805
  20.3 88.7 %all-gather.9.cloned.1.call-start = ((), (), s32[]{:S(2)}) async-start(), calls=%async_computation.10 | async-start | bytes 8650752 | tf_op jit(solution)/shard_map/all_gather | solution.py:936
  44.2 7.5 %collective-permute-start = (f32[2,512]{1,0:T(2,128)S(1)}, f32[2,512]{1,0:T(2,128)S(1)}, u32[]{:S(2)}, u32[]{:S(2)}) collective-permute-start(f32[2,512]{1,0:T(2,128)S(1)} %pad_maximum_fusion.10), channel_id=1, source_target_pairs={{0,2},{1,3},{2,0},{3,1},{4,6},{5,7},{6,4},{7,5},{8,10},{9,11},{10,... | collective-permute-start | bytes 12296 | tf_op jit(solution)/shard_map/ppermute | solution.py:815
  54.6 116.6 %all-gather.11.cloned.1.call-start = ((), (), s32[]{:S(2)}) async-start(), calls=%async_computation.11 | async-start | bytes 8650752 | tf_op jit(solution)/shard_map/all_gather | solution.py:943
  71.8 26.3 %collective-permute-start.3 = (bf16[1024,256]{1,0:T(8,128)(2,1)S(1)}, bf16[1024,256]{1,0:T(8,128)(2,1)S(1)}, u32[]{:S(2)}, u32[]{:S(2)}) collective-permute-start(bf16[1024,256]{1,0:T(8,128)(2,1)S(1)} %bitcast.113), channel_id=1, source_target_pairs={{0,1},{1,2},{2,3},{3,0},{4,5},{5,6},{6,7},{7,4},{8,9},{9,10},{10,1... | collective-permute-start | bytes 1572872 | tf_op jit(solution)/shard_map/ppermute | solution.py:815
  72.5 25.7 %collective-permute-start.4 = (bf16[1024,256]{1,0:T(8,128)(2,1)S(1)}, bf16[1024,256]{1,0:T(8,128)(2,1)S(1)}, u32[]{:S(2)}, u32[]{:S(2)}) collective-permute-start(bf16[1024,256]{1,0:T(8,128)(2,1)S(1)} %bitcast.114), channel_id=1, source_target_pairs={{0,2},{1,3},{2,0},{3,1},{4,6},{5,7},{6,4},{7,5},{8,10},{9,11},{10,... | collective-permute-start | bytes 1572872 | tf_op jit(solution)/shard_map/ppermute | solution.py:815
  74.2 24.6 %collective-permute-start.5 = (bf16[1024,256]{1,0:T(8,128)(2,1)S(1)}, bf16[1024,256]{1,0:T(8,128)(2,1)S(1)}, u32[]{:S(2)}, u32[]{:S(2)}) collective-permute-start(bf16[1024,256]{1,0:T(8,128)(2,1)S(1)} %bitcast.115), channel_id=1, source_target_pairs={{0,3},{1,0},{2,1},{3,2},{4,7},{5,4},{6,5},{7,6},{8,11},{9,8},{10,9... | collective-permute-start | bytes 1572872 | tf_op jit(solution)/shard_map/ppermute | solution.py:815
  133.7 5.8 %collective-permute-start.6 = (bf16[128,256]{1,0:T(8,128)(2,1)S(1)}, bf16[128,256]{1,0:T(8,128)(2,1)S(1)}, u32[]{:S(2)}, u32[]{:S(2)}) collective-permute-start(bf16[128,256]{1,0:T(8,128)(2,1)S(1)} %get-tuple-element.140), channel_id=1, source_target_pairs={{0,1},{1,2},{2,3},{3,0},{4,5},{5,6},{6,7},{7,4},{8,9},{9,10},{10,1... | collective-permute-start | bytes 196616 | tf_op jit(solution)/shard_map/ppermute | solution.py:834
  147.3 46.3 %all-to-all-start.2 = ((bf16[32,40,1024]{2,1,0:T(8,128)(2,1)}), bf16[32,40,1024]{2,1,0:T(8,128)(2,1)}, u32[]{:S(2)}, u32[]{:S(2)}) async-start(bf16[32,40,1024]{2,1,0:T(8,128)(2,1)} %bitcast.96), calls=%async_computation.2 | async-start | bytes 5242880 | tf_op jit(solution)/shard_map/all_to_all | solution.py:805
  156.7 95.8 %all-gather.15.cloned.1.call-start = ((), (), s32[]{:S(2)}) async-start(), calls=%async_computation.16 | async-start | bytes 2162688 | tf_op jit(solution)/shard_map/all_gather | solution.py:966
  202.2 44.1 %all-to-all-start.3 = ((bf16[32,40,1024]{2,1,0:T(8,128)(2,1)}), bf16[32,40,1024]{2,1,0:T(8,128)(2,1)}, u32[]{:S(2)}, u32[]{:S(2)}) async-start(bf16[32,40,1024]{2,1,0:T(8,128)(2,1)} %bitcast.108), calls=%async_computation.3 | async-start | bytes 5242880 | tf_op jit(solution)/shard_map/all_to_all | solution.py:805
  252.5 40.9 %all-to-all-start.4 = ((bf16[32,40,1024]{2,1,0:T(8,128)(2,1)}), bf16[32,40,1024]{2,1,0:T(8,128)(2,1)}, u32[]{:S(2)}, u32[]{:S(2)}) async-start(bf16[32,40,1024]{2,1,0:T(8,128)(2,1)} %bitcast.109), calls=%async_computation.4 | async-start | bytes 5242880 | tf_op jit(solution)/shard_map/all_to_all | solution.py:805
  257.3 53.9 %collective-permute-start.10 = (bf16[1024,512]{1,0:T(8,128)(2,1)}, bf16[1024,512]{1,0:T(8,128)(2,1)}, u32[]{:S(2)}, u32[]{:S(2)}) collective-permute-start(bf16[1024,512]{1,0:T(8,128)(2,1)} %bitcast.100), channel_id=1, source_target_pairs={{0,2},{1,3},{2,0},{3,1},{4,6},{5,7},{6,4},{7,5},{8,10},{9,11},{10,... | collective-permute-start | bytes 3145736 | tf_op jit(solution)/shard_map/ppermute | solution.py:815
  260.5 50.7 %collective-permute-start.11 = (bf16[1024,512]{1,0:T(8,128)(2,1)}, bf16[1024,512]{1,0:T(8,128)(2,1)}, u32[]{:S(2)}, u32[]{:S(2)}) collective-permute-start(bf16[1024,512]{1,0:T(8,128)(2,1)} %bitcast.101), channel_id=1, source_target_pairs={{0,3},{1,0},{2,1},{3,2},{4,7},{5,4},{6,5},{7,6},{8,11},{9,8},{10,9... | collective-permute-start | bytes 3145736 | tf_op jit(solution)/shard_map/ppermute | solution.py:815
  261.7 49.6 %collective-permute-start.9 = (bf16[1024,512]{1,0:T(8,128)(2,1)}, bf16[1024,512]{1,0:T(8,128)(2,1)}, u32[]{:S(2)}, u32[]{:S(2)}) collective-permute-start(bf16[1024,512]{1,0:T(8,128)(2,1)} %bitcast.102), channel_id=1, source_target_pairs={{0,1},{1,2},{2,3},{3,0},{4,5},{5,6},{6,7},{7,4},{8,9},{9,10},{10,1... | collective-permute-start | bytes 3145736 | tf_op jit(solution)/shard_map/ppermute | solution.py:815
  306.1 40.9 %all-to-all-start.5 = ((bf16[32,40,1024]{2,1,0:T(8,128)(2,1)}), bf16[32,40,1024]{2,1,0:T(8,128)(2,1)}, u32[]{:S(2)}, u32[]{:S(2)}) async-start(bf16[32,40,1024]{2,1,0:T(8,128)(2,1)} %bitcast.107), calls=%async_computation.5 | async-start | bytes 5242880 | tf_op jit(solution)/shard_map/all_to_all | solution.py:805
  311.0 102.1 %all-gather.17.cloned.1.call-start = ((), (), s32[]{:S(2)}) async-start(), calls=%async_computation.17 | async-start | bytes 9461760 | tf_op jit(solution)/shard_map/all_gather | solution.py:1056
  355.4 5.8 %collective-permute-start.13 = (bf16[128,256]{1,0:T(8,128)(2,1)S(1)}, bf16[128,256]{1,0:T(8,128)(2,1)S(1)}, u32[]{:S(2)}, u32[]{:S(2)}) collective-permute-start(bf16[128,256]{1,0:T(8,128)(2,1)S(1)} %get-tuple-element.135), channel_id=1, source_target_pairs={{0,2},{1,3},{2,0},{3,1},{4,6},{5,7},{6,4},{7,5},{8,10},{9,11},{10,... | collective-permute-start | bytes 196616 | tf_op jit(solution)/shard_map/ppermute | solution.py:1040
  363.1 151.8 %reduce-scatter.8.cloned.1.call-start = ((), (), s32[]{:S(2)}) async-start(), calls=%async_computation.14 | async-start | bytes 2621440 | tf_op jit(solution)/shard_map/reduce_scatter | solution.py:1072
  363.3 41.7 %collective-permute-start.15 = (bf16[128,1024]{1,0:T(8,128)(2,1)S(1)}, bf16[128,1024]{1,0:T(8,128)(2,1)S(1)}, u32[]{:S(2)}, u32[]{:S(2)}) collective-permute-start(bf16[128,1024]{1,0:T(8,128)(2,1)S(1)} %get-tuple-element.120), channel_id=1, source_target_pairs={{0,1},{1,2},{2,3},{3,0},{4,5},{5,6},{6,7},{7,4},{8,9},{9,10},{10,1... | collective-permute-start | bytes 786440 | tf_op jit(solution)/shard_map/ppermute | solution.py:815
  363.3 42.0 %collective-permute-start.17 = (bf16[128,1024]{1,0:T(8,128)(2,1)S(1)}, bf16[128,1024]{1,0:T(8,128)(2,1)S(1)}, u32[]{:S(2)}, u32[]{:S(2)}) collective-permute-start(bf16[128,1024]{1,0:T(8,128)(2,1)S(1)} %get-tuple-element.120), channel_id=1, source_target_pairs={{0,3},{1,0},{2,1},{3,2},{4,7},{5,4},{6,5},{7,6},{8,11},{9,8},{10,9... | collective-permute-start | bytes 786440 | tf_op jit(solution)/shard_map/ppermute | solution.py:815
  366.6 39.1 %collective-permute-start.16 = (bf16[128,1024]{1,0:T(8,128)(2,1)S(1)}, bf16[128,1024]{1,0:T(8,128)(2,1)S(1)}, u32[]{:S(2)}, u32[]{:S(2)}) collective-permute-start(bf16[128,1024]{1,0:T(8,128)(2,1)S(1)} %get-tuple-element.120), channel_id=1, source_target_pairs={{0,2},{1,3},{2,0},{3,1},{4,6},{5,7},{6,4},{7,5},{8,10},{9,11},{10,... | collective-permute-start | bytes 786440 | tf_op jit(solution)/shard_map/ppermute | solution.py:815
  413.1 101.9 %reduce-scatter.4.cloned.1.call-start = ((), (), s32[]{:S(2)}) async-start(), calls=%async_computation.12 | async-start | bytes 2621440 | tf_op jit(solution)/shard_map/reduce_scatter | solution.py:1070
  413.8 101.1 %reduce-scatter.6.cloned.1.call-start = ((), (), s32[]{:S(2)}) async-start(), calls=%async_computation.13 | async-start | bytes 2621440 | tf_op jit(solution)/shard_map/reduce_scatter | solution.py:1071
  458.9 6.4 %collective-permute-start.18 = (f32[32,128]{1,0:T(8,128)S(1)}, f32[32,128]{1,0:T(8,128)S(1)}, u32[]{:S(2)}, u32[]{:S(2)}) collective-permute-start(f32[32,128]{1,0:T(8,128)S(1)} %bitcast.138), channel_id=1, source_target_pairs={{0,2},{1,3},{2,0},{3,1},{4,6},{5,7},{6,4},{7,5},{8,10},{9,11},{10,... | collective-permute-start | bytes 49160 | tf_op jit(solution)/shard_map/ppermute | solution.py:815
  473.6 31.4 %all-to-all-start.6 = ((bf16[32,32,896]{2,1,0:T(8,128)(2,1)}), bf16[32,32,896]{2,1,0:T(8,128)(2,1)S(1)}, u32[]{:S(2)}, u32[]{:S(2)}) async-start(bf16[32,32,896]{2,1,0:T(8,128)(2,1)} %fusion.4), calls=%async_computation.6 | async-start | bytes 3670016 | tf_op jit(solution)/shard_map/all_to_all | solution.py:805
  478.2 7.2 %collective-permute-start.21 = (bf16[128,512]{1,0:T(8,128)(2,1)S(1)}, bf16[128,512]{1,0:T(8,128)(2,1)S(1)}, u32[]{:S(2)}, u32[]{:S(2)}) collective-permute-start(bf16[128,512]{1,0:T(8,128)(2,1)S(1)} %get-tuple-element.130), channel_id=1, source_target_pairs={{0,1},{1,2},{2,3},{3,0},{4,5},{5,6},{6,7},{7,4},{8,9},{9,10},{10,1... | collective-permute-start | bytes 393224 | tf_op jit(solution)/shard_map/ppermute | solution.py:834
  478.3 11.2 %collective-permute-start.22 = (bf16[128,512]{1,0:T(8,128)(2,1)S(1)}, bf16[128,512]{1,0:T(8,128)(2,1)}, u32[]{:S(2)}, u32[]{:S(2)}) collective-permute-start(bf16[128,512]{1,0:T(8,128)(2,1)S(1)} %get-tuple-element.129), channel_id=1, source_target_pairs={{0,2},{1,3},{2,0},{3,1},{4,6},{5,7},{6,4},{7,5},{8,10},{9,11},{10,... | collective-permute-start | bytes 393224 | tf_op jit(solution)/shard_map/ppermute | solution.py:834
  482.9 6.6 %collective-permute-start.23 = (bf16[128,512]{1,0:T(8,128)(2,1)S(1)}, bf16[128,512]{1,0:T(8,128)(2,1)}, u32[]{:S(2)}, u32[]{:S(2)}) collective-permute-start(bf16[128,512]{1,0:T(8,128)(2,1)S(1)} %get-tuple-element.131), channel_id=1, source_target_pairs={{0,3},{1,0},{2,1},{3,2},{4,7},{5,4},{6,5},{7,6},{8,11},{9,8},{10,9... | collective-permute-start | bytes 393224 | tf_op jit(solution)/shard_map/ppermute | solution.py:834
  506.8 7.5 %collective-permute-start.24 = (f32[32]{0:T(128)S(1)}, f32[32]{0:T(128)S(1)}, u32[]{:S(2)}, u32[]{:S(2)}) collective-permute-start(f32[32]{0:T(128)S(1)} %add_add_fusion.2), channel_id=1, source_target_pairs={{0,2},{1,3},{2,0},{3,1},{4,6},{5,7},{6,4},{7,5},{8,10},{9,11},{10,... | collective-permute-start | bytes 392 | tf_op jit(solution)/shard_map/ppermute | solution.py:815
  508.3 6.0 %collective-permute-start.25 = (f32[32]{0:T(128)S(1)}, f32[32]{0:T(128)S(1)}, u32[]{:S(2)}, u32[]{:S(2)}) collective-permute-start(f32[32]{0:T(128)S(1)} %add_add_fusion.2), channel_id=1, source_target_pairs={{0,1},{1,2},{2,3},{3,0},{4,5},{5,6},{6,7},{7,4},{8,9},{9,10},{10,1... | collective-permute-start | bytes 392 | tf_op jit(solution)/shard_map/ppermute | solution.py:815
  (56 other events, 602.7 us)
Sparse Core Ops, SparseCore 0:
  10.6 42.2 all-gather.12
  55.7 53.2 all-gather.8
  111.8 59.3 all-gather.10
  173.9 71.2 all-gather.14
  363.3 49.7 all-gather.16
  415.9 29.1 reduce-scatter.7
  448.2 29.7 reduce-scatter.3
  481.0 29.7 reduce-scatter.5

commit v10 on v9

--- a/solution.py
+++ b/solution.py
@@ -932,9 +932,8 @@
         cosine,
         sine,
     )
-    own_kv, expert = lax.optimization_barrier((own_kv, expert))
     kv_all = lax.all_gather(own_kv, "ctx", axis=0, tiled=True)
-    own_out, _ = lax.optimization_barrier((w_out, own_kv))
+    own_out, _, expert = lax.optimization_barrier((w_out, own_kv, expert))
     out_parts = shifted(
         spread(own_out, "ctx", ctx_count).reshape(model_width, head_cols), "exp", exp_count
     )

time: 531 us -> 531 us (level)
  Pallas kernels: 155 us -> 149 us
  starting transfers between devices: 84.1 us -> 90 us
    all_to_all x6, waiting for transfers between devices: 92.5 us -> 115 us  [exchange(): return lax.all_to_all(values, axis, split_axis=0, concat_axis=0, tiled=True)]
    pallas_call x2, Pallas kernels: 69.8 us -> 52.1 us  [pair_call(): pl.pallas_call(kernel, out_shape=tuple((out if out.dtype == F32 else pltp...]
    all_gather x1, waiting for transfers between devices: 13.8 us -> 0.01 us  [on_device(): q_all = lax.all_gather(later_q, 'ctx', axis=0, tiled=True)]
    pallas_call x3, Pallas kernels: 64.1 us -> 75.6 us  [kernel_call(): pl.pallas_call(kernel, out_shape=tuple(outs), grid_spec=pltpu.PrefetchSca...]
    all_gather x1, waiting for transfers between devices: 7.04 us -> 0.02 us  [on_device(): lax.all_gather(with_stats(out_grad, delta), 'ctx', axis=0, tiled=False)]
    all_to_all x6, starting transfers between devices: 37 us -> 42.9 us  [exchange(): return lax.all_to_all(values, axis, split_axis=0, concat_axis=0, tiled=True)]
  transfers between devices with their start and end apart: 41 -> 41, of which waited for: 21 -> 19; matrix products, arithmetic and copies ran while one was open for 15% -> 15% of each run, Pallas kernels for 30% -> 28%
where the time goes in v10:
time: 531 us; the launch traced here: 524 us
  waiting for transfers between devices  159 us (30%)
  Pallas kernels  149 us (28%)
  starting transfers between devices  90 us (17%)
  matrix products  38.5 us (7%)
  local copies, waits for them, and re-layouts  26.4 us (5%)
  other arithmetic  24.9 us (5%)
  between operations  19 us (4%)
  blocking collectives  17 us (3%)
    all_to_all x6, waiting for transfers between devices, exchange(): return lax.all_to_all(values, axis, split_axis=0, concat_axis=0, tiled=True)  115 us
    pallas_call x3, Pallas kernels, kernel_call(): pl.pallas_call(kernel, out_shape=tuple(outs), grid_spec=pltpu.PrefetchSca...  75.6 us
    pallas_call x2, Pallas kernels, pair_call(): pl.pallas_call(kernel, out_shape=tuple((out if out.dtype == F32 else pltp...  52.1 us
    all_to_all x6, starting transfers between devices, exchange(): return lax.all_to_all(values, axis, split_axis=0, concat_axis=0, tiled=True)  42.9 us
    dot_general x17, matrix products, dot(): return lax.dot_general(left, right, dims, preferred_element_type=F32)  38 us
    ppermute x18, starting transfers between devices, shifted(): lax.ppermute(values, axis, [(i, (i + step) % count) for i in range(count)])  31.5 us
    ppermute x18, waiting for transfers between devices, shifted(): lax.ppermute(values, axis, [(i, (i + step) % count) for i in range(count)])  24.4 us
    pallas_call x2, Pallas kernels, by_rows(): pl.pallas_call(kernel, out_shape=tuple((pltpu.HBM(out.shape, out.dtype) f...  21.4 us
  transfers between devices with their start and end apart: 41, of which 19 were waited for; matrix products, arithmetic and copies ran while one was open for 15% of the time, Pallas kernels for 28%

profile of v10, /device:TPU:0, one launch (start us, length us, event | category | flops | bytes accessed | tf_op | source)
XLA Modules:
  0.0 524.0 jit_solution(15162038665522446468)
XLA Ops:
  11.9 8.4 %all-to-all-start = ((bf16[32,40,512]{2,1,0:T(8,128)(2,1)}), bf16[32,40,512]{2,1,0:T(8,128)(2,1)S(1)}, u32[]{:S(2)}, u32[]{:S(2)}) async-start(bf16[32,40,512]{2,1,0:T(8,128)(2,1)} %broadcast_in_dim.59), calls=%async_computation | async-start | bytes 2621440 | tf_op jit(solution)/shard_map/all_to_all | solution.py:805
  22.3 18.8 %all-to-all-done = bf16[32,40,512]{2,1,0:T(8,128)(2,1)S(1)} async-done(((bf16[32,40,512]{2,1,0:T(8,128)(2,1)}), bf16[32,40,512]{2,1,0:T(8,128)(2,1)S(1)}, u32[]{:S(2)}, u32[]{:S(2)}) %all-to-all-start) | async-done | bytes 1310752 | tf_op jit(solution)/shard_map/all_to_all | solution.py:805
  44.2 3.3 collective-permute-start
  54.8 17.0 %all_to_all.35 = bf16[32,32,256]{2,1,0:T(8,128)(2,1)S(1)} all-to-all(bf16[32,32,256]{2,1,0:T(8,128)(2,1)S(1)} %broadcast_in_dim.102), channel_id=1, replica_groups=mesh['ctx'=32,'exp'=4] {'ctx'}, dimensions={0} | all-to-all | bytes 1048576 | tf_op jit(solution)/shard_map/all_to_all | solution.py:805
  76.8 21.3 %collective-permute-done.3 = bf16[1024,256]{1,0:T(8,128)(2,1)S(1)} collective-permute-done((bf16[1024,256]{1,0:T(8,128)(2,1)S(1)}, bf16[1024,256]{1,0:T(8,128)(2,1)S(1)}, u32[]{:S(2)}, u32[]{:S(2)}) %collective-permute-start.3) | collective-permute-done | bytes 524320 | tf_op jit(solution)/shard_map/ppermute | solution.py:815
  102.6 6.3 %all-gather.9.cloned.1.call-done.kv = bf16[16384,256]{1,0:T(8,128)(2,1)} async-done(((bf16[512,256]{1,0:T(8,128)(2,1)}), bf16[16384,256]{1,0:T(8,128)(2,1)}) %all-gather.9.cloned.1.call-update) | async-done | bytes 8388624 | tf_op jit(solution)/shard_map/all_gather | solution.py:935
  109.0 28.5 %attend.1 = (f32[512,256]{1,0:T(8,128)S(1)}, f32[2,4,256]{2,1,0:T(4,128)S(1)}) custom-call(s32[128]{0:T(128)S(1)} %copy-done, s32[5]{0:T(128)S(1)} %pad_add_fusion.own, bf16[512,256]{1,0:T(8,128)(2,1)} %get-tuple-element.67.q_in, bf16[16384,256]{1,0:T(8,128)(2,1)} %all-gather.9.cloned.1.call-done.kv), custom_call_target="tpu_custom_call" | custom-call | flops 20000000000 | bytes 8650752 | tf_op jit(solution)/shard_map/attend/pallas_call | solution.py:579
  151.0 4.8 all-to-all-start.2
  156.5 37.2 %all-to-all-done.2 = bf16[32,40,1024]{2,1,0:T(8,128)(2,1)} async-done(((bf16[32,40,1024]{2,1,0:T(8,128)(2,1)}), bf16[32,40,1024]{2,1,0:T(8,128)(2,1)}, u32[]{:S(2)}, u32[]{:S(2)}) %all-to-all-start.2) | async-done | bytes 2621472 | tf_op jit(solution)/shard_map/all_to_all | solution.py:805
  193.7 8.6 %expert.1 = (bf16[1280,1024]{1,0:T(8,128)(2,1)}, f32[1280,512]{1,0:T(8,128)}, f32[1280,512]{1,0:T(8,128)}) custom-call(bf16[1280,1024]{1,0:T(8,128)(2,1)} %bitcast.18.x_ref, bf16[4,1024,384]{2,1,0:T(8,128)(2,1)} %bitcast.104), custom_call_target="tpu_custom_call" | custom-call | flops 4026531840 | bytes 10000000 | tf_op jit(solution)/shard_map/expert/pallas_call | solution.py:601
  202.3 5.1 all-to-all-start.3
  209.4 4.7 copy.90
  219.7 26.8 %all-to-all-done.3 = bf16[32,40,1024]{2,1,0:T(8,128)(2,1)} async-done(((bf16[32,40,1024]{2,1,0:T(8,128)(2,1)}), bf16[32,40,1024]{2,1,0:T(8,128)(2,1)}, u32[]{:S(2)}, u32[]{:S(2)}) %all-to-all-start.3) | async-done | bytes 2621472 | tf_op jit(solution)/shard_map/all_to_all | solution.py:805
  252.7 4.8 all-to-all-start.4
  263.6 19.8 %pair_probs.1 = (bf16[16,1024,1024]{2,1,0:T(8,128)(2,1)}, bf16[2,2,512,512]{3,2,1,0:T(8,128)(2,1)}) custom-call(s32[128]{0:T(128)S(1)} %copy-done, s32[5]{0:T(128)S(1)} %pad_add_fusion.own, bf16[512,256]{1,0:T(8,128)(2,1)} %get-tuple-element.59.kv_in, bf16[16384,256]{1,0:T(8,128)(2,1)} %all-gather.11.cloned.1.call-done.q_all, ...), custom_call_target="tpu_custom_call" | custom-call | flops 20000000000 | bytes 40000000 | tf_op jit(solution)/shard_map/pair_probs/pallas_call | solution.py:708
  283.4 10.2 %all-to-all-done.4 = bf16[32,40,1024]{2,1,0:T(8,128)(2,1)} async-done(((bf16[32,40,1024]{2,1,0:T(8,128)(2,1)}), bf16[32,40,1024]{2,1,0:T(8,128)(2,1)}, u32[]{:S(2)}, u32[]{:S(2)}) %all-to-all-start.4) | async-done | bytes 2621472 | tf_op jit(solution)/shard_map/all_to_all | solution.py:805
  293.6 12.8 %expert_grad.1 = (bf16[1280,1024]{1,0:T(8,128)(2,1)}, bf16[1280,512]{1,0:T(8,128)(2,1)}, bf16[1280,512]{1,0:T(8,128)(2,1)}, bf16[1280,512]{1,0:T(8,128)(2,1)}) custom-call(bf16[1280,1024]{1,0:T(8,128)(2,1)} %bitcast.25.dy_ref, f32[1280,512]{1,0:T(8,128)} %get-tuple-element.81.gate_ref, f32[1280,512]{1,0:T(8,128)} %get-tuple-element.82.up_ref, ...), custom_call_target="tpu_custom_call" | custom-call | flops 4026531840 | bytes 10000000 | tf_op jit(solution)/shard_map/expert_grad/pallas_call | solution.py:601
  306.4 4.8 all-to-all-start.5
  311.5 3.9 pad_maximum_fusion
  315.4 4.7 fusion.106
  323.0 5.0 fusion.105
  330.9 5.0 fusion.107
  335.9 11.3 %all-to-all-done.5 = bf16[32,40,1024]{2,1,0:T(8,128)(2,1)} async-done(((bf16[32,40,1024]{2,1,0:T(8,128)(2,1)}), bf16[32,40,1024]{2,1,0:T(8,128)(2,1)}, u32[]{:S(2)}, u32[]{:S(2)}) %all-to-all-start.5) | async-done | bytes 2621472 | tf_op jit(solution)/shard_map/all_to_all | solution.py:805
  357.2 3.9 collective-permute-done.13
  367.0 45.7 %query_grad.1 = f32[512,256]{1,0:T(8,128)S(1)} custom-call(s32[128]{0:T(128)S(1)} %copy-done, s32[5]{0:T(128)S(1)} %pad_add_fusion.own, bf16[512,256]{1,0:T(8,128)(2,1)} %get-tuple-element.67.q_in, bf16[512,256]{1,0:T(8,128)(2,1)S(1)} %pad_maximum_fusion.6.do_in, f32[512,256]{1,0:T(8,128)S(1)} %get-tuple-element.63.o_in, ...), custom_call_target="tpu_custom_call" | custom-call | flops 30000001024 | bytes 9969664 | tf_op jit(solution)/shard_map/query_grad/pallas_call | solution.py:579
  415.4 32.3 %pair_grad.1 = f32[512,256]{1,0:T(8,128)S(1)} custom-call(s32[128]{0:T(128)S(1)} %copy-done, s32[5]{0:T(128)S(1)} %pad_add_fusion.own, bf16[512,256]{1,0:T(8,128)(2,1)} %get-tuple-element.59.kv_in, f32[512,128]{1,0:T(8,128)S(1)} %get-tuple-element.166.cos_ref, f32[512,128]{1,0:T(8,128)S(1)} %get-tuple-element.167.sin_ref, ...), custom_call_target="tpu_custom_call" | custom-call | flops 30000001024 | bytes 40000000 | tf_op jit(solution)/shard_map/pair_grad/pallas_call | solution.py:708
  448.9 3.6 collective-permute-start.18
  463.7 15.0 %all-to-all-start.6 = ((bf16[32,32,896]{2,1,0:T(8,128)(2,1)}), bf16[32,32,896]{2,1,0:T(8,128)(2,1)S(1)}, u32[]{:S(2)}, u32[]{:S(2)}) async-start(bf16[32,32,896]{2,1,0:T(8,128)(2,1)} %fusion.4), calls=%async_computation.6 | async-start | bytes 3670016 | tf_op jit(solution)/shard_map/all_to_all | solution.py:805
  478.9 4.7 collective-permute-start.22
  486.0 4.1 collective-permute-done.22
  490.1 4.0 fusion.19
  495.2 10.4 %all-to-all-done.6 = bf16[32,32,896]{2,1,0:T(8,128)(2,1)S(1)} async-done(((bf16[32,32,896]{2,1,0:T(8,128)(2,1)}), bf16[32,32,896]{2,1,0:T(8,128)(2,1)S(1)}, u32[]{:S(2)}, u32[]{:S(2)}) %all-to-all-start.6) | async-done | bytes 1835040 | tf_op jit(solution)/shard_map/all_to_all | solution.py:805
  (298 shorter events, 108.2 us)
Async XLA Ops:
  7.3 47.4 %all-gather.13.cloned.1.call-start = ((), (), s32[]{:S(2)}) async-start(), calls=%async_computation.15 | async-start | bytes 3932160 | tf_op jit(solution)/shard_map/all_gather | solution.py:903
  11.9 29.2 %all-to-all-start = ((bf16[32,40,512]{2,1,0:T(8,128)(2,1)}), bf16[32,40,512]{2,1,0:T(8,128)(2,1)S(1)}, u32[]{:S(2)}, u32[]{:S(2)}) async-start(bf16[32,40,512]{2,1,0:T(8,128)(2,1)} %broadcast_in_dim.59), calls=%async_computation | async-start | bytes 2621440 | tf_op jit(solution)/shard_map/all_to_all | solution.py:805
  20.3 88.7 %all-gather.9.cloned.1.call-start = ((), (), s32[]{:S(2)}) async-start(), calls=%async_computation.10 | async-start | bytes 8650752 | tf_op jit(solution)/shard_map/all_gather | solution.py:935
  44.2 7.5 %collective-permute-start = (f32[2,512]{1,0:T(2,128)S(1)}, f32[2,512]{1,0:T(2,128)S(1)}, u32[]{:S(2)}, u32[]{:S(2)}) collective-permute-start(f32[2,512]{1,0:T(2,128)S(1)} %pad_maximum_fusion.10), channel_id=1, source_target_pairs={{0,2},{1,3},{2,0},{3,1},{4,6},{5,7},{6,4},{7,5},{8,10},{9,11},{10,... | collective-permute-start | bytes 12296 | tf_op jit(solution)/shard_map/ppermute | solution.py:815
  54.6 139.1 %all-gather.11.cloned.1.call-start = ((), (), s32[]{:S(2)}) async-start(), calls=%async_computation.11 | async-start | bytes 8650752 | tf_op jit(solution)/shard_map/all_gather | solution.py:942
  71.8 26.3 %collective-permute-start.3 = (bf16[1024,256]{1,0:T(8,128)(2,1)S(1)}, bf16[1024,256]{1,0:T(8,128)(2,1)S(1)}, u32[]{:S(2)}, u32[]{:S(2)}) collective-permute-start(bf16[1024,256]{1,0:T(8,128)(2,1)S(1)} %bitcast.113), channel_id=1, source_target_pairs={{0,1},{1,2},{2,3},{3,0},{4,5},{5,6},{6,7},{7,4},{8,9},{9,10},{10,1... | collective-permute-start | bytes 1572872 | tf_op jit(solution)/shard_map/ppermute | solution.py:815
  72.4 25.7 %collective-permute-start.4 = (bf16[1024,256]{1,0:T(8,128)(2,1)S(1)}, bf16[1024,256]{1,0:T(8,128)(2,1)S(1)}, u32[]{:S(2)}, u32[]{:S(2)}) collective-permute-start(bf16[1024,256]{1,0:T(8,128)(2,1)S(1)} %bitcast.114), channel_id=1, source_target_pairs={{0,2},{1,3},{2,0},{3,1},{4,6},{5,7},{6,4},{7,5},{8,10},{9,11},{10,... | collective-permute-start | bytes 1572872 | tf_op jit(solution)/shard_map/ppermute | solution.py:815
  74.2 24.5 %collective-permute-start.5 = (bf16[1024,256]{1,0:T(8,128)(2,1)S(1)}, bf16[1024,256]{1,0:T(8,128)(2,1)S(1)}, u32[]{:S(2)}, u32[]{:S(2)}) collective-permute-start(bf16[1024,256]{1,0:T(8,128)(2,1)S(1)} %bitcast.115), channel_id=1, source_target_pairs={{0,3},{1,0},{2,1},{3,2},{4,7},{5,4},{6,5},{7,6},{8,11},{9,8},{10,9... | collective-permute-start | bytes 1572872 | tf_op jit(solution)/shard_map/ppermute | solution.py:815
  137.5 5.8 %collective-permute-start.6 = (bf16[128,256]{1,0:T(8,128)(2,1)S(1)}, bf16[128,256]{1,0:T(8,128)(2,1)S(1)}, u32[]{:S(2)}, u32[]{:S(2)}) collective-permute-start(bf16[128,256]{1,0:T(8,128)(2,1)S(1)} %get-tuple-element.138), channel_id=1, source_target_pairs={{0,1},{1,2},{2,3},{3,0},{4,5},{5,6},{6,7},{7,4},{8,9},{9,10},{10,1... | collective-permute-start | bytes 196616 | tf_op jit(solution)/shard_map/ppermute | solution.py:834
  151.0 42.7 %all-to-all-start.2 = ((bf16[32,40,1024]{2,1,0:T(8,128)(2,1)}), bf16[32,40,1024]{2,1,0:T(8,128)(2,1)}, u32[]{:S(2)}, u32[]{:S(2)}) async-start(bf16[32,40,1024]{2,1,0:T(8,128)(2,1)} %bitcast.96), calls=%async_computation.2 | async-start | bytes 5242880 | tf_op jit(solution)/shard_map/all_to_all | solution.py:805
  155.8 96.9 %all-gather.15.cloned.1.call-start = ((), (), s32[]{:S(2)}) async-start(), calls=%async_computation.16 | async-start | bytes 2162688 | tf_op jit(solution)/shard_map/all_gather | solution.py:965
  202.3 44.2 %all-to-all-start.3 = ((bf16[32,40,1024]{2,1,0:T(8,128)(2,1)}), bf16[32,40,1024]{2,1,0:T(8,128)(2,1)}, u32[]{:S(2)}, u32[]{:S(2)}) async-start(bf16[32,40,1024]{2,1,0:T(8,128)(2,1)} %bitcast.108), calls=%async_computation.3 | async-start | bytes 5242880 | tf_op jit(solution)/shard_map/all_to_all | solution.py:805
  252.7 40.9 %all-to-all-start.4 = ((bf16[32,40,1024]{2,1,0:T(8,128)(2,1)}), bf16[32,40,1024]{2,1,0:T(8,128)(2,1)}, u32[]{:S(2)}, u32[]{:S(2)}) async-start(bf16[32,40,1024]{2,1,0:T(8,128)(2,1)} %bitcast.109), calls=%async_computation.4 | async-start | bytes 5242880 | tf_op jit(solution)/shard_map/all_to_all | solution.py:805
  257.5 53.9 %collective-permute-start.10 = (bf16[1024,512]{1,0:T(8,128)(2,1)}, bf16[1024,512]{1,0:T(8,128)(2,1)}, u32[]{:S(2)}, u32[]{:S(2)}) collective-permute-start(bf16[1024,512]{1,0:T(8,128)(2,1)} %bitcast.100), channel_id=1, source_target_pairs={{0,2},{1,3},{2,0},{3,1},{4,6},{5,7},{6,4},{7,5},{8,10},{9,11},{10,... | collective-permute-start | bytes 3145736 | tf_op jit(solution)/shard_map/ppermute | solution.py:815
  260.5 51.0 %collective-permute-start.11 = (bf16[1024,512]{1,0:T(8,128)(2,1)}, bf16[1024,512]{1,0:T(8,128)(2,1)}, u32[]{:S(2)}, u32[]{:S(2)}) collective-permute-start(bf16[1024,512]{1,0:T(8,128)(2,1)} %bitcast.101), channel_id=1, source_target_pairs={{0,3},{1,0},{2,1},{3,2},{4,7},{5,4},{6,5},{7,6},{8,11},{9,8},{10,9... | collective-permute-start | bytes 3145736 | tf_op jit(solution)/shard_map/ppermute | solution.py:815
  261.6 49.8 %collective-permute-start.9 = (bf16[1024,512]{1,0:T(8,128)(2,1)}, bf16[1024,512]{1,0:T(8,128)(2,1)}, u32[]{:S(2)}, u32[]{:S(2)}) collective-permute-start(bf16[1024,512]{1,0:T(8,128)(2,1)} %bitcast.102), channel_id=1, source_target_pairs={{0,1},{1,2},{2,3},{3,0},{4,5},{5,6},{6,7},{7,4},{8,9},{9,10},{10,1... | collective-permute-start | bytes 3145736 | tf_op jit(solution)/shard_map/ppermute | solution.py:815
  306.4 40.9 %all-to-all-start.5 = ((bf16[32,40,1024]{2,1,0:T(8,128)(2,1)}), bf16[32,40,1024]{2,1,0:T(8,128)(2,1)}, u32[]{:S(2)}, u32[]{:S(2)}) async-start(bf16[32,40,1024]{2,1,0:T(8,128)(2,1)} %bitcast.107), calls=%async_computation.5 | async-start | bytes 5242880 | tf_op jit(solution)/shard_map/all_to_all | solution.py:805
  311.2 102.6 %all-gather.17.cloned.1.call-start = ((), (), s32[]{:S(2)}) async-start(), calls=%async_computation.17 | async-start | bytes 9461760 | tf_op jit(solution)/shard_map/all_gather | solution.py:1055
  355.3 5.8 %collective-permute-start.13 = (bf16[128,256]{1,0:T(8,128)(2,1)S(1)}, bf16[128,256]{1,0:T(8,128)(2,1)S(1)}, u32[]{:S(2)}, u32[]{:S(2)}) collective-permute-start(bf16[128,256]{1,0:T(8,128)(2,1)S(1)} %get-tuple-element.133), channel_id=1, source_target_pairs={{0,2},{1,3},{2,0},{3,1},{4,6},{5,7},{6,4},{7,5},{8,10},{9,11},{10,... | collective-permute-start | bytes 196616 | tf_op jit(solution)/shard_map/ppermute | solution.py:1039
  363.1 152.5 %reduce-scatter.8.cloned.1.call-start = ((), (), s32[]{:S(2)}) async-start(), calls=%async_computation.14 | async-start | bytes 2621440 | tf_op jit(solution)/shard_map/reduce_scatter | solution.py:1071
  363.2 49.5 %collective-permute-start.15 = (bf16[128,1024]{1,0:T(8,128)(2,1)S(1)}, bf16[128,1024]{1,0:T(8,128)(2,1)S(1)}, u32[]{:S(2)}, u32[]{:S(2)}) collective-permute-start(bf16[128,1024]{1,0:T(8,128)(2,1)S(1)} %get-tuple-element.118), channel_id=1, source_target_pairs={{0,1},{1,2},{2,3},{3,0},{4,5},{5,6},{6,7},{7,4},{8,9},{9,10},{10,1... | collective-permute-start | bytes 786440 | tf_op jit(solution)/shard_map/ppermute | solution.py:815
  363.3 49.8 %collective-permute-start.17 = (bf16[128,1024]{1,0:T(8,128)(2,1)S(1)}, bf16[128,1024]{1,0:T(8,128)(2,1)S(1)}, u32[]{:S(2)}, u32[]{:S(2)}) collective-permute-start(bf16[128,1024]{1,0:T(8,128)(2,1)S(1)} %get-tuple-element.118), channel_id=1, source_target_pairs={{0,3},{1,0},{2,1},{3,2},{4,7},{5,4},{6,5},{7,6},{8,11},{9,8},{10,9... | collective-permute-start | bytes 786440 | tf_op jit(solution)/shard_map/ppermute | solution.py:815
  366.5 46.9 %collective-permute-start.16 = (bf16[128,1024]{1,0:T(8,128)(2,1)S(1)}, bf16[128,1024]{1,0:T(8,128)(2,1)S(1)}, u32[]{:S(2)}, u32[]{:S(2)}) collective-permute-start(bf16[128,1024]{1,0:T(8,128)(2,1)S(1)} %get-tuple-element.118), channel_id=1, source_target_pairs={{0,2},{1,3},{2,0},{3,1},{4,6},{5,7},{6,4},{7,5},{8,10},{9,11},{10,... | collective-permute-start | bytes 786440 | tf_op jit(solution)/shard_map/ppermute | solution.py:815
  413.8 101.8 %reduce-scatter.4.cloned.1.call-start = ((), (), s32[]{:S(2)}) async-start(), calls=%async_computation.12 | async-start | bytes 2621440 | tf_op jit(solution)/shard_map/reduce_scatter | solution.py:1069
  414.5 101.0 %reduce-scatter.6.cloned.1.call-start = ((), (), s32[]{:S(2)}) async-start(), calls=%async_computation.13 | async-start | bytes 2621440 | tf_op jit(solution)/shard_map/reduce_scatter | solution.py:1070
  448.9 6.9 %collective-permute-start.18 = (f32[32,128]{1,0:T(8,128)S(1)}, f32[32,128]{1,0:T(8,128)S(1)}, u32[]{:S(2)}, u32[]{:S(2)}) collective-permute-start(f32[32,128]{1,0:T(8,128)S(1)} %bitcast.138), channel_id=1, source_target_pairs={{0,2},{1,3},{2,0},{3,1},{4,6},{5,7},{6,4},{7,5},{8,10},{9,11},{10,... | collective-permute-start | bytes 49160 | tf_op jit(solution)/shard_map/ppermute | solution.py:815
  463.7 41.9 %all-to-all-start.6 = ((bf16[32,32,896]{2,1,0:T(8,128)(2,1)}), bf16[32,32,896]{2,1,0:T(8,128)(2,1)S(1)}, u32[]{:S(2)}, u32[]{:S(2)}) async-start(bf16[32,32,896]{2,1,0:T(8,128)(2,1)} %fusion.4), calls=%async_computation.6 | async-start | bytes 3670016 | tf_op jit(solution)/shard_map/all_to_all | solution.py:805
  478.8 7.2 %collective-permute-start.21 = (bf16[128,512]{1,0:T(8,128)(2,1)S(1)}, bf16[128,512]{1,0:T(8,128)(2,1)S(1)}, u32[]{:S(2)}, u32[]{:S(2)}) collective-permute-start(bf16[128,512]{1,0:T(8,128)(2,1)S(1)} %get-tuple-element.128), channel_id=1, source_target_pairs={{0,1},{1,2},{2,3},{3,0},{4,5},{5,6},{6,7},{7,4},{8,9},{9,10},{10,1... | collective-permute-start | bytes 393224 | tf_op jit(solution)/shard_map/ppermute | solution.py:834
  478.9 11.2 %collective-permute-start.22 = (bf16[128,512]{1,0:T(8,128)(2,1)S(1)}, bf16[128,512]{1,0:T(8,128)(2,1)}, u32[]{:S(2)}, u32[]{:S(2)}) collective-permute-start(bf16[128,512]{1,0:T(8,128)(2,1)S(1)} %get-tuple-element.127), channel_id=1, source_target_pairs={{0,2},{1,3},{2,0},{3,1},{4,6},{5,7},{6,4},{7,5},{8,10},{9,11},{10,... | collective-permute-start | bytes 393224 | tf_op jit(solution)/shard_map/ppermute | solution.py:834
  483.5 6.6 %collective-permute-start.23 = (bf16[128,512]{1,0:T(8,128)(2,1)S(1)}, bf16[128,512]{1,0:T(8,128)(2,1)}, u32[]{:S(2)}, u32[]{:S(2)}) collective-permute-start(bf16[128,512]{1,0:T(8,128)(2,1)S(1)} %get-tuple-element.129), channel_id=1, source_target_pairs={{0,3},{1,0},{2,1},{3,2},{4,7},{5,4},{6,5},{7,6},{8,11},{9,8},{10,9... | collective-permute-start | bytes 393224 | tf_op jit(solution)/shard_map/ppermute | solution.py:834
  507.4 7.5 %collective-permute-start.24 = (f32[32]{0:T(128)S(1)}, f32[32]{0:T(128)S(1)}, u32[]{:S(2)}, u32[]{:S(2)}) collective-permute-start(f32[32]{0:T(128)S(1)} %add_add_fusion.2), channel_id=1, source_target_pairs={{0,2},{1,3},{2,0},{3,1},{4,6},{5,7},{6,4},{7,5},{8,10},{9,11},{10,... | collective-permute-start | bytes 392 | tf_op jit(solution)/shard_map/ppermute | solution.py:815
  508.9 6.0 %collective-permute-start.25 = (f32[32]{0:T(128)S(1)}, f32[32]{0:T(128)S(1)}, u32[]{:S(2)}, u32[]{:S(2)}) collective-permute-start(f32[32]{0:T(128)S(1)} %add_add_fusion.2), channel_id=1, source_target_pairs={{0,1},{1,2},{2,3},{3,0},{4,5},{5,6},{6,7},{7,4},{8,9},{9,10},{10,1... | collective-permute-start | bytes 392 | tf_op jit(solution)/shard_map/ppermute | solution.py:815
  (56 other events, 599.0 us)
Sparse Core Ops, SparseCore 0:
  10.6 42.2 all-gather.12
  55.7 53.2 all-gather.8
  111.8 68.0 all-gather.10
  182.6 62.6 all-gather.14
  363.2 49.7 all-gather.16
  415.8 29.1 reduce-scatter.7
  448.1 29.7 reduce-scatter.3
  480.9 29.5 reduce-scatter.5
